TPU v7x, 32 devices: a whole 2x2x4 slice. The times are simulated.
32 devices in a mesh: dp: 4 (over y, x), ctx: 8 (over z, core).
Axes of the slice: x: 2, y: 2, z: 4, core: 2. Of those that a mesh axis runs over, the one named last changes fastest.
Arguments:
- tokens: bfloat16 [4, 1024, 4096], P('dp', 'ctx'), may hold values from -6 to 6
- grad_attn: bfloat16 [4, 1024, 1024], P('dp', 'ctx'), may hold values from -6 to 6
- w_packed: bfloat16 [10240, 128], P('ctx'), may hold values from -0.1875 to 0.1875
- block_rows: int32 [10, 8], replicated, may hold values from 0 to 31, as said below
- span_pairs: int32 [8, 2], replicated, may hold values from 0 to 15, as said below
Outputs:
- grad_tokens: bfloat16 [4, 1024, 4096], P('dp', 'ctx')
- grad_weights: float32 [10240, 128], P('ctx')
Inputs may be any that keep to these rules, and one draw needn't show every extreme that they name: `block_rows`: row c lists the 8 row blocks in which column block c is nonzero, all different; rows 0 to 3 together list each of the 32 row blocks exactly once. Index k of ctx holds spans span_pairs[k, 0] and span_pairs[k, 1] = 15 - span_pairs[k, 0]; the first column takes each of 0 to 7 once.
All inputs are finite; a program needn't handle non-finite values.
Results may differ from a plain program's by a relative error of at most 0.0087.
Values may be sent and summed in bfloat16 or wider, within the bound.
No kernel may reach another device: no remote copies, remote signals or barrier semaphores. Data moves between devices by JAX's collectives and lax.ppermute only.
A program may use at most 64 MiB of HBM per device.

v0:
```python
import math

import jax
import jax.numpy as jnp
from jax import lax
from jax.sharding import PartitionSpec as P

D = 4096
HD = 128
BLK = 128
QPG = 8
GROUPS = 1
SPAN = 64
NRB = 32
NBR = 8
NCB = 10
NNZ = 80


EPSILON = 1e-06


def norm_forward(values):
    factor = lax.rsqrt(jnp.mean(values * values, axis=-1, keepdims=True) + EPSILON)
    return (values * factor, factor)


def norm_backward(values, factor, upstream):
    return factor * upstream - values * (factor * factor * factor) * jnp.mean(
        upstream * values, axis=-1, keepdims=True
    )


def span_part(array, which):
    return array[which * SPAN : (which + 1) * SPAN]


def positions_of(span_ids):
    return (span_ids[:, None] * SPAN + jnp.arange(SPAN, dtype=jnp.int32)[None, :]).reshape(-1)


def masked_scores(query_part, query_pos, key_part, key_pos):
    raw_scores = jnp.einsum(
        "tgqd,ugd->tgqu", query_part, key_part, preferred_element_type=jnp.float32
    ) / math.sqrt(HD)
    keep = key_pos[None, None, None, :] <= query_pos[:, None, None, None]
    return jnp.where(keep, jnp.exp(raw_scores), 0.0)


def forward_tile(query_part, query_pos, key_part, value_part, key_pos):
    exp_scores = masked_scores(query_part, query_pos, key_part, key_pos)
    weighted = jnp.einsum(
        "tgqu,ugd->tgqd",
        exp_scores.astype(jnp.bfloat16),
        value_part,
        preferred_element_type=jnp.float32,
    )
    return (jnp.sum(exp_scores, axis=-1), weighted)


def backward_tile(
    query_part, upstream_part, total_part, delta_part, query_pos, key_part, value_part, key_pos
):
    exp_scores = masked_scores(query_part, query_pos, key_part, key_pos)
    prob = exp_scores / total_part[..., None]
    dprob = jnp.einsum(
        "tgqd,ugd->tgqu", upstream_part, value_part, preferred_element_type=jnp.float32
    )
    dscore = (prob * (dprob - delta_part[..., None]) / math.sqrt(HD)).astype(jnp.bfloat16)
    part_query = jnp.einsum("tgqu,ugd->tgqd", dscore, key_part, preferred_element_type=jnp.float32)
    part_key = jnp.einsum("tgqu,tgqd->ugd", dscore, query_part, preferred_element_type=jnp.float32)
    part_value = jnp.einsum(
        "tgqu,tgqd->ugd",
        prob.astype(jnp.bfloat16),
        upstream_part,
        preferred_element_type=jnp.float32,
    )
    return (part_query, part_key, part_value)


def empty_forward():
    return (
        jnp.zeros((SPAN, GROUPS, QPG), jnp.float32),
        jnp.zeros((SPAN, GROUPS, QPG, HD), jnp.float32),
    )


def per_device(tokens, grad_attn, w_packed, block_rows, span_pairs):
    ndevices = lax.axis_size("ctx")
    my_index = lax.axis_index("ctx")
    tok_count = tokens.shape[1]
    nquery = GROUPS * QPG
    weights = lax.all_gather(w_packed, "ctx", axis=0, tiled=True).reshape(NCB, NBR, BLK, BLK)
    flat_ids = block_rows.reshape(-1)
    selected = jnp.take(tokens[0].reshape(tok_count, NRB, BLK), flat_ids, axis=1).reshape(
        tok_count, NCB, NBR, BLK
    )
    projected = jnp.einsum(
        "tcri,crio->tco", selected, weights, preferred_element_type=jnp.float32
    ).astype(jnp.bfloat16)
    query_raw = projected[:, :nquery].astype(jnp.float32).reshape(tok_count, GROUPS, QPG, HD)
    key_raw = projected[:, nquery : nquery + GROUPS].astype(jnp.float32)
    values = projected[:, nquery + GROUPS :]
    query_norm, query_factor = norm_forward(query_raw)
    key_norm, key_factor = norm_forward(key_raw)
    query_hat = query_norm.astype(jnp.bfloat16)
    key_hat = key_norm.astype(jnp.bfloat16)
    upstream = grad_attn[0].reshape(tok_count, GROUPS, QPG, HD)
    my_pair = span_pairs[my_index]
    query_pos = positions_of(my_pair)
    zero_rows, zero_out = empty_forward()
    gathered_keys, gathered_values = (
        lax.all_gather(key_hat, "ctx", axis=0, tiled=True),
        lax.all_gather(values, "ctx", axis=0, tiled=True),
    )
    all_positions = positions_of(span_pairs.reshape(-1))
    length = all_positions.shape[0]
    inverse = (
        jnp.zeros((length,), jnp.int32).at[all_positions].set(jnp.arange(length, dtype=jnp.int32))
    )
    sorted_keys = jnp.take(gathered_keys, inverse, axis=0)
    sorted_values = jnp.take(gathered_values, inverse, axis=0)
    key_block = math.gcd(512, length)
    total_parts = []
    weighted_parts = []
    for row_part in range(2):
        query_part = span_part(query_hat, row_part)
        pos_part = span_part(query_pos, row_part)
        block_count = ((my_pair[row_part] + 1) * SPAN + key_block - 1) // key_block

        def forward_loop(block_index, loop_state):
            first_row = block_index * key_block
            key_piece = lax.dynamic_slice_in_dim(sorted_keys, first_row, key_block, 0)
            value_piece = lax.dynamic_slice_in_dim(sorted_values, first_row, key_block, 0)
            key_pos = first_row + jnp.arange(key_block, dtype=jnp.int32)
            part_total, part_weighted = forward_tile(
                query_part, pos_part, key_piece, value_piece, key_pos
            )
            return (loop_state[0] + part_total, loop_state[1] + part_weighted)

        total_part, weighted_part = lax.fori_loop(
            0, block_count, forward_loop, (zero_rows, zero_out)
        )
        total_parts.append(total_part)
        weighted_parts.append(weighted_part)
    totals = jnp.concatenate(total_parts, axis=0)
    weighted = jnp.concatenate(weighted_parts, axis=0)
    attn_out = weighted / totals[..., None]
    deltas = jnp.sum(upstream.astype(jnp.float32) * attn_out, axis=-1)
    grad_keys_all = jnp.zeros((length, GROUPS, HD), jnp.float32)
    grad_values_all = jnp.zeros((length, GROUPS, HD), jnp.float32)
    query_parts = []
    for row_part in range(2):
        query_part = span_part(query_hat, row_part)
        upstream_part = span_part(upstream, row_part)
        total_part = span_part(totals, row_part)
        delta_part = span_part(deltas, row_part)
        pos_part = span_part(query_pos, row_part)
        block_count = ((my_pair[row_part] + 1) * SPAN + key_block - 1) // key_block

        def backward_loop(block_index, loop_state):
            grad_part, keys_acc, values_acc = loop_state
            first_row = block_index * key_block
            key_piece = lax.dynamic_slice_in_dim(sorted_keys, first_row, key_block, 0)
            value_piece = lax.dynamic_slice_in_dim(sorted_values, first_row, key_block, 0)
            key_pos = first_row + jnp.arange(key_block, dtype=jnp.int32)
            part_query, part_key, part_value = backward_tile(
                query_part,
                upstream_part,
                total_part,
                delta_part,
                pos_part,
                key_piece,
                value_piece,
                key_pos,
            )
            keys_acc = lax.dynamic_update_slice_in_dim(
                keys_acc,
                lax.dynamic_slice_in_dim(keys_acc, first_row, key_block, 0) + part_key,
                first_row,
                0,
            )
            values_acc = lax.dynamic_update_slice_in_dim(
                values_acc,
                lax.dynamic_slice_in_dim(values_acc, first_row, key_block, 0) + part_value,
                first_row,
                0,
            )
            return (grad_part + part_query, keys_acc, values_acc)

        grad_part, grad_keys_all, grad_values_all = lax.fori_loop(
            0, block_count, backward_loop, (zero_out, grad_keys_all, grad_values_all)
        )
        query_parts.append(grad_part)
    grad_query_hat = jnp.concatenate(query_parts, axis=0)
    owner_keys = jnp.take(grad_keys_all, all_positions, axis=0)
    owner_values = jnp.take(grad_values_all, all_positions, axis=0)
    grad_key_hat, grad_value = (
        lax.psum_scatter(owner_keys, "ctx", scatter_dimension=0, tiled=True),
        lax.psum_scatter(owner_values, "ctx", scatter_dimension=0, tiled=True),
    )
    grad_query = norm_backward(query_raw, query_factor, grad_query_hat).astype(jnp.bfloat16)
    grad_key = norm_backward(key_raw, key_factor, grad_key_hat).astype(jnp.bfloat16)
    grad_proj = jnp.concatenate(
        [grad_query.reshape(tok_count, nquery, HD), grad_key, grad_value.astype(jnp.bfloat16)],
        axis=1,
    )
    partial_w = jnp.einsum(
        "tcri,tco->crio", selected, grad_proj, preferred_element_type=jnp.float32
    ).astype(jnp.bfloat16)
    partial_w = partial_w.reshape(ndevices, NNZ * BLK // ndevices, BLK)
    received = lax.all_to_all(partial_w, "ctx", split_axis=0, concat_axis=0, tiled=True)
    summed = jnp.sum(received.astype(jnp.float32), axis=0)
    grad_weights = lax.psum(summed, "dp")
    placement = (block_rows[:, :, None] == jnp.arange(NRB, dtype=jnp.int32)[None, None, :]).astype(
        jnp.bfloat16
    )
    dense_weights = jnp.einsum(
        "crb,crio->cbio", placement, weights, preferred_element_type=jnp.float32
    ).astype(jnp.bfloat16)
    grad_tokens = jnp.einsum(
        "tco,cbio->tbi", grad_proj, dense_weights, preferred_element_type=jnp.float32
    )
    grad_tokens = grad_tokens.reshape(1, tok_count, D).astype(jnp.bfloat16)
    return (grad_tokens, grad_weights)


def solution(mesh):
    in_specs = (P("dp", "ctx", None), P("dp", "ctx", None), P("ctx", None), P(), P())
    out_specs = (P("dp", "ctx", None), P("ctx", None))
    return jax.shard_map(
        per_device, mesh=mesh, in_specs=in_specs, out_specs=out_specs, check_vma=False
    )
```

profile of v0, /device:TPU:0, one launch (start us, length us, event | category | flops | bytes accessed | tf_op | source)
XLA Modules:
  0.0 289.5 jit_solution(10172293427109092486)
XLA Ops:
  7.2 0.7 all-gather.2.cloned.1.call-update
  8.0 0.9 multiply_reduce_fusion
  8.8 0.5 fusion.129
  10.6 0.7 broadcast_multiply_fusion.1
  11.7 0.8 copy.28
  12.4 0.7 compare_and_fusion.2
  13.3 1.8 copy.33
  15.1 1.0 slice_bitcast_fusion.2
  16.2 0.7 copy.27
  16.9 0.7 copy.29
  17.6 2.6 gather_fusion
  20.1 4.5 %copy.30 = bf16[128,10,8,128]{0,3,2,1:T(8,128)(2,1)} copy(bf16[128,10,8,128]{3,0,2,1:T(8,128)(2,1)} %bitcast.434) | data formatting | bytes 5242880 | tf_op jit(solution)/shard_map/jit(_take)/gather | solution.py:95
  24.7 4.3 %scatter_custom_fusion = s32[1024]{0:T(1024)S(1)} fusion(s32[1024]{0:T(1024)S(1)} %bitcast.447, s32[1024]{0:T(1024)S(1)} %iota.33, s32[]{:T(128)} %constant.141.clone.1), kind=kCustom, calls=%fused_computation.186 | custom fusion | bytes 4100 | tf_op jit(solution)/shard_map/scatter | solution.py:119
  29.1 17.1 %all-gather.2.cloned.1.call-done = bf16[10240,128]{1,0:T(8,128)(2,1)} async-done(((bf16[1280,128]{1,0:T(8,128)(2,1)}), bf16[10240,128]{1,0:T(8,128)(2,1)}) %all-gather.2.cloned.1.call-update) | async-done | bytes 2621456 | tf_op jit(solution)/shard_map/all_gather | solution.py:93
  46.3 3.6 %fusion.98 = bf16[128,10,128]{2,0,1:T(8,128)(2,1)S(1)} fusion(bf16[10,8,128,128]{3,2,1,0:T(8,128)(2,1)} %bitcast.435, bf16[128,10,8,128]{0,3,2,1:T(8,128)(2,1)} %copy.30, pred[10,8]{1,0:T(8,128)(4,1)S(1)} %copy.26), kind=kOutput, calls=%fused_computation.130 | convolution fusion | flops 337018880 | bytes 5570640 | tf_op jit(solution)/shard_map/tcri,crio->tco/dot_general | solution.py:98
  50.3 14.2 %all_gather.11 = bf16[1024,1,128]{2,0,1:T(8,128)(2,1)S(1)} all-gather(bf16[128,1,128]{2,0,1:T(8,128)(2,1)S(1)} %slice.105), channel_id=1, replica_groups=mesh['dp'=4,'ctx'=8] {'ctx'}, dimensions={0}, use_global_device_ids=true | all-gather | bytes 294912 | tf_op jit(solution)/shard_map/all_gather | solution.py:114
  64.5 14.3 %all_gather.10 = bf16[1024,1,128]{2,0,1:T(8,128)(2,1)S(1)} all-gather(bf16[128,1,128]{2,0,1:T(8,128)(2,1)S(1)} %fusion.110), channel_id=1, replica_groups=mesh['dp'=4,'ctx'=8] {'ctx'}, dimensions={0}, use_global_device_ids=true | all-gather | bytes 294912 | tf_op jit(solution)/shard_map/all_gather | solution.py:113
  78.8 3.2 %gather_fusion.2 = bf16[1024,128]{1,0:T(8,128)(2,1)S(1)} fusion(bf16[1024,128]{1,0:T(8,128)(2,1)S(1)} %bitcast.429, s32[1024]{0:T(1024)S(1)} %fusion.118), kind=kCustom, calls=%fused_computation.2.clone | custom fusion | bytes 528384 | tf_op jit(solution)/shard_map/jit(_take)/gather | solution.py:122
  82.0 3.2 %gather_fusion.1 = bf16[1024,128]{1,0:T(8,128)(2,1)S(1)} fusion(bf16[1024,128]{1,0:T(8,128)(2,1)S(1)} %bitcast.428, s32[1024]{0:T(1024)S(1)} %fusion.118), kind=kCustom, calls=%fused_computation.clone | custom fusion | bytes 528384 | tf_op jit(solution)/shard_map/jit(_take)/gather | solution.py:121
  85.7 1.8 while.53
  85.8 0.5 fusion.179
  86.3 0.3 fusion.180
  86.7 0.5 fusion.179
  87.2 0.3 fusion.180
  87.6 0.9 while.52
  87.7 0.5 fusion.175
  88.2 0.3 fusion.176
  89.4 1.9 while.54
  89.6 0.4 fusion.191
  90.0 0.3 fusion.192
  90.3 0.4 fusion.195
  90.6 0.3 fusion.193
  91.0 0.3 fusion.194
  91.3 3.8 %while.55 = (s32[]{:T(128)}, f32[64,1,8,128]{3,0,2,1:T(8,128)S(1)}, f32[1024,1,128]{2,0,1:T(8,128)S(1)}, f32[1024,1,128]{2,0,1:T(8,128)S(1)}, s32[]{:T(128)}, /*...) while((s32[]{:T(128)}, f32[64,1,8,128]{3,0,2,1:T(8,128)S(1)}, ...), condition=%wide.region_13.15_spmd, body=%wide.region_12.14_spmd.sunk | while | flops 337871360 | bytes 7287259 | solution.py:191
  91.5 0.4 fusion.206
  91.9 0.3 fusion.207
  92.2 0.4 fusion.210
  92.6 0.3 fusion.208
  92.9 0.3 fusion.209
  93.4 0.4 fusion.206
  93.8 0.3 fusion.207
  94.1 0.4 fusion.210
  94.4 0.3 fusion.208
  94.8 0.4 fusion.209
  95.1 2.8 gather_fusion.4
  97.9 2.8 gather_fusion.3
  100.8 1.2 bitcast_select_fusion.1
  101.9 0.2 reduce-scatter.5.cloned.1.call-start
  102.2 0.5 reduce-scatter.5.cloned.1.call-update
  102.9 0.5 fusion.103
  103.4 28.6 %reduce-scatter.3.cloned.1.call-done = f32[128,1,128]{2,0,1:T(8,128)} async-done(((f32[1024,1,128]{2,0,1:T(8,128)}), f32[128,1,128]{2,0,1:T(8,128)}) %reduce-scatter.3.cloned.1.call-update) | async-done | bytes 65552 | tf_op jit(solution)/shard_map/reduce_scatter | solution.py:199
  132.0 0.9 fusion.114
  133.0 31.2 %reduce-scatter.5.cloned.1.call-done = f32[128,1,128]{2,0,1:T(8,128)} async-done(((f32[1024,1,128]{2,0,1:T(8,128)}), f32[128,1,128]{2,0,1:T(8,128)}) %reduce-scatter.5.cloned.1.call-update) | async-done | bytes 65552 | tf_op jit(solution)/shard_map/reduce_scatter | solution.py:200
  164.1 0.8 convert_element_type.99
  165.0 1.0 fusion.113
  165.9 4.1 %fusion.91 = bf16[10,8,128,128]{3,2,1,0:T(8,128)(2,1)} fusion(bf16[128,10,8,128]{0,3,2,1:T(8,128)(2,1)} %copy.30, pred[10,8]{1,0:T(8,128)(4,1)S(1)} %copy.26, bf16[128,1,128]{2,0,1:T(8,128)(2,1)S(1)} %convert_element_type.99, bf16[128,1,128]{2,0,1:T(8,128)(2,1)S(1)} %fusion.113, bf16[128,8,128]{2,0,1:T(8,128)(2,1)S(1)} %fusion.103), kind=kOutput, calls=%fused_computation.125 | convolution fusion | flops 338493440 | bytes 5570640 | tf_op jit(solution)/shard_map/tcri,tco->crio/dot_general | solution.py:208
  170.0 3.6 %all-to-all-start = ((bf16[8,1280,128]{2,1,0:T(8,128)(2,1)}), bf16[8,1280,128]{2,1,0:T(8,128)(2,1)S(1)}, u32[]{:S(2)}, u32[]{:S(2)}) async-start(bf16[8,1280,128]{2,1,0:T(8,128)(2,1)} %bitcast.438), calls=%async_computation.2 | async-start | bytes 5242880 | tf_op jit(solution)/shard_map/all_to_all | solution.py:212
  173.7 7.0 %convolution_convert_fusion = bf16[10,32,128,128]{3,1,2,0:T(8,128)(2,1)} fusion(bf16[10,8,128,128]{3,2,1,0:T(8,128)(2,1)} %bitcast.436, s32[10,8]{1,0:T(8,128)S(1)} %copy.28), kind=kOutput, calls=%fused_computation.118 | convolution fusion | flops 89131520 | bytes 13107520 | tf_op jit(solution)/shard_map/crb,crio->cbio/dot_general | solution.py:218
  180.7 53.2 %all-to-all-done = bf16[8,1280,128]{2,1,0:T(8,128)(2,1)S(1)} async-done(((bf16[8,1280,128]{2,1,0:T(8,128)(2,1)}), bf16[8,1280,128]{2,1,0:T(8,128)(2,1)S(1)}, u32[]{:S(2)}, u32[]{:S(2)}) %all-to-all-start) | async-done | bytes 2621472 | tf_op jit(solution)/shard_map/all_to_all | solution.py:212
  233.9 1.2 convert_reduce_fusion
  235.1 12.2 %bitcast_convert_fusion = bf16[128,32,128]{0,2,1:T(8,128)(2,1)S(1)} fusion(bf16[10,32,128,128]{3,1,2,0:T(8,128)(2,1)} %convolution_convert_fusion, bf16[128,1,128]{2,0,1:T(8,128)(2,1)S(1)} %convert_element_type.99, bf16[128,1,128]{2,0,1:T(8,128)(2,1)S(1)} %fusion.113, bf16[128,8,128]{2,0,1:T(8,128)(2,1)S(1)} %fusion.103), kind=kOutput, calls=%fused_computation.124 | convolution fusion | flops 1343684608 | bytes 11862016 | tf_op jit(solution)/shard_map/tco,cbio->tbi/dot_general | solution.py:221
  247.3 1.3 copy.41
  248.7 32.4 %all-reduce.2.cloned.1.call-done = f32[1280,128]{1,0:T(8,128)} async-done(((f32[1280,128]{1,0:T(8,128)}), f32[1280,128]{1,0:T(8,128)}) %all-reduce.2.cloned.1.call-update) | async-done | bytes 655376 | tf_op jit(solution)/shard_map/psum | solution.py:214
  281.0 2.0 copy.102
  (70 shorter events, 3.5 us)
Async XLA Ops:
  7.2 9.0 %copy-start.1 = (bf16[1,128,4096]{2,1,0:T(8,128)(2,1)S(1)}, bf16[1,128,4096]{2,1,0:T(8,128)(2,1)}, u32[]{:S(2)}) copy-start(bf16[1,128,4096]{2,1,0:T(8,128)(2,1)} %param.17) | copy-start | bytes 3145732
  7.2 39.1 %all-gather.2.cloned.1.call-start = ((), (), s32[]{:S(2)}) async-start(), calls=%async_computation.3 | async-start | bytes 2949120 | tf_op jit(solution)/shard_map/all_gather | solution.py:93
  7.9 124.1 %reduce-scatter.3.cloned.1.call-start = ((), (), s32[]{:S(2)}) async-start(), calls=%async_computation.4 | async-start | bytes 589824 | tf_op jit(solution)/shard_map/reduce_scatter | solution.py:199
  87.6 1.4 copy-start
  101.9 62.2 %reduce-scatter.5.cloned.1.call-start = ((), (), s32[]{:S(2)}) async-start(), calls=%async_computation.5 | async-start | bytes 589824 | tf_op jit(solution)/shard_map/reduce_scatter | solution.py:200
  170.0 63.9 %all-to-all-start = ((bf16[8,1280,128]{2,1,0:T(8,128)(2,1)}), bf16[8,1280,128]{2,1,0:T(8,128)(2,1)S(1)}, u32[]{:S(2)}, u32[]{:S(2)}) async-start(bf16[8,1280,128]{2,1,0:T(8,128)(2,1)} %bitcast.438), calls=%async_computation.2 | async-start | bytes 5242880 | tf_op jit(solution)/shard_map/all_to_all | solution.py:212
  173.7 107.4 %all-reduce.2.cloned.1.call-start = ((), (), s32[]{:S(2)}) async-start(), calls=%async_computation.6 | async-start | bytes 1310720 | tf_op jit(solution)/shard_map/psum | solution.py:214
Sparse Core Ops, SparseCore 0:
  9.6 36.5 all-gather.1
  102.1 29.8 reduce-scatter.2
  134.9 29.1 reduce-scatter.4
  235.2 45.7 all-reduce.1
where the time goes:
time: 290 us
  waiting for transfers between devices  164 us (57%)
  matrix products  34.4 us (12%)
  local copies, waits for them, and re-layouts  33.3 us (11%)
  blocking collectives  28.5 us (10%)
  between operations  15.4 us (5%)
  other arithmetic  9.92 us (3%)
  starting transfers between devices  3.97 us (1%)
    all_to_all x1, waiting for transfers between devices, per_device(): lax.all_to_all(partial_w, 'ctx', split_axis=0, concat_axis=0, tiled=True)  53.2 us
    psum x1, waiting for transfers between devices, per_device(): grad_weights = lax.psum(summed, 'dp')  32.4 us
    reduce_scatter x1, waiting for transfers between devices, per_device(): lax.psum_scatter(owner_values, 'ctx', scatter_dimension=0, tiled=True)  31.2 us
    reduce_scatter x1, waiting for transfers between devices, per_device(): lax.psum_scatter(owner_keys, 'ctx', scatter_dimension=0, tiled=True)  28.6 us
    all_gather x1, waiting for transfers between devices, per_device(): lax.all_gather(w_packed, 'ctx', axis=0, tiled=True)  17.1 us
    all_gather x1, blocking collectives, per_device(): lax.all_gather(key_hat, 'ctx', axis=0, tiled=True)  14.3 us
    all_gather x1, blocking collectives, per_device(): lax.all_gather(values, 'ctx', axis=0, tiled=True)  14.2 us
    dot_general x1, matrix products, per_device(): jnp.einsum('tco,cbio->tbi', grad_proj, dense_weights, preferred_element_t...  12.2 us
  transfers between devices with their start and end apart: 5, of which 5 were waited for; matrix products, arithmetic and copies ran while one was open for 14% of the time, Pallas kernels for 0%

commit v1 on v0

v1 whole, which is shorter than its diff:
```python
import functools
import math

import jax
import jax.numpy as jnp
from jax import lax
from jax.experimental import pallas as pl
from jax.experimental.pallas import tpu as pltpu
from jax.sharding import PartitionSpec as P

HD = 128
BLK = 128
QPG = 8
GROUPS = 1
SPAN = 64
NBR = 8
NCB = 10
NNZ = 80
NQ = GROUPS * QPG
KEYS = 128
EPSILON = 1e-06
SCALE = 1.0 / math.sqrt(HD)
LOG2E = math.log2(math.e)

F32 = jnp.float32
BF16 = jnp.bfloat16
VMEM = pl.BlockSpec(memory_space=pltpu.VMEM)
SMEM = pl.BlockSpec(memory_space=pltpu.SMEM)


def call(kernel, scalars, arrays, outs, scratch=(), flops=0, moved=0, exps=0):
    return pl.pallas_call(
        kernel,
        in_specs=[SMEM] * len(scalars) + [VMEM] * len(arrays),
        out_specs=[VMEM] * len(outs),
        out_shape=[jax.ShapeDtypeStruct(s, t) for s, t in outs],
        scratch_shapes=list(scratch),
        compiler_params=pltpu.CompilerParams(vmem_limit_bytes=56 * 2**20),
        cost_estimate=pl.CostEstimate(flops=flops, bytes_accessed=moved, transcendentals=exps),
    )(*scalars, *arrays)


def dot(a, b, contract=((1,), (0,))):
    return lax.dot_general(a, b, (contract, ((), ())), preferred_element_type=F32)


def rows_at(start, size, step):
    return pl.ds(pl.multiple_of(start, step), size)


def inverse_rms(values):
    return lax.rsqrt(jnp.mean(values * values, axis=-1, keepdims=True) + EPSILON)


def norm_backward(values, factor, upstream):
    return factor * upstream - values * (factor * factor * factor) * jnp.mean(
        upstream * values, axis=-1, keepdims=True
    )


def transpose_kernel(x_ref, out_ref):
    for b in range(x_ref.shape[1] // BLK):
        out_ref[b * BLK : (b + 1) * BLK, :] = x_ref[:, b * BLK : (b + 1) * BLK].T


def project_kernel(layout, ids, offsets, x_ref, *refs):
    pieces, (w_ref, q_ref, kv_ref, key_ref) = refs[: len(layout)], refs[len(layout) :]
    at = 0
    for piece, (parts, rows) in zip(pieces, layout):
        for part in range(parts):
            w_ref[rows_at(offsets[at], rows, 16), :] = piece[part * rows : (part + 1) * rows, :]
            at += 1
    wide = NBR * BLK
    for c in range(NCB):
        picked = jnp.concatenate(
            [x_ref[:, rows_at(ids[c * NBR + r] * BLK, BLK, BLK)] for r in range(NBR)], axis=1
        )
        out = dot(picked, w_ref[c * wide : (c + 1) * wide, :]).astype(BF16)
        if c < NQ:
            for p in range(2):
                at_row = (p * NQ + c) * SPAN
                q_ref[at_row : at_row + SPAN, :] = out[p * SPAN : (p + 1) * SPAN, :]
        elif c == NQ:
            key = out.astype(F32)
            key_ref[...] = out
            kv_ref[:, :HD] = (key * inverse_rms(key)).astype(BF16)
        else:
            kv_ref[:, HD:] = out


def attend_kernel(nz, meta, spans, q_ref, up_ref, *refs):
    pieces = refs[: 2 * nz]
    dq_ref = refs[2 * nz]
    keep = refs[2 * nz + 1 : 3 * nz + 1]
    send = refs[3 * nz + 1 : 4 * nz + 1]
    kv, qhat, up, expo, dprob, acc, dq_t = refs[4 * nz + 1 :]
    half = NQ * SPAN
    me, zi, core = meta[0], meta[1], meta[2]
    for k in range(nz):
        z_from = lax.rem(zi + nz - k, nz)
        for other in range(2):
            source = z_from * 2 + (core if other == 0 else 1 - core)
            for p in range(2):
                kv[rows_at(spans[2 * source + p] * SPAN, SPAN, SPAN), :] = pieces[2 * k + other][
                    p * SPAN : (p + 1) * SPAN, :
                ]
    query = q_ref[...].astype(F32)
    qhat[...] = (query * inverse_rms(query)).astype(BF16)
    for p in range(2):
        for h in range(NQ):
            at = (p * NQ + h) * SPAN
            up[at : at + SPAN, :] = up_ref[p * SPAN : (p + 1) * SPAN, h * HD : (h + 1) * HD]
    acc[...] = jnp.zeros_like(acc)
    key_row = lax.broadcasted_iota(jnp.int32, (KEYS, half), 0)
    query_at = lax.broadcasted_iota(jnp.int32, (KEYS, half), 1) % SPAN
    for p in range(2):
        span = spans[2 * me + p]
        blocks = ((span + 1) * SPAN + KEYS - 1) // KEYS
        q_part = qhat[p * half : (p + 1) * half, :]
        up_part = up[p * half : (p + 1) * half, :]
        limit = query_at + span * SPAN

        def forward(b, sums):
            rows = rows_at(b * KEYS, KEYS, KEYS)
            raw = dot(kv[rows, :HD], q_part, ((1,), (1,)))
            e = jnp.where(key_row + b * KEYS <= limit, jnp.exp2(raw * (SCALE * LOG2E)), 0.0)
            dp = dot(kv[rows, HD:], up_part, ((1,), (1,)))
            expo[rows, :] = e
            dprob[rows, :] = dp
            weighted = e.astype(BF16).astype(F32) * dp
            return (
                sums[0] + jnp.sum(e.reshape(KEYS // 8, 8, half), axis=0),
                sums[1] + jnp.sum(weighted.reshape(KEYS // 8, 8, half), axis=0),
            )

        zero = jnp.zeros((8, half), F32)
        total, weighted = lax.fori_loop(0, blocks, forward, (zero, zero))
        inverse = 1.0 / jnp.sum(total, axis=0, keepdims=True)
        delta = jnp.sum(weighted, axis=0, keepdims=True) * inverse
        dq_t[...] = jnp.zeros_like(dq_t)

        def backward(b, carry):
            rows = rows_at(b * KEYS, KEYS, KEYS)
            prob = expo[rows, :] * inverse
            dscore = (prob * (dprob[rows, :] - delta) * SCALE).astype(BF16)
            acc[rows, :HD] += dot(dscore, q_part)
            acc[rows, HD:] += dot(prob.astype(BF16), up_part)
            dq_t[...] += dot(kv[rows, :HD].T, dscore)
            return carry

        lax.fori_loop(0, blocks, backward, 0)
        q_rows = q_ref[p * half : (p + 1) * half, :].astype(F32)
        dq = norm_backward(q_rows, inverse_rms(q_rows), dq_t[...].T).astype(BF16)
        for h in range(NQ):
            dq_ref[h, p * SPAN : (p + 1) * SPAN, :] = dq[h * SPAN : (h + 1) * SPAN, :]
    for k in range(nz):
        z_to = lax.rem(zi + k, nz)
        for p in range(2):
            part = slice(p * SPAN, (p + 1) * SPAN)
            for out, owner in ((keep[k], z_to * 2 + core), (send[k], z_to * 2 + 1 - core)):
                rows = rows_at(spans[2 * owner + p] * SPAN, SPAN, SPAN)
                out[part, :] = acc[rows, :].astype(BF16)


def kv_grad(key_ref, terms, dkv_ref):
    total = terms[0][...].astype(F32)
    for term in terms[1:]:
        total = total + term[...].astype(F32)
    key = key_ref[...].astype(F32)
    dkv_ref[0, :, :] = norm_backward(key, inverse_rms(key), total[:, :HD]).astype(BF16)
    dkv_ref[1, :, :] = total[:, HD:].astype(BF16)


def block_products(first, last, ids, xt_ref, grad_of, work):
    for c in range(first // NBR, (last - 1) // NBR + 1):
        lo, hi = max(first, c * NBR), min(last, (c + 1) * NBR)
        picked = jnp.concatenate(
            [xt_ref[rows_at(ids[b] * BLK, BLK, BLK), :] for b in range(lo, hi)], axis=0
        )
        work[(lo - first) * BLK : (hi - first) * BLK, :] = dot(picked, grad_of(c)).astype(BF16)


def emit_terms(meta, work, keep, send, z_count, shard, piece):
    core, dp = meta[2], meta[3]
    for k in range(len(keep)):
        for z in range(z_count):
            rows = slice(z * piece, (z + 1) * piece)
            at = lax.bitwise_xor(dp, k) * piece + z * 2 * shard
            keep[k][rows, :] = work[rows_at(at + core * shard, piece, 16), :]
            send[k][rows, :] = work[rows_at(at + (1 - core) * shard, piece, 16), :]


def query_terms_kernel(ndp, z_count, shard, piece, meta, ids, xt_ref, dq_ref, *refs):
    keep, send, work = refs[:ndp], refs[ndp : 2 * ndp], refs[2 * ndp]
    block_products(0, z_count * 2 * shard // BLK, ids, xt_ref, lambda c: dq_ref[c], work)
    emit_terms(meta, work, keep, send, z_count, shard, piece)


def last_terms_kernel(ndp, nz, z_first, shard, piece, meta, ids, xt_ref, dq_ref, key_ref, *refs):
    terms, dkv_ref = refs[:nz], refs[nz]
    keep, send = refs[nz + 1 : nz + 1 + ndp], refs[nz + 1 + ndp : nz + 1 + 2 * ndp]
    work = refs[nz + 1 + 2 * ndp]
    kv_grad(key_ref, terms, dkv_ref)
    block_products(
        z_first * 2 * shard // BLK,
        NNZ,
        ids,
        xt_ref,
        lambda c: dq_ref[c] if c < NQ else dkv_ref[c - NQ],
        work,
    )
    emit_terms(meta, work, keep, send, nz - z_first, shard, piece)


def all_terms_kernel(nz, ids, xt_ref, dq_ref, key_ref, *refs):
    terms, (dkv_ref, out_ref) = refs[:nz], refs[nz:]
    kv_grad(key_ref, terms, dkv_ref)
    block_products(
        0, NNZ, ids, xt_ref, lambda c: dq_ref[c] if c < NQ else dkv_ref[c - NQ], out_ref
    )


def sum_kernel(ndp, nz, z_first, piece, meta, *refs):
    head, tail = refs[:ndp], refs[ndp : 2 * ndp]
    outs, work = refs[2 * ndp : 2 * ndp + nz], refs[2 * ndp + nz]
    for group, first, count in ((head, 0, z_first), (tail, z_first, nz - z_first)):
        total = group[0][...].astype(F32)
        for term in group[1:]:
            total = total + term[...].astype(F32)
        work[first * piece : (first + count) * piece, :] = total.astype(BF16)
    for k in range(nz):
        outs[k][...] = work[rows_at(lax.rem(meta[1] + k, nz) * piece, piece, 16), :]


def place_kernel(piece, meta, *refs):
    for k, ref in enumerate(refs[:-1]):
        at = lax.bitwise_xor(meta[3], k) * piece
        refs[-1][rows_at(at, piece, 16), :] = ref[...].astype(F32)


def token_grad_kernel(ids, dq_ref, dkv_ref, w_ref, out_ref, work):
    wide = NBR * BLK
    cover = out_ref.shape[1] // wide
    for c in range(NCB):
        grad = dq_ref[c] if c < NQ else dkv_ref[c - NQ]
        spread = dot(grad, w_ref[c * wide : (c + 1) * wide, :], ((1,), (1,)))
        for r in range(NBR):
            columns = rows_at(ids[c * NBR + r] * BLK, BLK, BLK)
            term = spread[:, r * BLK : (r + 1) * BLK]
            if c < cover:
                work[:, columns] = term
            else:
                work[:, columns] += term
    out_ref[...] = work[...].astype(BF16)


def per_device(ndp, tokens, grad_attn, w_packed, block_rows, span_pairs):
    nctx = lax.axis_size("ctx")
    nz = nctx // 2
    me = lax.axis_index("ctx")
    dp = lax.axis_index("dp")
    zi, core = me // 2, me % 2
    meta = jnp.stack([me, zi, core, dp]).astype(jnp.int32)
    ids, spans = block_rows.reshape(-1), span_pairs.reshape(-1)
    x, up = tokens[0], grad_attn[0]
    tok, width = x.shape
    length = span_pairs.shape[0] * 2 * SPAN
    shard = w_packed.shape[0]
    piece = shard // ndp
    z_first = NQ * NBR * BLK // (2 * shard)
    fast = shard % BLK == 0 and shard % (16 * ndp) == 0 and ndp & (ndp - 1) == 0

    def swap_core(v):
        return lax.ppermute(v, "ctx", [(i, i ^ 1) for i in range(nctx)])

    def shift_z(v, k):
        return lax.ppermute(
            v, "ctx", [(i, ((i // 2 + k) % nz) * 2 + i % 2) for i in range(nctx)]
        )

    def swap_dp(v, k):
        return lax.ppermute(v, "dp", [(i, i ^ k) for i in range(ndp)])

    (xt,) = call(transpose_kernel, (), (x,), [((width, tok), BF16)], moved=4 * x.size)

    if fast:
        mine = lax.dynamic_slice_in_dim(w_packed, dp * piece, piece, 0)
        from_z = [shift_z(mine, k) for k in range(1, nz)]
        gathered = [jnp.concatenate(from_z, axis=0)]
        gathered += [swap_dp(gathered[0], k) for k in range(1, ndp)]
        pieces, layout, offsets = [], [], []
        for other in range(2):
            parity = core if other == 0 else 1 - core
            pieces.append(w_packed if other == 0 else swap_core(w_packed))
            layout.append((1, shard))
            offsets.append(me * shard if other == 0 else (zi * 2 + parity) * shard)
            for k, part in enumerate(gathered):
                pieces.append(part if other == 0 else swap_core(part))
                layout.append((nz - 1, piece))
                for j in range(1, nz):
                    source = ((zi + nz - j) % nz) * 2 + parity
                    offsets.append(source * shard + (dp ^ k) * piece)
        offsets = jnp.stack(offsets).astype(jnp.int32)
    else:
        pieces = [lax.all_gather(w_packed, "ctx", axis=0, tiled=True)]
        layout = [(1, NNZ * BLK)]
        offsets = jnp.zeros((1,), jnp.int32)
    weights, query, kv, key = call(
        functools.partial(project_kernel, tuple(layout)),
        (ids, offsets),
        (x, *pieces),
        [
            ((NNZ * BLK, BLK), BF16),
            ((tok * NQ, HD), BF16),
            ((tok, 2 * HD), BF16),
            ((tok, HD), BF16),
        ],
        flops=2 * tok * NNZ * BLK * BLK,
        moved=8 * 2**20,
    )

    kv_pieces = []
    for k in range(nz):
        part = kv if k == 0 else shift_z(kv, k)
        kv_pieces += [part, swap_core(part)]
    half = NQ * SPAN
    outs = call(
        functools.partial(attend_kernel, nz),
        (meta, spans),
        (query, up, *kv_pieces),
        [((NQ, tok, HD), BF16)] + [((tok, 2 * HD), BF16)] * (2 * nz),
        scratch=[
            pltpu.VMEM((length, 2 * HD), BF16),
            pltpu.VMEM((tok * NQ, HD), BF16),
            pltpu.VMEM((tok * NQ, HD), BF16),
            pltpu.VMEM((length, half), F32),
            pltpu.VMEM((length, half), F32),
            pltpu.VMEM((length, 2 * HD), F32),
            pltpu.VMEM((HD, half), F32),
        ],
        flops=10 * tok * NQ * length * HD // 2,
        moved=4 * 2**20,
        exps=tok * NQ * length // 2,
    )
    dq, keep, send = outs[0], outs[1 : nz + 1], outs[nz + 1 :]

    def add(a, b):
        return (a.astype(F32) + b.astype(F32)).astype(BF16)

    sums = [add(keep[k], swap_core(send[k])) for k in range(nz)]
    terms = [sums[0]] + [shift_z(sums[k], k) for k in range(1, nz)]

    if fast:
        head = call(
            functools.partial(query_terms_kernel, ndp, z_first, shard, piece),
            (meta, ids),
            (xt, dq),
            [((z_first * piece, BLK), BF16)] * (2 * ndp),
            scratch=[pltpu.VMEM((z_first * 2 * shard, BLK), BF16)],
            flops=2 * tok * z_first * 2 * shard * BLK,
            moved=4 * 2**20,
        )
        head = [add(head[k], swap_core(head[ndp + k])) for k in range(ndp)]
        head = [head[0]] + [swap_dp(head[k], k) for k in range(1, ndp)]
        tail = call(
            functools.partial(last_terms_kernel, ndp, nz, z_first, shard, piece),
            (meta, ids),
            (xt, dq, key, *terms),
            [((2, tok, HD), BF16)] + [(((nz - z_first) * piece, BLK), BF16)] * (2 * ndp),
            scratch=[pltpu.VMEM(((nz - z_first) * 2 * shard, BLK), BF16)],
            flops=2 * tok * (nz - z_first) * 2 * shard * BLK,
            moved=3 * 2**20,
        )
        dkv, tail = tail[0], tail[1:]
        tail = [add(tail[k], swap_core(tail[ndp + k])) for k in range(ndp)]
        tail = [tail[0]] + [swap_dp(tail[k], k) for k in range(1, ndp)]
        by_z = call(
            functools.partial(sum_kernel, ndp, nz, z_first, piece),
            (meta,),
            (*head, *tail),
            [((piece, BLK), BF16)] * nz,
            scratch=[pltpu.VMEM((nz * piece, BLK), BF16)],
            moved=2 * 2**20,
        )
        owned = by_z[0].astype(F32)
        for k in range(1, nz):
            owned = owned + shift_z(by_z[k], k).astype(F32)
        owned = owned.astype(BF16)
        (grad_weights,) = call(
            functools.partial(place_kernel, piece),
            (meta,),
            [owned] + [swap_dp(owned, k) for k in range(1, ndp)],
            [((shard, BLK), F32)],
            moved=2**20,
        )
    else:
        dkv, partial_w = call(
            functools.partial(all_terms_kernel, nz),
            (ids,),
            (xt, dq, key, *terms),
            [((2, tok, HD), BF16), ((NNZ * BLK, BLK), BF16)],
            flops=2 * tok * NNZ * BLK * BLK,
            moved=4 * 2**20,
        )
        received = lax.all_to_all(
            partial_w.reshape(nctx, shard, BLK), "ctx", split_axis=0, concat_axis=0, tiled=True
        )
        grad_weights = lax.psum(jnp.sum(received.astype(F32), axis=0), "dp")

    (grad_tokens,) = call(
        token_grad_kernel,
        (ids,),
        (dq, dkv, weights),
        [((tok, width), BF16)],
        scratch=[pltpu.VMEM((tok, width), F32)],
        flops=2 * tok * NNZ * BLK * BLK,
        moved=4 * 2**20,
    )
    return (grad_tokens[None], grad_weights)


def solution(mesh):
    in_specs = (P("dp", "ctx", None), P("dp", "ctx", None), P("ctx", None), P(), P())
    out_specs = (P("dp", "ctx", None), P("ctx", None))
    return jax.shard_map(
        functools.partial(per_device, mesh.shape["dp"]),
        mesh=mesh,
        in_specs=in_specs,
        out_specs=out_specs,
        check_vma=False,
    )
```

time: 290 us -> 129 us (0.44)
  waiting for transfers between devices: 164 us -> 40.6 us
  matrix products: 34.4 us -> 0 us
  starting transfers between devices: 3.97 us -> 36.3 us
  Pallas kernels: 0 us -> 29.2 us
  blocking collectives: 28.5 us -> 0 us
  local copies, waits for them, and re-layouts: 33.3 us -> 8.69 us
  between operations: 15.4 us -> 1.03 us
    reduce_scatter x2 -> x0, waiting for transfers between devices: 59.8 us -> none  [the longest x1 31.2 us: per_device(): lax.psum_scatter(owner_values, 'ctx', scatter_dimension=0, tiled=True)]
    all_to_all x1 -> x0, waiting for transfers between devices: 53.2 us -> none  [per_device(): lax.all_to_all(partial_w, 'ctx', split_axis=0, concat_axis=0, tiled=True)]
    ppermute x0 -> x45, waiting for transfers between devices: none -> 40.6 us  [the longest x12 20.7 us: shift_z(): lax.ppermute(v, 'ctx', [(i, (i // 2 + k) % nz * 2 + i % 2) for i in range...]
    ppermute x0 -> x45, starting transfers between devices: none -> 36.3 us  [the longest x12 17.1 us: shift_z(): lax.ppermute(v, 'ctx', [(i, (i // 2 + k) % nz * 2 + i % 2) for i in range...]
    dot_general x25 -> x0, matrix products: 34.4 us -> none  [the longest x1 12.2 us: per_device(): jnp.einsum('tco,cbio->tbi', grad_proj, dense_weights, preferred_element_t...]
    psum x1 -> x0, waiting for transfers between devices: 32.4 us -> none  [per_device(): grad_weights = lax.psum(summed, 'dp')]
    pallas_call x0 -> x8, Pallas kernels: none -> 29.2 us  [call(): pl.pallas_call(kernel, in_specs=[SMEM] * len(scalars) + [VMEM] * len(arra...]
    all_gather x2 -> x0, blocking collectives: 28.5 us -> none  [the longest x1 14.3 us: per_device(): lax.all_gather(key_hat, 'ctx', axis=0, tiled=True)]
  transfers between devices with their start and end apart: 5 -> 45, of which waited for: 5 -> 14; matrix products, arithmetic and copies ran while one was open for 14% -> 11% of each run, Pallas kernels for 0% -> 8%
where the time goes in v1:
time: 129 us; the launch traced here: 128 us
  waiting for transfers between devices  40.6 us (31%)
  starting transfers between devices  36.3 us (28%)
  Pallas kernels  29.2 us (23%)
  other arithmetic  11.9 us (9%)
  local copies, waits for them, and re-layouts  8.69 us (7%)
    pallas_call x8, Pallas kernels, call(): pl.pallas_call(kernel, in_specs=[SMEM] * len(scalars) + [VMEM] * len(arra...  29.2 us
    ppermute x12, waiting for transfers between devices, shift_z(): lax.ppermute(v, 'ctx', [(i, (i // 2 + k) % nz * 2 + i % 2) for i in range...  20.7 us
    ppermute x12, waiting for transfers between devices, swap_dp(): return lax.ppermute(v, 'dp', [(i, i ^ k) for i in range(ndp)])  19.3 us
    ppermute x12, starting transfers between devices, shift_z(): lax.ppermute(v, 'ctx', [(i, (i // 2 + k) % nz * 2 + i % 2) for i in range...  17.1 us
    ppermute x12, starting transfers between devices, swap_dp(): return lax.ppermute(v, 'dp', [(i, i ^ k) for i in range(ndp)])  14.4 us
    convert_element_type x12, other arithmetic, add(): return (a.astype(F32) + b.astype(F32)).astype(BF16)  10.4 us
    unnamed x70, local copies, waits for them, and re-layouts  5.89 us
    ppermute x21, starting transfers between devices, swap_core(): return lax.ppermute(v, 'ctx', [(i, i ^ 1) for i in range(nctx)])  4.86 us
  transfers between devices with their start and end apart: 45, of which 14 were waited for; matrix products, arithmetic and copies ran while one was open for 11% of the time, Pallas kernels for 8%

profile of v1, /device:TPU:0, one launch (start us, length us, event | category | flops | bytes accessed | tf_op | source)
XLA Modules:
  0.0 127.8 jit_solution(10863228598820918406)
XLA Ops:
  0.6 0.9 constant_dynamic-slice_fusion
  1.5 3.0 %collective-permute-start = (bf16[320,128]{1,0:T(8,128)(2,1)S(1)}, bf16[320,128]{1,0:T(8,128)(2,1)S(1)}, u32[]{:S(2)}, u32[]{:S(2)}) collective-permute-start(bf16[320,128]{1,0:T(8,128)(2,1)S(1)} %constant_dynamic-slice_fusion), channel_id=1, source_target_pairs={{0,2},{1,3},{2,4},{3,5},{4,6},{5,7},{6,0},{7,1},{8,10},{9,11},{10,... | collective-permute-start | bytes 245768 | tf_op jit(solution)/shard_map/ppermute | solution.py:277
  4.6 2.1 %collective-permute-start.2 = (bf16[320,128]{1,0:T(8,128)(2,1)S(1)}, bf16[320,128]{1,0:T(8,128)(2,1)S(1)}, u32[]{:S(2)}, u32[]{:S(2)}) collective-permute-start(bf16[320,128]{1,0:T(8,128)(2,1)S(1)} %constant_dynamic-slice_fusion), channel_id=1, source_target_pairs={{0,6},{1,7},{2,0},{3,1},{4,2},{5,3},{6,4},{7,5},{8,14},{9,15},{10,... | collective-permute-start | bytes 245768 | tf_op jit(solution)/shard_map/ppermute | solution.py:277
  6.7 1.0 collective-permute-start.1
  7.6 1.8 %collective-permute-done = bf16[320,128]{1,0:T(8,128)(2,1)S(1)} collective-permute-done((bf16[320,128]{1,0:T(8,128)(2,1)S(1)}, bf16[320,128]{1,0:T(8,128)(2,1)S(1)}, u32[]{:S(2)}, u32[]{:S(2)}) %collective-permute-start) | collective-permute-done | bytes 81952 | tf_op jit(solution)/shard_map/ppermute | solution.py:277
  9.4 4.9 %collective-permute-done.1 = bf16[320,128]{1,0:T(8,128)(2,1)S(1)} collective-permute-done((bf16[320,128]{1,0:T(8,128)(2,1)S(1)}, bf16[320,128]{1,0:T(8,128)(2,1)S(1)}, u32[]{:S(2)}, u32[]{:S(2)}) %collective-permute-start.1) | collective-permute-done | bytes 81952 | tf_op jit(solution)/shard_map/ppermute | solution.py:277
  14.4 2.5 %collective-permute-start.5 = (bf16[960,128]{1,0:T(8,128)(2,1)S(1)}, bf16[960,128]{1,0:T(8,128)(2,1)S(1)}, u32[]{:S(2)}, u32[]{:S(2)}) collective-permute-start(bf16[960,128]{1,0:T(8,128)(2,1)S(1)} %constant_dynamic-update-slice_fusion.refs_1_), channel_id=1, source_target_pairs={{0,24},{8,16},{16,8},{24,0},{1,25},{9,17},{17,9},{25,1},{2,26},{10... | collective-permute-start | bytes 737288 | tf_op jit(solution)/shard_map/ppermute | solution.py:282
  17.4 0.5 collective-permute-start.3
  18.4 5.8 %collective-permute-done.5.refs_4_ = bf16[960,128]{1,0:T(8,128)(2,1)S(1)} collective-permute-done((bf16[960,128]{1,0:T(8,128)(2,1)S(1)}, bf16[960,128]{1,0:T(8,128)(2,1)S(1)}, u32[]{:S(2)}, u32[]{:S(2)}) %collective-permute-start.5) | collective-permute-done | bytes 245792 | tf_op jit(solution)/shard_map/ppermute | solution.py:282
  24.2 4.1 %collective-permute-done.4.refs_3_ = bf16[960,128]{1,0:T(8,128)(2,1)S(1)} collective-permute-done((bf16[960,128]{1,0:T(8,128)(2,1)S(1)}, bf16[960,128]{1,0:T(8,128)(2,1)S(1)}, u32[]{:S(2)}, u32[]{:S(2)}) %collective-permute-start.4) | collective-permute-done | bytes 245792 | tf_op jit(solution)/shard_map/ppermute | solution.py:282
  28.9 0.8 copy.9
  29.6 0.6 reshape.10.ids
  30.2 0.6 stack.127.offsets
  31.0 0.6 copy-done.10
  31.9 4.6 %shard_map.68 = (bf16[10240,128]{1,0:T(8,128)(2,1)}, bf16[1024,128]{1,0:T(8,128)(2,1)}, bf16[128,256]{1,0:T(8,128)(2,1)}, bf16[128,128]{1,0:T(8,128)(2,1)}) custom-call(s32[80]{0:T(128)} %reshape.10.ids, s32[26]{0:T(128)} %stack.127.offsets, bf16[128,4096]{1,0:T(8,128)(2,1)} %bitcast.33, bf16[1280,128]{1,0:T(8,128)(2,1)} %refs_0_.1, ...), custom_call_target="tpu_custom_call" | custom-call | flops 335544320 | bytes 8388608 | tf_op jit(solution)/shard_map/pallas_call | solution.py:32
  36.6 2.1 %collective-permute-start.16 = (bf16[128,256]{1,0:T(8,128)(2,1)}, bf16[128,256]{1,0:T(8,128)(2,1)S(1)}, u32[]{:S(2)}, u32[]{:S(2)}) collective-permute-start(bf16[128,256]{1,0:T(8,128)(2,1)} %get-tuple-element.37.refs_0_), channel_id=1, source_target_pairs={{0,6},{1,7},{2,0},{3,1},{4,2},{5,3},{6,4},{7,5},{8,14},{9,15},{10,... | collective-permute-start | bytes 196616 | tf_op jit(solution)/shard_map/ppermute | solution.py:277
  38.6 0.6 collective-permute-start.12
  39.3 0.7 reshape.11.spans
  40.0 1.4 %collective-permute-done.16.refs_6_ = bf16[128,256]{1,0:T(8,128)(2,1)S(1)} collective-permute-done((bf16[128,256]{1,0:T(8,128)(2,1)}, bf16[128,256]{1,0:T(8,128)(2,1)S(1)}, u32[]{:S(2)}, u32[]{:S(2)}) %collective-permute-start.16) | collective-permute-done | bytes 65568 | tf_op jit(solution)/shard_map/ppermute | solution.py:277
  41.4 4.3 %collective-permute-done.14.refs_4_ = bf16[128,256]{1,0:T(8,128)(2,1)S(1)} collective-permute-done((bf16[128,256]{1,0:T(8,128)(2,1)}, bf16[128,256]{1,0:T(8,128)(2,1)S(1)}, u32[]{:S(2)}, u32[]{:S(2)}) %collective-permute-start.14) | collective-permute-done | bytes 65568 | tf_op jit(solution)/shard_map/ppermute | solution.py:277
  46.3 0.6 pad_add_fusion.meta
  47.8 7.6 %shard_map.69 = (bf16[8,128,128]{2,1,0:T(8,128)(2,1)}, bf16[128,256]{1,0:T(8,128)(2,1)}, bf16[128,256]{1,0:T(8,128)(2,1)}, bf16[128,256]{1,0:T(8,128)(2,1)}, bf1...) custom-call(s32[4]{0:T(128)} %pad_add_fusion.meta, ...), custom_call_target="tpu_custom_call" | custom-call | flops 671088640 | bytes 4194304 | tf_op jit(solution)/shard_map/pallas_call | solution.py:32
  55.9 2.5 %shard_map.70.xt_ref = bf16[4096,128]{1,0:T(8,128)(2,1)} custom-call(bf16[128,4096]{1,0:T(8,128)(2,1)} %bitcast.34), custom_call_target="tpu_custom_call" | custom-call | bytes 2097152 | tf_op jit(solution)/shard_map/pallas_call | solution.py:32
  59.1 0.9 add_convert_fusion.11
  60.0 0.9 add_convert_fusion.10
  60.9 2.3 %collective-permute-start.22 = (bf16[128,256]{1,0:T(8,128)(2,1)S(1)}, bf16[128,256]{1,0:T(8,128)(2,1)S(1)}, u32[]{:S(2)}, u32[]{:S(2)}) collective-permute-start(bf16[128,256]{1,0:T(8,128)(2,1)S(1)} %add_convert_fusion.10), channel_id=1, source_target_pairs={{0,4},{1,5},{2,6},{3,7},{4,0},{5,1},{6,2},{7,3},{8,12},{9,13},{10,... | collective-permute-start | bytes 196616 | tf_op jit(solution)/shard_map/ppermute | solution.py:277
  63.2 0.9 add_convert_fusion.9
  64.0 2.1 %collective-permute-start.24 = (bf16[128,256]{1,0:T(8,128)(2,1)S(1)}, bf16[128,256]{1,0:T(8,128)(2,1)S(1)}, u32[]{:S(2)}, u32[]{:S(2)}) collective-permute-start(bf16[128,256]{1,0:T(8,128)(2,1)S(1)} %add_convert_fusion.9), channel_id=1, source_target_pairs={{0,6},{1,7},{2,0},{3,1},{4,2},{5,3},{6,4},{7,5},{8,14},{9,15},{10,... | collective-permute-start | bytes 196616 | tf_op jit(solution)/shard_map/ppermute | solution.py:277
  66.2 0.7 add_convert_fusion.12.refs_0_
  66.8 2.2 %collective-permute-done.22.refs_2_ = bf16[128,256]{1,0:T(8,128)(2,1)S(1)} collective-permute-done((bf16[128,256]{1,0:T(8,128)(2,1)S(1)}, bf16[128,256]{1,0:T(8,128)(2,1)S(1)}, u32[]{:S(2)}, u32[]{:S(2)}) %collective-permute-start.22) | collective-permute-done | bytes 65568 | tf_op jit(solution)/shard_map/ppermute | solution.py:277
  69.0 0.5 collective-permute-done.24.refs_3_
  69.7 0.5 copy-done.24
  70.2 2.7 %shard_map.71 = (bf16[2,128,128]{2,1,0:T(8,128)(2,1)}, bf16[320,128]{1,0:T(8,128)(2,1)}, bf16[320,128]{1,0:T(8,128)(2,1)}, bf16[320,128]{1,0:T(8,128)(2,1)}, bf1...) custom-call(s32[4]{0:T(128)} %pad_add_fusion.meta, ...), custom_call_target="tpu_custom_call" | custom-call | flops 83886080 | bytes 3145728 | tf_op jit(solution)/shard_map/pallas_call | solution.py:32
  72.9 3.3 %shard_map.73 = (bf16[960,128]{1,0:T(8,128)(2,1)}, bf16[960,128]{1,0:T(8,128)(2,1)}, bf16[960,128]{1,0:T(8,128)(2,1)}, bf16[960,128]{1,0:T(8,128)(2,1)}, bf16[96...) custom-call(s32[4]{0:T(128)} %pad_add_fusion.meta, ...), custom_call_target="tpu_custom_call" | custom-call | flops 251658240 | bytes 4194304 | tf_op jit(solution)/shard_map/pallas_call | solution.py:32
  77.7 1.5 %add_convert_fusion.8.refs_4_ = bf16[320,128]{1,0:T(8,128)(2,1)} fusion(bf16[320,128]{1,0:T(8,128)(2,1)S(1)} %collective-permute-done.32, bf16[320,128]{1,0:T(8,128)(2,1)} %get-tuple-element.58), kind=kLoop, calls=%fused_computation.8 | loop fusion | flops 163840 | bytes 245760 | tf_op jit(solution)/shard_map/convert_element_type | solution.py:348
  79.6 0.9 add_convert_fusion.7
  81.1 0.9 add_convert_fusion.6
  82.0 1.5 %collective-permute-start.34 = (bf16[320,128]{1,0:T(8,128)(2,1)S(1)}, bf16[320,128]{1,0:T(8,128)(2,1)S(1)}, u32[]{:S(2)}, u32[]{:S(2)}) collective-permute-start(bf16[320,128]{1,0:T(8,128)(2,1)S(1)} %add_convert_fusion.7), channel_id=1, source_target_pairs={{0,8},{8,0},{16,24},{24,16},{1,9},{9,1},{17,25},{25,17},{2,10},{10... | collective-permute-start | bytes 245768 | tf_op jit(solution)/shard_map/ppermute | solution.py:282
  83.5 1.0 add_convert_fusion.2
  84.5 0.7 collective-permute-start.27
  85.2 1.0 add_convert_fusion.1
  86.2 1.5 %collective-permute-start.29 = (bf16[960,128]{1,0:T(8,128)(2,1)S(1)}, bf16[960,128]{1,0:T(8,128)(2,1)S(1)}, u32[]{:S(2)}, u32[]{:S(2)}) collective-permute-start(bf16[960,128]{1,0:T(8,128)(2,1)S(1)} %add_convert_fusion.1), channel_id=1, source_target_pairs={{0,16},{8,24},{16,0},{24,8},{1,17},{9,25},{17,1},{25,9},{2,18},{10... | collective-permute-start | bytes 737288 | tf_op jit(solution)/shard_map/ppermute | solution.py:282
  87.7 1.0 add_convert_fusion
  88.8 1.5 %collective-permute-start.31 = (bf16[960,128]{1,0:T(8,128)(2,1)S(1)}, bf16[960,128]{1,0:T(8,128)(2,1)S(1)}, u32[]{:S(2)}, u32[]{:S(2)}) collective-permute-start(bf16[960,128]{1,0:T(8,128)(2,1)S(1)} %add_convert_fusion), channel_id=1, source_target_pairs={{0,24},{8,16},{16,8},{24,0},{1,25},{9,17},{17,9},{25,1},{2,26},{10... | collective-permute-start | bytes 737288 | tf_op jit(solution)/shard_map/ppermute | solution.py:282
  90.3 1.0 collective-permute-start.36
  91.3 1.2 collective-permute-start.38
  92.5 0.8 add_convert_fusion.3.refs_0_
  93.2 9.3 %collective-permute-done.36.refs_6_ = bf16[320,128]{1,0:T(8,128)(2,1)S(1)} collective-permute-done((bf16[320,128]{1,0:T(8,128)(2,1)S(1)}, bf16[320,128]{1,0:T(8,128)(2,1)S(1)}, u32[]{:S(2)}, u32[]{:S(2)}) %collective-permute-start.36) | collective-permute-done | bytes 81952 | tf_op jit(solution)/shard_map/ppermute | solution.py:282
  102.6 0.6 copy-done.15
  103.4 0.7 copy-done.5
  104.1 2.4 %shard_map.74 = (bf16[320,128]{1,0:T(8,128)(2,1)}, bf16[320,128]{1,0:T(8,128)(2,1)}, bf16[320,128]{1,0:T(8,128)(2,1)}, bf16[320,128]{1,0:T(8,128)(2,1)}) custom-call(s32[4]{0:T(128)} %pad_add_fusion.meta, bf16[960,128]{1,0:T(8,128)(2,1)} %add_convert_fusion.3.refs_0_, bf16[960,128]{1,0:T(8,128)(2,1)} %copy-done.3, bf16[960,128]{1,0:T(8,128)(2,1)} %copy-done.4, ...), custom_call_target="tpu_custom_call" | custom-call | bytes 2097152 | tf_op jit(solution)/shard_map/pallas_call | solution.py:32
  106.5 1.3 %collective-permute-start.39 = (bf16[320,128]{1,0:T(8,128)(2,1)}, bf16[320,128]{1,0:T(8,128)(2,1)S(1)}, u32[]{:S(2)}, u32[]{:S(2)}) collective-permute-start(bf16[320,128]{1,0:T(8,128)(2,1)} %get-tuple-element.67), channel_id=1, source_target_pairs={{0,2},{1,3},{2,4},{3,5},{4,6},{5,7},{6,0},{7,1},{8,10},{9,11},{10,... | collective-permute-start | bytes 245768 | tf_op jit(solution)/shard_map/ppermute | solution.py:277
  107.8 1.9 %collective-permute-start.40 = (bf16[320,128]{1,0:T(8,128)(2,1)}, bf16[320,128]{1,0:T(8,128)(2,1)S(1)}, u32[]{:S(2)}, u32[]{:S(2)}) collective-permute-start(bf16[320,128]{1,0:T(8,128)(2,1)} %get-tuple-element.68), channel_id=1, source_target_pairs={{0,4},{1,5},{2,6},{3,7},{4,0},{5,1},{6,2},{7,3},{8,12},{9,13},{10,... | collective-permute-start | bytes 245768 | tf_op jit(solution)/shard_map/ppermute | solution.py:277
  109.7 0.6 collective-permute-start.41
  110.3 3.1 %collective-permute-done.39 = bf16[320,128]{1,0:T(8,128)(2,1)S(1)} collective-permute-done((bf16[320,128]{1,0:T(8,128)(2,1)}, bf16[320,128]{1,0:T(8,128)(2,1)S(1)}, u32[]{:S(2)}, u32[]{:S(2)}) %collective-permute-start.39) | collective-permute-done | bytes 81952 | tf_op jit(solution)/shard_map/ppermute | solution.py:277
  113.4 2.5 %collective-permute-done.40 = bf16[320,128]{1,0:T(8,128)(2,1)S(1)} collective-permute-done((bf16[320,128]{1,0:T(8,128)(2,1)}, bf16[320,128]{1,0:T(8,128)(2,1)S(1)}, u32[]{:S(2)}, u32[]{:S(2)}) %collective-permute-start.40) | collective-permute-done | bytes 81952 | tf_op jit(solution)/shard_map/ppermute | solution.py:277
  115.9 0.9 add_convert_fusion.4.refs_0_
  116.8 1.8 %collective-permute-start.44 = (bf16[320,128]{1,0:T(8,128)(2,1)S(1)}, bf16[320,128]{1,0:T(8,128)(2,1)S(1)}, u32[]{:S(2)}, u32[]{:S(2)}) collective-permute-start(bf16[320,128]{1,0:T(8,128)(2,1)S(1)} %add_convert_fusion.4.refs_0_), channel_id=1, source_target_pairs={{0,24},{8,16},{16,8},{24,0},{1,25},{9,17},{17,9},{25,1},{2,26},{10... | collective-permute-start | bytes 245768 | tf_op jit(solution)/shard_map/ppermute | solution.py:282
  118.6 1.1 collective-permute-start.43
  119.8 0.6 collective-permute-start.42
  120.4 4.2 %shard_map.72 = bf16[128,4096]{1,0:T(8,128)(2,1)} custom-call(s32[80]{0:T(128)} %reshape.10.ids, bf16[8,128,128]{2,1,0:T(8,128)(2,1)} %get-tuple-element.38.dq_ref, bf16[2,128,128]{2,1,0:T(8,128)(2,1)} %get-tuple-element.48.dkv_ref, bf16[10240,128]{1,0:T(8,128)(2,1)} %get-tuple-element.49.w_ref), custom_call_target="tpu_custom_call" | custom-call | flops 335544320 | bytes 4194304 | tf_op jit(solution)/shard_map/pallas_call | solution.py:32
  124.7 0.6 copy-done.17
  125.3 0.6 copy-done.19
  125.9 1.9 %shard_map.75 = f32[1280,128]{1,0:T(8,128)} custom-call(s32[4]{0:T(128)} %pad_add_fusion.meta, bf16[320,128]{1,0:T(8,128)(2,1)} %copy-done.1, bf16[320,128]{1,0:T(8,128)(2,1)} %copy-done.19, bf16[320,128]{1,0:T(8,128)(2,1)} %copy-done.18, bf16[320,128]{1,0:T(8,128)(2,1)} %copy-done.17), custom_call_target="tpu_custom_call" | custom-call | bytes 1048576 | tf_op jit(solution)/shard_map/pallas_call | solution.py:32
  (123 shorter events, 7.6 us)
Async XLA Ops:
  0.6 38.6 %copy-start.25 = (s32[8,2]{0,1:T(2,128)S(1)}, s32[8,2]{0,1:T(2,128)}, u32[]{:S(2)}) copy-start(s32[8,2]{0,1:T(2,128)} %param.9) | copy-start | bytes 196
  1.5 7.8 %collective-permute-start = (bf16[320,128]{1,0:T(8,128)(2,1)S(1)}, bf16[320,128]{1,0:T(8,128)(2,1)S(1)}, u32[]{:S(2)}, u32[]{:S(2)}) collective-permute-start(bf16[320,128]{1,0:T(8,128)(2,1)S(1)} %constant_dynamic-slice_fusion), channel_id=1, source_target_pairs={{0,2},{1,3},{2,4},{3,5},{4,6},{5,7},{6,0},{7,1},{8,10},{9,11},{10,... | collective-permute-start | bytes 245768 | tf_op jit(solution)/shard_map/ppermute | solution.py:277
  4.6 9.8 %collective-permute-start.2 = (bf16[320,128]{1,0:T(8,128)(2,1)S(1)}, bf16[320,128]{1,0:T(8,128)(2,1)S(1)}, u32[]{:S(2)}, u32[]{:S(2)}) collective-permute-start(bf16[320,128]{1,0:T(8,128)(2,1)S(1)} %constant_dynamic-slice_fusion), channel_id=1, source_target_pairs={{0,6},{1,7},{2,0},{3,1},{4,2},{5,3},{6,4},{7,5},{8,14},{9,15},{10,... | collective-permute-start | bytes 245768 | tf_op jit(solution)/shard_map/ppermute | solution.py:277
  6.7 7.6 %collective-permute-start.1 = (bf16[320,128]{1,0:T(8,128)(2,1)S(1)}, bf16[320,128]{1,0:T(8,128)(2,1)S(1)}, u32[]{:S(2)}, u32[]{:S(2)}) collective-permute-start(bf16[320,128]{1,0:T(8,128)(2,1)S(1)} %constant_dynamic-slice_fusion), channel_id=1, source_target_pairs={{0,4},{1,5},{2,6},{3,7},{4,0},{5,1},{6,2},{7,3},{8,12},{9,13},{10,... | collective-permute-start | bytes 245768 | tf_op jit(solution)/shard_map/ppermute | solution.py:277
  14.3 16.6 %copy-start = (bf16[960,128]{1,0:T(8,128)(2,1)}, bf16[960,128]{1,0:T(8,128)(2,1)S(1)}, u32[]{:S(2)}) copy-start(bf16[960,128]{1,0:T(8,128)(2,1)S(1)} %constant_dynamic-update-slice_fusion.refs_1_) | copy-start | bytes 737284
  14.4 9.8 %collective-permute-start.5 = (bf16[960,128]{1,0:T(8,128)(2,1)S(1)}, bf16[960,128]{1,0:T(8,128)(2,1)S(1)}, u32[]{:S(2)}, u32[]{:S(2)}) collective-permute-start(bf16[960,128]{1,0:T(8,128)(2,1)S(1)} %constant_dynamic-update-slice_fusion.refs_1_), channel_id=1, source_target_pairs={{0,24},{8,16},{16,8},{24,0},{1,25},{9,17},{17,9},{25,1},{2,26},{10... | collective-permute-start | bytes 737288 | tf_op jit(solution)/shard_map/ppermute | solution.py:282
  16.9 11.5 %collective-permute-start.4 = (bf16[960,128]{1,0:T(8,128)(2,1)S(1)}, bf16[960,128]{1,0:T(8,128)(2,1)S(1)}, u32[]{:S(2)}, u32[]{:S(2)}) collective-permute-start(bf16[960,128]{1,0:T(8,128)(2,1)S(1)} %constant_dynamic-update-slice_fusion.refs_1_), channel_id=1, source_target_pairs={{0,16},{8,24},{16,0},{24,8},{1,17},{9,25},{17,1},{25,9},{2,18},{10... | collective-permute-start | bytes 737288 | tf_op jit(solution)/shard_map/ppermute | solution.py:282
  17.4 11.0 %collective-permute-start.3 = (bf16[960,128]{1,0:T(8,128)(2,1)S(1)}, bf16[960,128]{1,0:T(8,128)(2,1)S(1)}, u32[]{:S(2)}, u32[]{:S(2)}) collective-permute-start(bf16[960,128]{1,0:T(8,128)(2,1)S(1)} %constant_dynamic-update-slice_fusion.refs_1_), channel_id=1, source_target_pairs={{0,8},{8,0},{16,24},{24,16},{1,9},{9,1},{17,25},{25,17},{2,10},{10... | collective-permute-start | bytes 737288 | tf_op jit(solution)/shard_map/ppermute | solution.py:282
  17.9 12.9 %collective-permute-start.6 = (bf16[1280,128]{1,0:T(8,128)(2,1)}, bf16[1280,128]{1,0:T(8,128)(2,1)S(1)}, u32[]{:S(2)}, u32[]{:S(2)}) collective-permute-start(bf16[1280,128]{1,0:T(8,128)(2,1)} %refs_0_.1), channel_id=1, source_target_pairs={{0,1},{1,0},{2,3},{3,2},{4,5},{5,4},{6,7},{7,6},{8,9},{9,8},{10,11... | collective-permute-start | bytes 983048 | tf_op jit(solution)/shard_map/ppermute | solution.py:274
  17.9 12.9 %collective-permute-start.7 = (bf16[960,128]{1,0:T(8,128)(2,1)S(1)}, bf16[960,128]{1,0:T(8,128)(2,1)S(1)}, u32[]{:S(2)}, u32[]{:S(2)}) collective-permute-start(bf16[960,128]{1,0:T(8,128)(2,1)S(1)} %constant_dynamic-update-slice_fusion.refs_1_), channel_id=1, source_target_pairs={{0,1},{1,0},{2,3},{3,2},{4,5},{5,4},{6,7},{7,6},{8,9},{9,8},{10,11... | collective-permute-start | bytes 737288 | tf_op jit(solution)/shard_map/ppermute | solution.py:274
  24.2 6.7 %copy-start.7 = (bf16[960,128]{1,0:T(8,128)(2,1)}, bf16[960,128]{1,0:T(8,128)(2,1)S(1)}, u32[]{:S(2)}) copy-start(bf16[960,128]{1,0:T(8,128)(2,1)S(1)} %collective-permute-done.5.refs_4_) | copy-start | bytes 737284
  24.2 6.7 %collective-permute-start.10 = (bf16[960,128]{1,0:T(8,128)(2,1)S(1)}, bf16[960,128]{1,0:T(8,128)(2,1)S(1)}, u32[]{:S(2)}, u32[]{:S(2)}) collective-permute-start(bf16[960,128]{1,0:T(8,128)(2,1)S(1)} %collective-permute-done.5.refs_4_), channel_id=1, source_target_pairs={{0,1},{1,0},{2,3},{3,2},{4,5},{5,4},{6,7},{7,6},{8,9},{9,8},{10,11... | collective-permute-start | bytes 737288 | tf_op jit(solution)/shard_map/ppermute | solution.py:274
  28.3 2.6 %copy-start.8 = (bf16[960,128]{1,0:T(8,128)(2,1)}, bf16[960,128]{1,0:T(8,128)(2,1)S(1)}, u32[]{:S(2)}) copy-start(bf16[960,128]{1,0:T(8,128)(2,1)S(1)} %collective-permute-done.4.refs_3_) | copy-start | bytes 737284
  28.3 2.6 %collective-permute-start.9 = (bf16[960,128]{1,0:T(8,128)(2,1)S(1)}, bf16[960,128]{1,0:T(8,128)(2,1)S(1)}, u32[]{:S(2)}, u32[]{:S(2)}) collective-permute-start(bf16[960,128]{1,0:T(8,128)(2,1)S(1)} %collective-permute-done.4.refs_3_), channel_id=1, source_target_pairs={{0,1},{1,0},{2,3},{3,2},{4,5},{5,4},{6,7},{7,6},{8,9},{9,8},{10,11... | collective-permute-start | bytes 737288 | tf_op jit(solution)/shard_map/ppermute | solution.py:274
  28.4 2.6 %copy-start.9 = (bf16[960,128]{1,0:T(8,128)(2,1)}, bf16[960,128]{1,0:T(8,128)(2,1)S(1)}, u32[]{:S(2)}) copy-start(bf16[960,128]{1,0:T(8,128)(2,1)S(1)} %collective-permute-done.3.refs_2_) | copy-start | bytes 737284
  28.4 2.6 %collective-permute-start.8 = (bf16[960,128]{1,0:T(8,128)(2,1)S(1)}, bf16[960,128]{1,0:T(8,128)(2,1)S(1)}, u32[]{:S(2)}, u32[]{:S(2)}) collective-permute-start(bf16[960,128]{1,0:T(8,128)(2,1)S(1)} %collective-permute-done.3.refs_2_), channel_id=1, source_target_pairs={{0,1},{1,0},{2,3},{3,2},{4,5},{5,4},{6,7},{7,6},{8,9},{9,8},{10,11... | collective-permute-start | bytes 737288 | tf_op jit(solution)/shard_map/ppermute | solution.py:274
  30.9 0.8 copy-start.2
  30.9 0.9 copy-start.11
  30.9 0.9 copy-start.12
  30.9 1.0 copy-start.13
  36.6 4.9 %collective-permute-start.16 = (bf16[128,256]{1,0:T(8,128)(2,1)}, bf16[128,256]{1,0:T(8,128)(2,1)S(1)}, u32[]{:S(2)}, u32[]{:S(2)}) collective-permute-start(bf16[128,256]{1,0:T(8,128)(2,1)} %get-tuple-element.37.refs_0_), channel_id=1, source_target_pairs={{0,6},{1,7},{2,0},{3,1},{4,2},{5,3},{6,4},{7,5},{8,14},{9,15},{10,... | collective-permute-start | bytes 196616 | tf_op jit(solution)/shard_map/ppermute | solution.py:277
  38.6 7.1 %collective-permute-start.14 = (bf16[128,256]{1,0:T(8,128)(2,1)}, bf16[128,256]{1,0:T(8,128)(2,1)S(1)}, u32[]{:S(2)}, u32[]{:S(2)}) collective-permute-start(bf16[128,256]{1,0:T(8,128)(2,1)} %get-tuple-element.37.refs_0_), channel_id=1, source_target_pairs={{0,4},{1,5},{2,6},{3,7},{4,0},{5,1},{6,2},{7,3},{8,12},{9,13},{10,... | collective-permute-start | bytes 196616 | tf_op jit(solution)/shard_map/ppermute | solution.py:277
  38.6 7.1 %collective-permute-start.12 = (bf16[128,256]{1,0:T(8,128)(2,1)}, bf16[128,256]{1,0:T(8,128)(2,1)S(1)}, u32[]{:S(2)}, u32[]{:S(2)}) collective-permute-start(bf16[128,256]{1,0:T(8,128)(2,1)} %get-tuple-element.37.refs_0_), channel_id=1, source_target_pairs={{0,2},{1,3},{2,4},{3,5},{4,6},{5,7},{6,0},{7,1},{8,10},{9,11},{10,... | collective-permute-start | bytes 196616 | tf_op jit(solution)/shard_map/ppermute | solution.py:277
  40.0 6.9 %collective-permute-start.11 = (bf16[128,256]{1,0:T(8,128)(2,1)}, bf16[128,256]{1,0:T(8,128)(2,1)S(1)}, u32[]{:S(2)}, u32[]{:S(2)}) collective-permute-start(bf16[128,256]{1,0:T(8,128)(2,1)} %get-tuple-element.37.refs_0_), channel_id=1, source_target_pairs={{0,1},{1,0},{2,3},{3,2},{4,5},{5,4},{6,7},{7,6},{8,9},{9,8},{10,11... | collective-permute-start | bytes 196616 | tf_op jit(solution)/shard_map/ppermute | solution.py:274
  41.4 5.7 %copy-start.26 = (bf16[128,256]{1,0:T(8,128)(2,1)}, bf16[128,256]{1,0:T(8,128)(2,1)S(1)}, u32[]{:S(2)}) copy-start(bf16[128,256]{1,0:T(8,128)(2,1)S(1)} %collective-permute-done.16.refs_6_) | copy-start | bytes 196612
  41.4 5.4 %collective-permute-start.17 = (bf16[128,256]{1,0:T(8,128)(2,1)S(1)}, bf16[128,256]{1,0:T(8,128)(2,1)S(1)}, u32[]{:S(2)}, u32[]{:S(2)}) collective-permute-start(bf16[128,256]{1,0:T(8,128)(2,1)S(1)} %collective-permute-done.16.refs_6_), channel_id=1, source_target_pairs={{0,1},{1,0},{2,3},{3,2},{4,5},{5,4},{6,7},{7,6},{8,9},{9,8},{10,11... | collective-permute-start | bytes 196616 | tf_op jit(solution)/shard_map/ppermute | solution.py:274
  45.8 1.4 %copy-start.27 = (bf16[128,256]{1,0:T(8,128)(2,1)}, bf16[128,256]{1,0:T(8,128)(2,1)S(1)}, u32[]{:S(2)}) copy-start(bf16[128,256]{1,0:T(8,128)(2,1)S(1)} %collective-permute-done.14.refs_4_) | copy-start | bytes 196612
  45.8 1.3 collective-permute-start.15
  45.8 1.4 %copy-start.28 = (bf16[128,256]{1,0:T(8,128)(2,1)}, bf16[128,256]{1,0:T(8,128)(2,1)S(1)}, u32[]{:S(2)}) copy-start(bf16[128,256]{1,0:T(8,128)(2,1)S(1)} %collective-permute-done.12.refs_2_) | copy-start | bytes 196612
  45.8 1.4 %collective-permute-start.13 = (bf16[128,256]{1,0:T(8,128)(2,1)S(1)}, bf16[128,256]{1,0:T(8,128)(2,1)S(1)}, u32[]{:S(2)}, u32[]{:S(2)}) collective-permute-start(bf16[128,256]{1,0:T(8,128)(2,1)S(1)} %collective-permute-done.12.refs_2_), channel_id=1, source_target_pairs={{0,1},{1,0},{2,3},{3,2},{4,5},{5,4},{6,7},{7,6},{8,9},{9,8},{10,11... | collective-permute-start | bytes 196616 | tf_op jit(solution)/shard_map/ppermute | solution.py:274
  55.4 10.7 %copy-start.21 = (bf16[128,256]{1,0:T(8,128)(2,1)S(1)}, bf16[128,256]{1,0:T(8,128)(2,1)}, u32[]{:S(2)}) copy-start(bf16[128,256]{1,0:T(8,128)(2,1)} %get-tuple-element.40) | copy-start | bytes 196612
  55.4 3.6 %collective-permute-start.19 = (bf16[128,256]{1,0:T(8,128)(2,1)}, bf16[128,256]{1,0:T(8,128)(2,1)S(1)}, u32[]{:S(2)}, u32[]{:S(2)}) collective-permute-start(bf16[128,256]{1,0:T(8,128)(2,1)} %get-tuple-element.43), channel_id=1, source_target_pairs={{0,1},{1,0},{2,3},{3,2},{4,5},{5,4},{6,7},{7,6},{8,9},{9,8},{10,11... | collective-permute-start | bytes 196616 | tf_op jit(solution)/shard_map/ppermute | solution.py:274
  58.4 7.8 %collective-permute-start.18 = (bf16[128,256]{1,0:T(8,128)(2,1)}, bf16[128,256]{1,0:T(8,128)(2,1)S(1)}, u32[]{:S(2)}, u32[]{:S(2)}) collective-permute-start(bf16[128,256]{1,0:T(8,128)(2,1)} %get-tuple-element.41), channel_id=1, source_target_pairs={{0,1},{1,0},{2,3},{3,2},{4,5},{5,4},{6,7},{7,6},{8,9},{9,8},{10,11... | collective-permute-start | bytes 196616 | tf_op jit(solution)/shard_map/ppermute | solution.py:274
  58.5 1.5 %collective-permute-start.21 = (bf16[128,256]{1,0:T(8,128)(2,1)}, bf16[128,256]{1,0:T(8,128)(2,1)S(1)}, u32[]{:S(2)}, u32[]{:S(2)}) collective-permute-start(bf16[128,256]{1,0:T(8,128)(2,1)} %get-tuple-element.45), channel_id=1, source_target_pairs={{0,1},{1,0},{2,3},{3,2},{4,5},{5,4},{6,7},{7,6},{8,9},{9,8},{10,11... | collective-permute-start | bytes 196616 | tf_op jit(solution)/shard_map/ppermute | solution.py:274
  58.9 4.3 %collective-permute-start.23 = (bf16[128,256]{1,0:T(8,128)(2,1)}, bf16[128,256]{1,0:T(8,128)(2,1)S(1)}, u32[]{:S(2)}, u32[]{:S(2)}) collective-permute-start(bf16[128,256]{1,0:T(8,128)(2,1)} %get-tuple-element.47), channel_id=1, source_target_pairs={{0,1},{1,0},{2,3},{3,2},{4,5},{5,4},{6,7},{7,6},{8,9},{9,8},{10,11... | collective-permute-start | bytes 196616 | tf_op jit(solution)/shard_map/ppermute | solution.py:274
  59.9 6.9 %collective-permute-start.20 = (bf16[128,256]{1,0:T(8,128)(2,1)S(1)}, bf16[128,256]{1,0:T(8,128)(2,1)S(1)}, u32[]{:S(2)}, u32[]{:S(2)}) collective-permute-start(bf16[128,256]{1,0:T(8,128)(2,1)S(1)} %add_convert_fusion.11), channel_id=1, source_target_pairs={{0,2},{1,3},{2,4},{3,5},{4,6},{5,7},{6,0},{7,1},{8,10},{9,11},{10,... | collective-permute-start | bytes 196616 | tf_op jit(solution)/shard_map/ppermute | solution.py:277
  60.9 8.2 %collective-permute-start.22 = (bf16[128,256]{1,0:T(8,128)(2,1)S(1)}, bf16[128,256]{1,0:T(8,128)(2,1)S(1)}, u32[]{:S(2)}, u32[]{:S(2)}) collective-permute-start(bf16[128,256]{1,0:T(8,128)(2,1)S(1)} %add_convert_fusion.10), channel_id=1, source_target_pairs={{0,4},{1,5},{2,6},{3,7},{4,0},{5,1},{6,2},{7,3},{8,12},{9,13},{10,... | collective-permute-start | bytes 196616 | tf_op jit(solution)/shard_map/ppermute | solution.py:277
  64.0 5.5 %collective-permute-start.24 = (bf16[128,256]{1,0:T(8,128)(2,1)S(1)}, bf16[128,256]{1,0:T(8,128)(2,1)S(1)}, u32[]{:S(2)}, u32[]{:S(2)}) collective-permute-start(bf16[128,256]{1,0:T(8,128)(2,1)S(1)} %add_convert_fusion.9), channel_id=1, source_target_pairs={{0,6},{1,7},{2,0},{3,1},{4,2},{5,3},{6,4},{7,5},{8,14},{9,15},{10,... | collective-permute-start | bytes 196616 | tf_op jit(solution)/shard_map/ppermute | solution.py:277
  66.8 2.7 %copy-start.22 = (bf16[128,256]{1,0:T(8,128)(2,1)}, bf16[128,256]{1,0:T(8,128)(2,1)S(1)}, u32[]{:S(2)}) copy-start(bf16[128,256]{1,0:T(8,128)(2,1)S(1)} %collective-permute-done.20.refs_1_) | copy-start | bytes 196612
  72.9 17.4 %copy-start.20 = (bf16[320,128]{1,0:T(8,128)(2,1)S(1)}, bf16[320,128]{1,0:T(8,128)(2,1)}, u32[]{:S(2)}) copy-start(bf16[320,128]{1,0:T(8,128)(2,1)} %get-tuple-element.64) | copy-start | bytes 245764
  72.9 4.4 %collective-permute-start.32 = (bf16[320,128]{1,0:T(8,128)(2,1)}, bf16[320,128]{1,0:T(8,128)(2,1)S(1)}, u32[]{:S(2)}, u32[]{:S(2)}) collective-permute-start(bf16[320,128]{1,0:T(8,128)(2,1)} %get-tuple-element.59), channel_id=1, source_target_pairs={{0,1},{1,0},{2,3},{3,2},{4,5},{5,4},{6,7},{7,6},{8,9},{9,8},{10,11... | collective-permute-start | bytes 245768 | tf_op jit(solution)/shard_map/ppermute | solution.py:274
  76.2 16.2 %copy-start.6 = (bf16[960,128]{1,0:T(8,128)(2,1)S(1)}, bf16[960,128]{1,0:T(8,128)(2,1)}, u32[]{:S(2)}) copy-start(bf16[960,128]{1,0:T(8,128)(2,1)} %get-tuple-element.50) | copy-start | bytes 737284
  76.2 14.1 %collective-permute-start.25 = (bf16[960,128]{1,0:T(8,128)(2,1)}, bf16[960,128]{1,0:T(8,128)(2,1)S(1)}, u32[]{:S(2)}, u32[]{:S(2)}) collective-permute-start(bf16[960,128]{1,0:T(8,128)(2,1)} %get-tuple-element.51), channel_id=1, source_target_pairs={{0,1},{1,0},{2,3},{3,2},{4,5},{5,4},{6,7},{7,6},{8,9},{9,8},{10,11... | collective-permute-start | bytes 737288 | tf_op jit(solution)/shard_map/ppermute | solution.py:274
  76.7 5.3 %collective-permute-start.26 = (bf16[960,128]{1,0:T(8,128)(2,1)}, bf16[960,128]{1,0:T(8,128)(2,1)S(1)}, u32[]{:S(2)}, u32[]{:S(2)}) collective-permute-start(bf16[960,128]{1,0:T(8,128)(2,1)} %get-tuple-element.53), channel_id=1, source_target_pairs={{0,1},{1,0},{2,3},{3,2},{4,5},{5,4},{6,7},{7,6},{8,9},{9,8},{10,11... | collective-permute-start | bytes 737288 | tf_op jit(solution)/shard_map/ppermute | solution.py:274
  76.8 7.7 %collective-permute-start.28 = (bf16[960,128]{1,0:T(8,128)(2,1)}, bf16[960,128]{1,0:T(8,128)(2,1)S(1)}, u32[]{:S(2)}, u32[]{:S(2)}) collective-permute-start(bf16[960,128]{1,0:T(8,128)(2,1)} %get-tuple-element.55), channel_id=1, source_target_pairs={{0,1},{1,0},{2,3},{3,2},{4,5},{5,4},{6,7},{7,6},{8,9},{9,8},{10,11... | collective-permute-start | bytes 737288 | tf_op jit(solution)/shard_map/ppermute | solution.py:274
  77.2 9.0 %collective-permute-start.30 = (bf16[960,128]{1,0:T(8,128)(2,1)}, bf16[960,128]{1,0:T(8,128)(2,1)S(1)}, u32[]{:S(2)}, u32[]{:S(2)}) collective-permute-start(bf16[960,128]{1,0:T(8,128)(2,1)} %get-tuple-element.57), channel_id=1, source_target_pairs={{0,1},{1,0},{2,3},{3,2},{4,5},{5,4},{6,7},{7,6},{8,9},{9,8},{10,11... | collective-permute-start | bytes 737288 | tf_op jit(solution)/shard_map/ppermute | solution.py:274
  77.3 2.0 %collective-permute-start.33 = (bf16[320,128]{1,0:T(8,128)(2,1)}, bf16[320,128]{1,0:T(8,128)(2,1)S(1)}, u32[]{:S(2)}, u32[]{:S(2)}) collective-permute-start(bf16[320,128]{1,0:T(8,128)(2,1)} %get-tuple-element.61), channel_id=1, source_target_pairs={{0,1},{1,0},{2,3},{3,2},{4,5},{5,4},{6,7},{7,6},{8,9},{9,8},{10,11... | collective-permute-start | bytes 245768 | tf_op jit(solution)/shard_map/ppermute | solution.py:274
  79.3 1.5 %collective-permute-start.35 = (bf16[320,128]{1,0:T(8,128)(2,1)}, bf16[320,128]{1,0:T(8,128)(2,1)S(1)}, u32[]{:S(2)}, u32[]{:S(2)}) collective-permute-start(bf16[320,128]{1,0:T(8,128)(2,1)} %get-tuple-element.63), channel_id=1, source_target_pairs={{0,1},{1,0},{2,3},{3,2},{4,5},{5,4},{6,7},{7,6},{8,9},{9,8},{10,11... | collective-permute-start | bytes 245768 | tf_op jit(solution)/shard_map/ppermute | solution.py:274
  80.8 8.0 %collective-permute-start.37 = (bf16[320,128]{1,0:T(8,128)(2,1)}, bf16[320,128]{1,0:T(8,128)(2,1)S(1)}, u32[]{:S(2)}, u32[]{:S(2)}) collective-permute-start(bf16[320,128]{1,0:T(8,128)(2,1)} %get-tuple-element.65), channel_id=1, source_target_pairs={{0,1},{1,0},{2,3},{3,2},{4,5},{5,4},{6,7},{7,6},{8,9},{9,8},{10,11... | collective-permute-start | bytes 245768 | tf_op jit(solution)/shard_map/ppermute | solution.py:274
  82.0 9.2 %collective-permute-start.34 = (bf16[320,128]{1,0:T(8,128)(2,1)S(1)}, bf16[320,128]{1,0:T(8,128)(2,1)S(1)}, u32[]{:S(2)}, u32[]{:S(2)}) collective-permute-start(bf16[320,128]{1,0:T(8,128)(2,1)S(1)} %add_convert_fusion.7), channel_id=1, source_target_pairs={{0,8},{8,0},{16,24},{24,16},{1,9},{9,1},{17,25},{25,17},{2,10},{10... | collective-permute-start | bytes 245768 | tf_op jit(solution)/shard_map/ppermute | solution.py:282
  84.5 18.0 %collective-permute-start.27 = (bf16[960,128]{1,0:T(8,128)(2,1)S(1)}, bf16[960,128]{1,0:T(8,128)(2,1)S(1)}, u32[]{:S(2)}, u32[]{:S(2)}) collective-permute-start(bf16[960,128]{1,0:T(8,128)(2,1)S(1)} %add_convert_fusion.2), channel_id=1, source_target_pairs={{0,8},{8,0},{16,24},{24,16},{1,9},{9,1},{17,25},{25,17},{2,10},{10... | collective-permute-start | bytes 737288 | tf_op jit(solution)/shard_map/ppermute | solution.py:282
  86.2 16.3 %collective-permute-start.29 = (bf16[960,128]{1,0:T(8,128)(2,1)S(1)}, bf16[960,128]{1,0:T(8,128)(2,1)S(1)}, u32[]{:S(2)}, u32[]{:S(2)}) collective-permute-start(bf16[960,128]{1,0:T(8,128)(2,1)S(1)} %add_convert_fusion.1), channel_id=1, source_target_pairs={{0,16},{8,24},{16,0},{24,8},{1,17},{9,25},{17,1},{25,9},{2,18},{10... | collective-permute-start | bytes 737288 | tf_op jit(solution)/shard_map/ppermute | solution.py:282
  88.8 13.8 %collective-permute-start.31 = (bf16[960,128]{1,0:T(8,128)(2,1)S(1)}, bf16[960,128]{1,0:T(8,128)(2,1)S(1)}, u32[]{:S(2)}, u32[]{:S(2)}) collective-permute-start(bf16[960,128]{1,0:T(8,128)(2,1)S(1)} %add_convert_fusion), channel_id=1, source_target_pairs={{0,24},{8,16},{16,8},{24,0},{1,25},{9,17},{17,9},{25,1},{2,26},{10... | collective-permute-start | bytes 737288 | tf_op jit(solution)/shard_map/ppermute | solution.py:282
  90.3 12.3 %collective-permute-start.36 = (bf16[320,128]{1,0:T(8,128)(2,1)S(1)}, bf16[320,128]{1,0:T(8,128)(2,1)S(1)}, u32[]{:S(2)}, u32[]{:S(2)}) collective-permute-start(bf16[320,128]{1,0:T(8,128)(2,1)S(1)} %add_convert_fusion.6), channel_id=1, source_target_pairs={{0,16},{8,24},{16,0},{24,8},{1,17},{9,25},{17,1},{25,9},{2,18},{10... | collective-permute-start | bytes 245768 | tf_op jit(solution)/shard_map/ppermute | solution.py:282
  91.3 11.3 %copy-start.14 = (bf16[320,128]{1,0:T(8,128)(2,1)}, bf16[320,128]{1,0:T(8,128)(2,1)S(1)}, u32[]{:S(2)}) copy-start(bf16[320,128]{1,0:T(8,128)(2,1)S(1)} %collective-permute-done.34.refs_5_) | copy-start | bytes 245764
  91.3 11.3 %collective-permute-start.38 = (bf16[320,128]{1,0:T(8,128)(2,1)S(1)}, bf16[320,128]{1,0:T(8,128)(2,1)S(1)}, u32[]{:S(2)}, u32[]{:S(2)}) collective-permute-start(bf16[320,128]{1,0:T(8,128)(2,1)S(1)} %add_convert_fusion.5), channel_id=1, source_target_pairs={{0,24},{8,16},{16,8},{24,0},{1,25},{9,17},{17,9},{25,1},{2,26},{10... | collective-permute-start | bytes 245768 | tf_op jit(solution)/shard_map/ppermute | solution.py:282
  102.6 0.8 copy-start.4
  106.5 6.9 %collective-permute-start.39 = (bf16[320,128]{1,0:T(8,128)(2,1)}, bf16[320,128]{1,0:T(8,128)(2,1)S(1)}, u32[]{:S(2)}, u32[]{:S(2)}) collective-permute-start(bf16[320,128]{1,0:T(8,128)(2,1)} %get-tuple-element.67), channel_id=1, source_target_pairs={{0,2},{1,3},{2,4},{3,5},{4,6},{5,7},{6,0},{7,1},{8,10},{9,11},{10,... | collective-permute-start | bytes 245768 | tf_op jit(solution)/shard_map/ppermute | solution.py:277
  107.8 8.1 %collective-permute-start.40 = (bf16[320,128]{1,0:T(8,128)(2,1)}, bf16[320,128]{1,0:T(8,128)(2,1)S(1)}, u32[]{:S(2)}, u32[]{:S(2)}) collective-permute-start(bf16[320,128]{1,0:T(8,128)(2,1)} %get-tuple-element.68), channel_id=1, source_target_pairs={{0,4},{1,5},{2,6},{3,7},{4,0},{5,1},{6,2},{7,3},{8,12},{9,13},{10,... | collective-permute-start | bytes 245768 | tf_op jit(solution)/shard_map/ppermute | solution.py:277
  109.7 6.2 %collective-permute-start.41 = (bf16[320,128]{1,0:T(8,128)(2,1)}, bf16[320,128]{1,0:T(8,128)(2,1)S(1)}, u32[]{:S(2)}, u32[]{:S(2)}) collective-permute-start(bf16[320,128]{1,0:T(8,128)(2,1)} %get-tuple-element.69), channel_id=1, source_target_pairs={{0,6},{1,7},{2,0},{3,1},{4,2},{5,3},{6,4},{7,5},{8,14},{9,15},{10,... | collective-permute-start | bytes 245768 | tf_op jit(solution)/shard_map/ppermute | solution.py:277
  116.8 7.8 %copy-start.1 = (bf16[320,128]{1,0:T(8,128)(2,1)}, bf16[320,128]{1,0:T(8,128)(2,1)S(1)}, u32[]{:S(2)}) copy-start(bf16[320,128]{1,0:T(8,128)(2,1)S(1)} %add_convert_fusion.4.refs_0_) | copy-start | bytes 245764
  116.8 7.8 %collective-permute-start.44 = (bf16[320,128]{1,0:T(8,128)(2,1)S(1)}, bf16[320,128]{1,0:T(8,128)(2,1)S(1)}, u32[]{:S(2)}, u32[]{:S(2)}) collective-permute-start(bf16[320,128]{1,0:T(8,128)(2,1)S(1)} %add_convert_fusion.4.refs_0_), channel_id=1, source_target_pairs={{0,24},{8,16},{16,8},{24,0},{1,25},{9,17},{17,9},{25,1},{2,26},{10... | collective-permute-start | bytes 245768 | tf_op jit(solution)/shard_map/ppermute | solution.py:282
  118.6 6.0 %collective-permute-start.43 = (bf16[320,128]{1,0:T(8,128)(2,1)S(1)}, bf16[320,128]{1,0:T(8,128)(2,1)S(1)}, u32[]{:S(2)}, u32[]{:S(2)}) collective-permute-start(bf16[320,128]{1,0:T(8,128)(2,1)S(1)} %add_convert_fusion.4.refs_0_), channel_id=1, source_target_pairs={{0,16},{8,24},{16,0},{24,8},{1,17},{9,25},{17,1},{25,9},{2,18},{10... | collective-permute-start | bytes 245768 | tf_op jit(solution)/shard_map/ppermute | solution.py:282
  119.8 4.9 %collective-permute-start.42 = (bf16[320,128]{1,0:T(8,128)(2,1)S(1)}, bf16[320,128]{1,0:T(8,128)(2,1)S(1)}, u32[]{:S(2)}, u32[]{:S(2)}) collective-permute-start(bf16[320,128]{1,0:T(8,128)(2,1)S(1)} %add_convert_fusion.4.refs_0_), channel_id=1, source_target_pairs={{0,8},{8,0},{16,24},{24,16},{1,9},{9,1},{17,25},{25,17},{2,10},{10... | collective-permute-start | bytes 245768 | tf_op jit(solution)/shard_map/ppermute | solution.py:282
  (14 other events, 9.1 us)

commit v2 on v1

v2 whole, which is shorter than its diff:
```python
import functools
import math

import jax
import jax.numpy as jnp
from jax import lax
from jax.experimental import pallas as pl
from jax.experimental.pallas import tpu as pltpu
from jax.sharding import PartitionSpec as P

HD = 128
BLK = 128
QPG = 8
GROUPS = 1
SPAN = 64
NBR = 8
NCB = 10
NNZ = 80
NQ = GROUPS * QPG
KEYS = 128
EPSILON = 1e-06
SCALE = 1.0 / math.sqrt(HD)
LOG2E = math.log2(math.e)

F32 = jnp.float32
BF16 = jnp.bfloat16
VMEM = pl.BlockSpec(memory_space=pltpu.VMEM)
SMEM = pl.BlockSpec(memory_space=pltpu.SMEM)
ANY = pl.BlockSpec(memory_space=pl.ANY)


def nbytes(shape, dtype):
    return math.prod(shape) * jnp.dtype(dtype).itemsize


def call(kernel, scalars, arrays, outs, scratch=(), wait=(), flops=0, moved=0, exps=0):
    def body(*refs):
        at = len(scalars) + len(arrays)
        kernel(*refs[:at], *refs[at + len(wait) :])

    held = [(v.shape, v.dtype) for v in arrays] + [(s, t) for s, t in outs]
    held += [(v.shape, v.dtype) for v in scratch]
    need = sum(nbytes(s, t) for s, t in held)
    return pl.pallas_call(
        body,
        in_specs=[SMEM] * len(scalars) + [VMEM] * len(arrays) + [ANY] * len(wait),
        out_specs=[SMEM if t == jnp.int32 else VMEM for _, t in outs],
        out_shape=[jax.ShapeDtypeStruct(s, t) for s, t in outs],
        scratch_shapes=list(scratch),
        compiler_params=pltpu.CompilerParams(vmem_limit_bytes=need + need // 4 + 4 * 2**20),
        cost_estimate=pl.CostEstimate(flops=flops, bytes_accessed=moved, transcendentals=exps),
    )(*scalars, *arrays, *wait)


def dot(a, b, contract=((1,), (0,))):
    return lax.dot_general(a, b, (contract, ((), ())), preferred_element_type=F32)


def rows_at(start, size, step):
    return pl.ds(pl.multiple_of(start, step), size)


def inverse_rms(values):
    return lax.rsqrt(jnp.mean(values * values, axis=-1, keepdims=True) + EPSILON)


def norm_backward(values, factor, upstream):
    return factor * upstream - values * (factor * factor * factor) * jnp.mean(
        upstream * values, axis=-1, keepdims=True
    )


def prepare_kernel(ids, spans, x_ref, xt_ref, ids_out, spans_out):
    for b in range(x_ref.shape[1] // BLK):
        xt_ref[b * BLK : (b + 1) * BLK, :] = x_ref[:, b * BLK : (b + 1) * BLK].T
    for source, out in ((ids, ids_out), (spans, spans_out)):

        @pl.loop(0, source.shape[0])
        def _(i):
            for j in range(source.shape[1]):
                out[i, j] = source[i, j]


def arrange_kernel(z_lo, z_hi, *refs):
    pieces, out = refs[:-1], refs[-1]
    nz, rows = len(pieces), pieces[0].shape[0]
    me = lax.axis_index("ctx") // 2
    for z in range(z_lo, z_hi):
        at = (z - z_lo) * rows
        for k in range(nz):

            @pl.when(lax.rem(me + nz - k, nz) == z)
            def _():
                out[at : at + rows, :] = pieces[k][...]


def join_pieces(pieces, z_count, shard, piece, w_ref):
    core, dp = lax.axis_index("ctx") % 2, lax.axis_index("dp")
    for n, ref in enumerate(pieces):
        k, parity = n // 2, core if n % 2 == 0 else 1 - core
        for z in range(z_count):
            at = z * 2 * shard + parity * shard + lax.bitwise_xor(dp, k) * piece
            w_ref[rows_at(at, piece, 16), :] = ref[z * piece : (z + 1) * piece, :]


def column_of(c, ids, x_ref):
    return jnp.concatenate(
        [x_ref[:, rows_at(ids[c, r] * BLK, BLK, BLK)] for r in range(NBR)], axis=1
    )


def project_keys(ids, x_ref, w_ref, first, kv_ref, key_ref):
    wide = NBR * BLK
    for c in range(NQ, NCB):
        at = c * wide - first
        out = dot(column_of(c, ids, x_ref), w_ref[at : at + wide, :]).astype(BF16)
        if c == NQ:
            key = out.astype(F32)
            key_ref[...] = out
            kv_ref[:, :HD] = (key * inverse_rms(key)).astype(BF16)
        else:
            kv_ref[:, HD:] = out


def project_queries(ids, x_ref, rows_of, q_ref):
    wide = NBR * BLK
    for c in range(NQ):
        out = dot(column_of(c, ids, x_ref), rows_of(c * wide, (c + 1) * wide)).astype(BF16)
        for p in range(2):
            at = (p * NQ + c) * SPAN
            q_ref[at : at + SPAN, :] = out[p * SPAN : (p + 1) * SPAN, :]


def keys_kernel(z_count, shard, piece, ids, x_ref, *refs):
    pieces, (w_ref, kv_ref, key_ref) = refs[:-3], refs[-3:]
    join_pieces(pieces, z_count, shard, piece, w_ref)
    project_keys(ids, x_ref, w_ref, NNZ * BLK - z_count * 2 * shard, kv_ref, key_ref)


def queries_kernel(z_count, shard, piece, ids, x_ref, tail_ref, *refs):
    pieces, (w_ref, q_ref) = refs[:-2], refs[-2:]
    join_pieces(pieces, z_count, shard, piece, w_ref)
    cut = z_count * 2 * shard

    def rows_of(lo, hi):
        if hi <= cut:
            return w_ref[lo:hi, :]
        if lo >= cut:
            return tail_ref[lo - cut : hi - cut, :]
        return jnp.concatenate([w_ref[lo:cut, :], tail_ref[0 : hi - cut, :]], axis=0)

    project_queries(ids, x_ref, rows_of, q_ref)


def project_kernel(ids, x_ref, w_ref, q_ref, kv_ref, key_ref):
    project_keys(ids, x_ref, w_ref, 0, kv_ref, key_ref)
    project_queries(ids, x_ref, lambda lo, hi: w_ref[lo:hi, :], q_ref)


def attend_kernel(nz, spans, q_ref, up_ref, *refs):
    pieces = refs[: 2 * nz]
    dq_ref = refs[2 * nz]
    keep = refs[2 * nz + 1 : 3 * nz + 1]
    send = refs[3 * nz + 1 : 4 * nz + 1]
    kv, qhat, up, expo, dprob, acc, dq_t = refs[4 * nz + 1 :]
    half = NQ * SPAN
    me = lax.axis_index("ctx")
    zi, core = me // 2, me % 2
    for k in range(nz):
        z_from = lax.rem(zi + nz - k, nz)
        for other in range(2):
            source = z_from * 2 + (core if other == 0 else 1 - core)
            for p in range(2):
                kv[rows_at(spans[source, p] * SPAN, SPAN, SPAN), :] = pieces[2 * k + other][
                    p * SPAN : (p + 1) * SPAN, :
                ]
    query = q_ref[...].astype(F32)
    qhat[...] = (query * inverse_rms(query)).astype(BF16)
    for p in range(2):
        for h in range(NQ):
            at = (p * NQ + h) * SPAN
            up[at : at + SPAN, :] = up_ref[p * SPAN : (p + 1) * SPAN, h * HD : (h + 1) * HD]
    acc[...] = jnp.zeros_like(acc)
    key_row = lax.broadcasted_iota(jnp.int32, (KEYS, half), 0)
    query_at = lax.broadcasted_iota(jnp.int32, (KEYS, half), 1) % SPAN
    for p in range(2):
        span = spans[me, p]
        blocks = ((span + 1) * SPAN + KEYS - 1) // KEYS
        q_part = qhat[p * half : (p + 1) * half, :]
        up_part = up[p * half : (p + 1) * half, :]
        limit = query_at + span * SPAN

        def forward(b, sums):
            rows = rows_at(b * KEYS, KEYS, KEYS)
            raw = dot(kv[rows, :HD], q_part, ((1,), (1,)))
            e = jnp.where(key_row + b * KEYS <= limit, jnp.exp2(raw * (SCALE * LOG2E)), 0.0)
            dp = dot(kv[rows, HD:], up_part, ((1,), (1,)))
            expo[rows, :] = e
            dprob[rows, :] = dp
            weighted = e.astype(BF16).astype(F32) * dp
            return (
                sums[0] + jnp.sum(e.reshape(KEYS // 8, 8, half), axis=0),
                sums[1] + jnp.sum(weighted.reshape(KEYS // 8, 8, half), axis=0),
            )

        zero = jnp.zeros((8, half), F32)
        total, weighted = lax.fori_loop(0, blocks, forward, (zero, zero))
        inverse = 1.0 / jnp.sum(total, axis=0, keepdims=True)
        delta = jnp.sum(weighted, axis=0, keepdims=True) * inverse
        dq_t[...] = jnp.zeros_like(dq_t)

        def backward(b, carry):
            rows = rows_at(b * KEYS, KEYS, KEYS)
            prob = expo[rows, :] * inverse
            dscore = (prob * (dprob[rows, :] - delta) * SCALE).astype(BF16)
            acc[rows, :HD] += dot(dscore, q_part)
            acc[rows, HD:] += dot(prob.astype(BF16), up_part)
            dq_t[...] += dot(kv[rows, :HD].T, dscore)
            return carry

        lax.fori_loop(0, blocks, backward, 0)
        q_rows = q_ref[p * half : (p + 1) * half, :].astype(F32)
        dq = norm_backward(q_rows, inverse_rms(q_rows), dq_t[...].T).astype(BF16)
        for h in range(NQ):
            dq_ref[h, p * SPAN : (p + 1) * SPAN, :] = dq[h * SPAN : (h + 1) * SPAN, :]
    for k in range(nz):
        z_to = lax.rem(zi + k, nz)
        for p in range(2):
            part = slice(p * SPAN, (p + 1) * SPAN)
            for out, owner in ((keep[k], z_to * 2 + core), (send[k], z_to * 2 + 1 - core)):
                rows = rows_at(spans[owner, p] * SPAN, SPAN, SPAN)
                out[part, :] = acc[rows, :].astype(BF16)


def kv_grad_kernel(nz, key_ref, *refs):
    terms, dkv_ref = refs[:nz], refs[nz]
    total = terms[0][...].astype(F32)
    for term in terms[1:]:
        total = total + term[...].astype(F32)
    key = key_ref[...].astype(F32)
    dkv_ref[0, :, :] = norm_backward(key, inverse_rms(key), total[:, :HD]).astype(BF16)
    dkv_ref[1, :, :] = total[:, HD:].astype(BF16)


def terms_kernel(z_first, z_count, shard, piece, ids, xt, xt_other, *refs):
    tok = xt.shape[1]
    grads, work = refs[-2:]
    columns = grads.shape[0]
    first = z_first * 2 * shard // (NBR * BLK)
    ndp = shard // piece
    sources, outs = refs[: -2 - ndp], refs[-2 - ndp : -2]
    for n, ref in enumerate(sources):
        other = n % 2
        for i in range(ref.shape[0]):
            c = i - first if n < 2 else NQ + i - first
            if 0 <= c < columns:
                grads[c, other * tok : (other + 1) * tok, :] = ref[i]
    core, dp = lax.axis_index("ctx") % 2, lax.axis_index("dp")
    count = shard // BLK
    for z in range(z_count):
        for i in range(count):
            b = (2 * (z_first + z) + core) * count + i
            c = b // NBR
            rows = rows_at(ids[c, b % NBR] * BLK, BLK, BLK)
            picked = jnp.concatenate([xt[rows, :], xt_other[rows, :]], axis=1)
            at = (z * count + i) * BLK
            work[at : at + BLK, :] = dot(picked, grads[c - first]).astype(BF16)
    for k in range(ndp):
        for z in range(z_count):
            at = z * shard + lax.bitwise_xor(dp, k) * piece
            outs[k][z * piece : (z + 1) * piece, :] = work[rows_at(at, piece, 16), :]


def all_terms_kernel(ids, xt, dq_ref, dkv_ref, out_ref):
    for c in range(NCB):
        picked = jnp.concatenate(
            [xt[rows_at(ids[c, r] * BLK, BLK, BLK), :] for r in range(NBR)], axis=0
        )
        grad = dq_ref[c] if c < NQ else dkv_ref[c - NQ]
        out_ref[c * NBR * BLK : (c + 1) * NBR * BLK, :] = dot(picked, grad).astype(BF16)


def sum_kernel(ndp, nz, z_first, piece, *refs):
    head, tail = refs[:ndp], refs[ndp : 2 * ndp]
    outs, work = refs[2 * ndp : 2 * ndp + nz], refs[2 * ndp + nz]
    for group, first, count in ((head, 0, z_first), (tail, z_first, nz - z_first)):
        total = group[0][...].astype(F32)
        for term in group[1:]:
            total = total + term[...].astype(F32)
        work[first * piece : (first + count) * piece, :] = total.astype(BF16)
    for k in range(nz):
        at = lax.rem(lax.axis_index("ctx") // 2 + k, nz) * piece
        outs[k][...] = work[rows_at(at, piece, 16), :]


def place_kernel(piece, *refs):
    for k, ref in enumerate(refs[:-1]):
        at = lax.bitwise_xor(lax.axis_index("dp"), k) * piece
        refs[-1][rows_at(at, piece, 16), :] = ref[...].astype(F32)


def token_grad_kernel(ids, dq_ref, dkv_ref, *refs):
    parts, (out_ref, work) = refs[:-2], refs[-2:]
    wide = NBR * BLK
    cover = out_ref.shape[1] // wide
    first = 0
    done = 0
    for w_ref in parts:
        last = first + w_ref.shape[0] // BLK
        while done < last:
            c = done // NBR
            stop = min(last, (c + 1) * NBR)
            grad = dq_ref[c] if c < NQ else dkv_ref[c - NQ]
            spread = dot(grad, w_ref[(done - first) * BLK : (stop - first) * BLK, :], ((1,), (1,)))
            for b in range(done, stop):
                columns = rows_at(ids[c, b % NBR] * BLK, BLK, BLK)
                term = spread[:, (b - done) * BLK : (b - done + 1) * BLK]
                if c < cover:
                    work[:, columns] = term
                else:
                    work[:, columns] += term
            done = stop
        first = last
    out_ref[...] = work[...].astype(BF16)


def per_device(ndp, tokens, grad_attn, w_packed, ids, spans):
    nctx = lax.axis_size("ctx")
    nz = nctx // 2
    dp = lax.axis_index("dp")
    x, up = tokens[0], grad_attn[0]
    tok, width = x.shape
    length = spans.shape[0] * 2 * SPAN
    shard = w_packed.shape[0]
    piece = shard // ndp
    z_first = NQ * NBR * BLK // (2 * shard)
    z_last = nz - z_first
    cut = z_first * 2 * shard
    half = NQ * SPAN
    fast = shard % BLK == 0 and shard % (16 * ndp) == 0 and ndp & (ndp - 1) == 0

    def swap_core(v):
        return lax.ppermute(v, "ctx", [(i, i ^ 1) for i in range(nctx)])

    def shift_z(v, k):
        return lax.ppermute(
            v, "ctx", [(i, ((i // 2 + k) % nz) * 2 + i % 2) for i in range(nctx)]
        )

    def swap_dp(v, k):
        return lax.ppermute(v, "dp", [(i, i ^ k) for i in range(ndp)])

    def add(a, b):
        return (a.astype(F32) + b.astype(F32)).astype(BF16)

    xt, ids, spans = call(
        prepare_kernel,
        (ids, spans),
        (x,),
        [((width, tok), BF16), (ids.shape, jnp.int32), (spans.shape, jnp.int32)],
        moved=4 * x.size,
    )

    if fast:
        mine = lax.dynamic_slice_in_dim(w_packed, dp * piece, piece, 0)
        from_z = [mine] + [shift_z(mine, k) for k in range(1, nz)]

        def arrange(z_lo, z_hi, wait):
            return call(
                functools.partial(arrange_kernel, z_lo, z_hi),
                (),
                from_z,
                [(((z_hi - z_lo) * piece, BLK), BF16)],
                wait=wait,
                moved=4 * nz * piece * BLK,
            )[0]

        tail = arrange(z_first, nz, (ids,))
        tail = [tail] + [swap_dp(tail, k) for k in range(1, ndp)]
        head = arrange(0, z_first, tail[1:2])
        head = [head] + [swap_dp(head, k) for k in range(1, ndp)]
        w_tail, kv, key = call(
            functools.partial(keys_kernel, z_last, shard, piece),
            (ids,),
            [x] + [v for part in tail for v in (part, swap_core(part))],
            [((NNZ * BLK - cut, BLK), BF16), ((tok, 2 * HD), BF16), ((tok, HD), BF16)],
            flops=2 * tok * (NCB - NQ) * NBR * BLK * BLK,
            moved=3 * 2**20,
        )
        w_head, query = call(
            functools.partial(queries_kernel, z_first, shard, piece),
            (ids,),
            [x, w_tail] + [v for part in head for v in (part, swap_core(part))],
            [((cut, BLK), BF16), ((tok * NQ, HD), BF16)],
            flops=2 * tok * NQ * NBR * BLK * BLK,
            moved=6 * 2**20,
        )
        weights = [w_head, w_tail]
    else:
        weights = [lax.all_gather(w_packed, "ctx", axis=0, tiled=True)]
        query, kv, key = call(
            project_kernel,
            (ids,),
            (x, *weights),
            [((tok * NQ, HD), BF16), ((tok, 2 * HD), BF16), ((tok, HD), BF16)],
            flops=2 * tok * NNZ * BLK * BLK,
            moved=4 * 2**20,
        )

    kv_pieces = []
    for k in range(nz):
        part = kv if k == 0 else shift_z(kv, k)
        kv_pieces += [part, swap_core(part)]
    outs = call(
        functools.partial(attend_kernel, nz),
        (spans,),
        (query, up, *kv_pieces),
        [((NQ, tok, HD), BF16)] + [((tok, 2 * HD), BF16)] * (2 * nz),
        scratch=[
            pltpu.VMEM((length, 2 * HD), BF16),
            pltpu.VMEM((tok * NQ, HD), BF16),
            pltpu.VMEM((tok * NQ, HD), BF16),
            pltpu.VMEM((length, half), F32),
            pltpu.VMEM((length, half), F32),
            pltpu.VMEM((length, 2 * HD), F32),
            pltpu.VMEM((HD, half), F32),
        ],
        flops=10 * tok * NQ * length * HD // 2,
        moved=4 * 2**20,
        exps=tok * NQ * length // 2,
    )
    dq, keep, send = outs[0], outs[1 : nz + 1], outs[nz + 1 :]
    sums = [add(keep[k], swap_core(send[k])) for k in range(nz)]
    kv_terms = [sums[0]] + [shift_z(sums[k], k) for k in range(1, nz)]

    def weight_terms(z_lo, z_count, grads):
        first = z_lo * 2 * shard // (NBR * BLK)
        last = ((z_lo + z_count) * 2 * shard - 1) // (NBR * BLK)
        return call(
            functools.partial(terms_kernel, z_lo, z_count, shard, piece),
            (ids,),
            (xt, xt_other, *grads),
            [((z_count * piece, BLK), BF16)] * ndp,
            scratch=[
                pltpu.VMEM((last - first + 1, 2 * tok, HD), BF16),
                pltpu.VMEM((z_count * shard, BLK), BF16),
            ],
            flops=4 * tok * z_count * shard * BLK,
            moved=4 * 2**20,
        )

    if fast:
        xt_other = swap_core(xt)
        dq_pair = (dq, swap_core(dq))
        head = weight_terms(0, z_first, dq_pair)
        head = [head[0]] + [swap_dp(head[k], k) for k in range(1, ndp)]
    (dkv,) = call(
        functools.partial(kv_grad_kernel, nz),
        (),
        (key, *kv_terms),
        [((2, tok, HD), BF16)],
        moved=2**19,
    )
    if fast:
        tail = weight_terms(z_first, z_last, (*dq_pair, dkv, swap_core(dkv)))
        tail = [tail[0]] + [swap_dp(tail[k], k) for k in range(1, ndp)]
        by_z = call(
            functools.partial(sum_kernel, ndp, nz, z_first, piece),
            (),
            (*head, *tail),
            [((piece, BLK), BF16)] * nz,
            scratch=[pltpu.VMEM((nz * piece, BLK), BF16)],
            moved=2 * 2**20,
        )
        owned = by_z[0].astype(F32)
        for k in range(1, nz):
            owned = owned + shift_z(by_z[k], k).astype(F32)
        owned = owned.astype(BF16)
        (grad_weights,) = call(
            functools.partial(place_kernel, piece),
            (),
            [owned] + [swap_dp(owned, k) for k in range(1, ndp)],
            [((shard, BLK), F32)],
            moved=2**20,
        )
    else:
        (partial_w,) = call(
            all_terms_kernel,
            (ids,),
            (xt, dq, dkv),
            [((NNZ * BLK, BLK), BF16)],
            flops=2 * tok * NNZ * BLK * BLK,
            moved=4 * 2**20,
        )
        received = lax.all_to_all(
            partial_w.reshape(nctx, shard, BLK), "ctx", split_axis=0, concat_axis=0, tiled=True
        )
        grad_weights = lax.psum(jnp.sum(received.astype(F32), axis=0), "dp")

    (grad_tokens,) = call(
        token_grad_kernel,
        (ids,),
        (dq, dkv, *weights),
        [((tok, width), BF16)],
        scratch=[pltpu.VMEM((tok, width), F32)],
        flops=2 * tok * NNZ * BLK * BLK,
        moved=4 * 2**20,
    )
    return (grad_tokens[None], grad_weights)


def solution(mesh):
    in_specs = (P("dp", "ctx", None), P("dp", "ctx", None), P("ctx", None), P(), P())
    out_specs = (P("dp", "ctx", None), P("ctx", None))
    return jax.shard_map(
        functools.partial(per_device, mesh.shape["dp"]),
        mesh=mesh,
        in_specs=in_specs,
        out_specs=out_specs,
        check_vma=False,
    )
```

time: 129 us -> 102 us (0.79); the launches traced: 128 us -> 102 us
  other arithmetic: 11.9 us -> 0.12 us
  Pallas kernels: 29.2 us -> 17.8 us
  starting transfers between devices: 36.3 us -> 42.6 us
  local copies, waits for them, and re-layouts: 8.69 us -> 3.73 us
  waiting for transfers between devices: 40.6 us -> 37.2 us
    pallas_call x8 -> x12, Pallas kernels: 29.2 us -> 17.8 us  [call(): pl.pallas_call(body, in_specs=[SMEM] * len(scalars) + [VMEM] * len(arrays...]
    convert_element_type x12 -> x4, other arithmetic: 10.4 us -> 0.07 us  [add(): return (a.astype(F32) + b.astype(F32)).astype(BF16)]
    ppermute x12, waiting for transfers between devices: 20.7 us -> 13.2 us  [shift_z(): lax.ppermute(v, 'ctx', [(i, (i // 2 + k) % nz * 2 + i % 2) for i in range...]
    ppermute x12 -> x15, starting transfers between devices: 14.4 us -> 19.8 us  [swap_dp(): return lax.ppermute(v, 'dp', [(i, i ^ k) for i in range(ndp)])]
    ppermute x21 -> x19, waiting for transfers between devices: 0.59 us -> 3.22 us  [swap_core(): return lax.ppermute(v, 'ctx', [(i, i ^ 1) for i in range(nctx)])]
    unnamed x70 -> x10, local copies, waits for them, and re-layouts: 5.89 us -> 3.72 us
    ppermute x12, starting transfers between devices: 17.1 us -> 18.8 us  [shift_z(): lax.ppermute(v, 'ctx', [(i, (i // 2 + k) % nz * 2 + i % 2) for i in range...]
    ppermute x12 -> x15, waiting for transfers between devices: 19.3 us -> 20.8 us  [swap_dp(): return lax.ppermute(v, 'dp', [(i, i ^ k) for i in range(ndp)])]
  transfers between devices with their start and end apart: 45 -> 46, of which waited for: 14 -> 21; matrix products, arithmetic and copies ran while one was open for 11% -> 2% of each run, Pallas kernels for 8% -> 16%
where the time goes in v2:
time: 102 us
  starting transfers between devices  42.6 us (42%)
  waiting for transfers between devices  37.2 us (36%)
  Pallas kernels  17.8 us (17%)
  local copies, waits for them, and re-layouts  3.73 us (4%)
    ppermute x15, waiting for transfers between devices, swap_dp(): return lax.ppermute(v, 'dp', [(i, i ^ k) for i in range(ndp)])  20.8 us
    ppermute x15, starting transfers between devices, swap_dp(): return lax.ppermute(v, 'dp', [(i, i ^ k) for i in range(ndp)])  19.8 us
    ppermute x12, starting transfers between devices, shift_z(): lax.ppermute(v, 'ctx', [(i, (i // 2 + k) % nz * 2 + i % 2) for i in range...  18.8 us
    pallas_call x12, Pallas kernels, call(): pl.pallas_call(body, in_specs=[SMEM] * len(scalars) + [VMEM] * len(arrays...  17.8 us
    ppermute x12, waiting for transfers between devices, shift_z(): lax.ppermute(v, 'ctx', [(i, (i // 2 + k) % nz * 2 + i % 2) for i in range...  13.2 us
    ppermute x19, starting transfers between devices, swap_core(): return lax.ppermute(v, 'ctx', [(i, i ^ 1) for i in range(nctx)])  3.95 us
    unnamed x10, local copies, waits for them, and re-layouts  3.72 us
    ppermute x19, waiting for transfers between devices, swap_core(): return lax.ppermute(v, 'ctx', [(i, i ^ 1) for i in range(nctx)])  3.22 us
  transfers between devices with their start and end apart: 46, of which 21 were waited for; matrix products, arithmetic and copies ran while one was open for 2% of the time, Pallas kernels for 16%

profile of v2, /device:TPU:0, one launch (start us, length us, event | category | flops | bytes accessed | tf_op | source)
XLA Modules:
  0.0 102.2 jit_solution(2477606859235109897)
XLA Ops:
  0.6 1.0 copy-done
  1.6 3.0 %collective-permute-start = (bf16[320,128]{1,0:T(8,128)(2,1)S(1)}, bf16[320,128]{1,0:T(8,128)(2,1)S(1)}, u32[]{:S(2)}, u32[]{:S(2)}) collective-permute-start(bf16[320,128]{1,0:T(8,128)(2,1)S(1)} %constant_dynamic-slice_fusion.refs_0_), channel_id=1, source_target_pairs={{0,2},{1,3},{2,4},{3,5},{4,6},{5,7},{6,0},{7,1},{8,10},{9,11},{10,... | collective-permute-start | bytes 245768 | tf_op jit(solution)/shard_map/ppermute | solution.py:346
  4.6 2.6 %collective-permute-start.1 = (bf16[320,128]{1,0:T(8,128)(2,1)S(1)}, bf16[320,128]{1,0:T(8,128)(2,1)S(1)}, u32[]{:S(2)}, u32[]{:S(2)}) collective-permute-start(bf16[320,128]{1,0:T(8,128)(2,1)S(1)} %constant_dynamic-slice_fusion.refs_0_), channel_id=1, source_target_pairs={{0,4},{1,5},{2,6},{3,7},{4,0},{5,1},{6,2},{7,3},{8,12},{9,13},{10,... | collective-permute-start | bytes 245768 | tf_op jit(solution)/shard_map/ppermute | solution.py:346
  7.2 1.3 %collective-permute-start.2 = (bf16[320,128]{1,0:T(8,128)(2,1)S(1)}, bf16[320,128]{1,0:T(8,128)(2,1)S(1)}, u32[]{:S(2)}, u32[]{:S(2)}) collective-permute-start(bf16[320,128]{1,0:T(8,128)(2,1)S(1)} %constant_dynamic-slice_fusion.refs_0_), channel_id=1, source_target_pairs={{0,6},{1,7},{2,0},{3,1},{4,2},{5,3},{6,4},{7,5},{8,14},{9,15},{10,... | collective-permute-start | bytes 245768 | tf_op jit(solution)/shard_map/ppermute | solution.py:346
  8.6 0.8 copy.7.refs_0_
  9.3 0.8 copy.8.refs_1_
  10.1 1.2 %copy-done.1 = bf16[1,128,4096]{2,1,0:T(8,128)(2,1)S(1)} copy-done((bf16[1,128,4096]{2,1,0:T(8,128)(2,1)S(1)}, bf16[1,128,4096]{2,1,0:T(8,128)(2,1)}, u32[]{:S(2)}) %copy-start.1) | copy-done | bytes 1048600
  11.3 2.0 %shard_map.68 = (bf16[4096,128]{1,0:T(8,128)(2,1)S(1)}, s32[10,8]{1,0:T(8,128)S(1)}, s32[8,2]{1,0:T(8,128)S(1)}) custom-call(s32[10,8]{1,0:T(8,128)S(1)} %copy.7.refs_0_, s32[8,2]{1,0:T(8,128)S(1)} %copy.8.refs_1_, bf16[128,4096]{1,0:T(8,128)(2,1)S(1)} %bitcast.3), custom_call_target="tpu_custom_call" | custom-call | bytes 2097152 | tf_op jit(solution)/shard_map/pallas_call | solution.py:44
  13.4 1.6 %collective-permute-start.4 = (bf16[320,128]{1,0:T(8,128)(2,1)S(1)}, bf16[320,128]{1,0:T(8,128)(2,1)S(1)}, u32[]{:S(2)}, u32[]{:S(2)}) collective-permute-start(bf16[320,128]{1,0:T(8,128)(2,1)S(1)} %shard_map.69.refs_2_), channel_id=1, source_target_pairs={{0,8},{8,0},{16,24},{24,16},{1,9},{9,1},{17,25},{25,17},{2,10},{10... | collective-permute-start | bytes 245768 | tf_op jit(solution)/shard_map/ppermute | solution.py:351
  15.0 1.5 %collective-permute-start.6 = (bf16[320,128]{1,0:T(8,128)(2,1)S(1)}, bf16[320,128]{1,0:T(8,128)(2,1)S(1)}, u32[]{:S(2)}, u32[]{:S(2)}) collective-permute-start(bf16[320,128]{1,0:T(8,128)(2,1)S(1)} %shard_map.69.refs_2_), channel_id=1, source_target_pairs={{0,16},{8,24},{16,0},{24,8},{1,17},{9,25},{17,1},{25,9},{2,18},{10... | collective-permute-start | bytes 245768 | tf_op jit(solution)/shard_map/ppermute | solution.py:351
  16.5 1.4 %collective-permute-done.4.refs_4_ = bf16[320,128]{1,0:T(8,128)(2,1)S(1)} collective-permute-done((bf16[320,128]{1,0:T(8,128)(2,1)S(1)}, bf16[320,128]{1,0:T(8,128)(2,1)S(1)}, u32[]{:S(2)}, u32[]{:S(2)}) %collective-permute-start.4) | collective-permute-done | bytes 81952 | tf_op jit(solution)/shard_map/ppermute | solution.py:351
  18.0 1.6 %collective-permute-start.11 = (bf16[960,128]{1,0:T(8,128)(2,1)S(1)}, bf16[960,128]{1,0:T(8,128)(2,1)S(1)}, u32[]{:S(2)}, u32[]{:S(2)}) collective-permute-start(bf16[960,128]{1,0:T(8,128)(2,1)S(1)} %shard_map.71.refs_3_), channel_id=1, source_target_pairs={{0,8},{8,0},{16,24},{24,16},{1,9},{9,1},{17,25},{25,17},{2,10},{10... | collective-permute-start | bytes 737288 | tf_op jit(solution)/shard_map/ppermute | solution.py:351
  19.5 1.5 %collective-permute-start.13 = (bf16[960,128]{1,0:T(8,128)(2,1)S(1)}, bf16[960,128]{1,0:T(8,128)(2,1)S(1)}, u32[]{:S(2)}, u32[]{:S(2)}) collective-permute-start(bf16[960,128]{1,0:T(8,128)(2,1)S(1)} %shard_map.71.refs_3_), channel_id=1, source_target_pairs={{0,16},{8,24},{16,0},{24,8},{1,17},{9,25},{17,1},{25,9},{2,18},{10... | collective-permute-start | bytes 737288 | tf_op jit(solution)/shard_map/ppermute | solution.py:351
  21.1 0.5 collective-permute-start.15
  21.5 2.4 %collective-permute-start.8 = (bf16[320,128]{1,0:T(8,128)(2,1)S(1)}, bf16[320,128]{1,0:T(8,128)(2,1)S(1)}, u32[]{:S(2)}, u32[]{:S(2)}) collective-permute-start(bf16[320,128]{1,0:T(8,128)(2,1)S(1)} %shard_map.69.refs_2_), channel_id=1, source_target_pairs={{0,24},{8,16},{16,8},{24,0},{1,25},{9,17},{17,9},{25,1},{2,26},{10... | collective-permute-start | bytes 245768 | tf_op jit(solution)/shard_map/ppermute | solution.py:351
  24.0 7.9 %collective-permute-done.8.refs_8_ = bf16[320,128]{1,0:T(8,128)(2,1)S(1)} collective-permute-done((bf16[320,128]{1,0:T(8,128)(2,1)S(1)}, bf16[320,128]{1,0:T(8,128)(2,1)S(1)}, u32[]{:S(2)}, u32[]{:S(2)}) %collective-permute-start.8) | collective-permute-done | bytes 81952 | tf_op jit(solution)/shard_map/ppermute | solution.py:351
  31.9 0.5 collective-permute-start.9
  32.4 0.8 collective-permute-done.7.refs_7_
  33.4 1.0 %shard_map.70 = (bf16[2560,128]{1,0:T(8,128)(2,1)S(1)}, bf16[128,256]{1,0:T(8,128)(2,1)S(1)}, bf16[128,128]{1,0:T(8,128)(2,1)S(1)}) custom-call(s32[10,8]{1,0:T(8,128)S(1)} %get-tuple-element.31.refs_4_.refs_0_, bf16[128,4096]{1,0:T(8,128)(2,1)S(1)} %bitcast.4, bf16[320,128]{1,0:T(8,128)(2,1)S(1)} %shard_map.69.refs_2_, ...), custom_call_target="tpu_custom_call" | custom-call | flops 67108864 | bytes 3145728 | tf_op jit(solution)/shard_map/pallas_call | solution.py:44
  34.4 2.3 %collective-permute-start.18 = (bf16[128,256]{1,0:T(8,128)(2,1)S(1)}, bf16[128,256]{1,0:T(8,128)(2,1)S(1)}, u32[]{:S(2)}, u32[]{:S(2)}) collective-permute-start(bf16[128,256]{1,0:T(8,128)(2,1)S(1)} %get-tuple-element.35.refs_3_), channel_id=1, source_target_pairs={{0,2},{1,3},{2,4},{3,5},{4,6},{5,7},{6,0},{7,1},{8,10},{9,11},{10,... | collective-permute-start | bytes 196616 | tf_op jit(solution)/shard_map/ppermute | solution.py:346
  36.8 0.9 collective-permute-start.20
  37.7 3.5 %collective-permute-done.18.refs_5_ = bf16[128,256]{1,0:T(8,128)(2,1)S(1)} collective-permute-done((bf16[128,256]{1,0:T(8,128)(2,1)S(1)}, bf16[128,256]{1,0:T(8,128)(2,1)S(1)}, u32[]{:S(2)}, u32[]{:S(2)}) %collective-permute-start.18) | collective-permute-done | bytes 65568 | tf_op jit(solution)/shard_map/ppermute | solution.py:346
  41.2 0.5 collective-permute-start.12
  41.8 0.4 collective-permute-start.16
  42.2 1.2 %collective-permute-done.20.refs_7_ = bf16[128,256]{1,0:T(8,128)(2,1)S(1)} collective-permute-done((bf16[128,256]{1,0:T(8,128)(2,1)S(1)}, bf16[128,256]{1,0:T(8,128)(2,1)S(1)}, u32[]{:S(2)}, u32[]{:S(2)}) %collective-permute-start.20) | collective-permute-done | bytes 65568 | tf_op jit(solution)/shard_map/ppermute | solution.py:346
  43.4 1.2 %collective-permute-start.22 = (bf16[128,256]{1,0:T(8,128)(2,1)S(1)}, bf16[128,256]{1,0:T(8,128)(2,1)S(1)}, u32[]{:S(2)}, u32[]{:S(2)}) collective-permute-start(bf16[128,256]{1,0:T(8,128)(2,1)S(1)} %get-tuple-element.35.refs_3_), channel_id=1, source_target_pairs={{0,6},{1,7},{2,0},{3,1},{4,2},{5,3},{6,4},{7,5},{8,14},{9,15},{10,... | collective-permute-start | bytes 196616 | tf_op jit(solution)/shard_map/ppermute | solution.py:346
  44.7 3.0 %collective-permute-done.22.refs_9_ = bf16[128,256]{1,0:T(8,128)(2,1)S(1)} collective-permute-done((bf16[128,256]{1,0:T(8,128)(2,1)S(1)}, bf16[128,256]{1,0:T(8,128)(2,1)S(1)}, u32[]{:S(2)}, u32[]{:S(2)}) %collective-permute-start.22) | collective-permute-done | bytes 65568 | tf_op jit(solution)/shard_map/ppermute | solution.py:346
  47.7 0.5 collective-permute-start.17
  48.3 0.4 collective-permute-start.21
  48.8 1.6 %shard_map.72 = (bf16[7680,128]{1,0:T(8,128)(2,1)S(1)}, bf16[1024,128]{1,0:T(8,128)(2,1)S(1)}) custom-call(s32[10,8]{1,0:T(8,128)S(1)} %get-tuple-element.31.refs_4_.refs_0_, bf16[128,4096]{1,0:T(8,128)(2,1)S(1)} %bitcast.5, bf16[2560,128]{1,0:T(8,128)(2,1)S(1)} %get-tuple-element.33.refs_2_.refs_4_, bf16[960,128]{1,0:T(8,128)(2,1)S(1)} %shard_map.71.refs_3_, ...), custom_call_target="tpu_custom_call" | custom-call | flops 268435456 | bytes 6291456 | tf_op jit(solution)/shard_map/pallas_call | solution.py:44
  50.7 6.3 %shard_map.73 = (bf16[8,128,128]{2,1,0:T(8,128)(2,1)S(1)}, bf16[128,256]{1,0:T(8,128)(2,1)S(1)}, bf16[128,256]{1,0:T(8,128)(2,1)S(1)}, bf16[128,256]{1,0:T(8,128...) custom-call(s32[8,2]{1,0:T(8,128)S(1)} %get-tuple-element.32.refs_0_, ...), custom_call_target="tpu_custom_call" | custom-call | flops 671088640 | bytes 4194304 | tf_op jit(solution)/shard_map/pallas_call | solution.py:44
  57.0 0.2 collective-permute-start.25
  57.2 0.3 collective-permute-start.24
  57.6 0.2 collective-permute-start.27
  57.7 0.3 collective-permute-start.29
  58.1 0.2 collective-permute-done.25
  58.3 0.2 collective-permute-start.32
  58.5 0.3 collective-permute-done.27
  59.0 3.5 %collective-permute-start.28 = (bf16[128,256]{1,0:T(8,128)(2,1)S(1)}, bf16[128,256]{1,0:T(8,128)(2,1)S(1)}, u32[]{:S(2)}, u32[]{:S(2)}) collective-permute-start(bf16[128,256]{1,0:T(8,128)(2,1)S(1)} %add_convert_fusion.2), channel_id=1, source_target_pairs={{0,4},{1,5},{2,6},{3,7},{4,0},{5,1},{6,2},{7,3},{8,12},{9,13},{10,... | collective-permute-start | bytes 196616 | tf_op jit(solution)/shard_map/ppermute | solution.py:346
  62.6 0.3 collective-permute-start.30
  62.9 1.5 %shard_map.76 = (bf16[960,128]{1,0:T(8,128)(2,1)S(1)}, bf16[960,128]{1,0:T(8,128)(2,1)S(1)}, bf16[960,128]{1,0:T(8,128)(2,1)S(1)}, bf16[960,128]{1,0:T(8,128)(2,1)S(1)}) custom-call(s32[10,8]{1,0:T(8,128)S(1)} %get-tuple-element.31.refs_4_.refs_0_, bf16[4096,128]{1,0:T(8,128)(2,1)S(1)} %get-tuple-element.47.refs_1_, ...), custom_call_target="tpu_custom_call" | custom-call | flops 251658240 | bytes 4194304 | tf_op jit(solution)/shard_map/pallas_call | solution.py:44
  64.4 1.5 %collective-permute-start.33 = (bf16[960,128]{1,0:T(8,128)(2,1)S(1)}, bf16[960,128]{1,0:T(8,128)(2,1)S(1)}, u32[]{:S(2)}, u32[]{:S(2)}) collective-permute-start(bf16[960,128]{1,0:T(8,128)(2,1)S(1)} %get-tuple-element.49), channel_id=1, source_target_pairs={{0,8},{8,0},{16,24},{24,16},{1,9},{9,1},{17,25},{25,17},{2,10},{10... | collective-permute-start | bytes 737288 | tf_op jit(solution)/shard_map/ppermute | solution.py:351
  65.9 0.6 collective-permute-start.34
  66.5 1.4 %collective-permute-start.35 = (bf16[960,128]{1,0:T(8,128)(2,1)S(1)}, bf16[960,128]{1,0:T(8,128)(2,1)S(1)}, u32[]{:S(2)}, u32[]{:S(2)}) collective-permute-start(bf16[960,128]{1,0:T(8,128)(2,1)S(1)} %get-tuple-element.51), channel_id=1, source_target_pairs={{0,24},{8,16},{16,8},{24,0},{1,25},{9,17},{17,9},{25,1},{2,26},{10... | collective-permute-start | bytes 737288 | tf_op jit(solution)/shard_map/ppermute | solution.py:351
  68.2 1.2 %collective-permute-done.36.refs_6_ = bf16[2,128,128]{2,1,0:T(8,128)(2,1)S(1)} collective-permute-done((bf16[2,128,128]{2,1,0:T(8,128)(2,1)S(1)}, bf16[2,128,128]{2,1,0:T(8,128)(2,1)S(1)}, u32[]{:S(2)}, u32[]{:S(2)}) %collective-permute-start.36) | collective-permute-done | bytes 65568 | tf_op jit(solution)/shard_map/ppermute | solution.py:343
  69.4 1.0 %shard_map.77 = (bf16[320,128]{1,0:T(8,128)(2,1)S(1)}, bf16[320,128]{1,0:T(8,128)(2,1)S(1)}, bf16[320,128]{1,0:T(8,128)(2,1)S(1)}, bf16[320,128]{1,0:T(8,128)(2,1)S(1)}) custom-call(s32[10,8]{1,0:T(8,128)S(1)} %get-tuple-element.31.refs_4_.refs_0_, bf16[4096,128]{1,0:T(8,128)(2,1)S(1)} %get-tuple-element.47.refs_1_, ...), custom_call_target="tpu_custom_call" | custom-call | flops 83886080 | bytes 4194304 | tf_op jit(solution)/shard_map/pallas_call | solution.py:44
  70.5 1.5 %collective-permute-start.37 = (bf16[320,128]{1,0:T(8,128)(2,1)S(1)}, bf16[320,128]{1,0:T(8,128)(2,1)S(1)}, u32[]{:S(2)}, u32[]{:S(2)}) collective-permute-start(bf16[320,128]{1,0:T(8,128)(2,1)S(1)} %get-tuple-element.53), channel_id=1, source_target_pairs={{0,8},{8,0},{16,24},{24,16},{1,9},{9,1},{17,25},{25,17},{2,10},{10... | collective-permute-start | bytes 245768 | tf_op jit(solution)/shard_map/ppermute | solution.py:351
  72.0 0.6 collective-permute-start.38
  72.6 6.6 %collective-permute-done.37.refs_5_ = bf16[320,128]{1,0:T(8,128)(2,1)S(1)} collective-permute-done((bf16[320,128]{1,0:T(8,128)(2,1)S(1)}, bf16[320,128]{1,0:T(8,128)(2,1)S(1)}, u32[]{:S(2)}, u32[]{:S(2)}) %collective-permute-start.37) | collective-permute-done | bytes 81952 | tf_op jit(solution)/shard_map/ppermute | solution.py:351
  79.3 1.5 %collective-permute-start.39 = (bf16[320,128]{1,0:T(8,128)(2,1)S(1)}, bf16[320,128]{1,0:T(8,128)(2,1)S(1)}, u32[]{:S(2)}, u32[]{:S(2)}) collective-permute-start(bf16[320,128]{1,0:T(8,128)(2,1)S(1)} %get-tuple-element.55), channel_id=1, source_target_pairs={{0,24},{8,16},{16,8},{24,0},{1,25},{9,17},{17,9},{25,1},{2,26},{10... | collective-permute-start | bytes 245768 | tf_op jit(solution)/shard_map/ppermute | solution.py:351
  80.7 3.9 %collective-permute-done.39.refs_7_ = bf16[320,128]{1,0:T(8,128)(2,1)S(1)} collective-permute-done((bf16[320,128]{1,0:T(8,128)(2,1)S(1)}, bf16[320,128]{1,0:T(8,128)(2,1)S(1)}, u32[]{:S(2)}, u32[]{:S(2)}) %collective-permute-start.39) | collective-permute-done | bytes 81952 | tf_op jit(solution)/shard_map/ppermute | solution.py:351
  84.6 0.3 shard_map.78
  84.9 1.0 collective-permute-start.42
  85.9 1.7 %collective-permute-start.41 = (bf16[320,128]{1,0:T(8,128)(2,1)S(1)}, bf16[320,128]{1,0:T(8,128)(2,1)S(1)}, u32[]{:S(2)}, u32[]{:S(2)}) collective-permute-start(bf16[320,128]{1,0:T(8,128)(2,1)S(1)} %get-tuple-element.58), channel_id=1, source_target_pairs={{0,4},{1,5},{2,6},{3,7},{4,0},{5,1},{6,2},{7,3},{8,12},{9,13},{10,... | collective-permute-start | bytes 245768 | tf_op jit(solution)/shard_map/ppermute | solution.py:346
  87.6 0.8 collective-permute-start.40
  88.4 1.9 %collective-permute-done.42 = bf16[320,128]{1,0:T(8,128)(2,1)S(1)} collective-permute-done((bf16[320,128]{1,0:T(8,128)(2,1)S(1)}, bf16[320,128]{1,0:T(8,128)(2,1)S(1)}, u32[]{:S(2)}, u32[]{:S(2)}) %collective-permute-start.42) | collective-permute-done | bytes 81952 | tf_op jit(solution)/shard_map/ppermute | solution.py:346
  90.3 1.9 %collective-permute-done.41 = bf16[320,128]{1,0:T(8,128)(2,1)S(1)} collective-permute-done((bf16[320,128]{1,0:T(8,128)(2,1)S(1)}, bf16[320,128]{1,0:T(8,128)(2,1)S(1)}, u32[]{:S(2)}, u32[]{:S(2)}) %collective-permute-start.41) | collective-permute-done | bytes 81952 | tf_op jit(solution)/shard_map/ppermute | solution.py:346
  92.2 1.6 %collective-permute-done.40 = bf16[320,128]{1,0:T(8,128)(2,1)S(1)} collective-permute-done((bf16[320,128]{1,0:T(8,128)(2,1)S(1)}, bf16[320,128]{1,0:T(8,128)(2,1)S(1)}, u32[]{:S(2)}, u32[]{:S(2)}) %collective-permute-start.40) | collective-permute-done | bytes 81952 | tf_op jit(solution)/shard_map/ppermute | solution.py:346
  93.9 1.6 %collective-permute-start.43 = (bf16[320,128]{1,0:T(8,128)(2,1)S(1)}, bf16[320,128]{1,0:T(8,128)(2,1)S(1)}, u32[]{:S(2)}, u32[]{:S(2)}) collective-permute-start(bf16[320,128]{1,0:T(8,128)(2,1)S(1)} %add_convert_fusion.refs_0_), channel_id=1, source_target_pairs={{0,8},{8,0},{16,24},{24,16},{1,9},{9,1},{17,25},{25,17},{2,10},{10... | collective-permute-start | bytes 245768 | tf_op jit(solution)/shard_map/ppermute | solution.py:351
  95.5 0.6 collective-permute-start.44
  96.0 1.4 %collective-permute-start.45 = (bf16[320,128]{1,0:T(8,128)(2,1)S(1)}, bf16[320,128]{1,0:T(8,128)(2,1)S(1)}, u32[]{:S(2)}, u32[]{:S(2)}) collective-permute-start(bf16[320,128]{1,0:T(8,128)(2,1)S(1)} %add_convert_fusion.refs_0_), channel_id=1, source_target_pairs={{0,24},{8,16},{16,8},{24,0},{1,25},{9,17},{17,9},{25,1},{2,26},{10... | collective-permute-start | bytes 245768 | tf_op jit(solution)/shard_map/ppermute | solution.py:351
  97.4 3.0 %shard_map.75 = bf16[128,4096]{1,0:T(8,128)(2,1)} custom-call(s32[10,8]{1,0:T(8,128)S(1)} %get-tuple-element.31.refs_4_.refs_0_, bf16[8,128,128]{2,1,0:T(8,128)(2,1)S(1)} %get-tuple-element.36.refs_1_.refs_3_, bf16[2,128,128]{2,1,0:T(8,128)(2,1)S(1)} %shard_map.74.refs_2_.refs_5_, bf16[7680,128]{1,0:T(8,128)(2,1)S(1)} %get-tuple-element.46.refs_3_, ...), custom_call_target="tpu_custom_call" | custom-call | flops 335544320 | bytes 4194304 | tf_op jit(solution)/shard_map/pallas_call | solution.py:44
  100.5 0.9 collective-permute-done.45.refs_3_
  101.3 0.9 shard_map.79
  (56 shorter events, 1.3 us)
Async XLA Ops:
  0.6 1.0 copy-start
  1.6 11.7 %collective-permute-start = (bf16[320,128]{1,0:T(8,128)(2,1)S(1)}, bf16[320,128]{1,0:T(8,128)(2,1)S(1)}, u32[]{:S(2)}, u32[]{:S(2)}) collective-permute-start(bf16[320,128]{1,0:T(8,128)(2,1)S(1)} %constant_dynamic-slice_fusion.refs_0_), channel_id=1, source_target_pairs={{0,2},{1,3},{2,4},{3,5},{4,6},{5,7},{6,0},{7,1},{8,10},{9,11},{10,... | collective-permute-start | bytes 245768 | tf_op jit(solution)/shard_map/ppermute | solution.py:346
  4.6 8.7 %collective-permute-start.1 = (bf16[320,128]{1,0:T(8,128)(2,1)S(1)}, bf16[320,128]{1,0:T(8,128)(2,1)S(1)}, u32[]{:S(2)}, u32[]{:S(2)}) collective-permute-start(bf16[320,128]{1,0:T(8,128)(2,1)S(1)} %constant_dynamic-slice_fusion.refs_0_), channel_id=1, source_target_pairs={{0,4},{1,5},{2,6},{3,7},{4,0},{5,1},{6,2},{7,3},{8,12},{9,13},{10,... | collective-permute-start | bytes 245768 | tf_op jit(solution)/shard_map/ppermute | solution.py:346
  7.2 6.1 %collective-permute-start.2 = (bf16[320,128]{1,0:T(8,128)(2,1)S(1)}, bf16[320,128]{1,0:T(8,128)(2,1)S(1)}, u32[]{:S(2)}, u32[]{:S(2)}) collective-permute-start(bf16[320,128]{1,0:T(8,128)(2,1)S(1)} %constant_dynamic-slice_fusion.refs_0_), channel_id=1, source_target_pairs={{0,6},{1,7},{2,0},{3,1},{4,2},{5,3},{6,4},{7,5},{8,14},{9,15},{10,... | collective-permute-start | bytes 245768 | tf_op jit(solution)/shard_map/ppermute | solution.py:346
  10.1 1.2 %copy-start.1 = (bf16[1,128,4096]{2,1,0:T(8,128)(2,1)S(1)}, bf16[1,128,4096]{2,1,0:T(8,128)(2,1)}, u32[]{:S(2)}) copy-start(bf16[1,128,4096]{2,1,0:T(8,128)(2,1)} %param.5) | copy-start | bytes 3145732
  11.3 22.0 %copy-start.2 = (bf16[1,128,4096]{2,1,0:T(8,128)(2,1)S(1)}, bf16[1,128,4096]{2,1,0:T(8,128)(2,1)}, u32[]{:S(2)}) copy-start(bf16[1,128,4096]{2,1,0:T(8,128)(2,1)} %param.5) | copy-start | bytes 3145732
  13.4 4.5 %collective-permute-start.4 = (bf16[320,128]{1,0:T(8,128)(2,1)S(1)}, bf16[320,128]{1,0:T(8,128)(2,1)S(1)}, u32[]{:S(2)}, u32[]{:S(2)}) collective-permute-start(bf16[320,128]{1,0:T(8,128)(2,1)S(1)} %shard_map.69.refs_2_), channel_id=1, source_target_pairs={{0,8},{8,0},{16,24},{24,16},{1,9},{9,1},{17,25},{25,17},{2,10},{10... | collective-permute-start | bytes 245768 | tf_op jit(solution)/shard_map/ppermute | solution.py:351
  15.0 6.5 %collective-permute-start.3 = (bf16[320,128]{1,0:T(8,128)(2,1)S(1)}, bf16[320,128]{1,0:T(8,128)(2,1)S(1)}, u32[]{:S(2)}, u32[]{:S(2)}) collective-permute-start(bf16[320,128]{1,0:T(8,128)(2,1)S(1)} %shard_map.69.refs_2_), channel_id=1, source_target_pairs={{0,1},{1,0},{2,3},{3,2},{4,5},{5,4},{6,7},{7,6},{8,9},{9,8},{10,11... | collective-permute-start | bytes 245768 | tf_op jit(solution)/shard_map/ppermute | solution.py:343
  15.0 9.0 %collective-permute-start.6 = (bf16[320,128]{1,0:T(8,128)(2,1)S(1)}, bf16[320,128]{1,0:T(8,128)(2,1)S(1)}, u32[]{:S(2)}, u32[]{:S(2)}) collective-permute-start(bf16[320,128]{1,0:T(8,128)(2,1)S(1)} %shard_map.69.refs_2_), channel_id=1, source_target_pairs={{0,16},{8,24},{16,0},{24,8},{1,17},{9,25},{17,1},{25,9},{2,18},{10... | collective-permute-start | bytes 245768 | tf_op jit(solution)/shard_map/ppermute | solution.py:351
  18.0 23.2 %collective-permute-start.11 = (bf16[960,128]{1,0:T(8,128)(2,1)S(1)}, bf16[960,128]{1,0:T(8,128)(2,1)S(1)}, u32[]{:S(2)}, u32[]{:S(2)}) collective-permute-start(bf16[960,128]{1,0:T(8,128)(2,1)S(1)} %shard_map.71.refs_3_), channel_id=1, source_target_pairs={{0,8},{8,0},{16,24},{24,16},{1,9},{9,1},{17,25},{25,17},{2,10},{10... | collective-permute-start | bytes 737288 | tf_op jit(solution)/shard_map/ppermute | solution.py:351
  19.5 22.2 %collective-permute-start.13 = (bf16[960,128]{1,0:T(8,128)(2,1)S(1)}, bf16[960,128]{1,0:T(8,128)(2,1)S(1)}, u32[]{:S(2)}, u32[]{:S(2)}) collective-permute-start(bf16[960,128]{1,0:T(8,128)(2,1)S(1)} %shard_map.71.refs_3_), channel_id=1, source_target_pairs={{0,16},{8,24},{16,0},{24,8},{1,17},{9,25},{17,1},{25,9},{2,18},{10... | collective-permute-start | bytes 737288 | tf_op jit(solution)/shard_map/ppermute | solution.py:351
  21.1 20.7 %collective-permute-start.15 = (bf16[960,128]{1,0:T(8,128)(2,1)S(1)}, bf16[960,128]{1,0:T(8,128)(2,1)S(1)}, u32[]{:S(2)}, u32[]{:S(2)}) collective-permute-start(bf16[960,128]{1,0:T(8,128)(2,1)S(1)} %shard_map.71.refs_3_), channel_id=1, source_target_pairs={{0,24},{8,16},{16,8},{24,0},{1,25},{9,17},{17,9},{25,1},{2,26},{10... | collective-permute-start | bytes 737288 | tf_op jit(solution)/shard_map/ppermute | solution.py:351
  21.5 10.4 %collective-permute-start.8 = (bf16[320,128]{1,0:T(8,128)(2,1)S(1)}, bf16[320,128]{1,0:T(8,128)(2,1)S(1)}, u32[]{:S(2)}, u32[]{:S(2)}) collective-permute-start(bf16[320,128]{1,0:T(8,128)(2,1)S(1)} %shard_map.69.refs_2_), channel_id=1, source_target_pairs={{0,24},{8,16},{16,8},{24,0},{1,25},{9,17},{17,9},{25,1},{2,26},{10... | collective-permute-start | bytes 245768 | tf_op jit(solution)/shard_map/ppermute | solution.py:351
  24.0 7.9 %collective-permute-start.5 = (bf16[320,128]{1,0:T(8,128)(2,1)S(1)}, bf16[320,128]{1,0:T(8,128)(2,1)S(1)}, u32[]{:S(2)}, u32[]{:S(2)}) collective-permute-start(bf16[320,128]{1,0:T(8,128)(2,1)S(1)} %collective-permute-done.4.refs_4_), channel_id=1, source_target_pairs={{0,1},{1,0},{2,3},{3,2},{4,5},{5,4},{6,7},{7,6},{8,9},{9,8},{10,11... | collective-permute-start | bytes 245768 | tf_op jit(solution)/shard_map/ppermute | solution.py:343
  31.9 1.3 %collective-permute-start.7 = (bf16[320,128]{1,0:T(8,128)(2,1)S(1)}, bf16[320,128]{1,0:T(8,128)(2,1)S(1)}, u32[]{:S(2)}, u32[]{:S(2)}) collective-permute-start(bf16[320,128]{1,0:T(8,128)(2,1)S(1)} %collective-permute-done.6.refs_6_), channel_id=1, source_target_pairs={{0,1},{1,0},{2,3},{3,2},{4,5},{5,4},{6,7},{7,6},{8,9},{9,8},{10,11... | collective-permute-start | bytes 245768 | tf_op jit(solution)/shard_map/ppermute | solution.py:343
  31.9 1.4 %collective-permute-start.9 = (bf16[320,128]{1,0:T(8,128)(2,1)S(1)}, bf16[320,128]{1,0:T(8,128)(2,1)S(1)}, u32[]{:S(2)}, u32[]{:S(2)}) collective-permute-start(bf16[320,128]{1,0:T(8,128)(2,1)S(1)} %collective-permute-done.8.refs_8_), channel_id=1, source_target_pairs={{0,1},{1,0},{2,3},{3,2},{4,5},{5,4},{6,7},{7,6},{8,9},{9,8},{10,11... | collective-permute-start | bytes 245768 | tf_op jit(solution)/shard_map/ppermute | solution.py:343
  34.4 16.3 %copy-start.3 = (bf16[1,128,1024]{2,1,0:T(8,128)(2,1)S(1)}, bf16[1,128,1024]{2,1,0:T(8,128)(2,1)}, u32[]{:S(2)}) copy-start(bf16[1,128,1024]{2,1,0:T(8,128)(2,1)} %param.6) | copy-start | bytes 786436
  34.4 6.8 %collective-permute-start.18 = (bf16[128,256]{1,0:T(8,128)(2,1)S(1)}, bf16[128,256]{1,0:T(8,128)(2,1)S(1)}, u32[]{:S(2)}, u32[]{:S(2)}) collective-permute-start(bf16[128,256]{1,0:T(8,128)(2,1)S(1)} %get-tuple-element.35.refs_3_), channel_id=1, source_target_pairs={{0,2},{1,3},{2,4},{3,5},{4,6},{5,7},{6,0},{7,1},{8,10},{9,11},{10,... | collective-permute-start | bytes 196616 | tf_op jit(solution)/shard_map/ppermute | solution.py:346
  36.8 6.7 %collective-permute-start.20 = (bf16[128,256]{1,0:T(8,128)(2,1)S(1)}, bf16[128,256]{1,0:T(8,128)(2,1)S(1)}, u32[]{:S(2)}, u32[]{:S(2)}) collective-permute-start(bf16[128,256]{1,0:T(8,128)(2,1)S(1)} %get-tuple-element.35.refs_3_), channel_id=1, source_target_pairs={{0,4},{1,5},{2,6},{3,7},{4,0},{5,1},{6,2},{7,3},{8,12},{9,13},{10,... | collective-permute-start | bytes 196616 | tf_op jit(solution)/shard_map/ppermute | solution.py:346
  41.2 6.5 %collective-permute-start.10 = (bf16[960,128]{1,0:T(8,128)(2,1)S(1)}, bf16[960,128]{1,0:T(8,128)(2,1)S(1)}, u32[]{:S(2)}, u32[]{:S(2)}) collective-permute-start(bf16[960,128]{1,0:T(8,128)(2,1)S(1)} %shard_map.71.refs_3_), channel_id=1, source_target_pairs={{0,1},{1,0},{2,3},{3,2},{4,5},{5,4},{6,7},{7,6},{8,9},{9,8},{10,11... | collective-permute-start | bytes 737288 | tf_op jit(solution)/shard_map/ppermute | solution.py:343
  41.2 7.0 %collective-permute-start.12 = (bf16[960,128]{1,0:T(8,128)(2,1)S(1)}, bf16[960,128]{1,0:T(8,128)(2,1)S(1)}, u32[]{:S(2)}, u32[]{:S(2)}) collective-permute-start(bf16[960,128]{1,0:T(8,128)(2,1)S(1)} %collective-permute-done.11.refs_5_), channel_id=1, source_target_pairs={{0,1},{1,0},{2,3},{3,2},{4,5},{5,4},{6,7},{7,6},{8,9},{9,8},{10,11... | collective-permute-start | bytes 737288 | tf_op jit(solution)/shard_map/ppermute | solution.py:343
  41.7 6.6 %collective-permute-start.14 = (bf16[960,128]{1,0:T(8,128)(2,1)S(1)}, bf16[960,128]{1,0:T(8,128)(2,1)S(1)}, u32[]{:S(2)}, u32[]{:S(2)}) collective-permute-start(bf16[960,128]{1,0:T(8,128)(2,1)S(1)} %collective-permute-done.13.refs_7_), channel_id=1, source_target_pairs={{0,1},{1,0},{2,3},{3,2},{4,5},{5,4},{6,7},{7,6},{8,9},{9,8},{10,11... | collective-permute-start | bytes 737288 | tf_op jit(solution)/shard_map/ppermute | solution.py:343
  41.8 6.9 %collective-permute-start.16 = (bf16[960,128]{1,0:T(8,128)(2,1)S(1)}, bf16[960,128]{1,0:T(8,128)(2,1)S(1)}, u32[]{:S(2)}, u32[]{:S(2)}) collective-permute-start(bf16[960,128]{1,0:T(8,128)(2,1)S(1)} %collective-permute-done.15.refs_9_), channel_id=1, source_target_pairs={{0,1},{1,0},{2,3},{3,2},{4,5},{5,4},{6,7},{7,6},{8,9},{9,8},{10,11... | collective-permute-start | bytes 737288 | tf_op jit(solution)/shard_map/ppermute | solution.py:343
  43.4 4.3 %collective-permute-start.22 = (bf16[128,256]{1,0:T(8,128)(2,1)S(1)}, bf16[128,256]{1,0:T(8,128)(2,1)S(1)}, u32[]{:S(2)}, u32[]{:S(2)}) collective-permute-start(bf16[128,256]{1,0:T(8,128)(2,1)S(1)} %get-tuple-element.35.refs_3_), channel_id=1, source_target_pairs={{0,6},{1,7},{2,0},{3,1},{4,2},{5,3},{6,4},{7,5},{8,14},{9,15},{10,... | collective-permute-start | bytes 196616 | tf_op jit(solution)/shard_map/ppermute | solution.py:346
  47.7 15.2 %collective-permute-start.31 = (bf16[4096,128]{1,0:T(8,128)(2,1)S(1)}, bf16[4096,128]{1,0:T(8,128)(2,1)S(1)}, u32[]{:S(2)}, u32[]{:S(2)}) collective-permute-start(bf16[4096,128]{1,0:T(8,128)(2,1)S(1)} %get-tuple-element.47.refs_1_), channel_id=1, source_target_pairs={{0,1},{1,0},{2,3},{3,2},{4,5},{5,4},{6,7},{7,6},{8,9},{9,8},{10,11... | collective-permute-start | bytes 3145736 | tf_op jit(solution)/shard_map/ppermute | solution.py:343
  47.7 2.7 %collective-permute-start.17 = (bf16[128,256]{1,0:T(8,128)(2,1)S(1)}, bf16[128,256]{1,0:T(8,128)(2,1)S(1)}, u32[]{:S(2)}, u32[]{:S(2)}) collective-permute-start(bf16[128,256]{1,0:T(8,128)(2,1)S(1)} %get-tuple-element.35.refs_3_), channel_id=1, source_target_pairs={{0,1},{1,0},{2,3},{3,2},{4,5},{5,4},{6,7},{7,6},{8,9},{9,8},{10,11... | collective-permute-start | bytes 196616 | tf_op jit(solution)/shard_map/ppermute | solution.py:343
  48.2 2.3 %collective-permute-start.19 = (bf16[128,256]{1,0:T(8,128)(2,1)S(1)}, bf16[128,256]{1,0:T(8,128)(2,1)S(1)}, u32[]{:S(2)}, u32[]{:S(2)}) collective-permute-start(bf16[128,256]{1,0:T(8,128)(2,1)S(1)} %collective-permute-done.18.refs_5_), channel_id=1, source_target_pairs={{0,1},{1,0},{2,3},{3,2},{4,5},{5,4},{6,7},{7,6},{8,9},{9,8},{10,11... | collective-permute-start | bytes 196616 | tf_op jit(solution)/shard_map/ppermute | solution.py:343
  48.3 2.4 %collective-permute-start.21 = (bf16[128,256]{1,0:T(8,128)(2,1)S(1)}, bf16[128,256]{1,0:T(8,128)(2,1)S(1)}, u32[]{:S(2)}, u32[]{:S(2)}) collective-permute-start(bf16[128,256]{1,0:T(8,128)(2,1)S(1)} %collective-permute-done.20.refs_7_), channel_id=1, source_target_pairs={{0,1},{1,0},{2,3},{3,2},{4,5},{5,4},{6,7},{7,6},{8,9},{9,8},{10,11... | collective-permute-start | bytes 196616 | tf_op jit(solution)/shard_map/ppermute | solution.py:343
  48.7 2.0 %collective-permute-start.23 = (bf16[128,256]{1,0:T(8,128)(2,1)S(1)}, bf16[128,256]{1,0:T(8,128)(2,1)S(1)}, u32[]{:S(2)}, u32[]{:S(2)}) collective-permute-start(bf16[128,256]{1,0:T(8,128)(2,1)S(1)} %collective-permute-done.22.refs_9_), channel_id=1, source_target_pairs={{0,1},{1,0},{2,3},{3,2},{4,5},{5,4},{6,7},{7,6},{8,9},{9,8},{10,11... | collective-permute-start | bytes 196616 | tf_op jit(solution)/shard_map/ppermute | solution.py:343
  57.0 1.3 %collective-permute-start.25 = (bf16[128,256]{1,0:T(8,128)(2,1)S(1)}, bf16[128,256]{1,0:T(8,128)(2,1)S(1)}, u32[]{:S(2)}, u32[]{:S(2)}) collective-permute-start(bf16[128,256]{1,0:T(8,128)(2,1)S(1)} %get-tuple-element.41), channel_id=1, source_target_pairs={{0,1},{1,0},{2,3},{3,2},{4,5},{5,4},{6,7},{7,6},{8,9},{9,8},{10,11... | collective-permute-start | bytes 196616 | tf_op jit(solution)/shard_map/ppermute | solution.py:343
  57.2 8.7 %collective-permute-start.24 = (bf16[128,256]{1,0:T(8,128)(2,1)S(1)}, bf16[128,256]{1,0:T(8,128)(2,1)S(1)}, u32[]{:S(2)}, u32[]{:S(2)}) collective-permute-start(bf16[128,256]{1,0:T(8,128)(2,1)S(1)} %get-tuple-element.39), channel_id=1, source_target_pairs={{0,1},{1,0},{2,3},{3,2},{4,5},{5,4},{6,7},{7,6},{8,9},{9,8},{10,11... | collective-permute-start | bytes 196616 | tf_op jit(solution)/shard_map/ppermute | solution.py:343
  57.6 1.3 %collective-permute-start.27 = (bf16[128,256]{1,0:T(8,128)(2,1)S(1)}, bf16[128,256]{1,0:T(8,128)(2,1)S(1)}, u32[]{:S(2)}, u32[]{:S(2)}) collective-permute-start(bf16[128,256]{1,0:T(8,128)(2,1)S(1)} %get-tuple-element.43), channel_id=1, source_target_pairs={{0,1},{1,0},{2,3},{3,2},{4,5},{5,4},{6,7},{7,6},{8,9},{9,8},{10,11... | collective-permute-start | bytes 196616 | tf_op jit(solution)/shard_map/ppermute | solution.py:343
  57.7 1.3 %collective-permute-start.29 = (bf16[128,256]{1,0:T(8,128)(2,1)S(1)}, bf16[128,256]{1,0:T(8,128)(2,1)S(1)}, u32[]{:S(2)}, u32[]{:S(2)}) collective-permute-start(bf16[128,256]{1,0:T(8,128)(2,1)S(1)} %get-tuple-element.45), channel_id=1, source_target_pairs={{0,1},{1,0},{2,3},{3,2},{4,5},{5,4},{6,7},{7,6},{8,9},{9,8},{10,11... | collective-permute-start | bytes 196616 | tf_op jit(solution)/shard_map/ppermute | solution.py:343
  58.3 4.2 %collective-permute-start.32 = (bf16[8,128,128]{2,1,0:T(8,128)(2,1)S(1)}, bf16[8,128,128]{2,1,0:T(8,128)(2,1)S(1)}, u32[]{:S(2)}, u32[]{:S(2)}) collective-permute-start(bf16[8,128,128]{2,1,0:T(8,128)(2,1)S(1)} %get-tuple-element.36.refs_1_.refs_3_), channel_id=1, source_target_pairs={{0,1},{1,0},{2,3},{3,2},{4,5},{5,4},{6,7},{7,6},{8,9},{9,8},{10,11... | collective-permute-start | bytes 786440 | tf_op jit(solution)/shard_map/ppermute | solution.py:343
  58.8 7.7 %collective-permute-start.26 = (bf16[128,256]{1,0:T(8,128)(2,1)S(1)}, bf16[128,256]{1,0:T(8,128)(2,1)S(1)}, u32[]{:S(2)}, u32[]{:S(2)}) collective-permute-start(bf16[128,256]{1,0:T(8,128)(2,1)S(1)} %add_convert_fusion.3), channel_id=1, source_target_pairs={{0,2},{1,3},{2,4},{3,5},{4,6},{5,7},{6,0},{7,1},{8,10},{9,11},{10,... | collective-permute-start | bytes 196616 | tf_op jit(solution)/shard_map/ppermute | solution.py:346
  59.0 9.0 %collective-permute-start.28 = (bf16[128,256]{1,0:T(8,128)(2,1)S(1)}, bf16[128,256]{1,0:T(8,128)(2,1)S(1)}, u32[]{:S(2)}, u32[]{:S(2)}) collective-permute-start(bf16[128,256]{1,0:T(8,128)(2,1)S(1)} %add_convert_fusion.2), channel_id=1, source_target_pairs={{0,4},{1,5},{2,6},{3,7},{4,0},{5,1},{6,2},{7,3},{8,12},{9,13},{10,... | collective-permute-start | bytes 196616 | tf_op jit(solution)/shard_map/ppermute | solution.py:346
  62.6 5.4 %collective-permute-start.30 = (bf16[128,256]{1,0:T(8,128)(2,1)S(1)}, bf16[128,256]{1,0:T(8,128)(2,1)S(1)}, u32[]{:S(2)}, u32[]{:S(2)}) collective-permute-start(bf16[128,256]{1,0:T(8,128)(2,1)S(1)} %add_convert_fusion.1), channel_id=1, source_target_pairs={{0,6},{1,7},{2,0},{3,1},{4,2},{5,3},{6,4},{7,5},{8,14},{9,15},{10,... | collective-permute-start | bytes 196616 | tf_op jit(solution)/shard_map/ppermute | solution.py:346
  64.4 20.2 %collective-permute-start.33 = (bf16[960,128]{1,0:T(8,128)(2,1)S(1)}, bf16[960,128]{1,0:T(8,128)(2,1)S(1)}, u32[]{:S(2)}, u32[]{:S(2)}) collective-permute-start(bf16[960,128]{1,0:T(8,128)(2,1)S(1)} %get-tuple-element.49), channel_id=1, source_target_pairs={{0,8},{8,0},{16,24},{24,16},{1,9},{9,1},{17,25},{25,17},{2,10},{10... | collective-permute-start | bytes 737288 | tf_op jit(solution)/shard_map/ppermute | solution.py:351
  65.9 18.7 %collective-permute-start.34 = (bf16[960,128]{1,0:T(8,128)(2,1)S(1)}, bf16[960,128]{1,0:T(8,128)(2,1)S(1)}, u32[]{:S(2)}, u32[]{:S(2)}) collective-permute-start(bf16[960,128]{1,0:T(8,128)(2,1)S(1)} %get-tuple-element.50), channel_id=1, source_target_pairs={{0,16},{8,24},{16,0},{24,8},{1,17},{9,25},{17,1},{25,9},{2,18},{10... | collective-permute-start | bytes 737288 | tf_op jit(solution)/shard_map/ppermute | solution.py:351
  66.5 18.1 %collective-permute-start.35 = (bf16[960,128]{1,0:T(8,128)(2,1)S(1)}, bf16[960,128]{1,0:T(8,128)(2,1)S(1)}, u32[]{:S(2)}, u32[]{:S(2)}) collective-permute-start(bf16[960,128]{1,0:T(8,128)(2,1)S(1)} %get-tuple-element.51), channel_id=1, source_target_pairs={{0,24},{8,16},{16,8},{24,0},{1,25},{9,17},{17,9},{25,1},{2,26},{10... | collective-permute-start | bytes 737288 | tf_op jit(solution)/shard_map/ppermute | solution.py:351
  68.1 1.3 %collective-permute-start.36 = (bf16[2,128,128]{2,1,0:T(8,128)(2,1)S(1)}, bf16[2,128,128]{2,1,0:T(8,128)(2,1)S(1)}, u32[]{:S(2)}, u32[]{:S(2)}) collective-permute-start(bf16[2,128,128]{2,1,0:T(8,128)(2,1)S(1)} %shard_map.74.refs_2_.refs_5_), channel_id=1, source_target_pairs={{0,1},{1,0},{2,3},{3,2},{4,5},{5,4},{6,7},{7,6},{8,9},{9,8},{10,11... | collective-permute-start | bytes 196616 | tf_op jit(solution)/shard_map/ppermute | solution.py:343
  70.5 8.8 %collective-permute-start.37 = (bf16[320,128]{1,0:T(8,128)(2,1)S(1)}, bf16[320,128]{1,0:T(8,128)(2,1)S(1)}, u32[]{:S(2)}, u32[]{:S(2)}) collective-permute-start(bf16[320,128]{1,0:T(8,128)(2,1)S(1)} %get-tuple-element.53), channel_id=1, source_target_pairs={{0,8},{8,0},{16,24},{24,16},{1,9},{9,1},{17,25},{25,17},{2,10},{10... | collective-permute-start | bytes 245768 | tf_op jit(solution)/shard_map/ppermute | solution.py:351
  72.0 8.7 %collective-permute-start.38 = (bf16[320,128]{1,0:T(8,128)(2,1)S(1)}, bf16[320,128]{1,0:T(8,128)(2,1)S(1)}, u32[]{:S(2)}, u32[]{:S(2)}) collective-permute-start(bf16[320,128]{1,0:T(8,128)(2,1)S(1)} %get-tuple-element.54), channel_id=1, source_target_pairs={{0,16},{8,24},{16,0},{24,8},{1,17},{9,25},{17,1},{25,9},{2,18},{10... | collective-permute-start | bytes 245768 | tf_op jit(solution)/shard_map/ppermute | solution.py:351
  79.3 5.3 %collective-permute-start.39 = (bf16[320,128]{1,0:T(8,128)(2,1)S(1)}, bf16[320,128]{1,0:T(8,128)(2,1)S(1)}, u32[]{:S(2)}, u32[]{:S(2)}) collective-permute-start(bf16[320,128]{1,0:T(8,128)(2,1)S(1)} %get-tuple-element.55), channel_id=1, source_target_pairs={{0,24},{8,16},{16,8},{24,0},{1,25},{9,17},{17,9},{25,1},{2,26},{10... | collective-permute-start | bytes 245768 | tf_op jit(solution)/shard_map/ppermute | solution.py:351
  84.9 5.4 %collective-permute-start.42 = (bf16[320,128]{1,0:T(8,128)(2,1)S(1)}, bf16[320,128]{1,0:T(8,128)(2,1)S(1)}, u32[]{:S(2)}, u32[]{:S(2)}) collective-permute-start(bf16[320,128]{1,0:T(8,128)(2,1)S(1)} %get-tuple-element.59), channel_id=1, source_target_pairs={{0,6},{1,7},{2,0},{3,1},{4,2},{5,3},{6,4},{7,5},{8,14},{9,15},{10,... | collective-permute-start | bytes 245768 | tf_op jit(solution)/shard_map/ppermute | solution.py:346
  85.9 6.3 %collective-permute-start.41 = (bf16[320,128]{1,0:T(8,128)(2,1)S(1)}, bf16[320,128]{1,0:T(8,128)(2,1)S(1)}, u32[]{:S(2)}, u32[]{:S(2)}) collective-permute-start(bf16[320,128]{1,0:T(8,128)(2,1)S(1)} %get-tuple-element.58), channel_id=1, source_target_pairs={{0,4},{1,5},{2,6},{3,7},{4,0},{5,1},{6,2},{7,3},{8,12},{9,13},{10,... | collective-permute-start | bytes 245768 | tf_op jit(solution)/shard_map/ppermute | solution.py:346
  87.6 6.2 %collective-permute-start.40 = (bf16[320,128]{1,0:T(8,128)(2,1)S(1)}, bf16[320,128]{1,0:T(8,128)(2,1)S(1)}, u32[]{:S(2)}, u32[]{:S(2)}) collective-permute-start(bf16[320,128]{1,0:T(8,128)(2,1)S(1)} %get-tuple-element.57), channel_id=1, source_target_pairs={{0,2},{1,3},{2,4},{3,5},{4,6},{5,7},{6,0},{7,1},{8,10},{9,11},{10,... | collective-permute-start | bytes 245768 | tf_op jit(solution)/shard_map/ppermute | solution.py:346
  93.9 6.6 %collective-permute-start.43 = (bf16[320,128]{1,0:T(8,128)(2,1)S(1)}, bf16[320,128]{1,0:T(8,128)(2,1)S(1)}, u32[]{:S(2)}, u32[]{:S(2)}) collective-permute-start(bf16[320,128]{1,0:T(8,128)(2,1)S(1)} %add_convert_fusion.refs_0_), channel_id=1, source_target_pairs={{0,8},{8,0},{16,24},{24,16},{1,9},{9,1},{17,25},{25,17},{2,10},{10... | collective-permute-start | bytes 245768 | tf_op jit(solution)/shard_map/ppermute | solution.py:351
  95.5 5.0 %collective-permute-start.44 = (bf16[320,128]{1,0:T(8,128)(2,1)S(1)}, bf16[320,128]{1,0:T(8,128)(2,1)S(1)}, u32[]{:S(2)}, u32[]{:S(2)}) collective-permute-start(bf16[320,128]{1,0:T(8,128)(2,1)S(1)} %add_convert_fusion.refs_0_), channel_id=1, source_target_pairs={{0,16},{8,24},{16,0},{24,8},{1,17},{9,25},{17,1},{25,9},{2,18},{10... | collective-permute-start | bytes 245768 | tf_op jit(solution)/shard_map/ppermute | solution.py:351
  96.0 5.3 %collective-permute-start.45 = (bf16[320,128]{1,0:T(8,128)(2,1)S(1)}, bf16[320,128]{1,0:T(8,128)(2,1)S(1)}, u32[]{:S(2)}, u32[]{:S(2)}) collective-permute-start(bf16[320,128]{1,0:T(8,128)(2,1)S(1)} %add_convert_fusion.refs_0_), channel_id=1, source_target_pairs={{0,24},{8,16},{16,8},{24,0},{1,25},{9,17},{17,9},{25,1},{2,26},{10... | collective-permute-start | bytes 245768 | tf_op jit(solution)/shard_map/ppermute | solution.py:351

commit v3 on v2

--- a/solution.py
+++ b/solution.py
@@ -52,6 +52,17 @@
     )(*scalars, *arrays, *wait)
 
 
+def after(value, *wait):
+    return pl.pallas_call(
+        lambda *refs: None,
+        in_specs=[ANY] * (1 + len(wait)),
+        out_specs=ANY,
+        out_shape=jax.ShapeDtypeStruct(value.shape, value.dtype),
+        input_output_aliases={0: 0},
+        compiler_params=pltpu.CompilerParams(vmem_limit_bytes=2**20),
+    )(value, *wait)
+
+
 def dot(a, b, contract=((1,), (0,))):
     return lax.dot_general(a, b, (contract, ((), ())), preferred_element_type=F32)
 
@@ -81,26 +92,25 @@
                 out[i, j] = source[i, j]
 
 
-def arrange_kernel(z_lo, z_hi, *refs):
-    pieces, out = refs[:-1], refs[-1]
-    nz, rows = len(pieces), pieces[0].shape[0]
-    me = lax.axis_index("ctx") // 2
-    for z in range(z_lo, z_hi):
-        at = (z - z_lo) * rows
-        for k in range(nz):
-
-            @pl.when(lax.rem(me + nz - k, nz) == z)
-            def _():
-                out[at : at + rows, :] = pieces[k][...]
-
-
-def join_pieces(pieces, z_count, shard, piece, w_ref):
+def stack_kernel(*refs):
+    rows = refs[0].shape[0]
+    for k, ref in enumerate(refs[:-1]):
+        refs[-1][k * rows : (k + 1) * rows, :] = ref[...]
+
+
+def join_shards(shards, base, w_ref):
+    core = lax.axis_index("ctx") % 2
+    shard = shards[0].shape[0]
+    for n, ref in enumerate(shards):
+        at = base + (core if n == 0 else 1 - core) * shard
+        w_ref[rows_at(at, shard, 128), :] = ref[...]
+
+
+def join_pieces(pieces, slot, shard, piece, base, w_ref):
     core, dp = lax.axis_index("ctx") % 2, lax.axis_index("dp")
     for n, ref in enumerate(pieces):
-        k, parity = n // 2, core if n % 2 == 0 else 1 - core
-        for z in range(z_count):
-            at = z * 2 * shard + parity * shard + lax.bitwise_xor(dp, k) * piece
-            w_ref[rows_at(at, piece, 16), :] = ref[z * piece : (z + 1) * piece, :]
+        at = base + (core if n % 2 == 0 else 1 - core) * shard + (dp ^ (n // 2)) * piece
+        w_ref[rows_at(at, piece, 16), :] = ref[slot * piece : (slot + 1) * piece, :]
 
 
 def column_of(c, ids, x_ref):
@@ -109,11 +119,10 @@
     )
 
 
-def project_keys(ids, x_ref, w_ref, first, kv_ref, key_ref):
+def project_keys(ids, x_ref, w_ref, kv_ref, key_ref):
     wide = NBR * BLK
     for c in range(NQ, NCB):
-        at = c * wide - first
-        out = dot(column_of(c, ids, x_ref), w_ref[at : at + wide, :]).astype(BF16)
+        out = dot(column_of(c, ids, x_ref), w_ref[c * wide : (c + 1) * wide, :]).astype(BF16)
         if c == NQ:
             key = out.astype(F32)
             key_ref[...] = out
@@ -122,39 +131,29 @@
             kv_ref[:, HD:] = out
 
 
-def project_queries(ids, x_ref, rows_of, q_ref):
+def keys_kernel(nz, ids, x_ref, *refs):
+    shards, pieces, (w_ref, kv_ref, key_ref) = refs[:2], refs[2:-3], refs[-3:]
+    shard, piece = shards[0].shape[0], pieces[0].shape[0] // (nz - 1)
+    zi = lax.axis_index("ctx") // 2
+    join_shards(shards, zi * 2 * shard, w_ref)
+    for k in range(1, nz):
+        base = lax.rem(zi + nz - k, nz) * 2 * shard
+        join_pieces(pieces, k - 1, shard, piece, base, w_ref)
+    project_keys(ids, x_ref, w_ref, kv_ref, key_ref)
+
+
+def queries_kernel(ids, x_ref, w_ref, q_ref):
     wide = NBR * BLK
     for c in range(NQ):
-        out = dot(column_of(c, ids, x_ref), rows_of(c * wide, (c + 1) * wide)).astype(BF16)
+        out = dot(column_of(c, ids, x_ref), w_ref[c * wide : (c + 1) * wide, :]).astype(BF16)
         for p in range(2):
             at = (p * NQ + c) * SPAN
             q_ref[at : at + SPAN, :] = out[p * SPAN : (p + 1) * SPAN, :]
 
 
-def keys_kernel(z_count, shard, piece, ids, x_ref, *refs):
-    pieces, (w_ref, kv_ref, key_ref) = refs[:-3], refs[-3:]
-    join_pieces(pieces, z_count, shard, piece, w_ref)
-    project_keys(ids, x_ref, w_ref, NNZ * BLK - z_count * 2 * shard, kv_ref, key_ref)
-
-
-def queries_kernel(z_count, shard, piece, ids, x_ref, tail_ref, *refs):
-    pieces, (w_ref, q_ref) = refs[:-2], refs[-2:]
-    join_pieces(pieces, z_count, shard, piece, w_ref)
-    cut = z_count * 2 * shard
-
-    def rows_of(lo, hi):
-        if hi <= cut:
-            return w_ref[lo:hi, :]
-        if lo >= cut:
-            return tail_ref[lo - cut : hi - cut, :]
-        return jnp.concatenate([w_ref[lo:cut, :], tail_ref[0 : hi - cut, :]], axis=0)
-
-    project_queries(ids, x_ref, rows_of, q_ref)
-
-
 def project_kernel(ids, x_ref, w_ref, q_ref, kv_ref, key_ref):
-    project_keys(ids, x_ref, w_ref, 0, kv_ref, key_ref)
-    project_queries(ids, x_ref, lambda lo, hi: w_ref[lo:hi, :], q_ref)
+    project_keys(ids, x_ref, w_ref, kv_ref, key_ref)
+    queries_kernel(ids, x_ref, w_ref, q_ref)
 
 
 def attend_kernel(nz, spans, q_ref, up_ref, *refs):
@@ -280,10 +279,10 @@
         out_ref[c * NBR * BLK : (c + 1) * NBR * BLK, :] = dot(picked, grad).astype(BF16)
 
 
-def sum_kernel(ndp, nz, z_first, piece, *refs):
+def sum_kernel(ndp, nz, piece, *refs):
     head, tail = refs[:ndp], refs[ndp : 2 * ndp]
     outs, work = refs[2 * ndp : 2 * ndp + nz], refs[2 * ndp + nz]
-    for group, first, count in ((head, 0, z_first), (tail, z_first, nz - z_first)):
+    for group, first, count in ((head, 0, nz - 1), (tail, nz - 1, 1)):
         total = group[0][...].astype(F32)
         for term in group[1:]:
             total = total + term[...].astype(F32)
@@ -299,28 +298,19 @@
         refs[-1][rows_at(at, piece, 16), :] = ref[...].astype(F32)
 
 
-def token_grad_kernel(ids, dq_ref, dkv_ref, *refs):
-    parts, (out_ref, work) = refs[:-2], refs[-2:]
+def token_grad_kernel(ids, dq_ref, dkv_ref, w_ref, out_ref, work):
     wide = NBR * BLK
     cover = out_ref.shape[1] // wide
-    first = 0
-    done = 0
-    for w_ref in parts:
-        last = first + w_ref.shape[0] // BLK
-        while done < last:
-            c = done // NBR
-            stop = min(last, (c + 1) * NBR)
-            grad = dq_ref[c] if c < NQ else dkv_ref[c - NQ]
-            spread = dot(grad, w_ref[(done - first) * BLK : (stop - first) * BLK, :], ((1,), (1,)))
-            for b in range(done, stop):
-                columns = rows_at(ids[c, b % NBR] * BLK, BLK, BLK)
-                term = spread[:, (b - done) * BLK : (b - done + 1) * BLK]
-                if c < cover:
-                    work[:, columns] = term
-                else:
-                    work[:, columns] += term
-            done = stop
-        first = last
+    for c in range(NCB):
+        grad = dq_ref[c] if c < NQ else dkv_ref[c - NQ]
+        spread = dot(grad, w_ref[c * wide : (c + 1) * wide, :], ((1,), (1,)))
+        for r in range(NBR):
+            columns = rows_at(ids[c, r] * BLK, BLK, BLK)
+            term = spread[:, r * BLK : (r + 1) * BLK]
+            if c < cover:
+                work[:, columns] = term
+            else:
+                work[:, columns] += term
     out_ref[...] = work[...].astype(BF16)
 
 
@@ -333,11 +323,10 @@
     length = spans.shape[0] * 2 * SPAN
     shard = w_packed.shape[0]
     piece = shard // ndp
-    z_first = NQ * NBR * BLK // (2 * shard)
-    z_last = nz - z_first
-    cut = z_first * 2 * shard
+    cut = (nz - 1) * 2 * shard
     half = NQ * SPAN
-    fast = shard % BLK == 0 and shard % (16 * ndp) == 0 and ndp & (ndp - 1) == 0
+    fast = 2 < nz and cut <= NQ * NBR * BLK and shard % BLK == 0
+    fast = fast and shard % (16 * ndp) == 0 and 1 < ndp and ndp & (ndp - 1) == 0
 
     def swap_core(v):
         return lax.ppermute(v, "ctx", [(i, i ^ 1) for i in range(nctx)])
@@ -363,45 +352,45 @@
 
     if fast:
         mine = lax.dynamic_slice_in_dim(w_packed, dp * piece, piece, 0)
-        from_z = [mine] + [shift_z(mine, k) for k in range(1, nz)]
-
-        def arrange(z_lo, z_hi, wait):
-            return call(
-                functools.partial(arrange_kernel, z_lo, z_hi),
-                (),
-                from_z,
-                [(((z_hi - z_lo) * piece, BLK), BF16)],
-                wait=wait,
-                moved=4 * nz * piece * BLK,
-            )[0]
-
-        tail = arrange(z_first, nz, (ids,))
-        tail = [tail] + [swap_dp(tail, k) for k in range(1, ndp)]
-        head = arrange(0, z_first, tail[1:2])
-        head = [head] + [swap_dp(head, k) for k in range(1, ndp)]
-        w_tail, kv, key = call(
-            functools.partial(keys_kernel, z_last, shard, piece),
+        from_z = [shift_z(mine, k) for k in range(1, nz)]
+
+        def both_cores(parts):
+            return [v for part in parts for v in (part, swap_core(part))]
+
+        shards = both_cores([w_packed])
+        (stacked,) = call(
+            stack_kernel,
+            (),
+            from_z,
+            [(((nz - 1) * piece, BLK), BF16)],
+            wait=(ids, shards[1]),
+            moved=4 * nz * piece * BLK,
+        )
+        xt_other = swap_core(after(xt, stacked))
+        pieces = [stacked] + [swap_dp(stacked, k) for k in range(1, ndp)]
+        weights, kv, key = call(
+            functools.partial(keys_kernel, nz),
             (ids,),
-            [x] + [v for part in tail for v in (part, swap_core(part))],
-            [((NNZ * BLK - cut, BLK), BF16), ((tok, 2 * HD), BF16), ((tok, HD), BF16)],
+            (x, *shards, *both_cores(pieces)),
+            [((NNZ * BLK, BLK), BF16), ((tok, 2 * HD), BF16), ((tok, HD), BF16)],
+            wait=(xt_other,),
             flops=2 * tok * (NCB - NQ) * NBR * BLK * BLK,
+            moved=6 * 2**20,
+        )
+        (query,) = call(
+            queries_kernel,
+            (ids,),
+            (x, weights),
+            [((tok * NQ, HD), BF16)],
+            flops=2 * tok * NQ * NBR * BLK * BLK,
             moved=3 * 2**20,
         )
-        w_head, query = call(
-            functools.partial(queries_kernel, z_first, shard, piece),
-            (ids,),
-            [x, w_tail] + [v for part in head for v in (part, swap_core(part))],
-            [((cut, BLK), BF16), ((tok * NQ, HD), BF16)],
-            flops=2 * tok * NQ * NBR * BLK * BLK,
-            moved=6 * 2**20,
-        )
-        weights = [w_head, w_tail]
     else:
-        weights = [lax.all_gather(w_packed, "ctx", axis=0, tiled=True)]
+        weights = lax.all_gather(w_packed, "ctx", axis=0, tiled=True)
         query, kv, key = call(
             project_kernel,
             (ids,),
-            (x, *weights),
+            (x, weights),
             [((tok * NQ, HD), BF16), ((tok, 2 * HD), BF16), ((tok, HD), BF16)],
             flops=2 * tok * NNZ * BLK * BLK,
             moved=4 * 2**20,
@@ -450,9 +439,8 @@
         )
 
     if fast:
-        xt_other = swap_core(xt)
         dq_pair = (dq, swap_core(dq))
-        head = weight_terms(0, z_first, dq_pair)
+        head = weight_terms(0, nz - 1, dq_pair)
         head = [head[0]] + [swap_dp(head[k], k) for k in range(1, ndp)]
     (dkv,) = call(
         functools.partial(kv_grad_kernel, nz),
@@ -462,10 +450,10 @@
         moved=2**19,
     )
     if fast:
-        tail = weight_terms(z_first, z_last, (*dq_pair, dkv, swap_core(dkv)))
+        tail = weight_terms(nz - 1, 1, (*dq_pair, dkv, swap_core(dkv)))
         tail = [tail[0]] + [swap_dp(tail[k], k) for k in range(1, ndp)]
         by_z = call(
-            functools.partial(sum_kernel, ndp, nz, z_first, piece),
+            functools.partial(sum_kernel, ndp, nz, piece),
             (),
             (*head, *tail),
             [((piece, BLK), BF16)] * nz,
@@ -500,7 +488,7 @@
     (grad_tokens,) = call(
         token_grad_kernel,
         (ids,),
-        (dq, dkv, *weights),
+        (dq, dkv, weights),
         [((tok, width), BF16)],
         scratch=[pltpu.VMEM((tok, width), F32)],
         flops=2 * tok * NNZ * BLK * BLK,

time: 102 us -> 94 us (0.922)
  starting transfers between devices: 42.6 us -> 35.8 us
  waiting for transfers between devices: 37.2 us -> 35.5 us
    ppermute x15 -> x12, starting transfers between devices: 19.8 us -> 14.9 us  [swap_dp(): return lax.ppermute(v, 'dp', [(i, i ^ k) for i in range(ndp)])]
    ppermute x12, waiting for transfers between devices: 13.2 us -> 11 us  [shift_z(): lax.ppermute(v, 'ctx', [(i, (i // 2 + k) % nz * 2 + i % 2) for i in range...]
    ppermute x19 -> x16, starting transfers between devices: 3.95 us -> 2.84 us  [swap_core(): return lax.ppermute(v, 'ctx', [(i, i ^ 1) for i in range(nctx)])]
    unnamed x10 -> x11, local copies, waits for them, and re-layouts: 3.72 us -> 2.83 us
    ppermute x15 -> x12, waiting for transfers between devices: 20.8 us -> 21.3 us  [swap_dp(): return lax.ppermute(v, 'dp', [(i, i ^ k) for i in range(ndp)])]
    pallas_call x12 -> x11, Pallas kernels: 17.8 us -> 17.7 us  [call(): pl.pallas_call(body, in_specs=[SMEM] * len(scalars) + [VMEM] * len(arrays...]
    ppermute x19 -> x16, waiting for transfers between devices: 3.22 us -> 3.19 us  [swap_core(): return lax.ppermute(v, 'ctx', [(i, i ^ 1) for i in range(nctx)])]
  transfers between devices with their start and end apart: 46 -> 40, of which waited for: 21 -> 16; matrix products, arithmetic and copies ran while one was open for 2% -> 3% of each run, Pallas kernels for 16% -> 10%
where the time goes in v3:
time: 94 us; the launch traced here: 93.7 us
  starting transfers between devices  35.8 us (38%)
  waiting for transfers between devices  35.5 us (38%)
  Pallas kernels  17.7 us (19%)
  local copies, waits for them, and re-layouts  3.73 us (4%)
    ppermute x12, waiting for transfers between devices, swap_dp(): return lax.ppermute(v, 'dp', [(i, i ^ k) for i in range(ndp)])  21.3 us
    ppermute x12, starting transfers between devices, shift_z(): lax.ppermute(v, 'ctx', [(i, (i // 2 + k) % nz * 2 + i % 2) for i in range...  18.1 us
    pallas_call x11, Pallas kernels, call(): pl.pallas_call(body, in_specs=[SMEM] * len(scalars) + [VMEM] * len(arrays...  17.7 us
    ppermute x12, starting transfers between devices, swap_dp(): return lax.ppermute(v, 'dp', [(i, i ^ k) for i in range(ndp)])  14.9 us
    ppermute x12, waiting for transfers between devices, shift_z(): lax.ppermute(v, 'ctx', [(i, (i // 2 + k) % nz * 2 + i % 2) for i in range...  11 us
    ppermute x16, waiting for transfers between devices, swap_core(): return lax.ppermute(v, 'ctx', [(i, i ^ 1) for i in range(nctx)])  3.19 us
    ppermute x16, starting transfers between devices, swap_core(): return lax.ppermute(v, 'ctx', [(i, i ^ 1) for i in range(nctx)])  2.84 us
    unnamed x11, local copies, waits for them, and re-layouts  2.83 us
  transfers between devices with their start and end apart: 40, of which 16 were waited for; matrix products, arithmetic and copies ran while one was open for 3% of the time, Pallas kernels for 10%

profile of v3, /device:TPU:0, one launch (start us, length us, event | category | flops | bytes accessed | tf_op | source)
XLA Modules:
  0.0 93.7 jit_solution(11367340229167948551)
XLA Ops:
  0.6 0.5 collective-permute-start
  1.1 0.9 constant_dynamic-slice_fusion
  2.0 4.6 %collective-permute-start.3 = (bf16[320,128]{1,0:T(8,128)(2,1)S(1)}, bf16[320,128]{1,0:T(8,128)(2,1)S(1)}, u32[]{:S(2)}, u32[]{:S(2)}) collective-permute-start(bf16[320,128]{1,0:T(8,128)(2,1)S(1)} %constant_dynamic-slice_fusion), channel_id=1, source_target_pairs={{0,6},{1,7},{2,0},{3,1},{4,2},{5,3},{6,4},{7,5},{8,14},{9,15},{10,... | collective-permute-start | bytes 245768 | tf_op jit(solution)/shard_map/ppermute | solution.py:335
  6.7 1.0 %collective-permute-start.1 = (bf16[320,128]{1,0:T(8,128)(2,1)S(1)}, bf16[320,128]{1,0:T(8,128)(2,1)S(1)}, u32[]{:S(2)}, u32[]{:S(2)}) collective-permute-start(bf16[320,128]{1,0:T(8,128)(2,1)S(1)} %constant_dynamic-slice_fusion), channel_id=1, source_target_pairs={{0,2},{1,3},{2,4},{3,5},{4,6},{5,7},{6,0},{7,1},{8,10},{9,11},{10,... | collective-permute-start | bytes 245768 | tf_op jit(solution)/shard_map/ppermute | solution.py:335
  7.7 0.8 copy.9.refs_1_
  8.4 0.8 copy.8.refs_0_
  9.2 1.2 %copy-done = bf16[1,128,4096]{2,1,0:T(8,128)(2,1)S(1)} copy-done((bf16[1,128,4096]{2,1,0:T(8,128)(2,1)S(1)}, bf16[1,128,4096]{2,1,0:T(8,128)(2,1)}, u32[]{:S(2)}) %copy-start) | copy-done | bytes 1048600
  10.4 2.0 %shard_map.68 = (bf16[4096,128]{1,0:T(8,128)(2,1)S(1)}, s32[10,8]{1,0:T(8,128)S(1)}, s32[8,2]{1,0:T(8,128)S(1)}) custom-call(s32[10,8]{1,0:T(8,128)S(1)} %copy.8.refs_0_, s32[8,2]{1,0:T(8,128)S(1)} %copy.9.refs_1_, bf16[128,4096]{1,0:T(8,128)(2,1)S(1)} %bitcast.3), custom_call_target="tpu_custom_call" | custom-call | bytes 2097152 | tf_op jit(solution)/shard_map/pallas_call | solution.py:44
  12.5 0.1 copy.10.refs_0_
  12.6 2.6 %collective-permute-done.2.refs_1_ = bf16[320,128]{1,0:T(8,128)(2,1)S(1)} collective-permute-done((bf16[320,128]{1,0:T(8,128)(2,1)S(1)}, bf16[320,128]{1,0:T(8,128)(2,1)S(1)}, u32[]{:S(2)}, u32[]{:S(2)}) %collective-permute-start.2) | collective-permute-done | bytes 81952 | tf_op jit(solution)/shard_map/ppermute | solution.py:335
  15.2 0.1 collective-permute-start.11
  15.3 2.5 %collective-permute-start.9 = (bf16[960,128]{1,0:T(8,128)(2,1)S(1)}, bf16[960,128]{1,0:T(8,128)(2,1)S(1)}, u32[]{:S(2)}, u32[]{:S(2)}) collective-permute-start(bf16[960,128]{1,0:T(8,128)(2,1)S(1)} %shard_map.69.refs_1_.refs_4_), channel_id=1, source_target_pairs={{0,24},{8,16},{16,8},{24,0},{1,25},{9,17},{17,9},{25,1},{2,26},{10... | collective-permute-start | bytes 737288 | tf_op jit(solution)/shard_map/ppermute | solution.py:340
  17.8 0.5 collective-permute-start.7
  18.3 0.5 collective-permute-start.5
  18.9 6.2 %collective-permute-done.9.refs_10_ = bf16[960,128]{1,0:T(8,128)(2,1)S(1)} collective-permute-done((bf16[960,128]{1,0:T(8,128)(2,1)S(1)}, bf16[960,128]{1,0:T(8,128)(2,1)S(1)}, u32[]{:S(2)}, u32[]{:S(2)}) %collective-permute-start.9) | collective-permute-done | bytes 245792 | tf_op jit(solution)/shard_map/ppermute | solution.py:340
  25.1 4.8 %collective-permute-done.7.refs_8_ = bf16[960,128]{1,0:T(8,128)(2,1)S(1)} collective-permute-done((bf16[960,128]{1,0:T(8,128)(2,1)S(1)}, bf16[960,128]{1,0:T(8,128)(2,1)S(1)}, u32[]{:S(2)}, u32[]{:S(2)}) %collective-permute-start.7) | collective-permute-done | bytes 245792 | tf_op jit(solution)/shard_map/ppermute | solution.py:340
  29.9 0.1 collective-permute-done.5.refs_6_
  29.9 0.4 collective-permute-start.6
  30.4 1.0 %collective-permute-done.8.refs_9_ = bf16[960,128]{1,0:T(8,128)(2,1)S(1)} collective-permute-done((bf16[960,128]{1,0:T(8,128)(2,1)S(1)}, bf16[960,128]{1,0:T(8,128)(2,1)S(1)}, u32[]{:S(2)}, u32[]{:S(2)}) %collective-permute-start.8) | collective-permute-done | bytes 245792 | tf_op jit(solution)/shard_map/ppermute | solution.py:332
  31.4 0.4 collective-permute-done.6.refs_7_
  31.7 1.2 %shard_map.71 = (bf16[10240,128]{1,0:T(8,128)(2,1)S(1)}, bf16[128,256]{1,0:T(8,128)(2,1)S(1)}, bf16[128,128]{1,0:T(8,128)(2,1)S(1)}) custom-call(s32[10,8]{1,0:T(8,128)S(1)} %get-tuple-element.29.refs_3_.refs_0_, bf16[128,4096]{1,0:T(8,128)(2,1)S(1)} %bitcast.4, bf16[1280,128]{1,0:T(8,128)(2,1)S(1)} %copy-done.2, ...), custom_call_target="tpu_custom_call" | custom-call | flops 67108864 | bytes 6291456 | tf_op jit(solution)/shard_map/pallas_call | solution.py:44
  32.9 1.7 %collective-permute-start.17 = (bf16[128,256]{1,0:T(8,128)(2,1)S(1)}, bf16[128,256]{1,0:T(8,128)(2,1)S(1)}, u32[]{:S(2)}, u32[]{:S(2)}) collective-permute-start(bf16[128,256]{1,0:T(8,128)(2,1)S(1)} %get-tuple-element.33.refs_3_), channel_id=1, source_target_pairs={{0,6},{1,7},{2,0},{3,1},{4,2},{5,3},{6,4},{7,5},{8,14},{9,15},{10,... | collective-permute-start | bytes 196616 | tf_op jit(solution)/shard_map/ppermute | solution.py:335
  34.6 0.2 collective-permute-start.15
  34.8 1.9 %collective-permute-start.13 = (bf16[128,256]{1,0:T(8,128)(2,1)S(1)}, bf16[128,256]{1,0:T(8,128)(2,1)S(1)}, u32[]{:S(2)}, u32[]{:S(2)}) collective-permute-start(bf16[128,256]{1,0:T(8,128)(2,1)S(1)} %get-tuple-element.33.refs_3_), channel_id=1, source_target_pairs={{0,2},{1,3},{2,4},{3,5},{4,6},{5,7},{6,0},{7,1},{8,10},{9,11},{10,... | collective-permute-start | bytes 196616 | tf_op jit(solution)/shard_map/ppermute | solution.py:335
  36.7 0.5 collective-permute-done.17.refs_9_
  37.3 4.8 %collective-permute-done.15.refs_7_ = bf16[128,256]{1,0:T(8,128)(2,1)S(1)} collective-permute-done((bf16[128,256]{1,0:T(8,128)(2,1)S(1)}, bf16[128,256]{1,0:T(8,128)(2,1)S(1)}, u32[]{:S(2)}, u32[]{:S(2)}) %collective-permute-start.15) | collective-permute-done | bytes 65568 | tf_op jit(solution)/shard_map/ppermute | solution.py:335
  42.1 0.5 collective-permute-start.14
  42.6 1.5 %shard_map.72.refs_1_ = bf16[1024,128]{1,0:T(8,128)(2,1)S(1)} custom-call(s32[10,8]{1,0:T(8,128)S(1)} %get-tuple-element.29.refs_3_.refs_0_, bf16[128,4096]{1,0:T(8,128)(2,1)S(1)} %bitcast.5, bf16[10240,128]{1,0:T(8,128)(2,1)S(1)} %get-tuple-element.32.refs_2_.refs_3_), custom_call_target="tpu_custom_call" | custom-call | flops 268435456 | bytes 3145728 | tf_op jit(solution)/shard_map/pallas_call | solution.py:44
  44.1 6.3 %shard_map.73 = (bf16[8,128,128]{2,1,0:T(8,128)(2,1)S(1)}, bf16[128,256]{1,0:T(8,128)(2,1)S(1)}, bf16[128,256]{1,0:T(8,128)(2,1)S(1)}, bf16[128,256]{1,0:T(8,128...) custom-call(s32[8,2]{1,0:T(8,128)S(1)} %get-tuple-element.30.refs_0_, ...), custom_call_target="tpu_custom_call" | custom-call | flops 671088640 | bytes 4194304 | tf_op jit(solution)/shard_map/pallas_call | solution.py:44
  50.4 0.1 collective-permute-start.20
  50.5 0.5 collective-permute-start.19
  51.0 0.1 collective-permute-start.22
  51.0 0.4 collective-permute-start.24
  51.5 0.1 collective-permute-start.26
  51.6 0.2 collective-permute-done.20
  51.7 0.1 collective-permute-start.21
  51.8 0.4 collective-permute-done.22
  52.2 1.5 %collective-permute-start.23 = (bf16[128,256]{1,0:T(8,128)(2,1)S(1)}, bf16[128,256]{1,0:T(8,128)(2,1)S(1)}, u32[]{:S(2)}, u32[]{:S(2)}) collective-permute-start(bf16[128,256]{1,0:T(8,128)(2,1)S(1)} %add_convert_fusion.2), channel_id=1, source_target_pairs={{0,4},{1,5},{2,6},{3,7},{4,0},{5,1},{6,2},{7,3},{8,12},{9,13},{10,... | collective-permute-start | bytes 196616 | tf_op jit(solution)/shard_map/ppermute | solution.py:335
  53.8 2.6 %collective-permute-start.25 = (bf16[128,256]{1,0:T(8,128)(2,1)S(1)}, bf16[128,256]{1,0:T(8,128)(2,1)S(1)}, u32[]{:S(2)}, u32[]{:S(2)}) collective-permute-start(bf16[128,256]{1,0:T(8,128)(2,1)S(1)} %add_convert_fusion.1), channel_id=1, source_target_pairs={{0,6},{1,7},{2,0},{3,1},{4,2},{5,3},{6,4},{7,5},{8,14},{9,15},{10,... | collective-permute-start | bytes 196616 | tf_op jit(solution)/shard_map/ppermute | solution.py:335
  56.4 1.5 %shard_map.76 = (bf16[960,128]{1,0:T(8,128)(2,1)S(1)}, bf16[960,128]{1,0:T(8,128)(2,1)S(1)}, bf16[960,128]{1,0:T(8,128)(2,1)S(1)}, bf16[960,128]{1,0:T(8,128)(2,1)S(1)}) custom-call(s32[10,8]{1,0:T(8,128)S(1)} %get-tuple-element.29.refs_3_.refs_0_, bf16[4096,128]{1,0:T(8,128)(2,1)S(1)} %get-tuple-element.31.refs_1_, ...), custom_call_target="tpu_custom_call" | custom-call | flops 251658240 | bytes 4194304 | tf_op jit(solution)/shard_map/pallas_call | solution.py:44
  57.9 1.6 %collective-permute-start.27 = (bf16[960,128]{1,0:T(8,128)(2,1)S(1)}, bf16[960,128]{1,0:T(8,128)(2,1)S(1)}, u32[]{:S(2)}, u32[]{:S(2)}) collective-permute-start(bf16[960,128]{1,0:T(8,128)(2,1)S(1)} %get-tuple-element.45), channel_id=1, source_target_pairs={{0,8},{8,0},{16,24},{24,16},{1,9},{9,1},{17,25},{25,17},{2,10},{10... | collective-permute-start | bytes 737288 | tf_op jit(solution)/shard_map/ppermute | solution.py:340
  59.4 0.9 collective-permute-start.28
  60.3 1.1 %collective-permute-start.29 = (bf16[960,128]{1,0:T(8,128)(2,1)S(1)}, bf16[960,128]{1,0:T(8,128)(2,1)S(1)}, u32[]{:S(2)}, u32[]{:S(2)}) collective-permute-start(bf16[960,128]{1,0:T(8,128)(2,1)S(1)} %get-tuple-element.47), channel_id=1, source_target_pairs={{0,24},{8,16},{16,8},{24,0},{1,25},{9,17},{17,9},{25,1},{2,26},{10... | collective-permute-start | bytes 737288 | tf_op jit(solution)/shard_map/ppermute | solution.py:340
  61.5 0.1 shard_map.74.refs_2_.refs_5_
  61.6 0.1 collective-permute-start.30
  61.7 1.2 %collective-permute-done.30.refs_6_ = bf16[2,128,128]{2,1,0:T(8,128)(2,1)S(1)} collective-permute-done((bf16[2,128,128]{2,1,0:T(8,128)(2,1)S(1)}, bf16[2,128,128]{2,1,0:T(8,128)(2,1)S(1)}, u32[]{:S(2)}, u32[]{:S(2)}) %collective-permute-start.30) | collective-permute-done | bytes 65568 | tf_op jit(solution)/shard_map/ppermute | solution.py:332
  62.9 1.0 %shard_map.77 = (bf16[320,128]{1,0:T(8,128)(2,1)S(1)}, bf16[320,128]{1,0:T(8,128)(2,1)S(1)}, bf16[320,128]{1,0:T(8,128)(2,1)S(1)}, bf16[320,128]{1,0:T(8,128)(2,1)S(1)}) custom-call(s32[10,8]{1,0:T(8,128)S(1)} %get-tuple-element.29.refs_3_.refs_0_, bf16[4096,128]{1,0:T(8,128)(2,1)S(1)} %get-tuple-element.31.refs_1_, ...), custom_call_target="tpu_custom_call" | custom-call | flops 83886080 | bytes 4194304 | tf_op jit(solution)/shard_map/pallas_call | solution.py:44
  64.0 1.6 %collective-permute-start.31 = (bf16[320,128]{1,0:T(8,128)(2,1)S(1)}, bf16[320,128]{1,0:T(8,128)(2,1)S(1)}, u32[]{:S(2)}, u32[]{:S(2)}) collective-permute-start(bf16[320,128]{1,0:T(8,128)(2,1)S(1)} %get-tuple-element.49), channel_id=1, source_target_pairs={{0,8},{8,0},{16,24},{24,16},{1,9},{9,1},{17,25},{25,17},{2,10},{10... | collective-permute-start | bytes 245768 | tf_op jit(solution)/shard_map/ppermute | solution.py:340
  65.5 0.9 collective-permute-start.32
  66.4 5.8 %collective-permute-done.31.refs_5_ = bf16[320,128]{1,0:T(8,128)(2,1)S(1)} collective-permute-done((bf16[320,128]{1,0:T(8,128)(2,1)S(1)}, bf16[320,128]{1,0:T(8,128)(2,1)S(1)}, u32[]{:S(2)}, u32[]{:S(2)}) %collective-permute-start.31) | collective-permute-done | bytes 81952 | tf_op jit(solution)/shard_map/ppermute | solution.py:340
  72.3 1.8 %collective-permute-start.33 = (bf16[320,128]{1,0:T(8,128)(2,1)S(1)}, bf16[320,128]{1,0:T(8,128)(2,1)S(1)}, u32[]{:S(2)}, u32[]{:S(2)}) collective-permute-start(bf16[320,128]{1,0:T(8,128)(2,1)S(1)} %get-tuple-element.51), channel_id=1, source_target_pairs={{0,24},{8,16},{16,8},{24,0},{1,25},{9,17},{17,9},{25,1},{2,26},{10... | collective-permute-start | bytes 245768 | tf_op jit(solution)/shard_map/ppermute | solution.py:340
  74.1 3.5 %collective-permute-done.33.refs_7_ = bf16[320,128]{1,0:T(8,128)(2,1)S(1)} collective-permute-done((bf16[320,128]{1,0:T(8,128)(2,1)S(1)}, bf16[320,128]{1,0:T(8,128)(2,1)S(1)}, u32[]{:S(2)}, u32[]{:S(2)}) %collective-permute-start.33) | collective-permute-done | bytes 81952 | tf_op jit(solution)/shard_map/ppermute | solution.py:340
  77.6 0.3 shard_map.78
  77.9 0.3 collective-permute-start.34
  78.2 1.2 %collective-permute-start.35 = (bf16[320,128]{1,0:T(8,128)(2,1)S(1)}, bf16[320,128]{1,0:T(8,128)(2,1)S(1)}, u32[]{:S(2)}, u32[]{:S(2)}) collective-permute-start(bf16[320,128]{1,0:T(8,128)(2,1)S(1)} %get-tuple-element.54), channel_id=1, source_target_pairs={{0,4},{1,5},{2,6},{3,7},{4,0},{5,1},{6,2},{7,3},{8,12},{9,13},{10,... | collective-permute-start | bytes 245768 | tf_op jit(solution)/shard_map/ppermute | solution.py:335
  79.5 2.8 %collective-permute-start.36 = (bf16[320,128]{1,0:T(8,128)(2,1)S(1)}, bf16[320,128]{1,0:T(8,128)(2,1)S(1)}, u32[]{:S(2)}, u32[]{:S(2)}) collective-permute-start(bf16[320,128]{1,0:T(8,128)(2,1)S(1)} %get-tuple-element.55), channel_id=1, source_target_pairs={{0,6},{1,7},{2,0},{3,1},{4,2},{5,3},{6,4},{7,5},{8,14},{9,15},{10,... | collective-permute-start | bytes 245768 | tf_op jit(solution)/shard_map/ppermute | solution.py:335
  82.3 2.0 %collective-permute-done.34 = bf16[320,128]{1,0:T(8,128)(2,1)S(1)} collective-permute-done((bf16[320,128]{1,0:T(8,128)(2,1)S(1)}, bf16[320,128]{1,0:T(8,128)(2,1)S(1)}, u32[]{:S(2)}, u32[]{:S(2)}) %collective-permute-start.34) | collective-permute-done | bytes 81952 | tf_op jit(solution)/shard_map/ppermute | solution.py:335
  84.3 1.0 %collective-permute-done.35 = bf16[320,128]{1,0:T(8,128)(2,1)S(1)} collective-permute-done((bf16[320,128]{1,0:T(8,128)(2,1)S(1)}, bf16[320,128]{1,0:T(8,128)(2,1)S(1)}, u32[]{:S(2)}, u32[]{:S(2)}) %collective-permute-start.35) | collective-permute-done | bytes 81952 | tf_op jit(solution)/shard_map/ppermute | solution.py:335
  85.4 1.9 %collective-permute-start.39 = (bf16[320,128]{1,0:T(8,128)(2,1)S(1)}, bf16[320,128]{1,0:T(8,128)(2,1)S(1)}, u32[]{:S(2)}, u32[]{:S(2)}) collective-permute-start(bf16[320,128]{1,0:T(8,128)(2,1)S(1)} %add_convert_fusion.refs_0_), channel_id=1, source_target_pairs={{0,24},{8,16},{16,8},{24,0},{1,25},{9,17},{17,9},{25,1},{2,26},{10... | collective-permute-start | bytes 245768 | tf_op jit(solution)/shard_map/ppermute | solution.py:340
  87.3 1.2 %collective-permute-start.38 = (bf16[320,128]{1,0:T(8,128)(2,1)S(1)}, bf16[320,128]{1,0:T(8,128)(2,1)S(1)}, u32[]{:S(2)}, u32[]{:S(2)}) collective-permute-start(bf16[320,128]{1,0:T(8,128)(2,1)S(1)} %add_convert_fusion.refs_0_), channel_id=1, source_target_pairs={{0,16},{8,24},{16,0},{24,8},{1,17},{9,25},{17,1},{25,9},{2,18},{10... | collective-permute-start | bytes 245768 | tf_op jit(solution)/shard_map/ppermute | solution.py:340
  88.4 0.5 collective-permute-start.37
  89.0 3.0 %shard_map.75 = bf16[128,4096]{1,0:T(8,128)(2,1)} custom-call(s32[10,8]{1,0:T(8,128)S(1)} %get-tuple-element.29.refs_3_.refs_0_, bf16[8,128,128]{2,1,0:T(8,128)(2,1)S(1)} %get-tuple-element.34.refs_1_.refs_3_, bf16[2,128,128]{2,1,0:T(8,128)(2,1)S(1)} %shard_map.74.refs_2_.refs_5_, bf16[10240,128]{1,0:T(8,128)(2,1)S(1)} %get-tuple-element.32.refs_2_.refs_3_), custom_call_target="tpu_custom_call" | custom-call | flops 335544320 | bytes 4194304 | tf_op jit(solution)/shard_map/pallas_call | solution.py:44
  92.0 0.9 collective-permute-done.37.refs_1_
  92.9 0.9 shard_map.79
  (45 shorter events, 0.3 us)
Async XLA Ops:
  0.6 14.6 %collective-permute-start = (bf16[1280,128]{1,0:T(8,128)(2,1)}, bf16[1280,128]{1,0:T(8,128)(2,1)S(1)}, u32[]{:S(2)}, u32[]{:S(2)}) collective-permute-start(bf16[1280,128]{1,0:T(8,128)(2,1)} %refs_2_.1), channel_id=1, source_target_pairs={{0,1},{1,0},{2,3},{3,2},{4,5},{5,4},{6,7},{7,6},{8,9},{9,8},{10,11... | collective-permute-start | bytes 983048 | tf_op jit(solution)/shard_map/ppermute | solution.py:332
  2.0 10.5 %collective-permute-start.3 = (bf16[320,128]{1,0:T(8,128)(2,1)S(1)}, bf16[320,128]{1,0:T(8,128)(2,1)S(1)}, u32[]{:S(2)}, u32[]{:S(2)}) collective-permute-start(bf16[320,128]{1,0:T(8,128)(2,1)S(1)} %constant_dynamic-slice_fusion), channel_id=1, source_target_pairs={{0,6},{1,7},{2,0},{3,1},{4,2},{5,3},{6,4},{7,5},{8,14},{9,15},{10,... | collective-permute-start | bytes 245768 | tf_op jit(solution)/shard_map/ppermute | solution.py:335
  6.7 8.5 %collective-permute-start.2 = (bf16[320,128]{1,0:T(8,128)(2,1)S(1)}, bf16[320,128]{1,0:T(8,128)(2,1)S(1)}, u32[]{:S(2)}, u32[]{:S(2)}) collective-permute-start(bf16[320,128]{1,0:T(8,128)(2,1)S(1)} %constant_dynamic-slice_fusion), channel_id=1, source_target_pairs={{0,4},{1,5},{2,6},{3,7},{4,0},{5,1},{6,2},{7,3},{8,12},{9,13},{10,... | collective-permute-start | bytes 245768 | tf_op jit(solution)/shard_map/ppermute | solution.py:335
  6.7 8.5 %collective-permute-start.1 = (bf16[320,128]{1,0:T(8,128)(2,1)S(1)}, bf16[320,128]{1,0:T(8,128)(2,1)S(1)}, u32[]{:S(2)}, u32[]{:S(2)}) collective-permute-start(bf16[320,128]{1,0:T(8,128)(2,1)S(1)} %constant_dynamic-slice_fusion), channel_id=1, source_target_pairs={{0,2},{1,3},{2,4},{3,5},{4,6},{5,7},{6,0},{7,1},{8,10},{9,11},{10,... | collective-permute-start | bytes 245768 | tf_op jit(solution)/shard_map/ppermute | solution.py:335
  9.2 1.2 %copy-start = (bf16[1,128,4096]{2,1,0:T(8,128)(2,1)S(1)}, bf16[1,128,4096]{2,1,0:T(8,128)(2,1)}, u32[]{:S(2)}) copy-start(bf16[1,128,4096]{2,1,0:T(8,128)(2,1)} %param.5) | copy-start | bytes 3145732
  12.4 19.3 %copy-start.1 = (bf16[1,128,4096]{2,1,0:T(8,128)(2,1)S(1)}, bf16[1,128,4096]{2,1,0:T(8,128)(2,1)}, u32[]{:S(2)}) copy-start(bf16[1,128,4096]{2,1,0:T(8,128)(2,1)} %param.5) | copy-start | bytes 3145732
  12.5 19.3 %copy-start.2 = (bf16[1280,128]{1,0:T(8,128)(2,1)S(1)}, bf16[1280,128]{1,0:T(8,128)(2,1)}, u32[]{:S(2)}) copy-start(bf16[1280,128]{1,0:T(8,128)(2,1)} %refs_2_.1) | copy-start | bytes 983044
  15.2 16.5 %collective-permute-start.11 = (bf16[4096,128]{1,0:T(8,128)(2,1)S(1)}, bf16[4096,128]{1,0:T(8,128)(2,1)S(1)}, u32[]{:S(2)}, u32[]{:S(2)}) collective-permute-start(bf16[4096,128]{1,0:T(8,128)(2,1)S(1)} %shard_map.70), channel_id=1, source_target_pairs={{0,1},{1,0},{2,3},{3,2},{4,5},{5,4},{6,7},{7,6},{8,9},{9,8},{10,11... | collective-permute-start | bytes 3145736 | tf_op jit(solution)/shard_map/ppermute | solution.py:332
  15.3 9.7 %collective-permute-start.9 = (bf16[960,128]{1,0:T(8,128)(2,1)S(1)}, bf16[960,128]{1,0:T(8,128)(2,1)S(1)}, u32[]{:S(2)}, u32[]{:S(2)}) collective-permute-start(bf16[960,128]{1,0:T(8,128)(2,1)S(1)} %shard_map.69.refs_1_.refs_4_), channel_id=1, source_target_pairs={{0,24},{8,16},{16,8},{24,0},{1,25},{9,17},{17,9},{25,1},{2,26},{10... | collective-permute-start | bytes 737288 | tf_op jit(solution)/shard_map/ppermute | solution.py:340
  17.8 12.0 %collective-permute-start.7 = (bf16[960,128]{1,0:T(8,128)(2,1)S(1)}, bf16[960,128]{1,0:T(8,128)(2,1)S(1)}, u32[]{:S(2)}, u32[]{:S(2)}) collective-permute-start(bf16[960,128]{1,0:T(8,128)(2,1)S(1)} %shard_map.69.refs_1_.refs_4_), channel_id=1, source_target_pairs={{0,16},{8,24},{16,0},{24,8},{1,17},{9,25},{17,1},{25,9},{2,18},{10... | collective-permute-start | bytes 737288 | tf_op jit(solution)/shard_map/ppermute | solution.py:340
  18.3 11.6 %collective-permute-start.5 = (bf16[960,128]{1,0:T(8,128)(2,1)S(1)}, bf16[960,128]{1,0:T(8,128)(2,1)S(1)}, u32[]{:S(2)}, u32[]{:S(2)}) collective-permute-start(bf16[960,128]{1,0:T(8,128)(2,1)S(1)} %shard_map.69.refs_1_.refs_4_), channel_id=1, source_target_pairs={{0,8},{8,0},{16,24},{24,16},{1,9},{9,1},{17,25},{25,17},{2,10},{10... | collective-permute-start | bytes 737288 | tf_op jit(solution)/shard_map/ppermute | solution.py:340
  18.9 11.5 %collective-permute-start.4 = (bf16[960,128]{1,0:T(8,128)(2,1)S(1)}, bf16[960,128]{1,0:T(8,128)(2,1)S(1)}, u32[]{:S(2)}, u32[]{:S(2)}) collective-permute-start(bf16[960,128]{1,0:T(8,128)(2,1)S(1)} %shard_map.69.refs_1_.refs_4_), channel_id=1, source_target_pairs={{0,1},{1,0},{2,3},{3,2},{4,5},{5,4},{6,7},{7,6},{8,9},{9,8},{10,11... | collective-permute-start | bytes 737288 | tf_op jit(solution)/shard_map/ppermute | solution.py:332
  25.1 5.3 %collective-permute-start.10 = (bf16[960,128]{1,0:T(8,128)(2,1)S(1)}, bf16[960,128]{1,0:T(8,128)(2,1)S(1)}, u32[]{:S(2)}, u32[]{:S(2)}) collective-permute-start(bf16[960,128]{1,0:T(8,128)(2,1)S(1)} %collective-permute-done.9.refs_10_), channel_id=1, source_target_pairs={{0,1},{1,0},{2,3},{3,2},{4,5},{5,4},{6,7},{7,6},{8,9},{9,8},{10,11... | collective-permute-start | bytes 737288 | tf_op jit(solution)/shard_map/ppermute | solution.py:332
  29.8 1.5 %collective-permute-start.8 = (bf16[960,128]{1,0:T(8,128)(2,1)S(1)}, bf16[960,128]{1,0:T(8,128)(2,1)S(1)}, u32[]{:S(2)}, u32[]{:S(2)}) collective-permute-start(bf16[960,128]{1,0:T(8,128)(2,1)S(1)} %collective-permute-done.7.refs_8_), channel_id=1, source_target_pairs={{0,1},{1,0},{2,3},{3,2},{4,5},{5,4},{6,7},{7,6},{8,9},{9,8},{10,11... | collective-permute-start | bytes 737288 | tf_op jit(solution)/shard_map/ppermute | solution.py:332
  29.9 1.8 %collective-permute-start.6 = (bf16[960,128]{1,0:T(8,128)(2,1)S(1)}, bf16[960,128]{1,0:T(8,128)(2,1)S(1)}, u32[]{:S(2)}, u32[]{:S(2)}) collective-permute-start(bf16[960,128]{1,0:T(8,128)(2,1)S(1)} %collective-permute-done.5.refs_6_), channel_id=1, source_target_pairs={{0,1},{1,0},{2,3},{3,2},{4,5},{5,4},{6,7},{7,6},{8,9},{9,8},{10,11... | collective-permute-start | bytes 737288 | tf_op jit(solution)/shard_map/ppermute | solution.py:332
  32.9 11.2 %copy-start.3 = (bf16[1,128,1024]{2,1,0:T(8,128)(2,1)S(1)}, bf16[1,128,1024]{2,1,0:T(8,128)(2,1)}, u32[]{:S(2)}) copy-start(bf16[1,128,1024]{2,1,0:T(8,128)(2,1)} %param.6) | copy-start | bytes 786436
  32.9 4.3 %collective-permute-start.17 = (bf16[128,256]{1,0:T(8,128)(2,1)S(1)}, bf16[128,256]{1,0:T(8,128)(2,1)S(1)}, u32[]{:S(2)}, u32[]{:S(2)}) collective-permute-start(bf16[128,256]{1,0:T(8,128)(2,1)S(1)} %get-tuple-element.33.refs_3_), channel_id=1, source_target_pairs={{0,6},{1,7},{2,0},{3,1},{4,2},{5,3},{6,4},{7,5},{8,14},{9,15},{10,... | collective-permute-start | bytes 196616 | tf_op jit(solution)/shard_map/ppermute | solution.py:335
  34.6 7.5 %collective-permute-start.15 = (bf16[128,256]{1,0:T(8,128)(2,1)S(1)}, bf16[128,256]{1,0:T(8,128)(2,1)S(1)}, u32[]{:S(2)}, u32[]{:S(2)}) collective-permute-start(bf16[128,256]{1,0:T(8,128)(2,1)S(1)} %get-tuple-element.33.refs_3_), channel_id=1, source_target_pairs={{0,4},{1,5},{2,6},{3,7},{4,0},{5,1},{6,2},{7,3},{8,12},{9,13},{10,... | collective-permute-start | bytes 196616 | tf_op jit(solution)/shard_map/ppermute | solution.py:335
  34.8 7.3 %collective-permute-start.13 = (bf16[128,256]{1,0:T(8,128)(2,1)S(1)}, bf16[128,256]{1,0:T(8,128)(2,1)S(1)}, u32[]{:S(2)}, u32[]{:S(2)}) collective-permute-start(bf16[128,256]{1,0:T(8,128)(2,1)S(1)} %get-tuple-element.33.refs_3_), channel_id=1, source_target_pairs={{0,2},{1,3},{2,4},{3,5},{4,6},{5,7},{6,0},{7,1},{8,10},{9,11},{10,... | collective-permute-start | bytes 196616 | tf_op jit(solution)/shard_map/ppermute | solution.py:335
  36.7 7.3 %collective-permute-start.12 = (bf16[128,256]{1,0:T(8,128)(2,1)S(1)}, bf16[128,256]{1,0:T(8,128)(2,1)S(1)}, u32[]{:S(2)}, u32[]{:S(2)}) collective-permute-start(bf16[128,256]{1,0:T(8,128)(2,1)S(1)} %get-tuple-element.33.refs_3_), channel_id=1, source_target_pairs={{0,1},{1,0},{2,3},{3,2},{4,5},{5,4},{6,7},{7,6},{8,9},{9,8},{10,11... | collective-permute-start | bytes 196616 | tf_op jit(solution)/shard_map/ppermute | solution.py:332
  37.2 6.8 %collective-permute-start.18 = (bf16[128,256]{1,0:T(8,128)(2,1)S(1)}, bf16[128,256]{1,0:T(8,128)(2,1)S(1)}, u32[]{:S(2)}, u32[]{:S(2)}) collective-permute-start(bf16[128,256]{1,0:T(8,128)(2,1)S(1)} %collective-permute-done.17.refs_9_), channel_id=1, source_target_pairs={{0,1},{1,0},{2,3},{3,2},{4,5},{5,4},{6,7},{7,6},{8,9},{9,8},{10,11... | collective-permute-start | bytes 196616 | tf_op jit(solution)/shard_map/ppermute | solution.py:332
  42.1 2.0 %collective-permute-start.16 = (bf16[128,256]{1,0:T(8,128)(2,1)S(1)}, bf16[128,256]{1,0:T(8,128)(2,1)S(1)}, u32[]{:S(2)}, u32[]{:S(2)}) collective-permute-start(bf16[128,256]{1,0:T(8,128)(2,1)S(1)} %collective-permute-done.15.refs_7_), channel_id=1, source_target_pairs={{0,1},{1,0},{2,3},{3,2},{4,5},{5,4},{6,7},{7,6},{8,9},{9,8},{10,11... | collective-permute-start | bytes 196616 | tf_op jit(solution)/shard_map/ppermute | solution.py:332
  42.1 2.0 %collective-permute-start.14 = (bf16[128,256]{1,0:T(8,128)(2,1)S(1)}, bf16[128,256]{1,0:T(8,128)(2,1)S(1)}, u32[]{:S(2)}, u32[]{:S(2)}) collective-permute-start(bf16[128,256]{1,0:T(8,128)(2,1)S(1)} %collective-permute-done.13.refs_5_), channel_id=1, source_target_pairs={{0,1},{1,0},{2,3},{3,2},{4,5},{5,4},{6,7},{7,6},{8,9},{9,8},{10,11... | collective-permute-start | bytes 196616 | tf_op jit(solution)/shard_map/ppermute | solution.py:332
  50.4 1.3 %collective-permute-start.20 = (bf16[128,256]{1,0:T(8,128)(2,1)S(1)}, bf16[128,256]{1,0:T(8,128)(2,1)S(1)}, u32[]{:S(2)}, u32[]{:S(2)}) collective-permute-start(bf16[128,256]{1,0:T(8,128)(2,1)S(1)} %get-tuple-element.39), channel_id=1, source_target_pairs={{0,1},{1,0},{2,3},{3,2},{4,5},{5,4},{6,7},{7,6},{8,9},{9,8},{10,11... | collective-permute-start | bytes 196616 | tf_op jit(solution)/shard_map/ppermute | solution.py:332
  50.5 9.0 %collective-permute-start.19 = (bf16[128,256]{1,0:T(8,128)(2,1)S(1)}, bf16[128,256]{1,0:T(8,128)(2,1)S(1)}, u32[]{:S(2)}, u32[]{:S(2)}) collective-permute-start(bf16[128,256]{1,0:T(8,128)(2,1)S(1)} %get-tuple-element.37), channel_id=1, source_target_pairs={{0,1},{1,0},{2,3},{3,2},{4,5},{5,4},{6,7},{7,6},{8,9},{9,8},{10,11... | collective-permute-start | bytes 196616 | tf_op jit(solution)/shard_map/ppermute | solution.py:332
  51.0 1.3 %collective-permute-start.22 = (bf16[128,256]{1,0:T(8,128)(2,1)S(1)}, bf16[128,256]{1,0:T(8,128)(2,1)S(1)}, u32[]{:S(2)}, u32[]{:S(2)}) collective-permute-start(bf16[128,256]{1,0:T(8,128)(2,1)S(1)} %get-tuple-element.41), channel_id=1, source_target_pairs={{0,1},{1,0},{2,3},{3,2},{4,5},{5,4},{6,7},{7,6},{8,9},{9,8},{10,11... | collective-permute-start | bytes 196616 | tf_op jit(solution)/shard_map/ppermute | solution.py:332
  51.0 2.7 %collective-permute-start.24 = (bf16[128,256]{1,0:T(8,128)(2,1)S(1)}, bf16[128,256]{1,0:T(8,128)(2,1)S(1)}, u32[]{:S(2)}, u32[]{:S(2)}) collective-permute-start(bf16[128,256]{1,0:T(8,128)(2,1)S(1)} %get-tuple-element.43), channel_id=1, source_target_pairs={{0,1},{1,0},{2,3},{3,2},{4,5},{5,4},{6,7},{7,6},{8,9},{9,8},{10,11... | collective-permute-start | bytes 196616 | tf_op jit(solution)/shard_map/ppermute | solution.py:332
  51.5 4.9 %collective-permute-start.26 = (bf16[8,128,128]{2,1,0:T(8,128)(2,1)S(1)}, bf16[8,128,128]{2,1,0:T(8,128)(2,1)S(1)}, u32[]{:S(2)}, u32[]{:S(2)}) collective-permute-start(bf16[8,128,128]{2,1,0:T(8,128)(2,1)S(1)} %get-tuple-element.34.refs_1_.refs_3_), channel_id=1, source_target_pairs={{0,1},{1,0},{2,3},{3,2},{4,5},{5,4},{6,7},{7,6},{8,9},{9,8},{10,11... | collective-permute-start | bytes 786440 | tf_op jit(solution)/shard_map/ppermute | solution.py:332
  51.7 8.6 %collective-permute-start.21 = (bf16[128,256]{1,0:T(8,128)(2,1)S(1)}, bf16[128,256]{1,0:T(8,128)(2,1)S(1)}, u32[]{:S(2)}, u32[]{:S(2)}) collective-permute-start(bf16[128,256]{1,0:T(8,128)(2,1)S(1)} %add_convert_fusion.3), channel_id=1, source_target_pairs={{0,2},{1,3},{2,4},{3,5},{4,6},{5,7},{6,0},{7,1},{8,10},{9,11},{10,... | collective-permute-start | bytes 196616 | tf_op jit(solution)/shard_map/ppermute | solution.py:335
  52.2 9.2 %collective-permute-start.23 = (bf16[128,256]{1,0:T(8,128)(2,1)S(1)}, bf16[128,256]{1,0:T(8,128)(2,1)S(1)}, u32[]{:S(2)}, u32[]{:S(2)}) collective-permute-start(bf16[128,256]{1,0:T(8,128)(2,1)S(1)} %add_convert_fusion.2), channel_id=1, source_target_pairs={{0,4},{1,5},{2,6},{3,7},{4,0},{5,1},{6,2},{7,3},{8,12},{9,13},{10,... | collective-permute-start | bytes 196616 | tf_op jit(solution)/shard_map/ppermute | solution.py:335
  53.8 7.7 %collective-permute-start.25 = (bf16[128,256]{1,0:T(8,128)(2,1)S(1)}, bf16[128,256]{1,0:T(8,128)(2,1)S(1)}, u32[]{:S(2)}, u32[]{:S(2)}) collective-permute-start(bf16[128,256]{1,0:T(8,128)(2,1)S(1)} %add_convert_fusion.1), channel_id=1, source_target_pairs={{0,6},{1,7},{2,0},{3,1},{4,2},{5,3},{6,4},{7,5},{8,14},{9,15},{10,... | collective-permute-start | bytes 196616 | tf_op jit(solution)/shard_map/ppermute | solution.py:335
  57.9 19.7 %collective-permute-start.27 = (bf16[960,128]{1,0:T(8,128)(2,1)S(1)}, bf16[960,128]{1,0:T(8,128)(2,1)S(1)}, u32[]{:S(2)}, u32[]{:S(2)}) collective-permute-start(bf16[960,128]{1,0:T(8,128)(2,1)S(1)} %get-tuple-element.45), channel_id=1, source_target_pairs={{0,8},{8,0},{16,24},{24,16},{1,9},{9,1},{17,25},{25,17},{2,10},{10... | collective-permute-start | bytes 737288 | tf_op jit(solution)/shard_map/ppermute | solution.py:340
  59.4 18.2 %collective-permute-start.28 = (bf16[960,128]{1,0:T(8,128)(2,1)S(1)}, bf16[960,128]{1,0:T(8,128)(2,1)S(1)}, u32[]{:S(2)}, u32[]{:S(2)}) collective-permute-start(bf16[960,128]{1,0:T(8,128)(2,1)S(1)} %get-tuple-element.46), channel_id=1, source_target_pairs={{0,16},{8,24},{16,0},{24,8},{1,17},{9,25},{17,1},{25,9},{2,18},{10... | collective-permute-start | bytes 737288 | tf_op jit(solution)/shard_map/ppermute | solution.py:340
  60.3 17.3 %collective-permute-start.29 = (bf16[960,128]{1,0:T(8,128)(2,1)S(1)}, bf16[960,128]{1,0:T(8,128)(2,1)S(1)}, u32[]{:S(2)}, u32[]{:S(2)}) collective-permute-start(bf16[960,128]{1,0:T(8,128)(2,1)S(1)} %get-tuple-element.47), channel_id=1, source_target_pairs={{0,24},{8,16},{16,8},{24,0},{1,25},{9,17},{17,9},{25,1},{2,26},{10... | collective-permute-start | bytes 737288 | tf_op jit(solution)/shard_map/ppermute | solution.py:340
  61.6 1.3 %collective-permute-start.30 = (bf16[2,128,128]{2,1,0:T(8,128)(2,1)S(1)}, bf16[2,128,128]{2,1,0:T(8,128)(2,1)S(1)}, u32[]{:S(2)}, u32[]{:S(2)}) collective-permute-start(bf16[2,128,128]{2,1,0:T(8,128)(2,1)S(1)} %shard_map.74.refs_2_.refs_5_), channel_id=1, source_target_pairs={{0,1},{1,0},{2,3},{3,2},{4,5},{5,4},{6,7},{7,6},{8,9},{9,8},{10,11... | collective-permute-start | bytes 196616 | tf_op jit(solution)/shard_map/ppermute | solution.py:332
  64.0 8.3 %collective-permute-start.31 = (bf16[320,128]{1,0:T(8,128)(2,1)S(1)}, bf16[320,128]{1,0:T(8,128)(2,1)S(1)}, u32[]{:S(2)}, u32[]{:S(2)}) collective-permute-start(bf16[320,128]{1,0:T(8,128)(2,1)S(1)} %get-tuple-element.49), channel_id=1, source_target_pairs={{0,8},{8,0},{16,24},{24,16},{1,9},{9,1},{17,25},{25,17},{2,10},{10... | collective-permute-start | bytes 245768 | tf_op jit(solution)/shard_map/ppermute | solution.py:340
  65.5 8.5 %collective-permute-start.32 = (bf16[320,128]{1,0:T(8,128)(2,1)S(1)}, bf16[320,128]{1,0:T(8,128)(2,1)S(1)}, u32[]{:S(2)}, u32[]{:S(2)}) collective-permute-start(bf16[320,128]{1,0:T(8,128)(2,1)S(1)} %get-tuple-element.50), channel_id=1, source_target_pairs={{0,16},{8,24},{16,0},{24,8},{1,17},{9,25},{17,1},{25,9},{2,18},{10... | collective-permute-start | bytes 245768 | tf_op jit(solution)/shard_map/ppermute | solution.py:340
  72.3 5.3 %collective-permute-start.33 = (bf16[320,128]{1,0:T(8,128)(2,1)S(1)}, bf16[320,128]{1,0:T(8,128)(2,1)S(1)}, u32[]{:S(2)}, u32[]{:S(2)}) collective-permute-start(bf16[320,128]{1,0:T(8,128)(2,1)S(1)} %get-tuple-element.51), channel_id=1, source_target_pairs={{0,24},{8,16},{16,8},{24,0},{1,25},{9,17},{17,9},{25,1},{2,26},{10... | collective-permute-start | bytes 245768 | tf_op jit(solution)/shard_map/ppermute | solution.py:340
  77.9 6.4 %collective-permute-start.34 = (bf16[320,128]{1,0:T(8,128)(2,1)S(1)}, bf16[320,128]{1,0:T(8,128)(2,1)S(1)}, u32[]{:S(2)}, u32[]{:S(2)}) collective-permute-start(bf16[320,128]{1,0:T(8,128)(2,1)S(1)} %get-tuple-element.53), channel_id=1, source_target_pairs={{0,2},{1,3},{2,4},{3,5},{4,6},{5,7},{6,0},{7,1},{8,10},{9,11},{10,... | collective-permute-start | bytes 245768 | tf_op jit(solution)/shard_map/ppermute | solution.py:335
  78.2 7.1 %collective-permute-start.35 = (bf16[320,128]{1,0:T(8,128)(2,1)S(1)}, bf16[320,128]{1,0:T(8,128)(2,1)S(1)}, u32[]{:S(2)}, u32[]{:S(2)}) collective-permute-start(bf16[320,128]{1,0:T(8,128)(2,1)S(1)} %get-tuple-element.54), channel_id=1, source_target_pairs={{0,4},{1,5},{2,6},{3,7},{4,0},{5,1},{6,2},{7,3},{8,12},{9,13},{10,... | collective-permute-start | bytes 245768 | tf_op jit(solution)/shard_map/ppermute | solution.py:335
  79.5 5.9 %collective-permute-start.36 = (bf16[320,128]{1,0:T(8,128)(2,1)S(1)}, bf16[320,128]{1,0:T(8,128)(2,1)S(1)}, u32[]{:S(2)}, u32[]{:S(2)}) collective-permute-start(bf16[320,128]{1,0:T(8,128)(2,1)S(1)} %get-tuple-element.55), channel_id=1, source_target_pairs={{0,6},{1,7},{2,0},{3,1},{4,2},{5,3},{6,4},{7,5},{8,14},{9,15},{10,... | collective-permute-start | bytes 245768 | tf_op jit(solution)/shard_map/ppermute | solution.py:335
  85.4 6.6 %collective-permute-start.39 = (bf16[320,128]{1,0:T(8,128)(2,1)S(1)}, bf16[320,128]{1,0:T(8,128)(2,1)S(1)}, u32[]{:S(2)}, u32[]{:S(2)}) collective-permute-start(bf16[320,128]{1,0:T(8,128)(2,1)S(1)} %add_convert_fusion.refs_0_), channel_id=1, source_target_pairs={{0,24},{8,16},{16,8},{24,0},{1,25},{9,17},{17,9},{25,1},{2,26},{10... | collective-permute-start | bytes 245768 | tf_op jit(solution)/shard_map/ppermute | solution.py:340
  87.3 4.7 %collective-permute-start.38 = (bf16[320,128]{1,0:T(8,128)(2,1)S(1)}, bf16[320,128]{1,0:T(8,128)(2,1)S(1)}, u32[]{:S(2)}, u32[]{:S(2)}) collective-permute-start(bf16[320,128]{1,0:T(8,128)(2,1)S(1)} %add_convert_fusion.refs_0_), channel_id=1, source_target_pairs={{0,16},{8,24},{16,0},{24,8},{1,17},{9,25},{17,1},{25,9},{2,18},{10... | collective-permute-start | bytes 245768 | tf_op jit(solution)/shard_map/ppermute | solution.py:340
  88.4 4.4 %collective-permute-start.37 = (bf16[320,128]{1,0:T(8,128)(2,1)S(1)}, bf16[320,128]{1,0:T(8,128)(2,1)S(1)}, u32[]{:S(2)}, u32[]{:S(2)}) collective-permute-start(bf16[320,128]{1,0:T(8,128)(2,1)S(1)} %add_convert_fusion.refs_0_), channel_id=1, source_target_pairs={{0,8},{8,0},{16,24},{24,16},{1,9},{9,1},{17,25},{25,17},{2,10},{10... | collective-permute-start | bytes 245768 | tf_op jit(solution)/shard_map/ppermute | solution.py:340

commit v4 on v3

--- a/solution.py
+++ b/solution.py
@@ -17,7 +17,6 @@
 NCB = 10
 NNZ = 80
 NQ = GROUPS * QPG
-KEYS = 128
 EPSILON = 1e-06
 SCALE = 1.0 / math.sqrt(HD)
 LOG2E = math.log2(math.e)
@@ -81,7 +80,14 @@
     )
 
 
-def prepare_kernel(ids, spans, x_ref, xt_ref, ids_out, spans_out):
+def head_rows(p, c):
+    return slice((p * NQ + c) * SPAN, (p * NQ + c + 1) * SPAN)
+
+
+def prepare_kernel(ids, spans, x_ref, up_ref, xt_ref, up_out, ids_out, spans_out):
+    for p in range(2):
+        for h in range(NQ):
+            up_out[head_rows(p, h), :] = up_ref[p * SPAN : (p + 1) * SPAN, h * HD : (h + 1) * HD]
     for b in range(x_ref.shape[1] // BLK):
         xt_ref[b * BLK : (b + 1) * BLK, :] = x_ref[:, b * BLK : (b + 1) * BLK].T
     for source, out in ((ids, ids_out), (spans, spans_out)):
@@ -142,26 +148,28 @@
     project_keys(ids, x_ref, w_ref, kv_ref, key_ref)
 
 
-def queries_kernel(ids, x_ref, w_ref, q_ref):
+def queries_kernel(ids, x_ref, w_ref, q_ref, qhat_ref):
     wide = NBR * BLK
     for c in range(NQ):
         out = dot(column_of(c, ids, x_ref), w_ref[c * wide : (c + 1) * wide, :]).astype(BF16)
+        query = out.astype(F32)
+        normed = (query * inverse_rms(query)).astype(BF16)
         for p in range(2):
-            at = (p * NQ + c) * SPAN
-            q_ref[at : at + SPAN, :] = out[p * SPAN : (p + 1) * SPAN, :]
-
-
-def project_kernel(ids, x_ref, w_ref, q_ref, kv_ref, key_ref):
+            q_ref[head_rows(p, c), :] = out[p * SPAN : (p + 1) * SPAN, :]
+            qhat_ref[head_rows(p, c), :] = normed[p * SPAN : (p + 1) * SPAN, :]
+
+
+def project_kernel(ids, x_ref, w_ref, q_ref, qhat_ref, kv_ref, key_ref):
     project_keys(ids, x_ref, w_ref, kv_ref, key_ref)
-    queries_kernel(ids, x_ref, w_ref, q_ref)
-
-
-def attend_kernel(nz, spans, q_ref, up_ref, *refs):
+    queries_kernel(ids, x_ref, w_ref, q_ref, qhat_ref)
+
+
+def attend_kernel(nz, keys, spans, q_ref, qhat, up, *refs):
     pieces = refs[: 2 * nz]
     dq_ref = refs[2 * nz]
     keep = refs[2 * nz + 1 : 3 * nz + 1]
     send = refs[3 * nz + 1 : 4 * nz + 1]
-    kv, qhat, up, expo, dprob, acc, dq_t = refs[4 * nz + 1 :]
+    kv, expo, dprob, acc, dq_t = refs[4 * nz + 1 :]
     half = NQ * SPAN
     me = lax.axis_index("ctx")
     zi, core = me // 2, me % 2
@@ -173,33 +181,27 @@
                 kv[rows_at(spans[source, p] * SPAN, SPAN, SPAN), :] = pieces[2 * k + other][
                     p * SPAN : (p + 1) * SPAN, :
                 ]
-    query = q_ref[...].astype(F32)
-    qhat[...] = (query * inverse_rms(query)).astype(BF16)
-    for p in range(2):
-        for h in range(NQ):
-            at = (p * NQ + h) * SPAN
-            up[at : at + SPAN, :] = up_ref[p * SPAN : (p + 1) * SPAN, h * HD : (h + 1) * HD]
     acc[...] = jnp.zeros_like(acc)
-    key_row = lax.broadcasted_iota(jnp.int32, (KEYS, half), 0)
-    query_at = lax.broadcasted_iota(jnp.int32, (KEYS, half), 1) % SPAN
+    key_row = lax.broadcasted_iota(jnp.int32, (keys, half), 0)
+    query_at = lax.broadcasted_iota(jnp.int32, (keys, half), 1) % SPAN
     for p in range(2):
         span = spans[me, p]
-        blocks = ((span + 1) * SPAN + KEYS - 1) // KEYS
+        blocks = ((span + 1) * SPAN + keys - 1) // keys
         q_part = qhat[p * half : (p + 1) * half, :]
         up_part = up[p * half : (p + 1) * half, :]
         limit = query_at + span * SPAN
 
         def forward(b, sums):
-            rows = rows_at(b * KEYS, KEYS, KEYS)
+            rows = rows_at(b * keys, keys, keys)
             raw = dot(kv[rows, :HD], q_part, ((1,), (1,)))
-            e = jnp.where(key_row + b * KEYS <= limit, jnp.exp2(raw * (SCALE * LOG2E)), 0.0)
+            e = jnp.where(key_row + b * keys <= limit, jnp.exp2(raw * (SCALE * LOG2E)), 0.0)
             dp = dot(kv[rows, HD:], up_part, ((1,), (1,)))
             expo[rows, :] = e
             dprob[rows, :] = dp
             weighted = e.astype(BF16).astype(F32) * dp
             return (
-                sums[0] + jnp.sum(e.reshape(KEYS // 8, 8, half), axis=0),
-                sums[1] + jnp.sum(weighted.reshape(KEYS // 8, 8, half), axis=0),
+                sums[0] + jnp.sum(e.reshape(keys // 8, 8, half), axis=0),
+                sums[1] + jnp.sum(weighted.reshape(keys // 8, 8, half), axis=0),
             )
 
         zero = jnp.zeros((8, half), F32)
@@ -209,7 +211,7 @@
         dq_t[...] = jnp.zeros_like(dq_t)
 
         def backward(b, carry):
-            rows = rows_at(b * KEYS, KEYS, KEYS)
+            rows = rows_at(b * keys, keys, keys)
             prob = expo[rows, :] * inverse
             dscore = (prob * (dprob[rows, :] - delta) * SCALE).astype(BF16)
             acc[rows, :HD] += dot(dscore, q_part)
@@ -318,7 +320,7 @@
     nctx = lax.axis_size("ctx")
     nz = nctx // 2
     dp = lax.axis_index("dp")
-    x, up = tokens[0], grad_attn[0]
+    x = tokens[0]
     tok, width = x.shape
     length = spans.shape[0] * 2 * SPAN
     shard = w_packed.shape[0]
@@ -342,11 +344,16 @@
     def add(a, b):
         return (a.astype(F32) + b.astype(F32)).astype(BF16)
 
-    xt, ids, spans = call(
+    xt, up, ids, spans = call(
         prepare_kernel,
         (ids, spans),
-        (x,),
-        [((width, tok), BF16), (ids.shape, jnp.int32), (spans.shape, jnp.int32)],
+        (x, grad_attn[0]),
+        [
+            ((width, tok), BF16),
+            ((tok * NQ, HD), BF16),
+            (ids.shape, jnp.int32),
+            (spans.shape, jnp.int32),
+        ],
         moved=4 * x.size,
     )
 
@@ -377,21 +384,21 @@
             flops=2 * tok * (NCB - NQ) * NBR * BLK * BLK,
             moved=6 * 2**20,
         )
-        (query,) = call(
+        query, qhat = call(
             queries_kernel,
             (ids,),
             (x, weights),
-            [((tok * NQ, HD), BF16)],
-            flops=2 * tok * NQ * NBR * BLK * BLK,
+            [((tok * NQ, HD), BF16)] * 2,
+            flops=16 * tok * NQ * NBR * BLK * BLK,
             moved=3 * 2**20,
         )
     else:
         weights = lax.all_gather(w_packed, "ctx", axis=0, tiled=True)
-        query, kv, key = call(
+        query, qhat, kv, key = call(
             project_kernel,
             (ids,),
             (x, weights),
-            [((tok * NQ, HD), BF16), ((tok, 2 * HD), BF16), ((tok, HD), BF16)],
+            [((tok * NQ, HD), BF16)] * 2 + [((tok, 2 * HD), BF16), ((tok, HD), BF16)],
             flops=2 * tok * NNZ * BLK * BLK,
             moved=4 * 2**20,
         )
@@ -399,16 +406,14 @@
     kv_pieces = []
     for k in range(nz):
         part = kv if k == 0 else shift_z(kv, k)
-        kv_pieces += [part, swap_core(part)]
+        kv_pieces += [part, swap_core(after(part, query) if k == nz - 1 else part)]
     outs = call(
-        functools.partial(attend_kernel, nz),
+        functools.partial(attend_kernel, nz, math.gcd(512, length)),
         (spans,),
-        (query, up, *kv_pieces),
+        (query, qhat, up, *kv_pieces),
         [((NQ, tok, HD), BF16)] + [((tok, 2 * HD), BF16)] * (2 * nz),
         scratch=[
             pltpu.VMEM((length, 2 * HD), BF16),
-            pltpu.VMEM((tok * NQ, HD), BF16),
-            pltpu.VMEM((tok * NQ, HD), BF16),
             pltpu.VMEM((length, half), F32),
             pltpu.VMEM((length, half), F32),
             pltpu.VMEM((length, 2 * HD), F32),
@@ -451,7 +456,9 @@
     )
     if fast:
         tail = weight_terms(nz - 1, 1, (*dq_pair, dkv, swap_core(dkv)))
-        tail = [tail[0]] + [swap_dp(tail[k], k) for k in range(1, ndp)]
+        tail = [tail[0]] + [
+            swap_dp(after(tail[k], head[1]) if k == ndp - 1 else tail[k], k) for k in range(1, ndp)
+        ]
         by_z = call(
             functools.partial(sum_kernel, ndp, nz, piece),
             (),

time: 94 us -> 91 us (0.968)
  waiting for transfers between devices: 35.5 us -> 33.1 us
  Pallas kernels: 17.7 us -> 16.1 us
  local copies, waits for them, and re-layouts: 3.73 us -> 4.68 us
    ppermute x12, waiting for transfers between devices: 21.3 us -> 18 us  [swap_dp(): return lax.ppermute(v, 'dp', [(i, i ^ k) for i in range(ndp)])]
    pallas_call x11, Pallas kernels: 17.7 us -> 16.1 us  [call(): pl.pallas_call(body, in_specs=[SMEM] * len(scalars) + [VMEM] * len(arrays...]
    ppermute x16, waiting for transfers between devices: 3.19 us -> 4.34 us  [swap_core(): return lax.ppermute(v, 'ctx', [(i, i ^ 1) for i in range(nctx)])]
    unnamed x11 -> x12, local copies, waits for them, and re-layouts: 2.83 us -> 3.78 us
  transfers between devices with their start and end apart: 40 -> 40, of which waited for: 16 -> 18; matrix products, arithmetic and copies ran while one was open for 3% -> 3% of each run, Pallas kernels for 10% -> 10%
where the time goes in v4:
time: 91 us; the launch traced here: 90.7 us
  starting transfers between devices  35.9 us (39%)
  waiting for transfers between devices  33.1 us (36%)
  Pallas kernels  16.1 us (18%)
  local copies, waits for them, and re-layouts  4.68 us (5%)
    ppermute x12, starting transfers between devices, shift_z(): lax.ppermute(v, 'ctx', [(i, (i // 2 + k) % nz * 2 + i % 2) for i in range...  18.1 us
    ppermute x12, waiting for transfers between devices, swap_dp(): return lax.ppermute(v, 'dp', [(i, i ^ k) for i in range(ndp)])  18 us
    pallas_call x11, Pallas kernels, call(): pl.pallas_call(body, in_specs=[SMEM] * len(scalars) + [VMEM] * len(arrays...  16.1 us
    ppermute x12, starting transfers between devices, swap_dp(): return lax.ppermute(v, 'dp', [(i, i ^ k) for i in range(ndp)])  14.9 us
    ppermute x12, waiting for transfers between devices, shift_z(): lax.ppermute(v, 'ctx', [(i, (i // 2 + k) % nz * 2 + i % 2) for i in range...  10.8 us
    ppermute x16, waiting for transfers between devices, swap_core(): return lax.ppermute(v, 'ctx', [(i, i ^ 1) for i in range(nctx)])  4.34 us
    unnamed x12, local copies, waits for them, and re-layouts  3.78 us
    ppermute x16, starting transfers between devices, swap_core(): return lax.ppermute(v, 'ctx', [(i, i ^ 1) for i in range(nctx)])  2.92 us
  transfers between devices with their start and end apart: 40, of which 18 were waited for; matrix products, arithmetic and copies ran while one was open for 3% of the time, Pallas kernels for 10%

profile of v4, /device:TPU:0, one launch (start us, length us, event | category | flops | bytes accessed | tf_op | source)
XLA Modules:
  0.0 90.7 jit_solution(477418768672056127)
XLA Ops:
  0.6 0.5 collective-permute-start
  1.1 0.9 constant_dynamic-slice_fusion
  2.0 4.6 %collective-permute-start.3 = (bf16[320,128]{1,0:T(8,128)(2,1)S(1)}, bf16[320,128]{1,0:T(8,128)(2,1)S(1)}, u32[]{:S(2)}, u32[]{:S(2)}) collective-permute-start(bf16[320,128]{1,0:T(8,128)(2,1)S(1)} %constant_dynamic-slice_fusion), channel_id=1, source_target_pairs={{0,6},{1,7},{2,0},{3,1},{4,2},{5,3},{6,4},{7,5},{8,14},{9,15},{10,... | collective-permute-start | bytes 245768 | tf_op jit(solution)/shard_map/ppermute | solution.py:337
  6.7 1.0 %collective-permute-start.1 = (bf16[320,128]{1,0:T(8,128)(2,1)S(1)}, bf16[320,128]{1,0:T(8,128)(2,1)S(1)}, u32[]{:S(2)}, u32[]{:S(2)}) collective-permute-start(bf16[320,128]{1,0:T(8,128)(2,1)S(1)} %constant_dynamic-slice_fusion), channel_id=1, source_target_pairs={{0,2},{1,3},{2,4},{3,5},{4,6},{5,7},{6,0},{7,1},{8,10},{9,11},{10,... | collective-permute-start | bytes 245768 | tf_op jit(solution)/shard_map/ppermute | solution.py:337
  7.7 0.8 copy.11.refs_1_
  8.4 0.8 copy.10.refs_0_
  9.2 1.2 %copy-done = bf16[1,128,4096]{2,1,0:T(8,128)(2,1)S(1)} copy-done((bf16[1,128,4096]{2,1,0:T(8,128)(2,1)S(1)}, bf16[1,128,4096]{2,1,0:T(8,128)(2,1)}, u32[]{:S(2)}) %copy-start) | copy-done | bytes 1048600
  10.4 0.9 %copy-done.3 = bf16[1,128,1024]{2,1,0:T(8,128)(2,1)S(1)} copy-done((bf16[1,128,1024]{2,1,0:T(8,128)(2,1)S(1)}, bf16[1,128,1024]{2,1,0:T(8,128)(2,1)}, u32[]{:S(2)}) %copy-start.3) | copy-done | bytes 262168
  11.4 2.0 %shard_map.68 = (bf16[4096,128]{1,0:T(8,128)(2,1)S(1)}, bf16[1024,128]{1,0:T(8,128)(2,1)S(1)}, s32[10,8]{1,0:T(8,128)S(1)}, s32[8,2]{1,0:T(8,128)S(1)}) custom-call(s32[10,8]{1,0:T(8,128)S(1)} %copy.10.refs_0_, s32[8,2]{1,0:T(8,128)S(1)} %copy.11.refs_1_, bf16[128,4096]{1,0:T(8,128)(2,1)S(1)} %bitcast.3, bf16[128,1024]{1,0:T(8,128)(2,1)S(1)} %bitcast.6), custom_call_target="tpu_custom_call" | custom-call | bytes 2097152 | tf_op jit(solution)/shard_map/pallas_call | solution.py:43
  13.4 0.1 copy.12.refs_0_
  13.5 1.7 %collective-permute-done.2.refs_1_ = bf16[320,128]{1,0:T(8,128)(2,1)S(1)} collective-permute-done((bf16[320,128]{1,0:T(8,128)(2,1)S(1)}, bf16[320,128]{1,0:T(8,128)(2,1)S(1)}, u32[]{:S(2)}, u32[]{:S(2)}) %collective-permute-start.2) | collective-permute-done | bytes 81952 | tf_op jit(solution)/shard_map/ppermute | solution.py:337
  15.2 0.1 collective-permute-start.11
  15.3 2.5 %collective-permute-start.9 = (bf16[960,128]{1,0:T(8,128)(2,1)S(1)}, bf16[960,128]{1,0:T(8,128)(2,1)S(1)}, u32[]{:S(2)}, u32[]{:S(2)}) collective-permute-start(bf16[960,128]{1,0:T(8,128)(2,1)S(1)} %shard_map.69.refs_1_.refs_4_), channel_id=1, source_target_pairs={{0,24},{8,16},{16,8},{24,0},{1,25},{9,17},{17,9},{25,1},{2,26},{10... | collective-permute-start | bytes 737288 | tf_op jit(solution)/shard_map/ppermute | solution.py:342
  17.8 0.5 collective-permute-start.7
  18.3 0.5 collective-permute-start.5
  18.9 6.2 %collective-permute-done.9.refs_10_ = bf16[960,128]{1,0:T(8,128)(2,1)S(1)} collective-permute-done((bf16[960,128]{1,0:T(8,128)(2,1)S(1)}, bf16[960,128]{1,0:T(8,128)(2,1)S(1)}, u32[]{:S(2)}, u32[]{:S(2)}) %collective-permute-start.9) | collective-permute-done | bytes 245792 | tf_op jit(solution)/shard_map/ppermute | solution.py:342
  25.1 4.8 %collective-permute-done.7.refs_8_ = bf16[960,128]{1,0:T(8,128)(2,1)S(1)} collective-permute-done((bf16[960,128]{1,0:T(8,128)(2,1)S(1)}, bf16[960,128]{1,0:T(8,128)(2,1)S(1)}, u32[]{:S(2)}, u32[]{:S(2)}) %collective-permute-start.7) | collective-permute-done | bytes 245792 | tf_op jit(solution)/shard_map/ppermute | solution.py:342
  29.9 0.4 collective-permute-start.6
  30.4 1.0 %collective-permute-done.8.refs_9_ = bf16[960,128]{1,0:T(8,128)(2,1)S(1)} collective-permute-done((bf16[960,128]{1,0:T(8,128)(2,1)S(1)}, bf16[960,128]{1,0:T(8,128)(2,1)S(1)}, u32[]{:S(2)}, u32[]{:S(2)}) %collective-permute-start.8) | collective-permute-done | bytes 245792 | tf_op jit(solution)/shard_map/ppermute | solution.py:334
  31.4 0.4 collective-permute-done.6.refs_7_
  31.7 1.2 %shard_map.71 = (bf16[10240,128]{1,0:T(8,128)(2,1)S(1)}, bf16[128,256]{1,0:T(8,128)(2,1)S(1)}, bf16[128,128]{1,0:T(8,128)(2,1)S(1)}) custom-call(s32[10,8]{1,0:T(8,128)S(1)} %get-tuple-element.32.refs_3_.refs_0_, bf16[128,4096]{1,0:T(8,128)(2,1)S(1)} %bitcast.4, bf16[1280,128]{1,0:T(8,128)(2,1)S(1)} %copy-done.2, ...), custom_call_target="tpu_custom_call" | custom-call | flops 67108864 | bytes 6291456 | tf_op jit(solution)/shard_map/pallas_call | solution.py:43
  32.9 1.7 %collective-permute-start.17 = (bf16[128,256]{1,0:T(8,128)(2,1)S(1)}, bf16[128,256]{1,0:T(8,128)(2,1)S(1)}, u32[]{:S(2)}, u32[]{:S(2)}) collective-permute-start(bf16[128,256]{1,0:T(8,128)(2,1)S(1)} %get-tuple-element.39.refs_4_), channel_id=1, source_target_pairs={{0,6},{1,7},{2,0},{3,1},{4,2},{5,3},{6,4},{7,5},{8,14},{9,15},{10,... | collective-permute-start | bytes 196616 | tf_op jit(solution)/shard_map/ppermute | solution.py:337
  34.6 0.7 collective-permute-start.15
  35.3 1.5 %collective-permute-start.13 = (bf16[128,256]{1,0:T(8,128)(2,1)S(1)}, bf16[128,256]{1,0:T(8,128)(2,1)S(1)}, u32[]{:S(2)}, u32[]{:S(2)}) collective-permute-start(bf16[128,256]{1,0:T(8,128)(2,1)S(1)} %get-tuple-element.39.refs_4_), channel_id=1, source_target_pairs={{0,2},{1,3},{2,4},{3,5},{4,6},{5,7},{6,0},{7,1},{8,10},{9,11},{10,... | collective-permute-start | bytes 196616 | tf_op jit(solution)/shard_map/ppermute | solution.py:337
  36.7 1.5 %shard_map.72 = (bf16[1024,128]{1,0:T(8,128)(2,1)S(1)}, bf16[1024,128]{1,0:T(8,128)(2,1)S(1)}) custom-call(s32[10,8]{1,0:T(8,128)S(1)} %get-tuple-element.32.refs_3_.refs_0_, bf16[128,4096]{1,0:T(8,128)(2,1)S(1)} %bitcast.5, bf16[10240,128]{1,0:T(8,128)(2,1)S(1)} %get-tuple-element.35.refs_2_.refs_3_), custom_call_target="tpu_custom_call" | custom-call | flops 2147483648 | bytes 3145728 | tf_op jit(solution)/shard_map/pallas_call | solution.py:43
  38.3 3.8 %collective-permute-done.15.refs_8_ = bf16[128,256]{1,0:T(8,128)(2,1)S(1)} collective-permute-done((bf16[128,256]{1,0:T(8,128)(2,1)S(1)}, bf16[128,256]{1,0:T(8,128)(2,1)S(1)}, u32[]{:S(2)}, u32[]{:S(2)}) %collective-permute-start.15) | collective-permute-done | bytes 65568 | tf_op jit(solution)/shard_map/ppermute | solution.py:337
  42.1 0.5 collective-permute-start.14
  42.6 0.7 collective-permute-done.16.refs_9_
  43.3 0.2 collective-permute-done.14.refs_7_
  43.5 0.4 collective-permute-done.18.refs_11_
  43.9 4.5 %shard_map.74 = (bf16[8,128,128]{2,1,0:T(8,128)(2,1)S(1)}, bf16[128,256]{1,0:T(8,128)(2,1)S(1)}, bf16[128,256]{1,0:T(8,128)(2,1)S(1)}, bf16[128,256]{1,0:T(8,128...) custom-call(s32[8,2]{1,0:T(8,128)S(1)} %get-tuple-element.33.refs_0_, ...), custom_call_target="tpu_custom_call" | custom-call | flops 671088640 | bytes 4194304 | tf_op jit(solution)/shard_map/pallas_call | solution.py:43
  48.3 0.2 collective-permute-start.20
  48.6 0.3 collective-permute-start.19
  48.9 0.2 collective-permute-start.22
  49.1 0.3 collective-permute-start.24
  49.4 0.2 collective-permute-start.26
  49.6 0.1 collective-permute-done.20
  49.7 0.4 collective-permute-done.22
  50.2 1.5 %collective-permute-start.23 = (bf16[128,256]{1,0:T(8,128)(2,1)S(1)}, bf16[128,256]{1,0:T(8,128)(2,1)S(1)}, u32[]{:S(2)}, u32[]{:S(2)}) collective-permute-start(bf16[128,256]{1,0:T(8,128)(2,1)S(1)} %add_convert_fusion.2), channel_id=1, source_target_pairs={{0,4},{1,5},{2,6},{3,7},{4,0},{5,1},{6,2},{7,3},{8,12},{9,13},{10,... | collective-permute-start | bytes 196616 | tf_op jit(solution)/shard_map/ppermute | solution.py:337
  51.8 2.6 %collective-permute-start.25 = (bf16[128,256]{1,0:T(8,128)(2,1)S(1)}, bf16[128,256]{1,0:T(8,128)(2,1)S(1)}, u32[]{:S(2)}, u32[]{:S(2)}) collective-permute-start(bf16[128,256]{1,0:T(8,128)(2,1)S(1)} %add_convert_fusion.1), channel_id=1, source_target_pairs={{0,6},{1,7},{2,0},{3,1},{4,2},{5,3},{6,4},{7,5},{8,14},{9,15},{10,... | collective-permute-start | bytes 196616 | tf_op jit(solution)/shard_map/ppermute | solution.py:337
  54.4 1.5 %shard_map.77 = (bf16[960,128]{1,0:T(8,128)(2,1)S(1)}, bf16[960,128]{1,0:T(8,128)(2,1)S(1)}, bf16[960,128]{1,0:T(8,128)(2,1)S(1)}, bf16[960,128]{1,0:T(8,128)(2,1)S(1)}) custom-call(s32[10,8]{1,0:T(8,128)S(1)} %get-tuple-element.32.refs_3_.refs_0_, bf16[4096,128]{1,0:T(8,128)(2,1)S(1)} %get-tuple-element.34.refs_1_, ...), custom_call_target="tpu_custom_call" | custom-call | flops 251658240 | bytes 4194304 | tf_op jit(solution)/shard_map/pallas_call | solution.py:43
  55.8 1.6 %collective-permute-start.27 = (bf16[960,128]{1,0:T(8,128)(2,1)S(1)}, bf16[960,128]{1,0:T(8,128)(2,1)S(1)}, u32[]{:S(2)}, u32[]{:S(2)}) collective-permute-start(bf16[960,128]{1,0:T(8,128)(2,1)S(1)} %get-tuple-element.51), channel_id=1, source_target_pairs={{0,8},{8,0},{16,24},{24,16},{1,9},{9,1},{17,25},{25,17},{2,10},{10... | collective-permute-start | bytes 737288 | tf_op jit(solution)/shard_map/ppermute | solution.py:342
  57.4 0.9 collective-permute-start.28
  58.3 1.1 %collective-permute-start.29 = (bf16[960,128]{1,0:T(8,128)(2,1)S(1)}, bf16[960,128]{1,0:T(8,128)(2,1)S(1)}, u32[]{:S(2)}, u32[]{:S(2)}) collective-permute-start(bf16[960,128]{1,0:T(8,128)(2,1)S(1)} %get-tuple-element.53), channel_id=1, source_target_pairs={{0,24},{8,16},{16,8},{24,0},{1,25},{9,17},{17,9},{25,1},{2,26},{10... | collective-permute-start | bytes 737288 | tf_op jit(solution)/shard_map/ppermute | solution.py:342
  59.4 0.1 shard_map.75.refs_2_.refs_5_
  59.6 0.1 collective-permute-start.30
  59.6 1.2 %collective-permute-done.30.refs_6_ = bf16[2,128,128]{2,1,0:T(8,128)(2,1)S(1)} collective-permute-done((bf16[2,128,128]{2,1,0:T(8,128)(2,1)S(1)}, bf16[2,128,128]{2,1,0:T(8,128)(2,1)S(1)}, u32[]{:S(2)}, u32[]{:S(2)}) %collective-permute-start.30) | collective-permute-done | bytes 65568 | tf_op jit(solution)/shard_map/ppermute | solution.py:334
  60.9 1.0 %shard_map.78 = (bf16[320,128]{1,0:T(8,128)(2,1)S(1)}, bf16[320,128]{1,0:T(8,128)(2,1)S(1)}, bf16[320,128]{1,0:T(8,128)(2,1)S(1)}, bf16[320,128]{1,0:T(8,128)(2,1)S(1)}) custom-call(s32[10,8]{1,0:T(8,128)S(1)} %get-tuple-element.32.refs_3_.refs_0_, bf16[4096,128]{1,0:T(8,128)(2,1)S(1)} %get-tuple-element.34.refs_1_, ...), custom_call_target="tpu_custom_call" | custom-call | flops 83886080 | bytes 4194304 | tf_op jit(solution)/shard_map/pallas_call | solution.py:43
  61.9 1.6 %collective-permute-start.31 = (bf16[320,128]{1,0:T(8,128)(2,1)S(1)}, bf16[320,128]{1,0:T(8,128)(2,1)S(1)}, u32[]{:S(2)}, u32[]{:S(2)}) collective-permute-start(bf16[320,128]{1,0:T(8,128)(2,1)S(1)} %get-tuple-element.55), channel_id=1, source_target_pairs={{0,8},{8,0},{16,24},{24,16},{1,9},{9,1},{17,25},{25,17},{2,10},{10... | collective-permute-start | bytes 245768 | tf_op jit(solution)/shard_map/ppermute | solution.py:342
  63.5 0.9 collective-permute-start.32
  64.4 0.4 collective-permute-done.27.refs_1_
  64.8 1.8 %collective-permute-start.33 = (bf16[320,128]{1,0:T(8,128)(2,1)S(1)}, bf16[320,128]{1,0:T(8,128)(2,1)S(1)}, u32[]{:S(2)}, u32[]{:S(2)}) collective-permute-start(bf16[320,128]{1,0:T(8,128)(2,1)S(1)} %shard_map.79), channel_id=1, source_target_pairs={{0,24},{8,16},{16,8},{24,0},{1,25},{9,17},{17,9},{25,1},{2,26},{10... | collective-permute-start | bytes 245768 | tf_op jit(solution)/shard_map/ppermute | solution.py:342
  66.6 4.5 %collective-permute-done.31.refs_5_ = bf16[320,128]{1,0:T(8,128)(2,1)S(1)} collective-permute-done((bf16[320,128]{1,0:T(8,128)(2,1)S(1)}, bf16[320,128]{1,0:T(8,128)(2,1)S(1)}, u32[]{:S(2)}, u32[]{:S(2)}) %collective-permute-start.31) | collective-permute-done | bytes 81952 | tf_op jit(solution)/shard_map/ppermute | solution.py:342
  71.1 2.0 %collective-permute-done.32.refs_6_ = bf16[320,128]{1,0:T(8,128)(2,1)S(1)} collective-permute-done((bf16[320,128]{1,0:T(8,128)(2,1)S(1)}, bf16[320,128]{1,0:T(8,128)(2,1)S(1)}, u32[]{:S(2)}, u32[]{:S(2)}) %collective-permute-start.32) | collective-permute-done | bytes 81952 | tf_op jit(solution)/shard_map/ppermute | solution.py:342
  73.1 0.3 shard_map.80
  73.4 0.3 collective-permute-start.34
  73.8 1.2 %collective-permute-start.35 = (bf16[320,128]{1,0:T(8,128)(2,1)S(1)}, bf16[320,128]{1,0:T(8,128)(2,1)S(1)}, u32[]{:S(2)}, u32[]{:S(2)}) collective-permute-start(bf16[320,128]{1,0:T(8,128)(2,1)S(1)} %get-tuple-element.60), channel_id=1, source_target_pairs={{0,4},{1,5},{2,6},{3,7},{4,0},{5,1},{6,2},{7,3},{8,12},{9,13},{10,... | collective-permute-start | bytes 245768 | tf_op jit(solution)/shard_map/ppermute | solution.py:337
  75.0 2.8 %collective-permute-start.36 = (bf16[320,128]{1,0:T(8,128)(2,1)S(1)}, bf16[320,128]{1,0:T(8,128)(2,1)S(1)}, u32[]{:S(2)}, u32[]{:S(2)}) collective-permute-start(bf16[320,128]{1,0:T(8,128)(2,1)S(1)} %get-tuple-element.61), channel_id=1, source_target_pairs={{0,6},{1,7},{2,0},{3,1},{4,2},{5,3},{6,4},{7,5},{8,14},{9,15},{10,... | collective-permute-start | bytes 245768 | tf_op jit(solution)/shard_map/ppermute | solution.py:337
  77.9 2.8 %collective-permute-done.34 = bf16[320,128]{1,0:T(8,128)(2,1)S(1)} collective-permute-done((bf16[320,128]{1,0:T(8,128)(2,1)S(1)}, bf16[320,128]{1,0:T(8,128)(2,1)S(1)}, u32[]{:S(2)}, u32[]{:S(2)}) %collective-permute-start.34) | collective-permute-done | bytes 81952 | tf_op jit(solution)/shard_map/ppermute | solution.py:337
  80.6 2.5 %collective-permute-done.35 = bf16[320,128]{1,0:T(8,128)(2,1)S(1)} collective-permute-done((bf16[320,128]{1,0:T(8,128)(2,1)S(1)}, bf16[320,128]{1,0:T(8,128)(2,1)S(1)}, u32[]{:S(2)}, u32[]{:S(2)}) %collective-permute-start.35) | collective-permute-done | bytes 81952 | tf_op jit(solution)/shard_map/ppermute | solution.py:337
  83.2 1.5 %collective-permute-start.39 = (bf16[320,128]{1,0:T(8,128)(2,1)S(1)}, bf16[320,128]{1,0:T(8,128)(2,1)S(1)}, u32[]{:S(2)}, u32[]{:S(2)}) collective-permute-start(bf16[320,128]{1,0:T(8,128)(2,1)S(1)} %add_convert_fusion.refs_0_), channel_id=1, source_target_pairs={{0,24},{8,16},{16,8},{24,0},{1,25},{9,17},{17,9},{25,1},{2,26},{10... | collective-permute-start | bytes 245768 | tf_op jit(solution)/shard_map/ppermute | solution.py:342
  84.7 2.0 %collective-permute-start.37 = (bf16[320,128]{1,0:T(8,128)(2,1)S(1)}, bf16[320,128]{1,0:T(8,128)(2,1)S(1)}, u32[]{:S(2)}, u32[]{:S(2)}) collective-permute-start(bf16[320,128]{1,0:T(8,128)(2,1)S(1)} %add_convert_fusion.refs_0_), channel_id=1, source_target_pairs={{0,8},{8,0},{16,24},{24,16},{1,9},{9,1},{17,25},{25,17},{2,10},{10... | collective-permute-start | bytes 245768 | tf_op jit(solution)/shard_map/ppermute | solution.py:342
  86.8 3.0 %shard_map.76 = bf16[128,4096]{1,0:T(8,128)(2,1)} custom-call(s32[10,8]{1,0:T(8,128)S(1)} %get-tuple-element.32.refs_3_.refs_0_, bf16[8,128,128]{2,1,0:T(8,128)(2,1)S(1)} %get-tuple-element.40.refs_1_.refs_3_, bf16[2,128,128]{2,1,0:T(8,128)(2,1)S(1)} %shard_map.75.refs_2_.refs_5_, bf16[10240,128]{1,0:T(8,128)(2,1)S(1)} %get-tuple-element.35.refs_2_.refs_3_), custom_call_target="tpu_custom_call" | custom-call | flops 335544320 | bytes 4194304 | tf_op jit(solution)/shard_map/pallas_call | solution.py:43
  89.8 0.9 shard_map.81
  (48 shorter events, 0.4 us)
Async XLA Ops:
  0.6 14.6 %collective-permute-start = (bf16[1280,128]{1,0:T(8,128)(2,1)}, bf16[1280,128]{1,0:T(8,128)(2,1)S(1)}, u32[]{:S(2)}, u32[]{:S(2)}) collective-permute-start(bf16[1280,128]{1,0:T(8,128)(2,1)} %refs_2_.1), channel_id=1, source_target_pairs={{0,1},{1,0},{2,3},{3,2},{4,5},{5,4},{6,7},{7,6},{8,9},{9,8},{10,11... | collective-permute-start | bytes 983048 | tf_op jit(solution)/shard_map/ppermute | solution.py:334
  2.0 11.5 %collective-permute-start.3 = (bf16[320,128]{1,0:T(8,128)(2,1)S(1)}, bf16[320,128]{1,0:T(8,128)(2,1)S(1)}, u32[]{:S(2)}, u32[]{:S(2)}) collective-permute-start(bf16[320,128]{1,0:T(8,128)(2,1)S(1)} %constant_dynamic-slice_fusion), channel_id=1, source_target_pairs={{0,6},{1,7},{2,0},{3,1},{4,2},{5,3},{6,4},{7,5},{8,14},{9,15},{10,... | collective-permute-start | bytes 245768 | tf_op jit(solution)/shard_map/ppermute | solution.py:337
  6.7 8.5 %collective-permute-start.2 = (bf16[320,128]{1,0:T(8,128)(2,1)S(1)}, bf16[320,128]{1,0:T(8,128)(2,1)S(1)}, u32[]{:S(2)}, u32[]{:S(2)}) collective-permute-start(bf16[320,128]{1,0:T(8,128)(2,1)S(1)} %constant_dynamic-slice_fusion), channel_id=1, source_target_pairs={{0,4},{1,5},{2,6},{3,7},{4,0},{5,1},{6,2},{7,3},{8,12},{9,13},{10,... | collective-permute-start | bytes 245768 | tf_op jit(solution)/shard_map/ppermute | solution.py:337
  6.7 8.5 %collective-permute-start.1 = (bf16[320,128]{1,0:T(8,128)(2,1)S(1)}, bf16[320,128]{1,0:T(8,128)(2,1)S(1)}, u32[]{:S(2)}, u32[]{:S(2)}) collective-permute-start(bf16[320,128]{1,0:T(8,128)(2,1)S(1)} %constant_dynamic-slice_fusion), channel_id=1, source_target_pairs={{0,2},{1,3},{2,4},{3,5},{4,6},{5,7},{6,0},{7,1},{8,10},{9,11},{10,... | collective-permute-start | bytes 245768 | tf_op jit(solution)/shard_map/ppermute | solution.py:337
  9.2 1.2 %copy-start = (bf16[1,128,4096]{2,1,0:T(8,128)(2,1)S(1)}, bf16[1,128,4096]{2,1,0:T(8,128)(2,1)}, u32[]{:S(2)}) copy-start(bf16[1,128,4096]{2,1,0:T(8,128)(2,1)} %param.5) | copy-start | bytes 3145732
  10.4 0.9 %copy-start.3 = (bf16[1,128,1024]{2,1,0:T(8,128)(2,1)S(1)}, bf16[1,128,1024]{2,1,0:T(8,128)(2,1)}, u32[]{:S(2)}) copy-start(bf16[1,128,1024]{2,1,0:T(8,128)(2,1)} %param.6) | copy-start | bytes 786436
  13.4 18.3 %copy-start.1 = (bf16[1,128,4096]{2,1,0:T(8,128)(2,1)S(1)}, bf16[1,128,4096]{2,1,0:T(8,128)(2,1)}, u32[]{:S(2)}) copy-start(bf16[1,128,4096]{2,1,0:T(8,128)(2,1)} %param.5) | copy-start | bytes 3145732
  13.4 18.3 %copy-start.2 = (bf16[1280,128]{1,0:T(8,128)(2,1)S(1)}, bf16[1280,128]{1,0:T(8,128)(2,1)}, u32[]{:S(2)}) copy-start(bf16[1280,128]{1,0:T(8,128)(2,1)} %refs_2_.1) | copy-start | bytes 983044
  15.2 16.5 %collective-permute-start.11 = (bf16[4096,128]{1,0:T(8,128)(2,1)S(1)}, bf16[4096,128]{1,0:T(8,128)(2,1)S(1)}, u32[]{:S(2)}, u32[]{:S(2)}) collective-permute-start(bf16[4096,128]{1,0:T(8,128)(2,1)S(1)} %shard_map.70), channel_id=1, source_target_pairs={{0,1},{1,0},{2,3},{3,2},{4,5},{5,4},{6,7},{7,6},{8,9},{9,8},{10,11... | collective-permute-start | bytes 3145736 | tf_op jit(solution)/shard_map/ppermute | solution.py:334
  15.3 9.7 %collective-permute-start.9 = (bf16[960,128]{1,0:T(8,128)(2,1)S(1)}, bf16[960,128]{1,0:T(8,128)(2,1)S(1)}, u32[]{:S(2)}, u32[]{:S(2)}) collective-permute-start(bf16[960,128]{1,0:T(8,128)(2,1)S(1)} %shard_map.69.refs_1_.refs_4_), channel_id=1, source_target_pairs={{0,24},{8,16},{16,8},{24,0},{1,25},{9,17},{17,9},{25,1},{2,26},{10... | collective-permute-start | bytes 737288 | tf_op jit(solution)/shard_map/ppermute | solution.py:342
  17.8 12.0 %collective-permute-start.7 = (bf16[960,128]{1,0:T(8,128)(2,1)S(1)}, bf16[960,128]{1,0:T(8,128)(2,1)S(1)}, u32[]{:S(2)}, u32[]{:S(2)}) collective-permute-start(bf16[960,128]{1,0:T(8,128)(2,1)S(1)} %shard_map.69.refs_1_.refs_4_), channel_id=1, source_target_pairs={{0,16},{8,24},{16,0},{24,8},{1,17},{9,25},{17,1},{25,9},{2,18},{10... | collective-permute-start | bytes 737288 | tf_op jit(solution)/shard_map/ppermute | solution.py:342
  18.3 11.6 %collective-permute-start.5 = (bf16[960,128]{1,0:T(8,128)(2,1)S(1)}, bf16[960,128]{1,0:T(8,128)(2,1)S(1)}, u32[]{:S(2)}, u32[]{:S(2)}) collective-permute-start(bf16[960,128]{1,0:T(8,128)(2,1)S(1)} %shard_map.69.refs_1_.refs_4_), channel_id=1, source_target_pairs={{0,8},{8,0},{16,24},{24,16},{1,9},{9,1},{17,25},{25,17},{2,10},{10... | collective-permute-start | bytes 737288 | tf_op jit(solution)/shard_map/ppermute | solution.py:342
  18.9 11.5 %collective-permute-start.4 = (bf16[960,128]{1,0:T(8,128)(2,1)S(1)}, bf16[960,128]{1,0:T(8,128)(2,1)S(1)}, u32[]{:S(2)}, u32[]{:S(2)}) collective-permute-start(bf16[960,128]{1,0:T(8,128)(2,1)S(1)} %shard_map.69.refs_1_.refs_4_), channel_id=1, source_target_pairs={{0,1},{1,0},{2,3},{3,2},{4,5},{5,4},{6,7},{7,6},{8,9},{9,8},{10,11... | collective-permute-start | bytes 737288 | tf_op jit(solution)/shard_map/ppermute | solution.py:334
  25.1 5.3 %collective-permute-start.10 = (bf16[960,128]{1,0:T(8,128)(2,1)S(1)}, bf16[960,128]{1,0:T(8,128)(2,1)S(1)}, u32[]{:S(2)}, u32[]{:S(2)}) collective-permute-start(bf16[960,128]{1,0:T(8,128)(2,1)S(1)} %collective-permute-done.9.refs_10_), channel_id=1, source_target_pairs={{0,1},{1,0},{2,3},{3,2},{4,5},{5,4},{6,7},{7,6},{8,9},{9,8},{10,11... | collective-permute-start | bytes 737288 | tf_op jit(solution)/shard_map/ppermute | solution.py:334
  29.8 1.5 %collective-permute-start.8 = (bf16[960,128]{1,0:T(8,128)(2,1)S(1)}, bf16[960,128]{1,0:T(8,128)(2,1)S(1)}, u32[]{:S(2)}, u32[]{:S(2)}) collective-permute-start(bf16[960,128]{1,0:T(8,128)(2,1)S(1)} %collective-permute-done.7.refs_8_), channel_id=1, source_target_pairs={{0,1},{1,0},{2,3},{3,2},{4,5},{5,4},{6,7},{7,6},{8,9},{9,8},{10,11... | collective-permute-start | bytes 737288 | tf_op jit(solution)/shard_map/ppermute | solution.py:334
  29.9 1.8 %collective-permute-start.6 = (bf16[960,128]{1,0:T(8,128)(2,1)S(1)}, bf16[960,128]{1,0:T(8,128)(2,1)S(1)}, u32[]{:S(2)}, u32[]{:S(2)}) collective-permute-start(bf16[960,128]{1,0:T(8,128)(2,1)S(1)} %collective-permute-done.5.refs_6_), channel_id=1, source_target_pairs={{0,1},{1,0},{2,3},{3,2},{4,5},{5,4},{6,7},{7,6},{8,9},{9,8},{10,11... | collective-permute-start | bytes 737288 | tf_op jit(solution)/shard_map/ppermute | solution.py:334
  32.9 5.4 %collective-permute-start.17 = (bf16[128,256]{1,0:T(8,128)(2,1)S(1)}, bf16[128,256]{1,0:T(8,128)(2,1)S(1)}, u32[]{:S(2)}, u32[]{:S(2)}) collective-permute-start(bf16[128,256]{1,0:T(8,128)(2,1)S(1)} %get-tuple-element.39.refs_4_), channel_id=1, source_target_pairs={{0,6},{1,7},{2,0},{3,1},{4,2},{5,3},{6,4},{7,5},{8,14},{9,15},{10,... | collective-permute-start | bytes 196616 | tf_op jit(solution)/shard_map/ppermute | solution.py:337
  34.6 7.5 %collective-permute-start.15 = (bf16[128,256]{1,0:T(8,128)(2,1)S(1)}, bf16[128,256]{1,0:T(8,128)(2,1)S(1)}, u32[]{:S(2)}, u32[]{:S(2)}) collective-permute-start(bf16[128,256]{1,0:T(8,128)(2,1)S(1)} %get-tuple-element.39.refs_4_), channel_id=1, source_target_pairs={{0,4},{1,5},{2,6},{3,7},{4,0},{5,1},{6,2},{7,3},{8,12},{9,13},{10,... | collective-permute-start | bytes 196616 | tf_op jit(solution)/shard_map/ppermute | solution.py:337
  35.3 6.8 %collective-permute-start.13 = (bf16[128,256]{1,0:T(8,128)(2,1)S(1)}, bf16[128,256]{1,0:T(8,128)(2,1)S(1)}, u32[]{:S(2)}, u32[]{:S(2)}) collective-permute-start(bf16[128,256]{1,0:T(8,128)(2,1)S(1)} %get-tuple-element.39.refs_4_), channel_id=1, source_target_pairs={{0,2},{1,3},{2,4},{3,5},{4,6},{5,7},{6,0},{7,1},{8,10},{9,11},{10,... | collective-permute-start | bytes 196616 | tf_op jit(solution)/shard_map/ppermute | solution.py:337
  36.7 5.9 %collective-permute-start.12 = (bf16[128,256]{1,0:T(8,128)(2,1)S(1)}, bf16[128,256]{1,0:T(8,128)(2,1)S(1)}, u32[]{:S(2)}, u32[]{:S(2)}) collective-permute-start(bf16[128,256]{1,0:T(8,128)(2,1)S(1)} %get-tuple-element.39.refs_4_), channel_id=1, source_target_pairs={{0,1},{1,0},{2,3},{3,2},{4,5},{5,4},{6,7},{7,6},{8,9},{9,8},{10,11... | collective-permute-start | bytes 196616 | tf_op jit(solution)/shard_map/ppermute | solution.py:334
  42.1 1.3 %collective-permute-start.16 = (bf16[128,256]{1,0:T(8,128)(2,1)S(1)}, bf16[128,256]{1,0:T(8,128)(2,1)S(1)}, u32[]{:S(2)}, u32[]{:S(2)}) collective-permute-start(bf16[128,256]{1,0:T(8,128)(2,1)S(1)} %collective-permute-done.15.refs_8_), channel_id=1, source_target_pairs={{0,1},{1,0},{2,3},{3,2},{4,5},{5,4},{6,7},{7,6},{8,9},{9,8},{10,11... | collective-permute-start | bytes 196616 | tf_op jit(solution)/shard_map/ppermute | solution.py:334
  42.1 1.4 %collective-permute-start.14 = (bf16[128,256]{1,0:T(8,128)(2,1)S(1)}, bf16[128,256]{1,0:T(8,128)(2,1)S(1)}, u32[]{:S(2)}, u32[]{:S(2)}) collective-permute-start(bf16[128,256]{1,0:T(8,128)(2,1)S(1)} %collective-permute-done.13.refs_6_), channel_id=1, source_target_pairs={{0,1},{1,0},{2,3},{3,2},{4,5},{5,4},{6,7},{7,6},{8,9},{9,8},{10,11... | collective-permute-start | bytes 196616 | tf_op jit(solution)/shard_map/ppermute | solution.py:334
  42.6 1.3 %collective-permute-start.18 = (bf16[128,256]{1,0:T(8,128)(2,1)S(1)}, bf16[128,256]{1,0:T(8,128)(2,1)S(1)}, u32[]{:S(2)}, u32[]{:S(2)}) collective-permute-start(bf16[128,256]{1,0:T(8,128)(2,1)S(1)} %shard_map.73), channel_id=1, source_target_pairs={{0,1},{1,0},{2,3},{3,2},{4,5},{5,4},{6,7},{7,6},{8,9},{9,8},{10,11... | collective-permute-start | bytes 196616 | tf_op jit(solution)/shard_map/ppermute | solution.py:334
  48.3 1.3 %collective-permute-start.20 = (bf16[128,256]{1,0:T(8,128)(2,1)S(1)}, bf16[128,256]{1,0:T(8,128)(2,1)S(1)}, u32[]{:S(2)}, u32[]{:S(2)}) collective-permute-start(bf16[128,256]{1,0:T(8,128)(2,1)S(1)} %get-tuple-element.45), channel_id=1, source_target_pairs={{0,1},{1,0},{2,3},{3,2},{4,5},{5,4},{6,7},{7,6},{8,9},{9,8},{10,11... | collective-permute-start | bytes 196616 | tf_op jit(solution)/shard_map/ppermute | solution.py:334
  48.6 8.8 %collective-permute-start.19 = (bf16[128,256]{1,0:T(8,128)(2,1)S(1)}, bf16[128,256]{1,0:T(8,128)(2,1)S(1)}, u32[]{:S(2)}, u32[]{:S(2)}) collective-permute-start(bf16[128,256]{1,0:T(8,128)(2,1)S(1)} %get-tuple-element.43), channel_id=1, source_target_pairs={{0,1},{1,0},{2,3},{3,2},{4,5},{5,4},{6,7},{7,6},{8,9},{9,8},{10,11... | collective-permute-start | bytes 196616 | tf_op jit(solution)/shard_map/ppermute | solution.py:334
  48.9 1.3 %collective-permute-start.22 = (bf16[128,256]{1,0:T(8,128)(2,1)S(1)}, bf16[128,256]{1,0:T(8,128)(2,1)S(1)}, u32[]{:S(2)}, u32[]{:S(2)}) collective-permute-start(bf16[128,256]{1,0:T(8,128)(2,1)S(1)} %get-tuple-element.47), channel_id=1, source_target_pairs={{0,1},{1,0},{2,3},{3,2},{4,5},{5,4},{6,7},{7,6},{8,9},{9,8},{10,11... | collective-permute-start | bytes 196616 | tf_op jit(solution)/shard_map/ppermute | solution.py:334
  49.1 2.7 %collective-permute-start.24 = (bf16[128,256]{1,0:T(8,128)(2,1)S(1)}, bf16[128,256]{1,0:T(8,128)(2,1)S(1)}, u32[]{:S(2)}, u32[]{:S(2)}) collective-permute-start(bf16[128,256]{1,0:T(8,128)(2,1)S(1)} %get-tuple-element.49), channel_id=1, source_target_pairs={{0,1},{1,0},{2,3},{3,2},{4,5},{5,4},{6,7},{7,6},{8,9},{9,8},{10,11... | collective-permute-start | bytes 196616 | tf_op jit(solution)/shard_map/ppermute | solution.py:334
  49.4 4.9 %collective-permute-start.26 = (bf16[8,128,128]{2,1,0:T(8,128)(2,1)S(1)}, bf16[8,128,128]{2,1,0:T(8,128)(2,1)S(1)}, u32[]{:S(2)}, u32[]{:S(2)}) collective-permute-start(bf16[8,128,128]{2,1,0:T(8,128)(2,1)S(1)} %get-tuple-element.40.refs_1_.refs_3_), channel_id=1, source_target_pairs={{0,1},{1,0},{2,3},{3,2},{4,5},{5,4},{6,7},{7,6},{8,9},{9,8},{10,11... | collective-permute-start | bytes 786440 | tf_op jit(solution)/shard_map/ppermute | solution.py:334
  49.7 8.6 %collective-permute-start.21 = (bf16[128,256]{1,0:T(8,128)(2,1)S(1)}, bf16[128,256]{1,0:T(8,128)(2,1)S(1)}, u32[]{:S(2)}, u32[]{:S(2)}) collective-permute-start(bf16[128,256]{1,0:T(8,128)(2,1)S(1)} %add_convert_fusion.3), channel_id=1, source_target_pairs={{0,2},{1,3},{2,4},{3,5},{4,6},{5,7},{6,0},{7,1},{8,10},{9,11},{10,... | collective-permute-start | bytes 196616 | tf_op jit(solution)/shard_map/ppermute | solution.py:337
  50.2 9.2 %collective-permute-start.23 = (bf16[128,256]{1,0:T(8,128)(2,1)S(1)}, bf16[128,256]{1,0:T(8,128)(2,1)S(1)}, u32[]{:S(2)}, u32[]{:S(2)}) collective-permute-start(bf16[128,256]{1,0:T(8,128)(2,1)S(1)} %add_convert_fusion.2), channel_id=1, source_target_pairs={{0,4},{1,5},{2,6},{3,7},{4,0},{5,1},{6,2},{7,3},{8,12},{9,13},{10,... | collective-permute-start | bytes 196616 | tf_op jit(solution)/shard_map/ppermute | solution.py:337
  51.8 7.7 %collective-permute-start.25 = (bf16[128,256]{1,0:T(8,128)(2,1)S(1)}, bf16[128,256]{1,0:T(8,128)(2,1)S(1)}, u32[]{:S(2)}, u32[]{:S(2)}) collective-permute-start(bf16[128,256]{1,0:T(8,128)(2,1)S(1)} %add_convert_fusion.1), channel_id=1, source_target_pairs={{0,6},{1,7},{2,0},{3,1},{4,2},{5,3},{6,4},{7,5},{8,14},{9,15},{10,... | collective-permute-start | bytes 196616 | tf_op jit(solution)/shard_map/ppermute | solution.py:337
  55.8 9.0 %collective-permute-start.27 = (bf16[960,128]{1,0:T(8,128)(2,1)S(1)}, bf16[960,128]{1,0:T(8,128)(2,1)S(1)}, u32[]{:S(2)}, u32[]{:S(2)}) collective-permute-start(bf16[960,128]{1,0:T(8,128)(2,1)S(1)} %get-tuple-element.51), channel_id=1, source_target_pairs={{0,8},{8,0},{16,24},{24,16},{1,9},{9,1},{17,25},{25,17},{2,10},{10... | collective-permute-start | bytes 737288 | tf_op jit(solution)/shard_map/ppermute | solution.py:342
  57.4 15.8 %collective-permute-start.28 = (bf16[960,128]{1,0:T(8,128)(2,1)S(1)}, bf16[960,128]{1,0:T(8,128)(2,1)S(1)}, u32[]{:S(2)}, u32[]{:S(2)}) collective-permute-start(bf16[960,128]{1,0:T(8,128)(2,1)S(1)} %get-tuple-element.52), channel_id=1, source_target_pairs={{0,16},{8,24},{16,0},{24,8},{1,17},{9,25},{17,1},{25,9},{2,18},{10... | collective-permute-start | bytes 737288 | tf_op jit(solution)/shard_map/ppermute | solution.py:342
  58.3 14.9 %collective-permute-start.29 = (bf16[960,128]{1,0:T(8,128)(2,1)S(1)}, bf16[960,128]{1,0:T(8,128)(2,1)S(1)}, u32[]{:S(2)}, u32[]{:S(2)}) collective-permute-start(bf16[960,128]{1,0:T(8,128)(2,1)S(1)} %get-tuple-element.53), channel_id=1, source_target_pairs={{0,24},{8,16},{16,8},{24,0},{1,25},{9,17},{17,9},{25,1},{2,26},{10... | collective-permute-start | bytes 737288 | tf_op jit(solution)/shard_map/ppermute | solution.py:342
  59.6 1.3 %collective-permute-start.30 = (bf16[2,128,128]{2,1,0:T(8,128)(2,1)S(1)}, bf16[2,128,128]{2,1,0:T(8,128)(2,1)S(1)}, u32[]{:S(2)}, u32[]{:S(2)}) collective-permute-start(bf16[2,128,128]{2,1,0:T(8,128)(2,1)S(1)} %shard_map.75.refs_2_.refs_5_), channel_id=1, source_target_pairs={{0,1},{1,0},{2,3},{3,2},{4,5},{5,4},{6,7},{7,6},{8,9},{9,8},{10,11... | collective-permute-start | bytes 196616 | tf_op jit(solution)/shard_map/ppermute | solution.py:334
  61.9 9.2 %collective-permute-start.31 = (bf16[320,128]{1,0:T(8,128)(2,1)S(1)}, bf16[320,128]{1,0:T(8,128)(2,1)S(1)}, u32[]{:S(2)}, u32[]{:S(2)}) collective-permute-start(bf16[320,128]{1,0:T(8,128)(2,1)S(1)} %get-tuple-element.55), channel_id=1, source_target_pairs={{0,8},{8,0},{16,24},{24,16},{1,9},{9,1},{17,25},{25,17},{2,10},{10... | collective-permute-start | bytes 245768 | tf_op jit(solution)/shard_map/ppermute | solution.py:342
  63.5 9.7 %collective-permute-start.32 = (bf16[320,128]{1,0:T(8,128)(2,1)S(1)}, bf16[320,128]{1,0:T(8,128)(2,1)S(1)}, u32[]{:S(2)}, u32[]{:S(2)}) collective-permute-start(bf16[320,128]{1,0:T(8,128)(2,1)S(1)} %get-tuple-element.56), channel_id=1, source_target_pairs={{0,16},{8,24},{16,0},{24,8},{1,17},{9,25},{17,1},{25,9},{2,18},{10... | collective-permute-start | bytes 245768 | tf_op jit(solution)/shard_map/ppermute | solution.py:342
  64.8 8.4 %collective-permute-start.33 = (bf16[320,128]{1,0:T(8,128)(2,1)S(1)}, bf16[320,128]{1,0:T(8,128)(2,1)S(1)}, u32[]{:S(2)}, u32[]{:S(2)}) collective-permute-start(bf16[320,128]{1,0:T(8,128)(2,1)S(1)} %shard_map.79), channel_id=1, source_target_pairs={{0,24},{8,16},{16,8},{24,0},{1,25},{9,17},{17,9},{25,1},{2,26},{10... | collective-permute-start | bytes 245768 | tf_op jit(solution)/shard_map/ppermute | solution.py:342
  73.4 7.2 %collective-permute-start.34 = (bf16[320,128]{1,0:T(8,128)(2,1)S(1)}, bf16[320,128]{1,0:T(8,128)(2,1)S(1)}, u32[]{:S(2)}, u32[]{:S(2)}) collective-permute-start(bf16[320,128]{1,0:T(8,128)(2,1)S(1)} %get-tuple-element.59), channel_id=1, source_target_pairs={{0,2},{1,3},{2,4},{3,5},{4,6},{5,7},{6,0},{7,1},{8,10},{9,11},{10,... | collective-permute-start | bytes 245768 | tf_op jit(solution)/shard_map/ppermute | solution.py:337
  73.8 9.4 %collective-permute-start.35 = (bf16[320,128]{1,0:T(8,128)(2,1)S(1)}, bf16[320,128]{1,0:T(8,128)(2,1)S(1)}, u32[]{:S(2)}, u32[]{:S(2)}) collective-permute-start(bf16[320,128]{1,0:T(8,128)(2,1)S(1)} %get-tuple-element.60), channel_id=1, source_target_pairs={{0,4},{1,5},{2,6},{3,7},{4,0},{5,1},{6,2},{7,3},{8,12},{9,13},{10,... | collective-permute-start | bytes 245768 | tf_op jit(solution)/shard_map/ppermute | solution.py:337
  75.0 8.2 %collective-permute-start.36 = (bf16[320,128]{1,0:T(8,128)(2,1)S(1)}, bf16[320,128]{1,0:T(8,128)(2,1)S(1)}, u32[]{:S(2)}, u32[]{:S(2)}) collective-permute-start(bf16[320,128]{1,0:T(8,128)(2,1)S(1)} %get-tuple-element.61), channel_id=1, source_target_pairs={{0,6},{1,7},{2,0},{3,1},{4,2},{5,3},{6,4},{7,5},{8,14},{9,15},{10,... | collective-permute-start | bytes 245768 | tf_op jit(solution)/shard_map/ppermute | solution.py:337
  83.2 6.6 %collective-permute-start.39 = (bf16[320,128]{1,0:T(8,128)(2,1)S(1)}, bf16[320,128]{1,0:T(8,128)(2,1)S(1)}, u32[]{:S(2)}, u32[]{:S(2)}) collective-permute-start(bf16[320,128]{1,0:T(8,128)(2,1)S(1)} %add_convert_fusion.refs_0_), channel_id=1, source_target_pairs={{0,24},{8,16},{16,8},{24,0},{1,25},{9,17},{17,9},{25,1},{2,26},{10... | collective-permute-start | bytes 245768 | tf_op jit(solution)/shard_map/ppermute | solution.py:342
  84.7 5.1 %collective-permute-start.38 = (bf16[320,128]{1,0:T(8,128)(2,1)S(1)}, bf16[320,128]{1,0:T(8,128)(2,1)S(1)}, u32[]{:S(2)}, u32[]{:S(2)}) collective-permute-start(bf16[320,128]{1,0:T(8,128)(2,1)S(1)} %add_convert_fusion.refs_0_), channel_id=1, source_target_pairs={{0,16},{8,24},{16,0},{24,8},{1,17},{9,25},{17,1},{25,9},{2,18},{10... | collective-permute-start | bytes 245768 | tf_op jit(solution)/shard_map/ppermute | solution.py:342
  84.7 5.1 %collective-permute-start.37 = (bf16[320,128]{1,0:T(8,128)(2,1)S(1)}, bf16[320,128]{1,0:T(8,128)(2,1)S(1)}, u32[]{:S(2)}, u32[]{:S(2)}) collective-permute-start(bf16[320,128]{1,0:T(8,128)(2,1)S(1)} %add_convert_fusion.refs_0_), channel_id=1, source_target_pairs={{0,8},{8,0},{16,24},{24,16},{1,9},{9,1},{17,25},{25,17},{2,10},{10... | collective-permute-start | bytes 245768 | tf_op jit(solution)/shard_map/ppermute | solution.py:342

commit v5 on v4

--- a/solution.py
+++ b/solution.py
@@ -98,6 +98,11 @@
                 out[i, j] = source[i, j]
 
 
+def part_kernel(w_ref, out):
+    rows = out.shape[0]
+    out[...] = w_ref[rows_at(lax.axis_index("dp") * rows, rows, 16), :]
+
+
 def stack_kernel(*refs):
     rows = refs[0].shape[0]
     for k, ref in enumerate(refs[:-1]):
@@ -125,10 +130,11 @@
     )
 
 
-def project_keys(ids, x_ref, w_ref, kv_ref, key_ref):
+def project_keys(ids, x_ref, w_ref, first, kv_ref, key_ref):
     wide = NBR * BLK
     for c in range(NQ, NCB):
-        out = dot(column_of(c, ids, x_ref), w_ref[c * wide : (c + 1) * wide, :]).astype(BF16)
+        at = c * wide - first
+        out = dot(column_of(c, ids, x_ref), w_ref[at : at + wide, :]).astype(BF16)
         if c == NQ:
             key = out.astype(F32)
             key_ref[...] = out
@@ -137,18 +143,7 @@
             kv_ref[:, HD:] = out
 
 
-def keys_kernel(nz, ids, x_ref, *refs):
-    shards, pieces, (w_ref, kv_ref, key_ref) = refs[:2], refs[2:-3], refs[-3:]
-    shard, piece = shards[0].shape[0], pieces[0].shape[0] // (nz - 1)
-    zi = lax.axis_index("ctx") // 2
-    join_shards(shards, zi * 2 * shard, w_ref)
-    for k in range(1, nz):
-        base = lax.rem(zi + nz - k, nz) * 2 * shard
-        join_pieces(pieces, k - 1, shard, piece, base, w_ref)
-    project_keys(ids, x_ref, w_ref, kv_ref, key_ref)
-
-
-def queries_kernel(ids, x_ref, w_ref, q_ref, qhat_ref):
+def project_queries(ids, x_ref, w_ref, q_ref, qhat_ref):
     wide = NBR * BLK
     for c in range(NQ):
         out = dot(column_of(c, ids, x_ref), w_ref[c * wide : (c + 1) * wide, :]).astype(BF16)
@@ -159,9 +154,40 @@
             qhat_ref[head_rows(p, c), :] = normed[p * SPAN : (p + 1) * SPAN, :]
 
 
+def join_planes(nz, shards, pieces, w_ref, last_ref):
+    shard, piece = shards[0].shape[0], pieces[0].shape[0] // (nz - 1)
+    zi = lax.axis_index("ctx") // 2
+    for k in range(nz):
+        plane = lax.rem(zi + nz - k, nz)
+
+        def place(base, out):
+            if k == 0:
+                join_shards(shards, base, out)
+            else:
+                join_pieces(pieces, k - 1, shard, piece, base, out)
+
+        if w_ref is None:
+            pl.when(plane == nz - 1)(lambda: place(0, last_ref))
+        else:
+            pl.when(plane < nz - 1)(lambda: place(plane * 2 * shard, w_ref))
+
+
+def keys_kernel(nz, ids, x_ref, *refs):
+    shards, pieces, (w_ref, kv_ref, key_ref) = refs[:2], refs[2:-3], refs[-3:]
+    join_planes(nz, shards, pieces, None, w_ref)
+    project_keys(ids, x_ref, w_ref, NNZ * BLK - w_ref.shape[0], kv_ref, key_ref)
+
+
+def queries_kernel(nz, ids, x_ref, last_ref, *refs):
+    shards, pieces, (w_ref, q_ref, qhat_ref) = refs[:2], refs[2:-3], refs[-3:]
+    join_planes(nz, shards, pieces, w_ref, None)
+    w_ref[NNZ * BLK - last_ref.shape[0] :, :] = last_ref[...]
+    project_queries(ids, x_ref, w_ref, q_ref, qhat_ref)
+
+
 def project_kernel(ids, x_ref, w_ref, q_ref, qhat_ref, kv_ref, key_ref):
-    project_keys(ids, x_ref, w_ref, kv_ref, key_ref)
-    queries_kernel(ids, x_ref, w_ref, q_ref, qhat_ref)
+    project_keys(ids, x_ref, w_ref, 0, kv_ref, key_ref)
+    project_queries(ids, x_ref, w_ref, q_ref, qhat_ref)
 
 
 def attend_kernel(nz, keys, spans, q_ref, qhat, up, *refs):
@@ -181,45 +207,46 @@
                 kv[rows_at(spans[source, p] * SPAN, SPAN, SPAN), :] = pieces[2 * k + other][
                     p * SPAN : (p + 1) * SPAN, :
                 ]
-    acc[...] = jnp.zeros_like(acc)
+    length = kv.shape[0]
     key_row = lax.broadcasted_iota(jnp.int32, (keys, half), 0)
     query_at = lax.broadcasted_iota(jnp.int32, (keys, half), 1) % SPAN
-    for p in range(2):
-        span = spans[me, p]
-        blocks = ((span + 1) * SPAN + keys - 1) // keys
+    for p in (1, 0):
+        reach = length if p == 1 else length // 2
+        sure = length // 2 if p == 1 else 0
         q_part = qhat[p * half : (p + 1) * half, :]
         up_part = up[p * half : (p + 1) * half, :]
-        limit = query_at + span * SPAN
-
-        def forward(b, sums):
-            rows = rows_at(b * keys, keys, keys)
-            raw = dot(kv[rows, :HD], q_part, ((1,), (1,)))
-            e = jnp.where(key_row + b * keys <= limit, jnp.exp2(raw * (SCALE * LOG2E)), 0.0)
+        limit = query_at + spans[me, p] * SPAN
+        total = jnp.zeros((8, half), F32)
+        weighted = jnp.zeros((8, half), F32)
+        for at in range(0, reach, keys):
+            rows = slice(at, at + keys)
+            e = jnp.exp2(dot(kv[rows, :HD], q_part, ((1,), (1,))) * (SCALE * LOG2E))
+            if at + keys > sure:
+                e = jnp.where(key_row + at <= limit, e, 0.0)
             dp = dot(kv[rows, HD:], up_part, ((1,), (1,)))
             expo[rows, :] = e
             dprob[rows, :] = dp
-            weighted = e.astype(BF16).astype(F32) * dp
-            return (
-                sums[0] + jnp.sum(e.reshape(keys // 8, 8, half), axis=0),
-                sums[1] + jnp.sum(weighted.reshape(keys // 8, 8, half), axis=0),
-            )
-
-        zero = jnp.zeros((8, half), F32)
-        total, weighted = lax.fori_loop(0, blocks, forward, (zero, zero))
+            term = e.astype(BF16).astype(F32) * dp
+            total = total + jnp.sum(e.reshape(keys // 8, 8, half), axis=0)
+            weighted = weighted + jnp.sum(term.reshape(keys // 8, 8, half), axis=0)
         inverse = 1.0 / jnp.sum(total, axis=0, keepdims=True)
         delta = jnp.sum(weighted, axis=0, keepdims=True) * inverse
-        dq_t[...] = jnp.zeros_like(dq_t)
-
-        def backward(b, carry):
-            rows = rows_at(b * keys, keys, keys)
+        for at in range(0, reach, keys):
+            rows = slice(at, at + keys)
             prob = expo[rows, :] * inverse
             dscore = (prob * (dprob[rows, :] - delta) * SCALE).astype(BF16)
-            acc[rows, :HD] += dot(dscore, q_part)
-            acc[rows, HD:] += dot(prob.astype(BF16), up_part)
-            dq_t[...] += dot(kv[rows, :HD].T, dscore)
-            return carry
-
-        lax.fori_loop(0, blocks, backward, 0)
+            dkey, dvalue = dot(dscore, q_part), dot(prob.astype(BF16), up_part)
+            dq_term = dot(kv[rows, :HD].T, dscore)
+            if p == 1:
+                acc[rows, :HD] = dkey
+                acc[rows, HD:] = dvalue
+            else:
+                acc[rows, :HD] += dkey
+                acc[rows, HD:] += dvalue
+            if at == 0:
+                dq_t[...] = dq_term
+            else:
+                dq_t[...] += dq_term
         q_rows = q_ref[p * half : (p + 1) * half, :].astype(F32)
         dq = norm_backward(q_rows, inverse_rms(q_rows), dq_t[...].T).astype(BF16)
         for h in range(NQ):
@@ -300,7 +327,8 @@
         refs[-1][rows_at(at, piece, 16), :] = ref[...].astype(F32)
 
 
-def token_grad_kernel(ids, dq_ref, dkv_ref, w_ref, out_ref, work):
+def token_grad_kernel(ids, dq_ref, dkv_ref, w_ref, out_ref, done_ref, work):
+    done_ref[...] = jnp.zeros_like(done_ref)
     wide = NBR * BLK
     cover = out_ref.shape[1] // wide
     for c in range(NCB):
@@ -319,7 +347,6 @@
 def per_device(ndp, tokens, grad_attn, w_packed, ids, spans):
     nctx = lax.axis_size("ctx")
     nz = nctx // 2
-    dp = lax.axis_index("dp")
     x = tokens[0]
     tok, width = x.shape
     length = spans.shape[0] * 2 * SPAN
@@ -358,7 +385,7 @@
     )
 
     if fast:
-        mine = lax.dynamic_slice_in_dim(w_packed, dp * piece, piece, 0)
+        (mine,) = call(part_kernel, (), (w_packed,), [((piece, BLK), BF16)], moved=4 * piece * BLK)
         from_z = [shift_z(mine, k) for k in range(1, nz)]
 
         def both_cores(parts):
@@ -375,22 +402,23 @@
         )
         xt_other = swap_core(after(xt, stacked))
         pieces = [stacked] + [swap_dp(stacked, k) for k in range(1, ndp)]
-        weights, kv, key = call(
+        pieces = both_cores(pieces)
+        w_last, kv, key = call(
             functools.partial(keys_kernel, nz),
             (ids,),
-            (x, *shards, *both_cores(pieces)),
-            [((NNZ * BLK, BLK), BF16), ((tok, 2 * HD), BF16), ((tok, HD), BF16)],
+            (x, *shards, *pieces),
+            [((2 * shard, BLK), BF16), ((tok, 2 * HD), BF16), ((tok, HD), BF16)],
             wait=(xt_other,),
             flops=2 * tok * (NCB - NQ) * NBR * BLK * BLK,
-            moved=6 * 2**20,
-        )
-        query, qhat = call(
-            queries_kernel,
+            moved=4 * 2**20,
+        )
+        weights, query, qhat = call(
+            functools.partial(queries_kernel, nz),
             (ids,),
-            (x, weights),
-            [((tok * NQ, HD), BF16)] * 2,
-            flops=16 * tok * NQ * NBR * BLK * BLK,
-            moved=3 * 2**20,
+            (x, w_last, *shards, *pieces),
+            [((NNZ * BLK, BLK), BF16)] + [((tok * NQ, HD), BF16)] * 2,
+            flops=2 * tok * NQ * NBR * BLK * BLK,
+            moved=8 * 2**20,
         )
     else:
         weights = lax.all_gather(w_packed, "ctx", axis=0, tiled=True)
@@ -408,7 +436,7 @@
         part = kv if k == 0 else shift_z(kv, k)
         kv_pieces += [part, swap_core(after(part, query) if k == nz - 1 else part)]
     outs = call(
-        functools.partial(attend_kernel, nz, math.gcd(512, length)),
+        functools.partial(attend_kernel, nz, math.gcd(512, length // 2)),
         (spans,),
         (query, qhat, up, *kv_pieces),
         [((NQ, tok, HD), BF16)] + [((tok, 2 * HD), BF16)] * (2 * nz),
@@ -454,6 +482,15 @@
         [((2, tok, HD), BF16)],
         moved=2**19,
     )
+    grad_tokens, done = call(
+        token_grad_kernel,
+        (ids,),
+        (dq, dkv, weights),
+        [((tok, width), BF16), ((8, BLK), F32)],
+        scratch=[pltpu.VMEM((tok, width), F32)],
+        flops=2 * tok * NNZ * BLK * BLK,
+        moved=4 * 2**20,
+    )
     if fast:
         tail = weight_terms(nz - 1, 1, (*dq_pair, dkv, swap_core(dkv)))
         tail = [tail[0]] + [
@@ -465,6 +502,7 @@
             (*head, *tail),
             [((piece, BLK), BF16)] * nz,
             scratch=[pltpu.VMEM((nz * piece, BLK), BF16)],
+            wait=(done,),
             moved=2 * 2**20,
         )
         owned = by_z[0].astype(F32)
@@ -492,15 +530,6 @@
         )
         grad_weights = lax.psum(jnp.sum(received.astype(F32), axis=0), "dp")
 
-    (grad_tokens,) = call(
-        token_grad_kernel,
-        (ids,),
-        (dq, dkv, weights),
-        [((tok, width), BF16)],
-        scratch=[pltpu.VMEM((tok, width), F32)],
-        flops=2 * tok * NNZ * BLK * BLK,
-        moved=4 * 2**20,
-    )
     return (grad_tokens[None], grad_weights)
 
 

time: 91 us -> 88.8 us (0.976)
  starting transfers between devices: 35.9 us -> 34.4 us
    unnamed x12 -> x14, local copies, waits for them, and re-layouts: 3.78 us -> 4.75 us
    pallas_call x11 -> x12, Pallas kernels: 16.1 us -> 15.5 us  [call(): pl.pallas_call(body, in_specs=[SMEM] * len(scalars) + [VMEM] * len(arrays...]
  transfers between devices with their start and end apart: 40 -> 40, of which waited for: 18 -> 17; matrix products, arithmetic and copies ran while one was open for 3% -> 2% of each run, Pallas kernels for 10% -> 11%
where the time goes in v5:
time: 88.8 us; the launch traced here: 88.6 us
  starting transfers between devices  34.4 us (39%)
  waiting for transfers between devices  32.9 us (37%)
  Pallas kernels  15.5 us (17%)
  local copies, waits for them, and re-layouts  4.75 us (5%)
    ppermute x12, waiting for transfers between devices, swap_dp(): return lax.ppermute(v, 'dp', [(i, i ^ k) for i in range(ndp)])  18.1 us
    ppermute x12, starting transfers between devices, shift_z(): lax.ppermute(v, 'ctx', [(i, (i // 2 + k) % nz * 2 + i % 2) for i in range...  17.2 us
    pallas_call x12, Pallas kernels, call(): pl.pallas_call(body, in_specs=[SMEM] * len(scalars) + [VMEM] * len(arrays...  15.5 us
    ppermute x12, starting transfers between devices, swap_dp(): return lax.ppermute(v, 'dp', [(i, i ^ k) for i in range(ndp)])  14.2 us
    ppermute x12, waiting for transfers between devices, shift_z(): lax.ppermute(v, 'ctx', [(i, (i // 2 + k) % nz * 2 + i % 2) for i in range...  10.9 us
    unnamed x14, local copies, waits for them, and re-layouts  4.75 us
    ppermute x16, waiting for transfers between devices, swap_core(): return lax.ppermute(v, 'ctx', [(i, i ^ 1) for i in range(nctx)])  3.91 us
    ppermute x16, starting transfers between devices, swap_core(): return lax.ppermute(v, 'ctx', [(i, i ^ 1) for i in range(nctx)])  2.99 us
  transfers between devices with their start and end apart: 40, of which 17 were waited for; matrix products, arithmetic and copies ran while one was open for 2% of the time, Pallas kernels for 11%

profile of v5, /device:TPU:0, one launch (start us, length us, event | category | flops | bytes accessed | tf_op | source)
XLA Modules:
  0.0 88.6 jit_solution(8743074381945758104)
XLA Ops:
  0.6 0.5 collective-permute-start
  1.1 1.0 %copy-done.2 = bf16[1280,128]{1,0:T(8,128)(2,1)S(1)} copy-done((bf16[1280,128]{1,0:T(8,128)(2,1)S(1)}, bf16[1280,128]{1,0:T(8,128)(2,1)}, u32[]{:S(2)}) %copy-start.2) | copy-done | bytes 327704
  2.1 2.6 %collective-permute-start.1 = (bf16[320,128]{1,0:T(8,128)(2,1)S(1)}, bf16[320,128]{1,0:T(8,128)(2,1)S(1)}, u32[]{:S(2)}, u32[]{:S(2)}) collective-permute-start(bf16[320,128]{1,0:T(8,128)(2,1)S(1)} %shard_map.69), channel_id=1, source_target_pairs={{0,2},{1,3},{2,4},{3,5},{4,6},{5,7},{6,0},{7,1},{8,10},{9,11},{10,... | collective-permute-start | bytes 245768 | tf_op jit(solution)/shard_map/ppermute | solution.py:364
  4.7 2.6 %collective-permute-start.2 = (bf16[320,128]{1,0:T(8,128)(2,1)S(1)}, bf16[320,128]{1,0:T(8,128)(2,1)S(1)}, u32[]{:S(2)}, u32[]{:S(2)}) collective-permute-start(bf16[320,128]{1,0:T(8,128)(2,1)S(1)} %shard_map.69), channel_id=1, source_target_pairs={{0,4},{1,5},{2,6},{3,7},{4,0},{5,1},{6,2},{7,3},{8,12},{9,13},{10,... | collective-permute-start | bytes 245768 | tf_op jit(solution)/shard_map/ppermute | solution.py:364
  7.3 1.3 %collective-permute-start.3 = (bf16[320,128]{1,0:T(8,128)(2,1)S(1)}, bf16[320,128]{1,0:T(8,128)(2,1)S(1)}, u32[]{:S(2)}, u32[]{:S(2)}) collective-permute-start(bf16[320,128]{1,0:T(8,128)(2,1)S(1)} %shard_map.69), channel_id=1, source_target_pairs={{0,6},{1,7},{2,0},{3,1},{4,2},{5,3},{6,4},{7,5},{8,14},{9,15},{10,... | collective-permute-start | bytes 245768 | tf_op jit(solution)/shard_map/ppermute | solution.py:364
  8.7 0.8 copy.10.refs_0_
  9.4 0.8 copy.11.refs_1_
  10.2 1.2 %copy-done = bf16[1,128,4096]{2,1,0:T(8,128)(2,1)S(1)} copy-done((bf16[1,128,4096]{2,1,0:T(8,128)(2,1)S(1)}, bf16[1,128,4096]{2,1,0:T(8,128)(2,1)}, u32[]{:S(2)}) %copy-start) | copy-done | bytes 1048600
  11.4 0.9 %copy-done.4 = bf16[1,128,1024]{2,1,0:T(8,128)(2,1)S(1)} copy-done((bf16[1,128,1024]{2,1,0:T(8,128)(2,1)S(1)}, bf16[1,128,1024]{2,1,0:T(8,128)(2,1)}, u32[]{:S(2)}) %copy-start.4) | copy-done | bytes 262168
  12.4 2.0 %shard_map.68 = (bf16[4096,128]{1,0:T(8,128)(2,1)S(1)}, bf16[1024,128]{1,0:T(8,128)(2,1)S(1)}, s32[10,8]{1,0:T(8,128)S(1)}, s32[8,2]{1,0:T(8,128)S(1)}) custom-call(s32[10,8]{1,0:T(8,128)S(1)} %copy.10.refs_0_, s32[8,2]{1,0:T(8,128)S(1)} %copy.11.refs_1_, bf16[128,4096]{1,0:T(8,128)(2,1)S(1)} %bitcast.3, bf16[128,1024]{1,0:T(8,128)(2,1)S(1)} %bitcast.6), custom_call_target="tpu_custom_call" | custom-call | bytes 2097152 | tf_op jit(solution)/shard_map/pallas_call | solution.py:43
  14.6 0.1 collective-permute-start.11
  14.6 2.5 %collective-permute-start.9 = (bf16[960,128]{1,0:T(8,128)(2,1)S(1)}, bf16[960,128]{1,0:T(8,128)(2,1)S(1)}, u32[]{:S(2)}, u32[]{:S(2)}) collective-permute-start(bf16[960,128]{1,0:T(8,128)(2,1)S(1)} %shard_map.70.refs_1_.refs_4_.refs_5_), channel_id=1, source_target_pairs={{0,24},{8,16},{16,8},{24,0},{1,25},{9,17},{17,9},{25,1},{2,26},{10... | collective-permute-start | bytes 737288 | tf_op jit(solution)/shard_map/ppermute | solution.py:369
  17.1 0.5 collective-permute-start.5
  17.7 0.5 collective-permute-start.7
  18.2 6.2 %collective-permute-done.9.refs_10_.refs_11_ = bf16[960,128]{1,0:T(8,128)(2,1)S(1)} collective-permute-done((bf16[960,128]{1,0:T(8,128)(2,1)S(1)}, bf16[960,128]{1,0:T(8,128)(2,1)S(1)}, u32[]{:S(2)}, u32[]{:S(2)}) %collective-permute-start.9) | collective-permute-done | bytes 245792 | tf_op jit(solution)/shard_map/ppermute | solution.py:369
  24.4 4.9 %collective-permute-done.5.refs_6_.refs_7_ = bf16[960,128]{1,0:T(8,128)(2,1)S(1)} collective-permute-done((bf16[960,128]{1,0:T(8,128)(2,1)S(1)}, bf16[960,128]{1,0:T(8,128)(2,1)S(1)}, u32[]{:S(2)}, u32[]{:S(2)}) %collective-permute-start.5) | collective-permute-done | bytes 245792 | tf_op jit(solution)/shard_map/ppermute | solution.py:369
  29.3 0.5 collective-permute-start.8
  29.8 1.0 %collective-permute-done.6.refs_7_.refs_8_ = bf16[960,128]{1,0:T(8,128)(2,1)S(1)} collective-permute-done((bf16[960,128]{1,0:T(8,128)(2,1)S(1)}, bf16[960,128]{1,0:T(8,128)(2,1)S(1)}, u32[]{:S(2)}, u32[]{:S(2)}) %collective-permute-start.6) | collective-permute-done | bytes 245792 | tf_op jit(solution)/shard_map/ppermute | solution.py:361
  30.8 0.4 collective-permute-done.8.refs_9_.refs_10_
  31.1 1.1 %shard_map.72 = (bf16[2560,128]{1,0:T(8,128)(2,1)S(1)}, bf16[128,256]{1,0:T(8,128)(2,1)S(1)}, bf16[128,128]{1,0:T(8,128)(2,1)S(1)}) custom-call(s32[10,8]{1,0:T(8,128)S(1)} %get-tuple-element.35.refs_3_.refs_0_, bf16[128,4096]{1,0:T(8,128)(2,1)S(1)} %bitcast.4, bf16[1280,128]{1,0:T(8,128)(2,1)S(1)} %copy-done.3, ...), custom_call_target="tpu_custom_call" | custom-call | flops 67108864 | bytes 4194304 | tf_op jit(solution)/shard_map/pallas_call | solution.py:43
  32.2 2.3 %collective-permute-start.17 = (bf16[128,256]{1,0:T(8,128)(2,1)S(1)}, bf16[128,256]{1,0:T(8,128)(2,1)S(1)}, u32[]{:S(2)}, u32[]{:S(2)}) collective-permute-start(bf16[128,256]{1,0:T(8,128)(2,1)S(1)} %get-tuple-element.42.refs_4_), channel_id=1, source_target_pairs={{0,6},{1,7},{2,0},{3,1},{4,2},{5,3},{6,4},{7,5},{8,14},{9,15},{10,... | collective-permute-start | bytes 196616 | tf_op jit(solution)/shard_map/ppermute | solution.py:364
  34.5 0.6 collective-permute-start.15
  35.2 1.8 %shard_map.73 = (bf16[10240,128]{1,0:T(8,128)(2,1)S(1)}, bf16[1024,128]{1,0:T(8,128)(2,1)S(1)}, bf16[1024,128]{1,0:T(8,128)(2,1)S(1)}) custom-call(s32[10,8]{1,0:T(8,128)S(1)} %get-tuple-element.35.refs_3_.refs_0_, bf16[128,4096]{1,0:T(8,128)(2,1)S(1)} %bitcast.5, bf16[2560,128]{1,0:T(8,128)(2,1)S(1)} %get-tuple-element.38.refs_2_, ...), custom_call_target="tpu_custom_call" | custom-call | flops 268435456 | bytes 8388608 | tf_op jit(solution)/shard_map/pallas_call | solution.py:43
  37.0 0.6 collective-permute-start.18
  37.5 3.5 %collective-permute-done.13.refs_6_ = bf16[128,256]{1,0:T(8,128)(2,1)S(1)} collective-permute-done((bf16[128,256]{1,0:T(8,128)(2,1)S(1)}, bf16[128,256]{1,0:T(8,128)(2,1)S(1)}, u32[]{:S(2)}, u32[]{:S(2)}) %collective-permute-start.13) | collective-permute-done | bytes 65568 | tf_op jit(solution)/shard_map/ppermute | solution.py:364
  41.0 1.3 %collective-permute-done.15.refs_8_ = bf16[128,256]{1,0:T(8,128)(2,1)S(1)} collective-permute-done((bf16[128,256]{1,0:T(8,128)(2,1)S(1)}, bf16[128,256]{1,0:T(8,128)(2,1)S(1)}, u32[]{:S(2)}, u32[]{:S(2)}) %collective-permute-start.15) | collective-permute-done | bytes 65568 | tf_op jit(solution)/shard_map/ppermute | solution.py:364
  42.3 1.2 %collective-permute-done.16.refs_9_ = bf16[128,256]{1,0:T(8,128)(2,1)S(1)} collective-permute-done((bf16[128,256]{1,0:T(8,128)(2,1)S(1)}, bf16[128,256]{1,0:T(8,128)(2,1)S(1)}, u32[]{:S(2)}, u32[]{:S(2)}) %collective-permute-start.16) | collective-permute-done | bytes 65568 | tf_op jit(solution)/shard_map/ppermute | solution.py:361
  43.6 3.7 %shard_map.75 = (bf16[8,128,128]{2,1,0:T(8,128)(2,1)S(1)}, bf16[128,256]{1,0:T(8,128)(2,1)S(1)}, bf16[128,256]{1,0:T(8,128)(2,1)S(1)}, bf16[128,256]{1,0:T(8,128...) custom-call(s32[8,2]{1,0:T(8,128)S(1)} %get-tuple-element.36.refs_0_, ...), custom_call_target="tpu_custom_call" | custom-call | flops 671088640 | bytes 4194304 | tf_op jit(solution)/shard_map/pallas_call | solution.py:43
  47.3 0.2 collective-permute-start.24
  47.5 0.3 collective-permute-start.22
  47.9 0.2 collective-permute-start.20
  48.0 0.3 collective-permute-start.19
  48.4 0.2 collective-permute-start.26
  48.6 1.8 %collective-permute-start.25 = (bf16[128,256]{1,0:T(8,128)(2,1)S(1)}, bf16[128,256]{1,0:T(8,128)(2,1)S(1)}, u32[]{:S(2)}, u32[]{:S(2)}) collective-permute-start(bf16[128,256]{1,0:T(8,128)(2,1)S(1)} %add_convert_fusion.1), channel_id=1, source_target_pairs={{0,6},{1,7},{2,0},{3,1},{4,2},{5,3},{6,4},{7,5},{8,14},{9,15},{10,... | collective-permute-start | bytes 196616 | tf_op jit(solution)/shard_map/ppermute | solution.py:364
  50.5 0.1 collective-permute-start.23
  50.6 0.7 collective-permute-start.21
  51.3 1.5 %shard_map.78 = (bf16[960,128]{1,0:T(8,128)(2,1)S(1)}, bf16[960,128]{1,0:T(8,128)(2,1)S(1)}, bf16[960,128]{1,0:T(8,128)(2,1)S(1)}, bf16[960,128]{1,0:T(8,128)(2,1)S(1)}) custom-call(s32[10,8]{1,0:T(8,128)S(1)} %get-tuple-element.35.refs_3_.refs_0_, bf16[4096,128]{1,0:T(8,128)(2,1)S(1)} %get-tuple-element.37.refs_1_, ...), custom_call_target="tpu_custom_call" | custom-call | flops 251658240 | bytes 4194304 | tf_op jit(solution)/shard_map/pallas_call | solution.py:43
  52.8 1.6 %collective-permute-start.27 = (bf16[960,128]{1,0:T(8,128)(2,1)S(1)}, bf16[960,128]{1,0:T(8,128)(2,1)S(1)}, u32[]{:S(2)}, u32[]{:S(2)}) collective-permute-start(bf16[960,128]{1,0:T(8,128)(2,1)S(1)} %get-tuple-element.56), channel_id=1, source_target_pairs={{0,8},{8,0},{16,24},{24,16},{1,9},{9,1},{17,25},{25,17},{2,10},{10... | collective-permute-start | bytes 737288 | tf_op jit(solution)/shard_map/ppermute | solution.py:369
  54.3 1.1 %collective-permute-start.28 = (bf16[960,128]{1,0:T(8,128)(2,1)S(1)}, bf16[960,128]{1,0:T(8,128)(2,1)S(1)}, u32[]{:S(2)}, u32[]{:S(2)}) collective-permute-start(bf16[960,128]{1,0:T(8,128)(2,1)S(1)} %get-tuple-element.57), channel_id=1, source_target_pairs={{0,16},{8,24},{16,0},{24,8},{1,17},{9,25},{17,1},{25,9},{2,18},{10... | collective-permute-start | bytes 737288 | tf_op jit(solution)/shard_map/ppermute | solution.py:369
  55.4 0.9 %collective-permute-start.29 = (bf16[960,128]{1,0:T(8,128)(2,1)S(1)}, bf16[960,128]{1,0:T(8,128)(2,1)S(1)}, u32[]{:S(2)}, u32[]{:S(2)}) collective-permute-start(bf16[960,128]{1,0:T(8,128)(2,1)S(1)} %get-tuple-element.58), channel_id=1, source_target_pairs={{0,24},{8,16},{16,8},{24,0},{1,25},{9,17},{17,9},{25,1},{2,26},{10... | collective-permute-start | bytes 737288 | tf_op jit(solution)/shard_map/ppermute | solution.py:369
  56.4 1.6 %collective-permute-done.23.refs_3_ = bf16[128,256]{1,0:T(8,128)(2,1)S(1)} collective-permute-done((bf16[128,256]{1,0:T(8,128)(2,1)S(1)}, bf16[128,256]{1,0:T(8,128)(2,1)S(1)}, u32[]{:S(2)}, u32[]{:S(2)}) %collective-permute-start.23) | collective-permute-done | bytes 65568 | tf_op jit(solution)/shard_map/ppermute | solution.py:364
  58.0 0.1 shard_map.76.refs_2_.refs_5_
  58.1 0.1 collective-permute-start.30
  58.2 1.2 %collective-permute-done.30.refs_6_ = bf16[2,128,128]{2,1,0:T(8,128)(2,1)S(1)} collective-permute-done((bf16[2,128,128]{2,1,0:T(8,128)(2,1)S(1)}, bf16[2,128,128]{2,1,0:T(8,128)(2,1)S(1)}, u32[]{:S(2)}, u32[]{:S(2)}) %collective-permute-start.30) | collective-permute-done | bytes 65568 | tf_op jit(solution)/shard_map/ppermute | solution.py:361
  59.4 1.0 %shard_map.79 = (bf16[320,128]{1,0:T(8,128)(2,1)S(1)}, bf16[320,128]{1,0:T(8,128)(2,1)S(1)}, bf16[320,128]{1,0:T(8,128)(2,1)S(1)}, bf16[320,128]{1,0:T(8,128)(2,1)S(1)}) custom-call(s32[10,8]{1,0:T(8,128)S(1)} %get-tuple-element.35.refs_3_.refs_0_, bf16[4096,128]{1,0:T(8,128)(2,1)S(1)} %get-tuple-element.37.refs_1_, ...), custom_call_target="tpu_custom_call" | custom-call | flops 83886080 | bytes 4194304 | tf_op jit(solution)/shard_map/pallas_call | solution.py:43
  60.4 1.6 %collective-permute-start.31 = (bf16[320,128]{1,0:T(8,128)(2,1)S(1)}, bf16[320,128]{1,0:T(8,128)(2,1)S(1)}, u32[]{:S(2)}, u32[]{:S(2)}) collective-permute-start(bf16[320,128]{1,0:T(8,128)(2,1)S(1)} %get-tuple-element.60), channel_id=1, source_target_pairs={{0,8},{8,0},{16,24},{24,16},{1,9},{9,1},{17,25},{25,17},{2,10},{10... | collective-permute-start | bytes 245768 | tf_op jit(solution)/shard_map/ppermute | solution.py:369
  62.0 1.0 %collective-permute-start.32 = (bf16[320,128]{1,0:T(8,128)(2,1)S(1)}, bf16[320,128]{1,0:T(8,128)(2,1)S(1)}, u32[]{:S(2)}, u32[]{:S(2)}) collective-permute-start(bf16[320,128]{1,0:T(8,128)(2,1)S(1)} %get-tuple-element.61), channel_id=1, source_target_pairs={{0,16},{8,24},{16,0},{24,8},{1,17},{9,25},{17,1},{25,9},{2,18},{10... | collective-permute-start | bytes 245768 | tf_op jit(solution)/shard_map/ppermute | solution.py:369
  63.1 0.9 %collective-permute-start.33 = (bf16[320,128]{1,0:T(8,128)(2,1)S(1)}, bf16[320,128]{1,0:T(8,128)(2,1)S(1)}, u32[]{:S(2)}, u32[]{:S(2)}) collective-permute-start(bf16[320,128]{1,0:T(8,128)(2,1)S(1)} %shard_map.80), channel_id=1, source_target_pairs={{0,24},{8,16},{16,8},{24,0},{1,25},{9,17},{17,9},{25,1},{2,26},{10... | collective-permute-start | bytes 245768 | tf_op jit(solution)/shard_map/ppermute | solution.py:369
  64.0 3.0 %shard_map.77 = (bf16[128,4096]{1,0:T(8,128)(2,1)}, f32[8,128]{1,0:T(8,128)S(1)}) custom-call(s32[10,8]{1,0:T(8,128)S(1)} %get-tuple-element.35.refs_3_.refs_0_, bf16[8,128,128]{2,1,0:T(8,128)(2,1)S(1)} %get-tuple-element.43.refs_1_.refs_3_, bf16[2,128,128]{2,1,0:T(8,128)(2,1)S(1)} %shard_map.76.refs_2_.refs_5_, bf16[10240,128]{1,0:T(8,128)(2,1)S(1)} %get-tuple-element.53.refs_3_), custom_call_target="tpu_custom_call" | custom-call | flops 335544320 | bytes 4194304 | tf_op jit(solution)/shard_map/pallas_call | solution.py:43
  67.0 1.4 %collective-permute-done.31.refs_5_ = bf16[320,128]{1,0:T(8,128)(2,1)S(1)} collective-permute-done((bf16[320,128]{1,0:T(8,128)(2,1)S(1)}, bf16[320,128]{1,0:T(8,128)(2,1)S(1)}, u32[]{:S(2)}, u32[]{:S(2)}) %collective-permute-start.31) | collective-permute-done | bytes 81952 | tf_op jit(solution)/shard_map/ppermute | solution.py:369
  68.4 2.0 %collective-permute-done.32.refs_6_ = bf16[320,128]{1,0:T(8,128)(2,1)S(1)} collective-permute-done((bf16[320,128]{1,0:T(8,128)(2,1)S(1)}, bf16[320,128]{1,0:T(8,128)(2,1)S(1)}, u32[]{:S(2)}, u32[]{:S(2)}) %collective-permute-start.32) | collective-permute-done | bytes 81952 | tf_op jit(solution)/shard_map/ppermute | solution.py:369
  70.5 0.3 shard_map.81
  70.8 2.5 %collective-permute-start.34 = (bf16[320,128]{1,0:T(8,128)(2,1)S(1)}, bf16[320,128]{1,0:T(8,128)(2,1)S(1)}, u32[]{:S(2)}, u32[]{:S(2)}) collective-permute-start(bf16[320,128]{1,0:T(8,128)(2,1)S(1)} %get-tuple-element.65), channel_id=1, source_target_pairs={{0,2},{1,3},{2,4},{3,5},{4,6},{5,7},{6,0},{7,1},{8,10},{9,11},{10,... | collective-permute-start | bytes 245768 | tf_op jit(solution)/shard_map/ppermute | solution.py:364
  73.3 1.2 %collective-permute-start.35 = (bf16[320,128]{1,0:T(8,128)(2,1)S(1)}, bf16[320,128]{1,0:T(8,128)(2,1)S(1)}, u32[]{:S(2)}, u32[]{:S(2)}) collective-permute-start(bf16[320,128]{1,0:T(8,128)(2,1)S(1)} %get-tuple-element.66), channel_id=1, source_target_pairs={{0,4},{1,5},{2,6},{3,7},{4,0},{5,1},{6,2},{7,3},{8,12},{9,13},{10,... | collective-permute-start | bytes 245768 | tf_op jit(solution)/shard_map/ppermute | solution.py:364
  74.5 1.5 %collective-permute-start.36 = (bf16[320,128]{1,0:T(8,128)(2,1)S(1)}, bf16[320,128]{1,0:T(8,128)(2,1)S(1)}, u32[]{:S(2)}, u32[]{:S(2)}) collective-permute-start(bf16[320,128]{1,0:T(8,128)(2,1)S(1)} %get-tuple-element.67), channel_id=1, source_target_pairs={{0,6},{1,7},{2,0},{3,1},{4,2},{5,3},{6,4},{7,5},{8,14},{9,15},{10,... | collective-permute-start | bytes 245768 | tf_op jit(solution)/shard_map/ppermute | solution.py:364
  76.0 2.0 %collective-permute-done.34 = bf16[320,128]{1,0:T(8,128)(2,1)S(1)} collective-permute-done((bf16[320,128]{1,0:T(8,128)(2,1)S(1)}, bf16[320,128]{1,0:T(8,128)(2,1)S(1)}, u32[]{:S(2)}, u32[]{:S(2)}) %collective-permute-start.34) | collective-permute-done | bytes 81952 | tf_op jit(solution)/shard_map/ppermute | solution.py:364
  78.0 2.5 %collective-permute-done.35 = bf16[320,128]{1,0:T(8,128)(2,1)S(1)} collective-permute-done((bf16[320,128]{1,0:T(8,128)(2,1)S(1)}, bf16[320,128]{1,0:T(8,128)(2,1)S(1)}, u32[]{:S(2)}, u32[]{:S(2)}) %collective-permute-start.35) | collective-permute-done | bytes 81952 | tf_op jit(solution)/shard_map/ppermute | solution.py:364
  80.6 0.8 collective-permute-start.37
  81.4 0.9 %collective-permute-start.38 = (bf16[320,128]{1,0:T(8,128)(2,1)S(1)}, bf16[320,128]{1,0:T(8,128)(2,1)S(1)}, u32[]{:S(2)}, u32[]{:S(2)}) collective-permute-start(bf16[320,128]{1,0:T(8,128)(2,1)S(1)} %add_convert_fusion.refs_0_), channel_id=1, source_target_pairs={{0,16},{8,24},{16,0},{24,8},{1,17},{9,25},{17,1},{25,9},{2,18},{10... | collective-permute-start | bytes 245768 | tf_op jit(solution)/shard_map/ppermute | solution.py:369
  82.3 1.8 %collective-permute-start.39 = (bf16[320,128]{1,0:T(8,128)(2,1)S(1)}, bf16[320,128]{1,0:T(8,128)(2,1)S(1)}, u32[]{:S(2)}, u32[]{:S(2)}) collective-permute-start(bf16[320,128]{1,0:T(8,128)(2,1)S(1)} %add_convert_fusion.refs_0_), channel_id=1, source_target_pairs={{0,24},{8,16},{16,8},{24,0},{1,25},{9,17},{17,9},{25,1},{2,26},{10... | collective-permute-start | bytes 245768 | tf_op jit(solution)/shard_map/ppermute | solution.py:369
  84.1 1.7 %collective-permute-done.37.refs_1_ = bf16[320,128]{1,0:T(8,128)(2,1)S(1)} collective-permute-done((bf16[320,128]{1,0:T(8,128)(2,1)S(1)}, bf16[320,128]{1,0:T(8,128)(2,1)S(1)}, u32[]{:S(2)}, u32[]{:S(2)}) %collective-permute-start.37) | collective-permute-done | bytes 81952 | tf_op jit(solution)/shard_map/ppermute | solution.py:369
  85.8 0.6 collective-permute-done.38.refs_2_
  86.5 1.2 %collective-permute-done.39.refs_3_ = bf16[320,128]{1,0:T(8,128)(2,1)S(1)} collective-permute-done((bf16[320,128]{1,0:T(8,128)(2,1)S(1)}, bf16[320,128]{1,0:T(8,128)(2,1)S(1)}, u32[]{:S(2)}, u32[]{:S(2)}) %collective-permute-start.39) | collective-permute-done | bytes 81952 | tf_op jit(solution)/shard_map/ppermute | solution.py:369
  87.7 0.9 %shard_map.82 = f32[1280,128]{1,0:T(8,128)} custom-call(bf16[320,128]{1,0:T(8,128)(2,1)S(1)} %add_convert_fusion.refs_0_, bf16[320,128]{1,0:T(8,128)(2,1)S(1)} %collective-permute-done.37.refs_1_, bf16[320,128]{1,0:T(8,128)(2,1)S(1)} %collective-permute-done.38.refs_2_, bf16[320,128]{1,0:T(8,128)(2,1)S(1)} %collective-permute-done.39.refs_3_), custom_call_target="tpu_custom_call" | custom-call | bytes 1048576 | tf_op jit(solution)/shard_map/pallas_call | solution.py:43
  (50 shorter events, 0.4 us)
Async XLA Ops:
  0.6 13.9 %collective-permute-start = (bf16[1280,128]{1,0:T(8,128)(2,1)}, bf16[1280,128]{1,0:T(8,128)(2,1)S(1)}, u32[]{:S(2)}, u32[]{:S(2)}) collective-permute-start(bf16[1280,128]{1,0:T(8,128)(2,1)} %refs_3_.1), channel_id=1, source_target_pairs={{0,1},{1,0},{2,3},{3,2},{4,5},{5,4},{6,7},{7,6},{8,9},{9,8},{10,11... | collective-permute-start | bytes 983048 | tf_op jit(solution)/shard_map/ppermute | solution.py:361
  1.1 1.0 %copy-start.2 = (bf16[1280,128]{1,0:T(8,128)(2,1)S(1)}, bf16[1280,128]{1,0:T(8,128)(2,1)}, u32[]{:S(2)}) copy-start(bf16[1280,128]{1,0:T(8,128)(2,1)} %refs_3_.1) | copy-start | bytes 983044
  2.1 12.4 %collective-permute-start.1 = (bf16[320,128]{1,0:T(8,128)(2,1)S(1)}, bf16[320,128]{1,0:T(8,128)(2,1)S(1)}, u32[]{:S(2)}, u32[]{:S(2)}) collective-permute-start(bf16[320,128]{1,0:T(8,128)(2,1)S(1)} %shard_map.69), channel_id=1, source_target_pairs={{0,2},{1,3},{2,4},{3,5},{4,6},{5,7},{6,0},{7,1},{8,10},{9,11},{10,... | collective-permute-start | bytes 245768 | tf_op jit(solution)/shard_map/ppermute | solution.py:364
  4.7 9.8 %collective-permute-start.2 = (bf16[320,128]{1,0:T(8,128)(2,1)S(1)}, bf16[320,128]{1,0:T(8,128)(2,1)S(1)}, u32[]{:S(2)}, u32[]{:S(2)}) collective-permute-start(bf16[320,128]{1,0:T(8,128)(2,1)S(1)} %shard_map.69), channel_id=1, source_target_pairs={{0,4},{1,5},{2,6},{3,7},{4,0},{5,1},{6,2},{7,3},{8,12},{9,13},{10,... | collective-permute-start | bytes 245768 | tf_op jit(solution)/shard_map/ppermute | solution.py:364
  7.3 7.2 %collective-permute-start.3 = (bf16[320,128]{1,0:T(8,128)(2,1)S(1)}, bf16[320,128]{1,0:T(8,128)(2,1)S(1)}, u32[]{:S(2)}, u32[]{:S(2)}) collective-permute-start(bf16[320,128]{1,0:T(8,128)(2,1)S(1)} %shard_map.69), channel_id=1, source_target_pairs={{0,6},{1,7},{2,0},{3,1},{4,2},{5,3},{6,4},{7,5},{8,14},{9,15},{10,... | collective-permute-start | bytes 245768 | tf_op jit(solution)/shard_map/ppermute | solution.py:364
  10.2 1.2 %copy-start = (bf16[1,128,4096]{2,1,0:T(8,128)(2,1)S(1)}, bf16[1,128,4096]{2,1,0:T(8,128)(2,1)}, u32[]{:S(2)}) copy-start(bf16[1,128,4096]{2,1,0:T(8,128)(2,1)} %param.5) | copy-start | bytes 3145732
  11.4 0.9 %copy-start.4 = (bf16[1,128,1024]{2,1,0:T(8,128)(2,1)S(1)}, bf16[1,128,1024]{2,1,0:T(8,128)(2,1)}, u32[]{:S(2)}) copy-start(bf16[1,128,1024]{2,1,0:T(8,128)(2,1)} %param.6) | copy-start | bytes 786436
  14.4 16.8 %copy-start.1 = (bf16[1,128,4096]{2,1,0:T(8,128)(2,1)S(1)}, bf16[1,128,4096]{2,1,0:T(8,128)(2,1)}, u32[]{:S(2)}) copy-start(bf16[1,128,4096]{2,1,0:T(8,128)(2,1)} %param.5) | copy-start | bytes 3145732
  14.4 16.8 %copy-start.3 = (bf16[1280,128]{1,0:T(8,128)(2,1)S(1)}, bf16[1280,128]{1,0:T(8,128)(2,1)}, u32[]{:S(2)}) copy-start(bf16[1280,128]{1,0:T(8,128)(2,1)} %refs_3_.1) | copy-start | bytes 983044
  14.6 16.6 %collective-permute-start.11 = (bf16[4096,128]{1,0:T(8,128)(2,1)S(1)}, bf16[4096,128]{1,0:T(8,128)(2,1)S(1)}, u32[]{:S(2)}, u32[]{:S(2)}) collective-permute-start(bf16[4096,128]{1,0:T(8,128)(2,1)S(1)} %shard_map.71), channel_id=1, source_target_pairs={{0,1},{1,0},{2,3},{3,2},{4,5},{5,4},{6,7},{7,6},{8,9},{9,8},{10,11... | collective-permute-start | bytes 3145736 | tf_op jit(solution)/shard_map/ppermute | solution.py:361
  14.6 9.8 %collective-permute-start.9 = (bf16[960,128]{1,0:T(8,128)(2,1)S(1)}, bf16[960,128]{1,0:T(8,128)(2,1)S(1)}, u32[]{:S(2)}, u32[]{:S(2)}) collective-permute-start(bf16[960,128]{1,0:T(8,128)(2,1)S(1)} %shard_map.70.refs_1_.refs_4_.refs_5_), channel_id=1, source_target_pairs={{0,24},{8,16},{16,8},{24,0},{1,25},{9,17},{17,9},{25,1},{2,26},{10... | collective-permute-start | bytes 737288 | tf_op jit(solution)/shard_map/ppermute | solution.py:369
  17.1 12.1 %collective-permute-start.5 = (bf16[960,128]{1,0:T(8,128)(2,1)S(1)}, bf16[960,128]{1,0:T(8,128)(2,1)S(1)}, u32[]{:S(2)}, u32[]{:S(2)}) collective-permute-start(bf16[960,128]{1,0:T(8,128)(2,1)S(1)} %shard_map.70.refs_1_.refs_4_.refs_5_), channel_id=1, source_target_pairs={{0,8},{8,0},{16,24},{24,16},{1,9},{9,1},{17,25},{25,17},{2,10},{10... | collective-permute-start | bytes 737288 | tf_op jit(solution)/shard_map/ppermute | solution.py:369
  17.7 11.6 %collective-permute-start.7 = (bf16[960,128]{1,0:T(8,128)(2,1)S(1)}, bf16[960,128]{1,0:T(8,128)(2,1)S(1)}, u32[]{:S(2)}, u32[]{:S(2)}) collective-permute-start(bf16[960,128]{1,0:T(8,128)(2,1)S(1)} %shard_map.70.refs_1_.refs_4_.refs_5_), channel_id=1, source_target_pairs={{0,16},{8,24},{16,0},{24,8},{1,17},{9,25},{17,1},{25,9},{2,18},{10... | collective-permute-start | bytes 737288 | tf_op jit(solution)/shard_map/ppermute | solution.py:369
  18.2 11.6 %collective-permute-start.4 = (bf16[960,128]{1,0:T(8,128)(2,1)S(1)}, bf16[960,128]{1,0:T(8,128)(2,1)S(1)}, u32[]{:S(2)}, u32[]{:S(2)}) collective-permute-start(bf16[960,128]{1,0:T(8,128)(2,1)S(1)} %shard_map.70.refs_1_.refs_4_.refs_5_), channel_id=1, source_target_pairs={{0,1},{1,0},{2,3},{3,2},{4,5},{5,4},{6,7},{7,6},{8,9},{9,8},{10,11... | collective-permute-start | bytes 737288 | tf_op jit(solution)/shard_map/ppermute | solution.py:361
  24.4 5.4 %collective-permute-start.10 = (bf16[960,128]{1,0:T(8,128)(2,1)S(1)}, bf16[960,128]{1,0:T(8,128)(2,1)S(1)}, u32[]{:S(2)}, u32[]{:S(2)}) collective-permute-start(bf16[960,128]{1,0:T(8,128)(2,1)S(1)} %collective-permute-done.9.refs_10_.refs_11_), channel_id=1, source_target_pairs={{0,1},{1,0},{2,3},{3,2},{4,5},{5,4},{6,7},{7,6},{8,9},{9,8},{10,11... | collective-permute-start | bytes 737288 | tf_op jit(solution)/shard_map/ppermute | solution.py:361
  29.3 1.5 %collective-permute-start.6 = (bf16[960,128]{1,0:T(8,128)(2,1)S(1)}, bf16[960,128]{1,0:T(8,128)(2,1)S(1)}, u32[]{:S(2)}, u32[]{:S(2)}) collective-permute-start(bf16[960,128]{1,0:T(8,128)(2,1)S(1)} %collective-permute-done.5.refs_6_.refs_7_), channel_id=1, source_target_pairs={{0,1},{1,0},{2,3},{3,2},{4,5},{5,4},{6,7},{7,6},{8,9},{9,8},{10,11... | collective-permute-start | bytes 737288 | tf_op jit(solution)/shard_map/ppermute | solution.py:361
  29.3 1.9 %collective-permute-start.8 = (bf16[960,128]{1,0:T(8,128)(2,1)S(1)}, bf16[960,128]{1,0:T(8,128)(2,1)S(1)}, u32[]{:S(2)}, u32[]{:S(2)}) collective-permute-start(bf16[960,128]{1,0:T(8,128)(2,1)S(1)} %collective-permute-done.7.refs_8_.refs_9_), channel_id=1, source_target_pairs={{0,1},{1,0},{2,3},{3,2},{4,5},{5,4},{6,7},{7,6},{8,9},{9,8},{10,11... | collective-permute-start | bytes 737288 | tf_op jit(solution)/shard_map/ppermute | solution.py:361
  32.2 4.7 %collective-permute-start.17 = (bf16[128,256]{1,0:T(8,128)(2,1)S(1)}, bf16[128,256]{1,0:T(8,128)(2,1)S(1)}, u32[]{:S(2)}, u32[]{:S(2)}) collective-permute-start(bf16[128,256]{1,0:T(8,128)(2,1)S(1)} %get-tuple-element.42.refs_4_), channel_id=1, source_target_pairs={{0,6},{1,7},{2,0},{3,1},{4,2},{5,3},{6,4},{7,5},{8,14},{9,15},{10,... | collective-permute-start | bytes 196616 | tf_op jit(solution)/shard_map/ppermute | solution.py:364
  34.5 6.5 %collective-permute-start.13 = (bf16[128,256]{1,0:T(8,128)(2,1)S(1)}, bf16[128,256]{1,0:T(8,128)(2,1)S(1)}, u32[]{:S(2)}, u32[]{:S(2)}) collective-permute-start(bf16[128,256]{1,0:T(8,128)(2,1)S(1)} %get-tuple-element.42.refs_4_), channel_id=1, source_target_pairs={{0,2},{1,3},{2,4},{3,5},{4,6},{5,7},{6,0},{7,1},{8,10},{9,11},{10,... | collective-permute-start | bytes 196616 | tf_op jit(solution)/shard_map/ppermute | solution.py:364
  34.5 7.8 %collective-permute-start.15 = (bf16[128,256]{1,0:T(8,128)(2,1)S(1)}, bf16[128,256]{1,0:T(8,128)(2,1)S(1)}, u32[]{:S(2)}, u32[]{:S(2)}) collective-permute-start(bf16[128,256]{1,0:T(8,128)(2,1)S(1)} %get-tuple-element.42.refs_4_), channel_id=1, source_target_pairs={{0,4},{1,5},{2,6},{3,7},{4,0},{5,1},{6,2},{7,3},{8,12},{9,13},{10,... | collective-permute-start | bytes 196616 | tf_op jit(solution)/shard_map/ppermute | solution.py:364
  35.1 7.2 %collective-permute-start.12 = (bf16[128,256]{1,0:T(8,128)(2,1)S(1)}, bf16[128,256]{1,0:T(8,128)(2,1)S(1)}, u32[]{:S(2)}, u32[]{:S(2)}) collective-permute-start(bf16[128,256]{1,0:T(8,128)(2,1)S(1)} %get-tuple-element.42.refs_4_), channel_id=1, source_target_pairs={{0,1},{1,0},{2,3},{3,2},{4,5},{5,4},{6,7},{7,6},{8,9},{9,8},{10,11... | collective-permute-start | bytes 196616 | tf_op jit(solution)/shard_map/ppermute | solution.py:361
  37.0 5.3 %collective-permute-start.18 = (bf16[128,256]{1,0:T(8,128)(2,1)S(1)}, bf16[128,256]{1,0:T(8,128)(2,1)S(1)}, u32[]{:S(2)}, u32[]{:S(2)}) collective-permute-start(bf16[128,256]{1,0:T(8,128)(2,1)S(1)} %shard_map.74), channel_id=1, source_target_pairs={{0,1},{1,0},{2,3},{3,2},{4,5},{5,4},{6,7},{7,6},{8,9},{9,8},{10,11... | collective-permute-start | bytes 196616 | tf_op jit(solution)/shard_map/ppermute | solution.py:361
  41.0 1.3 %collective-permute-start.14 = (bf16[128,256]{1,0:T(8,128)(2,1)S(1)}, bf16[128,256]{1,0:T(8,128)(2,1)S(1)}, u32[]{:S(2)}, u32[]{:S(2)}) collective-permute-start(bf16[128,256]{1,0:T(8,128)(2,1)S(1)} %collective-permute-done.13.refs_6_), channel_id=1, source_target_pairs={{0,1},{1,0},{2,3},{3,2},{4,5},{5,4},{6,7},{7,6},{8,9},{9,8},{10,11... | collective-permute-start | bytes 196616 | tf_op jit(solution)/shard_map/ppermute | solution.py:361
  42.3 1.3 %collective-permute-start.16 = (bf16[128,256]{1,0:T(8,128)(2,1)S(1)}, bf16[128,256]{1,0:T(8,128)(2,1)S(1)}, u32[]{:S(2)}, u32[]{:S(2)}) collective-permute-start(bf16[128,256]{1,0:T(8,128)(2,1)S(1)} %collective-permute-done.15.refs_8_), channel_id=1, source_target_pairs={{0,1},{1,0},{2,3},{3,2},{4,5},{5,4},{6,7},{7,6},{8,9},{9,8},{10,11... | collective-permute-start | bytes 196616 | tf_op jit(solution)/shard_map/ppermute | solution.py:361
  47.3 1.3 %collective-permute-start.24 = (bf16[128,256]{1,0:T(8,128)(2,1)S(1)}, bf16[128,256]{1,0:T(8,128)(2,1)S(1)}, u32[]{:S(2)}, u32[]{:S(2)}) collective-permute-start(bf16[128,256]{1,0:T(8,128)(2,1)S(1)} %get-tuple-element.52), channel_id=1, source_target_pairs={{0,1},{1,0},{2,3},{3,2},{4,5},{5,4},{6,7},{7,6},{8,9},{9,8},{10,11... | collective-permute-start | bytes 196616 | tf_op jit(solution)/shard_map/ppermute | solution.py:361
  47.5 3.0 %collective-permute-start.22 = (bf16[128,256]{1,0:T(8,128)(2,1)S(1)}, bf16[128,256]{1,0:T(8,128)(2,1)S(1)}, u32[]{:S(2)}, u32[]{:S(2)}) collective-permute-start(bf16[128,256]{1,0:T(8,128)(2,1)S(1)} %get-tuple-element.50), channel_id=1, source_target_pairs={{0,1},{1,0},{2,3},{3,2},{4,5},{5,4},{6,7},{7,6},{8,9},{9,8},{10,11... | collective-permute-start | bytes 196616 | tf_op jit(solution)/shard_map/ppermute | solution.py:361
  47.9 2.7 %collective-permute-start.20 = (bf16[128,256]{1,0:T(8,128)(2,1)S(1)}, bf16[128,256]{1,0:T(8,128)(2,1)S(1)}, u32[]{:S(2)}, u32[]{:S(2)}) collective-permute-start(bf16[128,256]{1,0:T(8,128)(2,1)S(1)} %get-tuple-element.48), channel_id=1, source_target_pairs={{0,1},{1,0},{2,3},{3,2},{4,5},{5,4},{6,7},{7,6},{8,9},{9,8},{10,11... | collective-permute-start | bytes 196616 | tf_op jit(solution)/shard_map/ppermute | solution.py:361
  48.0 6.3 %collective-permute-start.19 = (bf16[128,256]{1,0:T(8,128)(2,1)S(1)}, bf16[128,256]{1,0:T(8,128)(2,1)S(1)}, u32[]{:S(2)}, u32[]{:S(2)}) collective-permute-start(bf16[128,256]{1,0:T(8,128)(2,1)S(1)} %get-tuple-element.46), channel_id=1, source_target_pairs={{0,1},{1,0},{2,3},{3,2},{4,5},{5,4},{6,7},{7,6},{8,9},{9,8},{10,11... | collective-permute-start | bytes 196616 | tf_op jit(solution)/shard_map/ppermute | solution.py:361
  48.4 2.9 %collective-permute-start.26 = (bf16[8,128,128]{2,1,0:T(8,128)(2,1)S(1)}, bf16[8,128,128]{2,1,0:T(8,128)(2,1)S(1)}, u32[]{:S(2)}, u32[]{:S(2)}) collective-permute-start(bf16[8,128,128]{2,1,0:T(8,128)(2,1)S(1)} %get-tuple-element.43.refs_1_.refs_3_), channel_id=1, source_target_pairs={{0,1},{1,0},{2,3},{3,2},{4,5},{5,4},{6,7},{7,6},{8,9},{9,8},{10,11... | collective-permute-start | bytes 786440 | tf_op jit(solution)/shard_map/ppermute | solution.py:361
  48.6 6.8 %collective-permute-start.25 = (bf16[128,256]{1,0:T(8,128)(2,1)S(1)}, bf16[128,256]{1,0:T(8,128)(2,1)S(1)}, u32[]{:S(2)}, u32[]{:S(2)}) collective-permute-start(bf16[128,256]{1,0:T(8,128)(2,1)S(1)} %add_convert_fusion.1), channel_id=1, source_target_pairs={{0,6},{1,7},{2,0},{3,1},{4,2},{5,3},{6,4},{7,5},{8,14},{9,15},{10,... | collective-permute-start | bytes 196616 | tf_op jit(solution)/shard_map/ppermute | solution.py:364
  50.5 7.5 %collective-permute-start.23 = (bf16[128,256]{1,0:T(8,128)(2,1)S(1)}, bf16[128,256]{1,0:T(8,128)(2,1)S(1)}, u32[]{:S(2)}, u32[]{:S(2)}) collective-permute-start(bf16[128,256]{1,0:T(8,128)(2,1)S(1)} %add_convert_fusion.2), channel_id=1, source_target_pairs={{0,4},{1,5},{2,6},{3,7},{4,0},{5,1},{6,2},{7,3},{8,12},{9,13},{10,... | collective-permute-start | bytes 196616 | tf_op jit(solution)/shard_map/ppermute | solution.py:364
  50.6 7.3 %collective-permute-start.21 = (bf16[128,256]{1,0:T(8,128)(2,1)S(1)}, bf16[128,256]{1,0:T(8,128)(2,1)S(1)}, u32[]{:S(2)}, u32[]{:S(2)}) collective-permute-start(bf16[128,256]{1,0:T(8,128)(2,1)S(1)} %add_convert_fusion.3), channel_id=1, source_target_pairs={{0,2},{1,3},{2,4},{3,5},{4,6},{5,7},{6,0},{7,1},{8,10},{9,11},{10,... | collective-permute-start | bytes 196616 | tf_op jit(solution)/shard_map/ppermute | solution.py:364
  52.8 10.3 %collective-permute-start.27 = (bf16[960,128]{1,0:T(8,128)(2,1)S(1)}, bf16[960,128]{1,0:T(8,128)(2,1)S(1)}, u32[]{:S(2)}, u32[]{:S(2)}) collective-permute-start(bf16[960,128]{1,0:T(8,128)(2,1)S(1)} %get-tuple-element.56), channel_id=1, source_target_pairs={{0,8},{8,0},{16,24},{24,16},{1,9},{9,1},{17,25},{25,17},{2,10},{10... | collective-permute-start | bytes 737288 | tf_op jit(solution)/shard_map/ppermute | solution.py:369
  54.3 16.2 %collective-permute-start.28 = (bf16[960,128]{1,0:T(8,128)(2,1)S(1)}, bf16[960,128]{1,0:T(8,128)(2,1)S(1)}, u32[]{:S(2)}, u32[]{:S(2)}) collective-permute-start(bf16[960,128]{1,0:T(8,128)(2,1)S(1)} %get-tuple-element.57), channel_id=1, source_target_pairs={{0,16},{8,24},{16,0},{24,8},{1,17},{9,25},{17,1},{25,9},{2,18},{10... | collective-permute-start | bytes 737288 | tf_op jit(solution)/shard_map/ppermute | solution.py:369
  55.4 15.1 %collective-permute-start.29 = (bf16[960,128]{1,0:T(8,128)(2,1)S(1)}, bf16[960,128]{1,0:T(8,128)(2,1)S(1)}, u32[]{:S(2)}, u32[]{:S(2)}) collective-permute-start(bf16[960,128]{1,0:T(8,128)(2,1)S(1)} %get-tuple-element.58), channel_id=1, source_target_pairs={{0,24},{8,16},{16,8},{24,0},{1,25},{9,17},{17,9},{25,1},{2,26},{10... | collective-permute-start | bytes 737288 | tf_op jit(solution)/shard_map/ppermute | solution.py:369
  58.1 1.3 %collective-permute-start.30 = (bf16[2,128,128]{2,1,0:T(8,128)(2,1)S(1)}, bf16[2,128,128]{2,1,0:T(8,128)(2,1)S(1)}, u32[]{:S(2)}, u32[]{:S(2)}) collective-permute-start(bf16[2,128,128]{2,1,0:T(8,128)(2,1)S(1)} %shard_map.76.refs_2_.refs_5_), channel_id=1, source_target_pairs={{0,1},{1,0},{2,3},{3,2},{4,5},{5,4},{6,7},{7,6},{8,9},{9,8},{10,11... | collective-permute-start | bytes 196616 | tf_op jit(solution)/shard_map/ppermute | solution.py:361
  60.4 8.0 %collective-permute-start.31 = (bf16[320,128]{1,0:T(8,128)(2,1)S(1)}, bf16[320,128]{1,0:T(8,128)(2,1)S(1)}, u32[]{:S(2)}, u32[]{:S(2)}) collective-permute-start(bf16[320,128]{1,0:T(8,128)(2,1)S(1)} %get-tuple-element.60), channel_id=1, source_target_pairs={{0,8},{8,0},{16,24},{24,16},{1,9},{9,1},{17,25},{25,17},{2,10},{10... | collective-permute-start | bytes 245768 | tf_op jit(solution)/shard_map/ppermute | solution.py:369
  62.0 8.5 %collective-permute-start.32 = (bf16[320,128]{1,0:T(8,128)(2,1)S(1)}, bf16[320,128]{1,0:T(8,128)(2,1)S(1)}, u32[]{:S(2)}, u32[]{:S(2)}) collective-permute-start(bf16[320,128]{1,0:T(8,128)(2,1)S(1)} %get-tuple-element.61), channel_id=1, source_target_pairs={{0,16},{8,24},{16,0},{24,8},{1,17},{9,25},{17,1},{25,9},{2,18},{10... | collective-permute-start | bytes 245768 | tf_op jit(solution)/shard_map/ppermute | solution.py:369
  63.1 7.4 %collective-permute-start.33 = (bf16[320,128]{1,0:T(8,128)(2,1)S(1)}, bf16[320,128]{1,0:T(8,128)(2,1)S(1)}, u32[]{:S(2)}, u32[]{:S(2)}) collective-permute-start(bf16[320,128]{1,0:T(8,128)(2,1)S(1)} %shard_map.80), channel_id=1, source_target_pairs={{0,24},{8,16},{16,8},{24,0},{1,25},{9,17},{17,9},{25,1},{2,26},{10... | collective-permute-start | bytes 245768 | tf_op jit(solution)/shard_map/ppermute | solution.py:369
  70.8 7.2 %collective-permute-start.34 = (bf16[320,128]{1,0:T(8,128)(2,1)S(1)}, bf16[320,128]{1,0:T(8,128)(2,1)S(1)}, u32[]{:S(2)}, u32[]{:S(2)}) collective-permute-start(bf16[320,128]{1,0:T(8,128)(2,1)S(1)} %get-tuple-element.65), channel_id=1, source_target_pairs={{0,2},{1,3},{2,4},{3,5},{4,6},{5,7},{6,0},{7,1},{8,10},{9,11},{10,... | collective-permute-start | bytes 245768 | tf_op jit(solution)/shard_map/ppermute | solution.py:364
  73.3 7.2 %collective-permute-start.35 = (bf16[320,128]{1,0:T(8,128)(2,1)S(1)}, bf16[320,128]{1,0:T(8,128)(2,1)S(1)}, u32[]{:S(2)}, u32[]{:S(2)}) collective-permute-start(bf16[320,128]{1,0:T(8,128)(2,1)S(1)} %get-tuple-element.66), channel_id=1, source_target_pairs={{0,4},{1,5},{2,6},{3,7},{4,0},{5,1},{6,2},{7,3},{8,12},{9,13},{10,... | collective-permute-start | bytes 245768 | tf_op jit(solution)/shard_map/ppermute | solution.py:364
  74.5 6.0 %collective-permute-start.36 = (bf16[320,128]{1,0:T(8,128)(2,1)S(1)}, bf16[320,128]{1,0:T(8,128)(2,1)S(1)}, u32[]{:S(2)}, u32[]{:S(2)}) collective-permute-start(bf16[320,128]{1,0:T(8,128)(2,1)S(1)} %get-tuple-element.67), channel_id=1, source_target_pairs={{0,6},{1,7},{2,0},{3,1},{4,2},{5,3},{6,4},{7,5},{8,14},{9,15},{10,... | collective-permute-start | bytes 245768 | tf_op jit(solution)/shard_map/ppermute | solution.py:364
  80.6 5.3 %collective-permute-start.37 = (bf16[320,128]{1,0:T(8,128)(2,1)S(1)}, bf16[320,128]{1,0:T(8,128)(2,1)S(1)}, u32[]{:S(2)}, u32[]{:S(2)}) collective-permute-start(bf16[320,128]{1,0:T(8,128)(2,1)S(1)} %add_convert_fusion.refs_0_), channel_id=1, source_target_pairs={{0,8},{8,0},{16,24},{24,16},{1,9},{9,1},{17,25},{25,17},{2,10},{10... | collective-permute-start | bytes 245768 | tf_op jit(solution)/shard_map/ppermute | solution.py:369
  81.4 5.1 %collective-permute-start.38 = (bf16[320,128]{1,0:T(8,128)(2,1)S(1)}, bf16[320,128]{1,0:T(8,128)(2,1)S(1)}, u32[]{:S(2)}, u32[]{:S(2)}) collective-permute-start(bf16[320,128]{1,0:T(8,128)(2,1)S(1)} %add_convert_fusion.refs_0_), channel_id=1, source_target_pairs={{0,16},{8,24},{16,0},{24,8},{1,17},{9,25},{17,1},{25,9},{2,18},{10... | collective-permute-start | bytes 245768 | tf_op jit(solution)/shard_map/ppermute | solution.py:369
  82.3 5.3 %collective-permute-start.39 = (bf16[320,128]{1,0:T(8,128)(2,1)S(1)}, bf16[320,128]{1,0:T(8,128)(2,1)S(1)}, u32[]{:S(2)}, u32[]{:S(2)}) collective-permute-start(bf16[320,128]{1,0:T(8,128)(2,1)S(1)} %add_convert_fusion.refs_0_), channel_id=1, source_target_pairs={{0,24},{8,16},{16,8},{24,0},{1,25},{9,17},{17,9},{25,1},{2,26},{10... | collective-permute-start | bytes 245768 | tf_op jit(solution)/shard_map/ppermute | solution.py:369

commit v6 on v5

--- a/solution.py
+++ b/solution.py
@@ -70,6 +70,10 @@
     return pl.ds(pl.multiple_of(start, step), size)
 
 
+def plane_at(k):
+    return lax.bitwise_xor(lax.axis_index("ctx") // 2, k)
+
+
 def inverse_rms(values):
     return lax.rsqrt(jnp.mean(values * values, axis=-1, keepdims=True) + EPSILON)
 
@@ -92,15 +96,42 @@
         xt_ref[b * BLK : (b + 1) * BLK, :] = x_ref[:, b * BLK : (b + 1) * BLK].T
     for source, out in ((ids, ids_out), (spans, spans_out)):
 
-        @pl.loop(0, source.shape[0])
-        def _(i):
-            for j in range(source.shape[1]):
+        @pl.loop(0, source.shape[1])
+        def _(j):
+            for i in range(source.shape[0]):
                 out[i, j] = source[i, j]
 
 
 def part_kernel(w_ref, out):
     rows = out.shape[0]
     out[...] = w_ref[rows_at(lax.axis_index("dp") * rows, rows, 16), :]
+
+
+def first_step(nz):
+    step = plane_at(nz - 1)
+    return jnp.where(step == 0, nz - 1, step)
+
+
+def first_kernel(*refs):
+    pieces, out = refs[:-1], refs[-1]
+    for k, ref in enumerate(pieces):
+
+        @pl.when(first_step(len(pieces) + 1) == k + 1)
+        def _():
+            out[...] = ref[...]
+
+
+def others_kernel(*refs):
+    pieces, out = refs[:-1], refs[-1]
+    rows = pieces[0].shape[0]
+    first = first_step(len(pieces) + 1)
+    for k, ref in enumerate(pieces):
+        for slot in (k - 1, k):
+            if 0 <= slot < len(pieces) - 1:
+
+                @pl.when(first < k + 1 if slot < k else first > k + 1)
+                def _():
+                    out[slot * rows : (slot + 1) * rows, :] = ref[...]
 
 
 def stack_kernel(*refs):
@@ -126,7 +157,7 @@
 
 def column_of(c, ids, x_ref):
     return jnp.concatenate(
-        [x_ref[:, rows_at(ids[c, r] * BLK, BLK, BLK)] for r in range(NBR)], axis=1
+        [x_ref[:, rows_at(ids[r, c] * BLK, BLK, BLK)] for r in range(NBR)], axis=1
     )
 
 
@@ -154,33 +185,31 @@
             qhat_ref[head_rows(p, c), :] = normed[p * SPAN : (p + 1) * SPAN, :]
 
 
-def join_planes(nz, shards, pieces, w_ref, last_ref):
-    shard, piece = shards[0].shape[0], pieces[0].shape[0] // (nz - 1)
-    zi = lax.axis_index("ctx") // 2
-    for k in range(nz):
-        plane = lax.rem(zi + nz - k, nz)
-
-        def place(base, out):
-            if k == 0:
-                join_shards(shards, base, out)
-            else:
-                join_pieces(pieces, k - 1, shard, piece, base, out)
-
-        if w_ref is None:
-            pl.when(plane == nz - 1)(lambda: place(0, last_ref))
-        else:
-            pl.when(plane < nz - 1)(lambda: place(plane * 2 * shard, w_ref))
-
-
 def keys_kernel(nz, ids, x_ref, *refs):
     shards, pieces, (w_ref, kv_ref, key_ref) = refs[:2], refs[2:-3], refs[-3:]
-    join_planes(nz, shards, pieces, None, w_ref)
+    shard, piece = shards[0].shape[0], pieces[0].shape[0]
+    last = lax.axis_index("ctx") // 2 == nz - 1
+    pl.when(last)(lambda: join_shards(shards, 0, w_ref))
+    pl.when(jnp.logical_not(last))(lambda: join_pieces(pieces, 0, shard, piece, 0, w_ref))
     project_keys(ids, x_ref, w_ref, NNZ * BLK - w_ref.shape[0], kv_ref, key_ref)
 
 
 def queries_kernel(nz, ids, x_ref, last_ref, *refs):
-    shards, pieces, (w_ref, q_ref, qhat_ref) = refs[:2], refs[2:-3], refs[-3:]
-    join_planes(nz, shards, pieces, w_ref, None)
+    shards, firsts, others, (w_ref, q_ref, qhat_ref) = refs[:2], refs[2:-5], refs[-5:-3], refs[-3:]
+    shard, piece = shards[0].shape[0], firsts[0].shape[0]
+    zi, core = lax.axis_index("ctx") // 2, lax.axis_index("ctx") % 2
+    last = zi == nz - 1
+    pl.when(last)(lambda: join_pieces(firsts, 0, shard, piece, 0, w_ref))
+    pl.when(jnp.logical_not(last))(lambda: join_shards(shards, zi * 2 * shard, w_ref))
+    for slot in range(nz - 2):
+        step = slot + 1 + (slot + 1 >= first_step(nz)).astype(jnp.int32)
+        base = plane_at(step) * 2 * shard
+        for k in range(len(firsts) // 2):
+            for n, ref in enumerate(others):
+                at = base + (core if n == 0 else 1 - core) * shard
+                at += lax.bitwise_xor(lax.axis_index("dp"), k) * piece
+                row = (k * (nz - 2) + slot) * piece
+                w_ref[rows_at(at, piece, 16), :] = ref[row : row + piece, :]
     w_ref[NNZ * BLK - last_ref.shape[0] :, :] = last_ref[...]
     project_queries(ids, x_ref, w_ref, q_ref, qhat_ref)
 
@@ -200,11 +229,11 @@
     me = lax.axis_index("ctx")
     zi, core = me // 2, me % 2
     for k in range(nz):
-        z_from = lax.rem(zi + nz - k, nz)
+        z_from = plane_at(k)
         for other in range(2):
             source = z_from * 2 + (core if other == 0 else 1 - core)
             for p in range(2):
-                kv[rows_at(spans[source, p] * SPAN, SPAN, SPAN), :] = pieces[2 * k + other][
+                kv[rows_at(spans[p, source] * SPAN, SPAN, SPAN), :] = pieces[2 * k + other][
                     p * SPAN : (p + 1) * SPAN, :
                 ]
     length = kv.shape[0]
@@ -215,7 +244,7 @@
         sure = length // 2 if p == 1 else 0
         q_part = qhat[p * half : (p + 1) * half, :]
         up_part = up[p * half : (p + 1) * half, :]
-        limit = query_at + spans[me, p] * SPAN
+        limit = query_at + spans[p, me] * SPAN
         total = jnp.zeros((8, half), F32)
         weighted = jnp.zeros((8, half), F32)
         for at in range(0, reach, keys):
@@ -252,11 +281,11 @@
         for h in range(NQ):
             dq_ref[h, p * SPAN : (p + 1) * SPAN, :] = dq[h * SPAN : (h + 1) * SPAN, :]
     for k in range(nz):
-        z_to = lax.rem(zi + k, nz)
+        z_to = plane_at(k)
         for p in range(2):
             part = slice(p * SPAN, (p + 1) * SPAN)
             for out, owner in ((keep[k], z_to * 2 + core), (send[k], z_to * 2 + 1 - core)):
-                rows = rows_at(spans[owner, p] * SPAN, SPAN, SPAN)
+                rows = rows_at(spans[p, owner] * SPAN, SPAN, SPAN)
                 out[part, :] = acc[rows, :].astype(BF16)
 
 
@@ -289,7 +318,7 @@
         for i in range(count):
             b = (2 * (z_first + z) + core) * count + i
             c = b // NBR
-            rows = rows_at(ids[c, b % NBR] * BLK, BLK, BLK)
+            rows = rows_at(ids[b % NBR, c] * BLK, BLK, BLK)
             picked = jnp.concatenate([xt[rows, :], xt_other[rows, :]], axis=1)
             at = (z * count + i) * BLK
             work[at : at + BLK, :] = dot(picked, grads[c - first]).astype(BF16)
@@ -302,7 +331,7 @@
 def all_terms_kernel(ids, xt, dq_ref, dkv_ref, out_ref):
     for c in range(NCB):
         picked = jnp.concatenate(
-            [xt[rows_at(ids[c, r] * BLK, BLK, BLK), :] for r in range(NBR)], axis=0
+            [xt[rows_at(ids[r, c] * BLK, BLK, BLK), :] for r in range(NBR)], axis=0
         )
         grad = dq_ref[c] if c < NQ else dkv_ref[c - NQ]
         out_ref[c * NBR * BLK : (c + 1) * NBR * BLK, :] = dot(picked, grad).astype(BF16)
@@ -317,7 +346,7 @@
             total = total + term[...].astype(F32)
         work[first * piece : (first + count) * piece, :] = total.astype(BF16)
     for k in range(nz):
-        at = lax.rem(lax.axis_index("ctx") // 2 + k, nz) * piece
+        at = plane_at(k) * piece
         outs[k][...] = work[rows_at(at, piece, 16), :]
 
 
@@ -335,7 +364,7 @@
         grad = dq_ref[c] if c < NQ else dkv_ref[c - NQ]
         spread = dot(grad, w_ref[c * wide : (c + 1) * wide, :], ((1,), (1,)))
         for r in range(NBR):
-            columns = rows_at(ids[c, r] * BLK, BLK, BLK)
+            columns = rows_at(ids[r, c] * BLK, BLK, BLK)
             term = spread[:, r * BLK : (r + 1) * BLK]
             if c < cover:
                 work[:, columns] = term
@@ -344,12 +373,13 @@
     out_ref[...] = work[...].astype(BF16)
 
 
-def per_device(ndp, tokens, grad_attn, w_packed, ids, spans):
+def per_device(ndp, tokens, grad_attn, w_packed, block_rows, span_pairs):
+    ids, spans = block_rows.T, span_pairs.T
     nctx = lax.axis_size("ctx")
     nz = nctx // 2
     x = tokens[0]
     tok, width = x.shape
-    length = spans.shape[0] * 2 * SPAN
+    length = spans.shape[1] * 2 * SPAN
     shard = w_packed.shape[0]
     piece = shard // ndp
     cut = (nz - 1) * 2 * shard
@@ -360,10 +390,11 @@
     def swap_core(v):
         return lax.ppermute(v, "ctx", [(i, i ^ 1) for i in range(nctx)])
 
-    def shift_z(v, k):
-        return lax.ppermute(
-            v, "ctx", [(i, ((i // 2 + k) % nz) * 2 + i % 2) for i in range(nctx)]
-        )
+    def both_cores(parts):
+        return [v for part in parts for v in (part, swap_core(part))]
+
+    def swap_z(v, k):
+        return lax.ppermute(v, "ctx", [(i, i ^ (2 * k)) for i in range(nctx)])
 
     def swap_dp(v, k):
         return lax.ppermute(v, "dp", [(i, i ^ k) for i in range(ndp)])
@@ -386,40 +417,54 @@
 
     if fast:
         (mine,) = call(part_kernel, (), (w_packed,), [((piece, BLK), BF16)], moved=4 * piece * BLK)
-        from_z = [shift_z(mine, k) for k in range(1, nz)]
-
-        def both_cores(parts):
-            return [v for part in parts for v in (part, swap_core(part))]
+        from_z = [swap_z(mine, k) for k in range(1, nz)]
+
+        def pick(kernel, count, wait):
+            return call(
+                kernel,
+                (),
+                from_z,
+                [((count * piece, BLK), BF16)],
+                wait=wait,
+                moved=4 * nz * piece * BLK,
+            )[0]
+
+        def to_all_dp(held):
+            return [held] + [swap_dp(held, k) for k in range(1, ndp)]
 
         shards = both_cores([w_packed])
+        first = pick(first_kernel, 1, (ids, shards[1]))
+        firsts = to_all_dp(first)
+        others = to_all_dp(pick(others_kernel, nz - 2, (first,)))
+        firsts = both_cores(firsts)
+        w_last, kv, key = call(
+            functools.partial(keys_kernel, nz),
+            (ids,),
+            (x, *shards, *firsts),
+            [((2 * shard, BLK), BF16), ((tok, 2 * HD), BF16), ((tok, HD), BF16)],
+            flops=2 * tok * (NCB - NQ) * NBR * BLK * BLK,
+            moved=3 * 2**20,
+        )
+        kv_from_z = [swap_z(kv, k) for k in range(1, nz)]
+        kv_pieces = both_cores([kv] + kv_from_z)
         (stacked,) = call(
             stack_kernel,
             (),
-            from_z,
-            [(((nz - 1) * piece, BLK), BF16)],
-            wait=(ids, shards[1]),
-            moved=4 * nz * piece * BLK,
-        )
-        xt_other = swap_core(after(xt, stacked))
-        pieces = [stacked] + [swap_dp(stacked, k) for k in range(1, ndp)]
-        pieces = both_cores(pieces)
-        w_last, kv, key = call(
-            functools.partial(keys_kernel, nz),
-            (ids,),
-            (x, *shards, *pieces),
-            [((2 * shard, BLK), BF16), ((tok, 2 * HD), BF16), ((tok, HD), BF16)],
-            wait=(xt_other,),
-            flops=2 * tok * (NCB - NQ) * NBR * BLK * BLK,
-            moved=4 * 2**20,
+            others,
+            [((ndp * (nz - 2) * piece, BLK), BF16)],
+            wait=kv_from_z,
+            moved=4 * nz * shard * BLK,
         )
         weights, query, qhat = call(
             functools.partial(queries_kernel, nz),
             (ids,),
-            (x, w_last, *shards, *pieces),
+            (x, w_last, *shards, *firsts, stacked, swap_core(stacked)),
             [((NNZ * BLK, BLK), BF16)] + [((tok * NQ, HD), BF16)] * 2,
+            wait=kv_pieces,
             flops=2 * tok * NQ * NBR * BLK * BLK,
             moved=8 * 2**20,
         )
+        xt_other = swap_core(after(xt, qhat))
     else:
         weights = lax.all_gather(w_packed, "ctx", axis=0, tiled=True)
         query, qhat, kv, key = call(
@@ -431,10 +476,8 @@
             moved=4 * 2**20,
         )
 
-    kv_pieces = []
-    for k in range(nz):
-        part = kv if k == 0 else shift_z(kv, k)
-        kv_pieces += [part, swap_core(after(part, query) if k == nz - 1 else part)]
+        kv_pieces = both_cores([kv] + [swap_z(kv, k) for k in range(1, nz)])
+
     outs = call(
         functools.partial(attend_kernel, nz, math.gcd(512, length // 2)),
         (spans,),
@@ -453,7 +496,7 @@
     )
     dq, keep, send = outs[0], outs[1 : nz + 1], outs[nz + 1 :]
     sums = [add(keep[k], swap_core(send[k])) for k in range(nz)]
-    kv_terms = [sums[0]] + [shift_z(sums[k], k) for k in range(1, nz)]
+    kv_terms = [sums[0]] + [swap_z(sums[k], k) for k in range(1, nz)]
 
     def weight_terms(z_lo, z_count, grads):
         first = z_lo * 2 * shard // (NBR * BLK)
@@ -507,7 +550,7 @@
         )
         owned = by_z[0].astype(F32)
         for k in range(1, nz):
-            owned = owned + shift_z(by_z[k], k).astype(F32)
+            owned = owned + swap_z(by_z[k], k).astype(F32)
         owned = owned.astype(BF16)
         (grad_weights,) = call(
             functools.partial(place_kernel, piece),

time: 88.8 us -> 86.9 us (0.979)
  waiting for transfers between devices: 32.9 us -> 23.6 us
  starting transfers between devices: 34.4 us -> 42.7 us
    ppermute x12 -> x15, waiting for transfers between devices: 18.1 us -> 9.78 us  [swap_dp(): return lax.ppermute(v, 'dp', [(i, i ^ k) for i in range(ndp)])]
    ppermute x12 -> x15, starting transfers between devices: 14.2 us -> 20.1 us  [swap_dp(): return lax.ppermute(v, 'dp', [(i, i ^ k) for i in range(ndp)])]
    ppermute x12, starting transfers between devices: 17.2 us -> 18.7 us  [swap_z(): return lax.ppermute(v, 'ctx', [(i, i ^ 2 * k) for i in range(nctx)])]
    ppermute x12, waiting for transfers between devices: 10.9 us -> 9.91 us  [swap_z(): return lax.ppermute(v, 'ctx', [(i, i ^ 2 * k) for i in range(nctx)])]
    ppermute x16 -> x17, starting transfers between devices: 2.99 us -> 3.91 us  [swap_core(): return lax.ppermute(v, 'ctx', [(i, i ^ 1) for i in range(nctx)])]
    pallas_call x12 -> x14, Pallas kernels: 15.5 us -> 14.8 us  [call(): pl.pallas_call(body, in_specs=[SMEM] * len(scalars) + [VMEM] * len(arrays...]
    unnamed x14 -> x15, local copies, waits for them, and re-layouts: 4.75 us -> 4.59 us
    ppermute x16 -> x17, waiting for transfers between devices: 3.91 us -> 3.86 us  [swap_core(): return lax.ppermute(v, 'ctx', [(i, i ^ 1) for i in range(nctx)])]
  transfers between devices with their start and end apart: 40 -> 44, of which waited for: 17 -> 23; matrix products, arithmetic and copies ran while one was open for 2% -> 0% of each run, Pallas kernels for 11% -> 14%
where the time goes in v6:
time: 86.9 us; the launch traced here: 86.7 us
  starting transfers between devices  42.7 us (49%)
  waiting for transfers between devices  23.6 us (27%)
  Pallas kernels  14.8 us (17%)
  local copies, waits for them, and re-layouts  4.59 us (5%)
    ppermute x15, starting transfers between devices, swap_dp(): return lax.ppermute(v, 'dp', [(i, i ^ k) for i in range(ndp)])  20.1 us
    ppermute x12, starting transfers between devices, swap_z(): return lax.ppermute(v, 'ctx', [(i, i ^ 2 * k) for i in range(nctx)])  18.7 us
    pallas_call x14, Pallas kernels, call(): pl.pallas_call(body, in_specs=[SMEM] * len(scalars) + [VMEM] * len(arrays...  14.8 us
    ppermute x12, waiting for transfers between devices, swap_z(): return lax.ppermute(v, 'ctx', [(i, i ^ 2 * k) for i in range(nctx)])  9.91 us
    ppermute x15, waiting for transfers between devices, swap_dp(): return lax.ppermute(v, 'dp', [(i, i ^ k) for i in range(ndp)])  9.78 us
    unnamed x15, local copies, waits for them, and re-layouts  4.59 us
    ppermute x17, starting transfers between devices, swap_core(): return lax.ppermute(v, 'ctx', [(i, i ^ 1) for i in range(nctx)])  3.91 us
    ppermute x17, waiting for transfers between devices, swap_core(): return lax.ppermute(v, 'ctx', [(i, i ^ 1) for i in range(nctx)])  3.86 us
  transfers between devices with their start and end apart: 44, of which 23 were waited for; matrix products, arithmetic and copies ran while one was open for 0% of the time, Pallas kernels for 14%

profile of v6, /device:TPU:0, one launch (start us, length us, event | category | flops | bytes accessed | tf_op | source)
XLA Modules:
  0.0 86.7 jit_solution(10905606797355789722)
XLA Ops:
  0.6 0.5 collective-permute-start
  1.1 1.0 %copy-done.2 = bf16[1280,128]{1,0:T(8,128)(2,1)S(1)} copy-done((bf16[1280,128]{1,0:T(8,128)(2,1)S(1)}, bf16[1280,128]{1,0:T(8,128)(2,1)}, u32[]{:S(2)}) %copy-start.2) | copy-done | bytes 327704
  2.1 4.7 %collective-permute-start.3 = (bf16[320,128]{1,0:T(8,128)(2,1)S(1)}, bf16[320,128]{1,0:T(8,128)(2,1)S(1)}, u32[]{:S(2)}, u32[]{:S(2)}) collective-permute-start(bf16[320,128]{1,0:T(8,128)(2,1)S(1)} %shard_map.69), channel_id=1, source_target_pairs={{0,6},{1,7},{2,4},{3,5},{4,2},{5,3},{6,0},{7,1},{8,14},{9,15},{10,... | collective-permute-start | bytes 245768 | tf_op jit(solution)/shard_map/ppermute | solution.py:397
  6.8 0.6 collective-permute-start.1
  7.5 1.2 %copy-done = bf16[1,128,4096]{2,1,0:T(8,128)(2,1)S(1)} copy-done((bf16[1,128,4096]{2,1,0:T(8,128)(2,1)S(1)}, bf16[1,128,4096]{2,1,0:T(8,128)(2,1)}, u32[]{:S(2)}) %copy-start) | copy-done | bytes 1048600
  8.7 0.9 %copy-done.4 = bf16[1,128,1024]{2,1,0:T(8,128)(2,1)S(1)} copy-done((bf16[1,128,1024]{2,1,0:T(8,128)(2,1)S(1)}, bf16[1,128,1024]{2,1,0:T(8,128)(2,1)}, u32[]{:S(2)}) %copy-start.4) | copy-done | bytes 262168
  9.6 0.7 copy-done.5
  10.3 0.7 copy-done.6
  11.0 1.8 %shard_map.68 = (bf16[4096,128]{1,0:T(8,128)(2,1)S(1)}, bf16[1024,128]{1,0:T(8,128)(2,1)S(1)}, s32[8,10]{1,0:T(8,128)S(1)}, s32[2,8]{1,0:T(2,128)S(1)}) custom-call(s32[8,10]{1,0:T(8,128)S(1)} %bitcast.9, s32[2,8]{1,0:T(2,128)S(1)} %bitcast.10, bf16[128,4096]{1,0:T(8,128)(2,1)S(1)} %bitcast.5, bf16[128,1024]{1,0:T(8,128)(2,1)S(1)} %bitcast.8), custom_call_target="tpu_custom_call" | custom-call | bytes 2097152 | tf_op jit(solution)/shard_map/pallas_call | solution.py:43
  12.8 1.5 %collective-permute-done.2.refs_1_ = bf16[320,128]{1,0:T(8,128)(2,1)S(1)} collective-permute-done((bf16[320,128]{1,0:T(8,128)(2,1)S(1)}, bf16[320,128]{1,0:T(8,128)(2,1)S(1)}, u32[]{:S(2)}, u32[]{:S(2)}) %collective-permute-start.2) | collective-permute-done | bytes 81952 | tf_op jit(solution)/shard_map/ppermute | solution.py:397
  14.3 2.5 %collective-permute-start.9 = (bf16[320,128]{1,0:T(8,128)(2,1)S(1)}, bf16[320,128]{1,0:T(8,128)(2,1)S(1)}, u32[]{:S(2)}, u32[]{:S(2)}) collective-permute-start(bf16[320,128]{1,0:T(8,128)(2,1)S(1)} %shard_map.70.refs_4_.refs_3_.refs_5_), channel_id=1, source_target_pairs={{0,24},{8,16},{16,8},{24,0},{1,25},{9,17},{17,9},{25,1},{2,26},{10... | collective-permute-start | bytes 245768 | tf_op jit(solution)/shard_map/ppermute | solution.py:400
  16.9 0.5 collective-permute-start.7
  17.4 0.5 collective-permute-start.5
  17.9 1.9 %collective-permute-done.9.refs_10_.refs_11_ = bf16[320,128]{1,0:T(8,128)(2,1)S(1)} collective-permute-done((bf16[320,128]{1,0:T(8,128)(2,1)S(1)}, bf16[320,128]{1,0:T(8,128)(2,1)S(1)}, u32[]{:S(2)}, u32[]{:S(2)}) %collective-permute-start.9) | collective-permute-done | bytes 81952 | tf_op jit(solution)/shard_map/ppermute | solution.py:400
  19.9 3.0 %collective-permute-start.13 = (bf16[640,128]{1,0:T(8,128)(2,1)S(1)}, bf16[640,128]{1,0:T(8,128)(2,1)S(1)}, u32[]{:S(2)}, u32[]{:S(2)}) collective-permute-start(bf16[640,128]{1,0:T(8,128)(2,1)S(1)} %shard_map.72.refs_0_), channel_id=1, source_target_pairs={{0,24},{8,16},{16,8},{24,0},{1,25},{9,17},{17,9},{25,1},{2,26},{10... | collective-permute-start | bytes 491528 | tf_op jit(solution)/shard_map/ppermute | solution.py:400
  22.8 0.6 collective-permute-start.12
  23.4 0.2 collective-permute-start.11
  23.6 0.5 collective-permute-start.6
  24.1 0.8 collective-permute-done.8.refs_9_.refs_10_
  24.9 0.2 collective-permute-done.6.refs_7_.refs_8_
  25.1 1.0 %shard_map.71 = (bf16[2560,128]{1,0:T(8,128)(2,1)S(1)}, bf16[128,256]{1,0:T(8,128)(2,1)S(1)}, bf16[128,128]{1,0:T(8,128)(2,1)S(1)}) custom-call(s32[8,10]{1,0:T(8,128)S(1)} %get-tuple-element.35.refs_3_.refs_0_, bf16[128,4096]{1,0:T(8,128)(2,1)S(1)} %bitcast.6, bf16[1280,128]{1,0:T(8,128)(2,1)S(1)} %copy-done.3, ...), custom_call_target="tpu_custom_call" | custom-call | flops 67108864 | bytes 3145728 | tf_op jit(solution)/shard_map/pallas_call | solution.py:43
  26.1 2.5 %collective-permute-start.16 = (bf16[128,256]{1,0:T(8,128)(2,1)S(1)}, bf16[128,256]{1,0:T(8,128)(2,1)S(1)}, u32[]{:S(2)}, u32[]{:S(2)}) collective-permute-start(bf16[128,256]{1,0:T(8,128)(2,1)S(1)} %get-tuple-element.38.refs_15_.refs_4_), channel_id=1, source_target_pairs={{0,6},{1,7},{2,4},{3,5},{4,2},{5,3},{6,0},{7,1},{8,14},{9,15},{10,... | collective-permute-start | bytes 196616 | tf_op jit(solution)/shard_map/ppermute | solution.py:397
  28.6 1.9 %collective-permute-start.14 = (bf16[128,256]{1,0:T(8,128)(2,1)S(1)}, bf16[128,256]{1,0:T(8,128)(2,1)S(1)}, u32[]{:S(2)}, u32[]{:S(2)}) collective-permute-start(bf16[128,256]{1,0:T(8,128)(2,1)S(1)} %get-tuple-element.38.refs_15_.refs_4_), channel_id=1, source_target_pairs={{0,2},{1,3},{2,0},{3,1},{4,6},{5,7},{6,4},{7,5},{8,10},{9,11},{10,... | collective-permute-start | bytes 196616 | tf_op jit(solution)/shard_map/ppermute | solution.py:397
  30.5 0.7 collective-permute-done.12.refs_2_
  31.2 0.4 collective-permute-done.11.refs_1_
  31.7 1.2 %collective-permute-done.16.refs_6_.refs_21_.refs_10_ = bf16[128,256]{1,0:T(8,128)(2,1)S(1)} collective-permute-done((bf16[128,256]{1,0:T(8,128)(2,1)S(1)}, bf16[128,256]{1,0:T(8,128)(2,1)S(1)}, u32[]{:S(2)}, u32[]{:S(2)}) %collective-permute-start.16) | collective-permute-done | bytes 65568 | tf_op jit(solution)/shard_map/ppermute | solution.py:397
  32.9 2.2 %collective-permute-done.15.refs_5_.refs_19_.refs_8_ = bf16[128,256]{1,0:T(8,128)(2,1)S(1)} collective-permute-done((bf16[128,256]{1,0:T(8,128)(2,1)S(1)}, bf16[128,256]{1,0:T(8,128)(2,1)S(1)}, u32[]{:S(2)}, u32[]{:S(2)}) %collective-permute-start.15) | collective-permute-done | bytes 65568 | tf_op jit(solution)/shard_map/ppermute | solution.py:397
  35.2 0.5 collective-permute-start.18
  35.8 0.4 collective-permute-start.20
  36.4 1.0 %collective-permute-done.18.refs_16_.refs_5_ = bf16[128,256]{1,0:T(8,128)(2,1)S(1)} collective-permute-done((bf16[128,256]{1,0:T(8,128)(2,1)S(1)}, bf16[128,256]{1,0:T(8,128)(2,1)S(1)}, u32[]{:S(2)}, u32[]{:S(2)}) %collective-permute-start.18) | collective-permute-done | bytes 65568 | tf_op jit(solution)/shard_map/ppermute | solution.py:391
  37.7 1.7 %shard_map.74 = (bf16[10240,128]{1,0:T(8,128)(2,1)S(1)}, bf16[1024,128]{1,0:T(8,128)(2,1)S(1)}, bf16[1024,128]{1,0:T(8,128)(2,1)S(1)}) custom-call(s32[8,10]{1,0:T(8,128)S(1)} %get-tuple-element.35.refs_3_.refs_0_, bf16[128,4096]{1,0:T(8,128)(2,1)S(1)} %bitcast.7, bf16[2560,128]{1,0:T(8,128)(2,1)S(1)} %get-tuple-element.37.refs_2_, ...), custom_call_target="tpu_custom_call" | custom-call | flops 268435456 | bytes 8388608 | tf_op jit(solution)/shard_map/pallas_call | solution.py:43
  39.4 0.2 collective-permute-start.29
  39.6 3.7 %shard_map.75 = (bf16[8,128,128]{2,1,0:T(8,128)(2,1)S(1)}, bf16[128,256]{1,0:T(8,128)(2,1)S(1)}, bf16[128,256]{1,0:T(8,128)(2,1)S(1)}, bf16[128,256]{1,0:T(8,128...) custom-call(s32[2,8]{1,0:T(2,128)S(1)} %get-tuple-element.36.refs_0_, ...), custom_call_target="tpu_custom_call" | custom-call | flops 671088640 | bytes 4194304 | tf_op jit(solution)/shard_map/pallas_call | solution.py:43
  43.3 0.4 collective-permute-start.23
  43.8 0.4 collective-permute-start.25
  44.3 0.2 collective-permute-done.23
  44.6 0.4 collective-permute-start.30
  45.1 0.7 collective-permute-start.24
  45.9 2.4 %collective-permute-start.26 = (bf16[128,256]{1,0:T(8,128)(2,1)S(1)}, bf16[128,256]{1,0:T(8,128)(2,1)S(1)}, u32[]{:S(2)}, u32[]{:S(2)}) collective-permute-start(bf16[128,256]{1,0:T(8,128)(2,1)S(1)} %add_convert_fusion.2), channel_id=1, source_target_pairs={{0,4},{1,5},{2,6},{3,7},{4,0},{5,1},{6,2},{7,3},{8,12},{9,13},{10,... | collective-permute-start | bytes 196616 | tf_op jit(solution)/shard_map/ppermute | solution.py:397
  48.3 1.4 %collective-permute-start.28 = (bf16[128,256]{1,0:T(8,128)(2,1)S(1)}, bf16[128,256]{1,0:T(8,128)(2,1)S(1)}, u32[]{:S(2)}, u32[]{:S(2)}) collective-permute-start(bf16[128,256]{1,0:T(8,128)(2,1)S(1)} %add_convert_fusion.1), channel_id=1, source_target_pairs={{0,6},{1,7},{2,4},{3,5},{4,2},{5,3},{6,0},{7,1},{8,14},{9,15},{10,... | collective-permute-start | bytes 196616 | tf_op jit(solution)/shard_map/ppermute | solution.py:397
  49.7 1.4 %shard_map.79 = (bf16[960,128]{1,0:T(8,128)(2,1)S(1)}, bf16[960,128]{1,0:T(8,128)(2,1)S(1)}, bf16[960,128]{1,0:T(8,128)(2,1)S(1)}, bf16[960,128]{1,0:T(8,128)(2,1)S(1)}) custom-call(s32[8,10]{1,0:T(8,128)S(1)} %get-tuple-element.35.refs_3_.refs_0_, bf16[4096,128]{1,0:T(8,128)(2,1)S(1)} %get-tuple-element.54.refs_1_, ...), custom_call_target="tpu_custom_call" | custom-call | flops 251658240 | bytes 4194304 | tf_op jit(solution)/shard_map/pallas_call | solution.py:43
  51.1 1.9 %collective-permute-start.31 = (bf16[960,128]{1,0:T(8,128)(2,1)S(1)}, bf16[960,128]{1,0:T(8,128)(2,1)S(1)}, u32[]{:S(2)}, u32[]{:S(2)}) collective-permute-start(bf16[960,128]{1,0:T(8,128)(2,1)S(1)} %get-tuple-element.56), channel_id=1, source_target_pairs={{0,8},{8,0},{16,24},{24,16},{1,9},{9,1},{17,25},{25,17},{2,10},{10... | collective-permute-start | bytes 737288 | tf_op jit(solution)/shard_map/ppermute | solution.py:400
  53.0 1.5 %collective-permute-start.32 = (bf16[960,128]{1,0:T(8,128)(2,1)S(1)}, bf16[960,128]{1,0:T(8,128)(2,1)S(1)}, u32[]{:S(2)}, u32[]{:S(2)}) collective-permute-start(bf16[960,128]{1,0:T(8,128)(2,1)S(1)} %get-tuple-element.57), channel_id=1, source_target_pairs={{0,16},{8,24},{16,0},{24,8},{1,17},{9,25},{17,1},{25,9},{2,18},{10... | collective-permute-start | bytes 737288 | tf_op jit(solution)/shard_map/ppermute | solution.py:400
  54.9 1.2 %collective-permute-done.34.refs_6_ = bf16[2,128,128]{2,1,0:T(8,128)(2,1)S(1)} collective-permute-done((bf16[2,128,128]{2,1,0:T(8,128)(2,1)S(1)}, bf16[2,128,128]{2,1,0:T(8,128)(2,1)S(1)}, u32[]{:S(2)}, u32[]{:S(2)}) %collective-permute-start.34) | collective-permute-done | bytes 65568 | tf_op jit(solution)/shard_map/ppermute | solution.py:391
  56.1 1.0 %shard_map.80 = (bf16[320,128]{1,0:T(8,128)(2,1)S(1)}, bf16[320,128]{1,0:T(8,128)(2,1)S(1)}, bf16[320,128]{1,0:T(8,128)(2,1)S(1)}, bf16[320,128]{1,0:T(8,128)(2,1)S(1)}) custom-call(s32[8,10]{1,0:T(8,128)S(1)} %get-tuple-element.35.refs_3_.refs_0_, bf16[4096,128]{1,0:T(8,128)(2,1)S(1)} %get-tuple-element.54.refs_1_, ...), custom_call_target="tpu_custom_call" | custom-call | flops 83886080 | bytes 4194304 | tf_op jit(solution)/shard_map/pallas_call | solution.py:43
  57.1 1.9 %collective-permute-start.35 = (bf16[320,128]{1,0:T(8,128)(2,1)S(1)}, bf16[320,128]{1,0:T(8,128)(2,1)S(1)}, u32[]{:S(2)}, u32[]{:S(2)}) collective-permute-start(bf16[320,128]{1,0:T(8,128)(2,1)S(1)} %get-tuple-element.60), channel_id=1, source_target_pairs={{0,8},{8,0},{16,24},{24,16},{1,9},{9,1},{17,25},{25,17},{2,10},{10... | collective-permute-start | bytes 245768 | tf_op jit(solution)/shard_map/ppermute | solution.py:400
  59.0 1.5 %collective-permute-start.36 = (bf16[320,128]{1,0:T(8,128)(2,1)S(1)}, bf16[320,128]{1,0:T(8,128)(2,1)S(1)}, u32[]{:S(2)}, u32[]{:S(2)}) collective-permute-start(bf16[320,128]{1,0:T(8,128)(2,1)S(1)} %get-tuple-element.61), channel_id=1, source_target_pairs={{0,16},{8,24},{16,0},{24,8},{1,17},{9,25},{17,1},{25,9},{2,18},{10... | collective-permute-start | bytes 245768 | tf_op jit(solution)/shard_map/ppermute | solution.py:400
  60.5 2.3 %collective-permute-start.37 = (bf16[320,128]{1,0:T(8,128)(2,1)S(1)}, bf16[320,128]{1,0:T(8,128)(2,1)S(1)}, u32[]{:S(2)}, u32[]{:S(2)}) collective-permute-start(bf16[320,128]{1,0:T(8,128)(2,1)S(1)} %shard_map.81), channel_id=1, source_target_pairs={{0,24},{8,16},{16,8},{24,0},{1,25},{9,17},{17,9},{25,1},{2,26},{10... | collective-permute-start | bytes 245768 | tf_op jit(solution)/shard_map/ppermute | solution.py:400
  62.8 2.9 %shard_map.77 = (bf16[128,4096]{1,0:T(8,128)(2,1)}, f32[8,128]{1,0:T(8,128)S(1)}) custom-call(s32[8,10]{1,0:T(8,128)S(1)} %get-tuple-element.35.refs_3_.refs_0_, bf16[8,128,128]{2,1,0:T(8,128)(2,1)S(1)} %get-tuple-element.42.refs_1_.refs_3_, bf16[2,128,128]{2,1,0:T(8,128)(2,1)S(1)} %shard_map.76.refs_2_.refs_5_, bf16[10240,128]{1,0:T(8,128)(2,1)S(1)} %get-tuple-element.52.refs_3_), custom_call_target="tpu_custom_call" | custom-call | flops 335544320 | bytes 4194304 | tf_op jit(solution)/shard_map/pallas_call | solution.py:43
  65.7 0.8 collective-permute-done.35.refs_5_
  66.6 2.3 %collective-permute-done.36.refs_6_ = bf16[320,128]{1,0:T(8,128)(2,1)S(1)} collective-permute-done((bf16[320,128]{1,0:T(8,128)(2,1)S(1)}, bf16[320,128]{1,0:T(8,128)(2,1)S(1)}, u32[]{:S(2)}, u32[]{:S(2)}) %collective-permute-start.36) | collective-permute-done | bytes 81952 | tf_op jit(solution)/shard_map/ppermute | solution.py:400
  68.9 0.3 shard_map.82
  69.3 3.0 %collective-permute-start.39 = (bf16[320,128]{1,0:T(8,128)(2,1)S(1)}, bf16[320,128]{1,0:T(8,128)(2,1)S(1)}, u32[]{:S(2)}, u32[]{:S(2)}) collective-permute-start(bf16[320,128]{1,0:T(8,128)(2,1)S(1)} %get-tuple-element.66), channel_id=1, source_target_pairs={{0,4},{1,5},{2,6},{3,7},{4,0},{5,1},{6,2},{7,3},{8,12},{9,13},{10,... | collective-permute-start | bytes 245768 | tf_op jit(solution)/shard_map/ppermute | solution.py:397
  72.3 1.4 %collective-permute-start.40 = (bf16[320,128]{1,0:T(8,128)(2,1)S(1)}, bf16[320,128]{1,0:T(8,128)(2,1)S(1)}, u32[]{:S(2)}, u32[]{:S(2)}) collective-permute-start(bf16[320,128]{1,0:T(8,128)(2,1)S(1)} %get-tuple-element.67), channel_id=1, source_target_pairs={{0,6},{1,7},{2,4},{3,5},{4,2},{5,3},{6,0},{7,1},{8,14},{9,15},{10,... | collective-permute-start | bytes 245768 | tf_op jit(solution)/shard_map/ppermute | solution.py:397
  73.6 0.5 collective-permute-done.38
  74.2 3.5 %collective-permute-done.39 = bf16[320,128]{1,0:T(8,128)(2,1)S(1)} collective-permute-done((bf16[320,128]{1,0:T(8,128)(2,1)S(1)}, bf16[320,128]{1,0:T(8,128)(2,1)S(1)}, u32[]{:S(2)}, u32[]{:S(2)}) %collective-permute-start.39) | collective-permute-done | bytes 81952 | tf_op jit(solution)/shard_map/ppermute | solution.py:397
  77.6 1.0 %collective-permute-done.40 = bf16[320,128]{1,0:T(8,128)(2,1)S(1)} collective-permute-done((bf16[320,128]{1,0:T(8,128)(2,1)S(1)}, bf16[320,128]{1,0:T(8,128)(2,1)S(1)}, u32[]{:S(2)}, u32[]{:S(2)}) %collective-permute-start.40) | collective-permute-done | bytes 81952 | tf_op jit(solution)/shard_map/ppermute | solution.py:397
  78.7 2.0 %collective-permute-start.43 = (bf16[320,128]{1,0:T(8,128)(2,1)S(1)}, bf16[320,128]{1,0:T(8,128)(2,1)S(1)}, u32[]{:S(2)}, u32[]{:S(2)}) collective-permute-start(bf16[320,128]{1,0:T(8,128)(2,1)S(1)} %add_convert_fusion.refs_0_), channel_id=1, source_target_pairs={{0,24},{8,16},{16,8},{24,0},{1,25},{9,17},{17,9},{25,1},{2,26},{10... | collective-permute-start | bytes 245768 | tf_op jit(solution)/shard_map/ppermute | solution.py:400
  80.7 0.7 collective-permute-start.42
  81.3 0.9 %collective-permute-start.41 = (bf16[320,128]{1,0:T(8,128)(2,1)S(1)}, bf16[320,128]{1,0:T(8,128)(2,1)S(1)}, u32[]{:S(2)}, u32[]{:S(2)}) collective-permute-start(bf16[320,128]{1,0:T(8,128)(2,1)S(1)} %add_convert_fusion.refs_0_), channel_id=1, source_target_pairs={{0,8},{8,0},{16,24},{24,16},{1,9},{9,1},{17,25},{25,17},{2,10},{10... | collective-permute-start | bytes 245768 | tf_op jit(solution)/shard_map/ppermute | solution.py:400
  82.2 1.9 %collective-permute-done.43.refs_3_ = bf16[320,128]{1,0:T(8,128)(2,1)S(1)} collective-permute-done((bf16[320,128]{1,0:T(8,128)(2,1)S(1)}, bf16[320,128]{1,0:T(8,128)(2,1)S(1)}, u32[]{:S(2)}, u32[]{:S(2)}) %collective-permute-start.43) | collective-permute-done | bytes 81952 | tf_op jit(solution)/shard_map/ppermute | solution.py:400
  84.1 1.0 %collective-permute-done.42.refs_2_ = bf16[320,128]{1,0:T(8,128)(2,1)S(1)} collective-permute-done((bf16[320,128]{1,0:T(8,128)(2,1)S(1)}, bf16[320,128]{1,0:T(8,128)(2,1)S(1)}, u32[]{:S(2)}, u32[]{:S(2)}) %collective-permute-start.42) | collective-permute-done | bytes 81952 | tf_op jit(solution)/shard_map/ppermute | solution.py:400
  85.1 0.7 collective-permute-done.41.refs_1_
  85.8 0.9 %shard_map.83 = f32[1280,128]{1,0:T(8,128)} custom-call(bf16[320,128]{1,0:T(8,128)(2,1)S(1)} %add_convert_fusion.refs_0_, bf16[320,128]{1,0:T(8,128)(2,1)S(1)} %collective-permute-done.41.refs_1_, bf16[320,128]{1,0:T(8,128)(2,1)S(1)} %collective-permute-done.42.refs_2_, bf16[320,128]{1,0:T(8,128)(2,1)S(1)} %collective-permute-done.43.refs_3_), custom_call_target="tpu_custom_call" | custom-call | bytes 1048576 | tf_op jit(solution)/shard_map/pallas_call | solution.py:43
  (60 shorter events, 1.7 us)
Async XLA Ops:
  0.6 13.7 %collective-permute-start = (bf16[1280,128]{1,0:T(8,128)(2,1)}, bf16[1280,128]{1,0:T(8,128)(2,1)S(1)}, u32[]{:S(2)}, u32[]{:S(2)}) collective-permute-start(bf16[1280,128]{1,0:T(8,128)(2,1)} %refs_3_.1), channel_id=1, source_target_pairs={{0,1},{1,0},{2,3},{3,2},{4,5},{5,4},{6,7},{7,6},{8,9},{9,8},{10,11... | collective-permute-start | bytes 983048 | tf_op jit(solution)/shard_map/ppermute | solution.py:391
  1.1 1.0 %copy-start.2 = (bf16[1280,128]{1,0:T(8,128)(2,1)S(1)}, bf16[1280,128]{1,0:T(8,128)(2,1)}, u32[]{:S(2)}) copy-start(bf16[1280,128]{1,0:T(8,128)(2,1)} %refs_3_.1) | copy-start | bytes 983044
  2.1 22.9 %copy-start.3 = (bf16[1280,128]{1,0:T(8,128)(2,1)S(1)}, bf16[1280,128]{1,0:T(8,128)(2,1)}, u32[]{:S(2)}) copy-start(bf16[1280,128]{1,0:T(8,128)(2,1)} %refs_3_.1) | copy-start | bytes 983044
  2.1 10.7 %collective-permute-start.3 = (bf16[320,128]{1,0:T(8,128)(2,1)S(1)}, bf16[320,128]{1,0:T(8,128)(2,1)S(1)}, u32[]{:S(2)}, u32[]{:S(2)}) collective-permute-start(bf16[320,128]{1,0:T(8,128)(2,1)S(1)} %shard_map.69), channel_id=1, source_target_pairs={{0,6},{1,7},{2,4},{3,5},{4,2},{5,3},{6,0},{7,1},{8,14},{9,15},{10,... | collective-permute-start | bytes 245768 | tf_op jit(solution)/shard_map/ppermute | solution.py:397
  6.8 7.5 %collective-permute-start.2 = (bf16[320,128]{1,0:T(8,128)(2,1)S(1)}, bf16[320,128]{1,0:T(8,128)(2,1)S(1)}, u32[]{:S(2)}, u32[]{:S(2)}) collective-permute-start(bf16[320,128]{1,0:T(8,128)(2,1)S(1)} %shard_map.69), channel_id=1, source_target_pairs={{0,4},{1,5},{2,6},{3,7},{4,0},{5,1},{6,2},{7,3},{8,12},{9,13},{10,... | collective-permute-start | bytes 245768 | tf_op jit(solution)/shard_map/ppermute | solution.py:397
  6.8 7.5 %collective-permute-start.1 = (bf16[320,128]{1,0:T(8,128)(2,1)S(1)}, bf16[320,128]{1,0:T(8,128)(2,1)S(1)}, u32[]{:S(2)}, u32[]{:S(2)}) collective-permute-start(bf16[320,128]{1,0:T(8,128)(2,1)S(1)} %shard_map.69), channel_id=1, source_target_pairs={{0,2},{1,3},{2,0},{3,1},{4,6},{5,7},{6,4},{7,5},{8,10},{9,11},{10,... | collective-permute-start | bytes 245768 | tf_op jit(solution)/shard_map/ppermute | solution.py:397
  7.5 1.2 %copy-start = (bf16[1,128,4096]{2,1,0:T(8,128)(2,1)S(1)}, bf16[1,128,4096]{2,1,0:T(8,128)(2,1)}, u32[]{:S(2)}) copy-start(bf16[1,128,4096]{2,1,0:T(8,128)(2,1)} %param.5) | copy-start | bytes 3145732
  8.7 0.9 %copy-start.4 = (bf16[1,128,1024]{2,1,0:T(8,128)(2,1)S(1)}, bf16[1,128,1024]{2,1,0:T(8,128)(2,1)}, u32[]{:S(2)}) copy-start(bf16[1,128,1024]{2,1,0:T(8,128)(2,1)} %param.6) | copy-start | bytes 786436
  9.6 0.7 copy-start.5
  10.3 0.7 copy-start.6
  11.0 14.1 %copy-start.1 = (bf16[1,128,4096]{2,1,0:T(8,128)(2,1)S(1)}, bf16[1,128,4096]{2,1,0:T(8,128)(2,1)}, u32[]{:S(2)}) copy-start(bf16[1,128,4096]{2,1,0:T(8,128)(2,1)} %param.5) | copy-start | bytes 3145732
  14.3 5.5 %collective-permute-start.9 = (bf16[320,128]{1,0:T(8,128)(2,1)S(1)}, bf16[320,128]{1,0:T(8,128)(2,1)S(1)}, u32[]{:S(2)}, u32[]{:S(2)}) collective-permute-start(bf16[320,128]{1,0:T(8,128)(2,1)S(1)} %shard_map.70.refs_4_.refs_3_.refs_5_), channel_id=1, source_target_pairs={{0,24},{8,16},{16,8},{24,0},{1,25},{9,17},{17,9},{25,1},{2,26},{10... | collective-permute-start | bytes 245768 | tf_op jit(solution)/shard_map/ppermute | solution.py:400
  16.9 6.0 %collective-permute-start.7 = (bf16[320,128]{1,0:T(8,128)(2,1)S(1)}, bf16[320,128]{1,0:T(8,128)(2,1)S(1)}, u32[]{:S(2)}, u32[]{:S(2)}) collective-permute-start(bf16[320,128]{1,0:T(8,128)(2,1)S(1)} %shard_map.70.refs_4_.refs_3_.refs_5_), channel_id=1, source_target_pairs={{0,16},{8,24},{16,0},{24,8},{1,17},{9,25},{17,1},{25,9},{2,18},{10... | collective-permute-start | bytes 245768 | tf_op jit(solution)/shard_map/ppermute | solution.py:400
  17.4 6.1 %collective-permute-start.5 = (bf16[320,128]{1,0:T(8,128)(2,1)S(1)}, bf16[320,128]{1,0:T(8,128)(2,1)S(1)}, u32[]{:S(2)}, u32[]{:S(2)}) collective-permute-start(bf16[320,128]{1,0:T(8,128)(2,1)S(1)} %shard_map.70.refs_4_.refs_3_.refs_5_), channel_id=1, source_target_pairs={{0,8},{8,0},{16,24},{24,16},{1,9},{9,1},{17,25},{25,17},{2,10},{10... | collective-permute-start | bytes 245768 | tf_op jit(solution)/shard_map/ppermute | solution.py:400
  17.9 5.7 %collective-permute-start.4 = (bf16[320,128]{1,0:T(8,128)(2,1)S(1)}, bf16[320,128]{1,0:T(8,128)(2,1)S(1)}, u32[]{:S(2)}, u32[]{:S(2)}) collective-permute-start(bf16[320,128]{1,0:T(8,128)(2,1)S(1)} %shard_map.70.refs_4_.refs_3_.refs_5_), channel_id=1, source_target_pairs={{0,1},{1,0},{2,3},{3,2},{4,5},{5,4},{6,7},{7,6},{8,9},{9,8},{10,11... | collective-permute-start | bytes 245768 | tf_op jit(solution)/shard_map/ppermute | solution.py:391
  19.8 3.8 %collective-permute-start.10 = (bf16[320,128]{1,0:T(8,128)(2,1)S(1)}, bf16[320,128]{1,0:T(8,128)(2,1)S(1)}, u32[]{:S(2)}, u32[]{:S(2)}) collective-permute-start(bf16[320,128]{1,0:T(8,128)(2,1)S(1)} %collective-permute-done.9.refs_10_.refs_11_), channel_id=1, source_target_pairs={{0,1},{1,0},{2,3},{3,2},{4,5},{5,4},{6,7},{7,6},{8,9},{9,8},{10,11... | collective-permute-start | bytes 245768 | tf_op jit(solution)/shard_map/ppermute | solution.py:391
  19.9 8.7 %collective-permute-start.13 = (bf16[640,128]{1,0:T(8,128)(2,1)S(1)}, bf16[640,128]{1,0:T(8,128)(2,1)S(1)}, u32[]{:S(2)}, u32[]{:S(2)}) collective-permute-start(bf16[640,128]{1,0:T(8,128)(2,1)S(1)} %shard_map.72.refs_0_), channel_id=1, source_target_pairs={{0,24},{8,16},{16,8},{24,0},{1,25},{9,17},{17,9},{25,1},{2,26},{10... | collective-permute-start | bytes 491528 | tf_op jit(solution)/shard_map/ppermute | solution.py:400
  22.8 8.4 %collective-permute-start.12 = (bf16[640,128]{1,0:T(8,128)(2,1)S(1)}, bf16[640,128]{1,0:T(8,128)(2,1)S(1)}, u32[]{:S(2)}, u32[]{:S(2)}) collective-permute-start(bf16[640,128]{1,0:T(8,128)(2,1)S(1)} %shard_map.72.refs_0_), channel_id=1, source_target_pairs={{0,16},{8,24},{16,0},{24,8},{1,17},{9,25},{17,1},{25,9},{2,18},{10... | collective-permute-start | bytes 491528 | tf_op jit(solution)/shard_map/ppermute | solution.py:400
  23.4 8.2 %collective-permute-start.11 = (bf16[640,128]{1,0:T(8,128)(2,1)S(1)}, bf16[640,128]{1,0:T(8,128)(2,1)S(1)}, u32[]{:S(2)}, u32[]{:S(2)}) collective-permute-start(bf16[640,128]{1,0:T(8,128)(2,1)S(1)} %shard_map.72.refs_0_), channel_id=1, source_target_pairs={{0,8},{8,0},{16,24},{24,16},{1,9},{9,1},{17,25},{25,17},{2,10},{10... | collective-permute-start | bytes 491528 | tf_op jit(solution)/shard_map/ppermute | solution.py:400
  23.6 1.3 %collective-permute-start.8 = (bf16[320,128]{1,0:T(8,128)(2,1)S(1)}, bf16[320,128]{1,0:T(8,128)(2,1)S(1)}, u32[]{:S(2)}, u32[]{:S(2)}) collective-permute-start(bf16[320,128]{1,0:T(8,128)(2,1)S(1)} %collective-permute-done.7.refs_8_.refs_9_), channel_id=1, source_target_pairs={{0,1},{1,0},{2,3},{3,2},{4,5},{5,4},{6,7},{7,6},{8,9},{9,8},{10,11... | collective-permute-start | bytes 245768 | tf_op jit(solution)/shard_map/ppermute | solution.py:391
  23.6 1.4 %collective-permute-start.6 = (bf16[320,128]{1,0:T(8,128)(2,1)S(1)}, bf16[320,128]{1,0:T(8,128)(2,1)S(1)}, u32[]{:S(2)}, u32[]{:S(2)}) collective-permute-start(bf16[320,128]{1,0:T(8,128)(2,1)S(1)} %collective-permute-done.5.refs_6_.refs_7_), channel_id=1, source_target_pairs={{0,1},{1,0},{2,3},{3,2},{4,5},{5,4},{6,7},{7,6},{8,9},{9,8},{10,11... | collective-permute-start | bytes 245768 | tf_op jit(solution)/shard_map/ppermute | solution.py:391
  26.1 6.8 %collective-permute-start.16 = (bf16[128,256]{1,0:T(8,128)(2,1)S(1)}, bf16[128,256]{1,0:T(8,128)(2,1)S(1)}, u32[]{:S(2)}, u32[]{:S(2)}) collective-permute-start(bf16[128,256]{1,0:T(8,128)(2,1)S(1)} %get-tuple-element.38.refs_15_.refs_4_), channel_id=1, source_target_pairs={{0,6},{1,7},{2,4},{3,5},{4,2},{5,3},{6,0},{7,1},{8,14},{9,15},{10,... | collective-permute-start | bytes 196616 | tf_op jit(solution)/shard_map/ppermute | solution.py:397
  28.6 6.5 %collective-permute-start.15 = (bf16[128,256]{1,0:T(8,128)(2,1)S(1)}, bf16[128,256]{1,0:T(8,128)(2,1)S(1)}, u32[]{:S(2)}, u32[]{:S(2)}) collective-permute-start(bf16[128,256]{1,0:T(8,128)(2,1)S(1)} %get-tuple-element.38.refs_15_.refs_4_), channel_id=1, source_target_pairs={{0,4},{1,5},{2,6},{3,7},{4,0},{5,1},{6,2},{7,3},{8,12},{9,13},{10,... | collective-permute-start | bytes 196616 | tf_op jit(solution)/shard_map/ppermute | solution.py:397
  28.6 6.5 %collective-permute-start.14 = (bf16[128,256]{1,0:T(8,128)(2,1)S(1)}, bf16[128,256]{1,0:T(8,128)(2,1)S(1)}, u32[]{:S(2)}, u32[]{:S(2)}) collective-permute-start(bf16[128,256]{1,0:T(8,128)(2,1)S(1)} %get-tuple-element.38.refs_15_.refs_4_), channel_id=1, source_target_pairs={{0,2},{1,3},{2,0},{3,1},{4,6},{5,7},{6,4},{7,5},{8,10},{9,11},{10,... | collective-permute-start | bytes 196616 | tf_op jit(solution)/shard_map/ppermute | solution.py:397
  35.1 2.5 %collective-permute-start.17 = (bf16[2560,128]{1,0:T(8,128)(2,1)S(1)}, bf16[2560,128]{1,0:T(8,128)(2,1)S(1)}, u32[]{:S(2)}, u32[]{:S(2)}) collective-permute-start(bf16[2560,128]{1,0:T(8,128)(2,1)S(1)} %shard_map.73.refs_13_), channel_id=1, source_target_pairs={{0,1},{1,0},{2,3},{3,2},{4,5},{5,4},{6,7},{7,6},{8,9},{9,8},{10,11... | collective-permute-start | bytes 1966088 | tf_op jit(solution)/shard_map/ppermute | solution.py:391
  35.2 2.2 %collective-permute-start.18 = (bf16[128,256]{1,0:T(8,128)(2,1)S(1)}, bf16[128,256]{1,0:T(8,128)(2,1)S(1)}, u32[]{:S(2)}, u32[]{:S(2)}) collective-permute-start(bf16[128,256]{1,0:T(8,128)(2,1)S(1)} %get-tuple-element.38.refs_15_.refs_4_), channel_id=1, source_target_pairs={{0,1},{1,0},{2,3},{3,2},{4,5},{5,4},{6,7},{7,6},{8,9},{9,8},{10,11... | collective-permute-start | bytes 196616 | tf_op jit(solution)/shard_map/ppermute | solution.py:391
  35.7 1.8 %collective-permute-start.21 = (bf16[128,256]{1,0:T(8,128)(2,1)S(1)}, bf16[128,256]{1,0:T(8,128)(2,1)S(1)}, u32[]{:S(2)}, u32[]{:S(2)}) collective-permute-start(bf16[128,256]{1,0:T(8,128)(2,1)S(1)} %collective-permute-done.16.refs_6_.refs_21_.refs_10_), channel_id=1, source_target_pairs={{0,1},{1,0},{2,3},{3,2},{4,5},{5,4},{6,7},{7,6},{8,9},{9,8},{10,11... | collective-permute-start | bytes 196616 | tf_op jit(solution)/shard_map/ppermute | solution.py:391
  35.8 1.8 %collective-permute-start.20 = (bf16[128,256]{1,0:T(8,128)(2,1)S(1)}, bf16[128,256]{1,0:T(8,128)(2,1)S(1)}, u32[]{:S(2)}, u32[]{:S(2)}) collective-permute-start(bf16[128,256]{1,0:T(8,128)(2,1)S(1)} %collective-permute-done.15.refs_5_.refs_19_.refs_8_), channel_id=1, source_target_pairs={{0,1},{1,0},{2,3},{3,2},{4,5},{5,4},{6,7},{7,6},{8,9},{9,8},{10,11... | collective-permute-start | bytes 196616 | tf_op jit(solution)/shard_map/ppermute | solution.py:391
  36.2 1.5 %collective-permute-start.19 = (bf16[128,256]{1,0:T(8,128)(2,1)S(1)}, bf16[128,256]{1,0:T(8,128)(2,1)S(1)}, u32[]{:S(2)}, u32[]{:S(2)}) collective-permute-start(bf16[128,256]{1,0:T(8,128)(2,1)S(1)} %collective-permute-done.14.refs_4_.refs_17_.refs_6_), channel_id=1, source_target_pairs={{0,1},{1,0},{2,3},{3,2},{4,5},{5,4},{6,7},{7,6},{8,9},{9,8},{10,11... | collective-permute-start | bytes 196616 | tf_op jit(solution)/shard_map/ppermute | solution.py:391
  39.4 10.3 %collective-permute-start.29 = (bf16[4096,128]{1,0:T(8,128)(2,1)S(1)}, bf16[4096,128]{1,0:T(8,128)(2,1)S(1)}, u32[]{:S(2)}, u32[]{:S(2)}) collective-permute-start(bf16[4096,128]{1,0:T(8,128)(2,1)S(1)} %shard_map.78), channel_id=1, source_target_pairs={{0,1},{1,0},{2,3},{3,2},{4,5},{5,4},{6,7},{7,6},{8,9},{9,8},{10,11... | collective-permute-start | bytes 3145736 | tf_op jit(solution)/shard_map/ppermute | solution.py:391
  43.3 1.3 %collective-permute-start.23 = (bf16[128,256]{1,0:T(8,128)(2,1)S(1)}, bf16[128,256]{1,0:T(8,128)(2,1)S(1)}, u32[]{:S(2)}, u32[]{:S(2)}) collective-permute-start(bf16[128,256]{1,0:T(8,128)(2,1)S(1)} %get-tuple-element.47), channel_id=1, source_target_pairs={{0,1},{1,0},{2,3},{3,2},{4,5},{5,4},{6,7},{7,6},{8,9},{9,8},{10,11... | collective-permute-start | bytes 196616 | tf_op jit(solution)/shard_map/ppermute | solution.py:391
  43.7 9.3 %collective-permute-start.22 = (bf16[128,256]{1,0:T(8,128)(2,1)S(1)}, bf16[128,256]{1,0:T(8,128)(2,1)S(1)}, u32[]{:S(2)}, u32[]{:S(2)}) collective-permute-start(bf16[128,256]{1,0:T(8,128)(2,1)S(1)} %get-tuple-element.45), channel_id=1, source_target_pairs={{0,1},{1,0},{2,3},{3,2},{4,5},{5,4},{6,7},{7,6},{8,9},{9,8},{10,11... | collective-permute-start | bytes 196616 | tf_op jit(solution)/shard_map/ppermute | solution.py:391
  43.8 1.3 %collective-permute-start.25 = (bf16[128,256]{1,0:T(8,128)(2,1)S(1)}, bf16[128,256]{1,0:T(8,128)(2,1)S(1)}, u32[]{:S(2)}, u32[]{:S(2)}) collective-permute-start(bf16[128,256]{1,0:T(8,128)(2,1)S(1)} %get-tuple-element.49), channel_id=1, source_target_pairs={{0,1},{1,0},{2,3},{3,2},{4,5},{5,4},{6,7},{7,6},{8,9},{9,8},{10,11... | collective-permute-start | bytes 196616 | tf_op jit(solution)/shard_map/ppermute | solution.py:391
  44.2 1.6 %collective-permute-start.27 = (bf16[128,256]{1,0:T(8,128)(2,1)S(1)}, bf16[128,256]{1,0:T(8,128)(2,1)S(1)}, u32[]{:S(2)}, u32[]{:S(2)}) collective-permute-start(bf16[128,256]{1,0:T(8,128)(2,1)S(1)} %get-tuple-element.51), channel_id=1, source_target_pairs={{0,1},{1,0},{2,3},{3,2},{4,5},{5,4},{6,7},{7,6},{8,9},{9,8},{10,11... | collective-permute-start | bytes 196616 | tf_op jit(solution)/shard_map/ppermute | solution.py:391
  44.6 3.7 %collective-permute-start.30 = (bf16[8,128,128]{2,1,0:T(8,128)(2,1)S(1)}, bf16[8,128,128]{2,1,0:T(8,128)(2,1)S(1)}, u32[]{:S(2)}, u32[]{:S(2)}) collective-permute-start(bf16[8,128,128]{2,1,0:T(8,128)(2,1)S(1)} %get-tuple-element.42.refs_1_.refs_3_), channel_id=1, source_target_pairs={{0,1},{1,0},{2,3},{3,2},{4,5},{5,4},{6,7},{7,6},{8,9},{9,8},{10,11... | collective-permute-start | bytes 786440 | tf_op jit(solution)/shard_map/ppermute | solution.py:391
  45.1 9.4 %collective-permute-start.24 = (bf16[128,256]{1,0:T(8,128)(2,1)S(1)}, bf16[128,256]{1,0:T(8,128)(2,1)S(1)}, u32[]{:S(2)}, u32[]{:S(2)}) collective-permute-start(bf16[128,256]{1,0:T(8,128)(2,1)S(1)} %add_convert_fusion.3), channel_id=1, source_target_pairs={{0,2},{1,3},{2,0},{3,1},{4,6},{5,7},{6,4},{7,5},{8,10},{9,11},{10,... | collective-permute-start | bytes 196616 | tf_op jit(solution)/shard_map/ppermute | solution.py:397
  45.9 8.8 %collective-permute-start.26 = (bf16[128,256]{1,0:T(8,128)(2,1)S(1)}, bf16[128,256]{1,0:T(8,128)(2,1)S(1)}, u32[]{:S(2)}, u32[]{:S(2)}) collective-permute-start(bf16[128,256]{1,0:T(8,128)(2,1)S(1)} %add_convert_fusion.2), channel_id=1, source_target_pairs={{0,4},{1,5},{2,6},{3,7},{4,0},{5,1},{6,2},{7,3},{8,12},{9,13},{10,... | collective-permute-start | bytes 196616 | tf_op jit(solution)/shard_map/ppermute | solution.py:397
  48.3 6.4 %collective-permute-start.28 = (bf16[128,256]{1,0:T(8,128)(2,1)S(1)}, bf16[128,256]{1,0:T(8,128)(2,1)S(1)}, u32[]{:S(2)}, u32[]{:S(2)}) collective-permute-start(bf16[128,256]{1,0:T(8,128)(2,1)S(1)} %add_convert_fusion.1), channel_id=1, source_target_pairs={{0,6},{1,7},{2,4},{3,5},{4,2},{5,3},{6,0},{7,1},{8,14},{9,15},{10,... | collective-permute-start | bytes 196616 | tf_op jit(solution)/shard_map/ppermute | solution.py:397
  51.1 9.5 %collective-permute-start.31 = (bf16[960,128]{1,0:T(8,128)(2,1)S(1)}, bf16[960,128]{1,0:T(8,128)(2,1)S(1)}, u32[]{:S(2)}, u32[]{:S(2)}) collective-permute-start(bf16[960,128]{1,0:T(8,128)(2,1)S(1)} %get-tuple-element.56), channel_id=1, source_target_pairs={{0,8},{8,0},{16,24},{24,16},{1,9},{9,1},{17,25},{25,17},{2,10},{10... | collective-permute-start | bytes 737288 | tf_op jit(solution)/shard_map/ppermute | solution.py:400
  53.0 15.9 %collective-permute-start.32 = (bf16[960,128]{1,0:T(8,128)(2,1)S(1)}, bf16[960,128]{1,0:T(8,128)(2,1)S(1)}, u32[]{:S(2)}, u32[]{:S(2)}) collective-permute-start(bf16[960,128]{1,0:T(8,128)(2,1)S(1)} %get-tuple-element.57), channel_id=1, source_target_pairs={{0,16},{8,24},{16,0},{24,8},{1,17},{9,25},{17,1},{25,9},{2,18},{10... | collective-permute-start | bytes 737288 | tf_op jit(solution)/shard_map/ppermute | solution.py:400
  54.5 14.4 %collective-permute-start.33 = (bf16[960,128]{1,0:T(8,128)(2,1)S(1)}, bf16[960,128]{1,0:T(8,128)(2,1)S(1)}, u32[]{:S(2)}, u32[]{:S(2)}) collective-permute-start(bf16[960,128]{1,0:T(8,128)(2,1)S(1)} %get-tuple-element.58), channel_id=1, source_target_pairs={{0,24},{8,16},{16,8},{24,0},{1,25},{9,17},{17,9},{25,1},{2,26},{10... | collective-permute-start | bytes 737288 | tf_op jit(solution)/shard_map/ppermute | solution.py:400
  54.8 1.3 %collective-permute-start.34 = (bf16[2,128,128]{2,1,0:T(8,128)(2,1)S(1)}, bf16[2,128,128]{2,1,0:T(8,128)(2,1)S(1)}, u32[]{:S(2)}, u32[]{:S(2)}) collective-permute-start(bf16[2,128,128]{2,1,0:T(8,128)(2,1)S(1)} %shard_map.76.refs_2_.refs_5_), channel_id=1, source_target_pairs={{0,1},{1,0},{2,3},{3,2},{4,5},{5,4},{6,7},{7,6},{8,9},{9,8},{10,11... | collective-permute-start | bytes 196616 | tf_op jit(solution)/shard_map/ppermute | solution.py:391
  57.1 9.5 %collective-permute-start.35 = (bf16[320,128]{1,0:T(8,128)(2,1)S(1)}, bf16[320,128]{1,0:T(8,128)(2,1)S(1)}, u32[]{:S(2)}, u32[]{:S(2)}) collective-permute-start(bf16[320,128]{1,0:T(8,128)(2,1)S(1)} %get-tuple-element.60), channel_id=1, source_target_pairs={{0,8},{8,0},{16,24},{24,16},{1,9},{9,1},{17,25},{25,17},{2,10},{10... | collective-permute-start | bytes 245768 | tf_op jit(solution)/shard_map/ppermute | solution.py:400
  59.0 9.9 %collective-permute-start.36 = (bf16[320,128]{1,0:T(8,128)(2,1)S(1)}, bf16[320,128]{1,0:T(8,128)(2,1)S(1)}, u32[]{:S(2)}, u32[]{:S(2)}) collective-permute-start(bf16[320,128]{1,0:T(8,128)(2,1)S(1)} %get-tuple-element.61), channel_id=1, source_target_pairs={{0,16},{8,24},{16,0},{24,8},{1,17},{9,25},{17,1},{25,9},{2,18},{10... | collective-permute-start | bytes 245768 | tf_op jit(solution)/shard_map/ppermute | solution.py:400
  60.5 8.4 %collective-permute-start.37 = (bf16[320,128]{1,0:T(8,128)(2,1)S(1)}, bf16[320,128]{1,0:T(8,128)(2,1)S(1)}, u32[]{:S(2)}, u32[]{:S(2)}) collective-permute-start(bf16[320,128]{1,0:T(8,128)(2,1)S(1)} %shard_map.81), channel_id=1, source_target_pairs={{0,24},{8,16},{16,8},{24,0},{1,25},{9,17},{17,9},{25,1},{2,26},{10... | collective-permute-start | bytes 245768 | tf_op jit(solution)/shard_map/ppermute | solution.py:400
  69.2 5.0 %collective-permute-start.38 = (bf16[320,128]{1,0:T(8,128)(2,1)S(1)}, bf16[320,128]{1,0:T(8,128)(2,1)S(1)}, u32[]{:S(2)}, u32[]{:S(2)}) collective-permute-start(bf16[320,128]{1,0:T(8,128)(2,1)S(1)} %get-tuple-element.65), channel_id=1, source_target_pairs={{0,2},{1,3},{2,0},{3,1},{4,6},{5,7},{6,4},{7,5},{8,10},{9,11},{10,... | collective-permute-start | bytes 245768 | tf_op jit(solution)/shard_map/ppermute | solution.py:397
  69.3 8.4 %collective-permute-start.39 = (bf16[320,128]{1,0:T(8,128)(2,1)S(1)}, bf16[320,128]{1,0:T(8,128)(2,1)S(1)}, u32[]{:S(2)}, u32[]{:S(2)}) collective-permute-start(bf16[320,128]{1,0:T(8,128)(2,1)S(1)} %get-tuple-element.66), channel_id=1, source_target_pairs={{0,4},{1,5},{2,6},{3,7},{4,0},{5,1},{6,2},{7,3},{8,12},{9,13},{10,... | collective-permute-start | bytes 245768 | tf_op jit(solution)/shard_map/ppermute | solution.py:397
  72.3 6.3 %collective-permute-start.40 = (bf16[320,128]{1,0:T(8,128)(2,1)S(1)}, bf16[320,128]{1,0:T(8,128)(2,1)S(1)}, u32[]{:S(2)}, u32[]{:S(2)}) collective-permute-start(bf16[320,128]{1,0:T(8,128)(2,1)S(1)} %get-tuple-element.67), channel_id=1, source_target_pairs={{0,6},{1,7},{2,4},{3,5},{4,2},{5,3},{6,0},{7,1},{8,14},{9,15},{10,... | collective-permute-start | bytes 245768 | tf_op jit(solution)/shard_map/ppermute | solution.py:397
  78.7 5.4 %collective-permute-start.43 = (bf16[320,128]{1,0:T(8,128)(2,1)S(1)}, bf16[320,128]{1,0:T(8,128)(2,1)S(1)}, u32[]{:S(2)}, u32[]{:S(2)}) collective-permute-start(bf16[320,128]{1,0:T(8,128)(2,1)S(1)} %add_convert_fusion.refs_0_), channel_id=1, source_target_pairs={{0,24},{8,16},{16,8},{24,0},{1,25},{9,17},{17,9},{25,1},{2,26},{10... | collective-permute-start | bytes 245768 | tf_op jit(solution)/shard_map/ppermute | solution.py:400
  80.7 4.4 %collective-permute-start.42 = (bf16[320,128]{1,0:T(8,128)(2,1)S(1)}, bf16[320,128]{1,0:T(8,128)(2,1)S(1)}, u32[]{:S(2)}, u32[]{:S(2)}) collective-permute-start(bf16[320,128]{1,0:T(8,128)(2,1)S(1)} %add_convert_fusion.refs_0_), channel_id=1, source_target_pairs={{0,16},{8,24},{16,0},{24,8},{1,17},{9,25},{17,1},{25,9},{2,18},{10... | collective-permute-start | bytes 245768 | tf_op jit(solution)/shard_map/ppermute | solution.py:400
  81.3 4.4 %collective-permute-start.41 = (bf16[320,128]{1,0:T(8,128)(2,1)S(1)}, bf16[320,128]{1,0:T(8,128)(2,1)S(1)}, u32[]{:S(2)}, u32[]{:S(2)}) collective-permute-start(bf16[320,128]{1,0:T(8,128)(2,1)S(1)} %add_convert_fusion.refs_0_), channel_id=1, source_target_pairs={{0,8},{8,0},{16,24},{24,16},{1,9},{9,1},{17,25},{25,17},{2,10},{10... | collective-permute-start | bytes 245768 | tf_op jit(solution)/shard_map/ppermute | solution.py:400

commit v7 on v6

--- a/solution.py
+++ b/solution.py
@@ -496,7 +496,6 @@
     )
     dq, keep, send = outs[0], outs[1 : nz + 1], outs[nz + 1 :]
     sums = [add(keep[k], swap_core(send[k])) for k in range(nz)]
-    kv_terms = [sums[0]] + [swap_z(sums[k], k) for k in range(1, nz)]
 
     def weight_terms(z_lo, z_count, grads):
         first = z_lo * 2 * shard // (NBR * BLK)
@@ -516,8 +515,11 @@
 
     if fast:
         dq_pair = (dq, swap_core(dq))
-        head = weight_terms(0, nz - 1, dq_pair)
-        head = [head[0]] + [swap_dp(head[k], k) for k in range(1, ndp)]
+        head_raw = weight_terms(0, nz - 1, dq_pair)
+        head = [head_raw[0]] + [swap_dp(head_raw[k], k) for k in range(1, ndp)]
+    gate = head_raw[:1] if fast else []
+    kv_terms = [sums[0], swap_z(after(sums[1], *gate), 1)]
+    kv_terms += [swap_z(sums[k], k) for k in range(2, nz)]
     (dkv,) = call(
         functools.partial(kv_grad_kernel, nz),
         (),

time: 86.9 us -> 86.3 us (level)
    ppermute x15, waiting for transfers between devices: 9.78 us -> 8.77 us  [swap_dp(): return lax.ppermute(v, 'dp', [(i, i ^ k) for i in range(ndp)])]
    ppermute x12, starting transfers between devices: 18.7 us -> 17.8 us  [swap_z(): return lax.ppermute(v, 'ctx', [(i, i ^ 2 * k) for i in range(nctx)])]
    ppermute x12, waiting for transfers between devices: 9.91 us -> 10.8 us  [swap_z(): return lax.ppermute(v, 'ctx', [(i, i ^ 2 * k) for i in range(nctx)])]
  transfers between devices with their start and end apart: 44 -> 44, of which waited for: 23 -> 21; matrix products, arithmetic and copies ran while one was open for 0% -> 0% of each run, Pallas kernels for 14% -> 14%
where the time goes in v7:
time: 86.3 us; the launch traced here: 86.1 us
  starting transfers between devices  41.9 us (49%)
  waiting for transfers between devices  23.8 us (28%)
  Pallas kernels  14.9 us (17%)
  local copies, waits for them, and re-layouts  4.59 us (5%)
    ppermute x15, starting transfers between devices, swap_dp(): return lax.ppermute(v, 'dp', [(i, i ^ k) for i in range(ndp)])  20.1 us
    ppermute x12, starting transfers between devices, swap_z(): return lax.ppermute(v, 'ctx', [(i, i ^ 2 * k) for i in range(nctx)])  17.8 us
    pallas_call x14, Pallas kernels, call(): pl.pallas_call(body, in_specs=[SMEM] * len(scalars) + [VMEM] * len(arrays...  14.8 us
    ppermute x12, waiting for transfers between devices, swap_z(): return lax.ppermute(v, 'ctx', [(i, i ^ 2 * k) for i in range(nctx)])  10.8 us
    ppermute x15, waiting for transfers between devices, swap_dp(): return lax.ppermute(v, 'dp', [(i, i ^ k) for i in range(ndp)])  8.77 us
    unnamed x15, local copies, waits for them, and re-layouts  4.59 us
    ppermute x17, waiting for transfers between devices, swap_core(): return lax.ppermute(v, 'ctx', [(i, i ^ 1) for i in range(nctx)])  4.23 us
    ppermute x17, starting transfers between devices, swap_core(): return lax.ppermute(v, 'ctx', [(i, i ^ 1) for i in range(nctx)])  3.9 us
  transfers between devices with their start and end apart: 44, of which 21 were waited for; matrix products, arithmetic and copies ran while one was open for 0% of the time, Pallas kernels for 14%

profile of v7, /device:TPU:0, one launch (start us, length us, event | category | flops | bytes accessed | tf_op | source)
XLA Modules:
  0.0 86.1 jit_solution(10279013830677689954)
XLA Ops:
  0.6 0.5 collective-permute-start
  1.1 1.0 %copy-done.2 = bf16[1280,128]{1,0:T(8,128)(2,1)S(1)} copy-done((bf16[1280,128]{1,0:T(8,128)(2,1)S(1)}, bf16[1280,128]{1,0:T(8,128)(2,1)}, u32[]{:S(2)}) %copy-start.2) | copy-done | bytes 327704
  2.1 4.7 %collective-permute-start.3 = (bf16[320,128]{1,0:T(8,128)(2,1)S(1)}, bf16[320,128]{1,0:T(8,128)(2,1)S(1)}, u32[]{:S(2)}, u32[]{:S(2)}) collective-permute-start(bf16[320,128]{1,0:T(8,128)(2,1)S(1)} %shard_map.69), channel_id=1, source_target_pairs={{0,6},{1,7},{2,4},{3,5},{4,2},{5,3},{6,0},{7,1},{8,14},{9,15},{10,... | collective-permute-start | bytes 245768 | tf_op jit(solution)/shard_map/ppermute | solution.py:397
  6.8 0.6 collective-permute-start.1
  7.5 1.2 %copy-done = bf16[1,128,4096]{2,1,0:T(8,128)(2,1)S(1)} copy-done((bf16[1,128,4096]{2,1,0:T(8,128)(2,1)S(1)}, bf16[1,128,4096]{2,1,0:T(8,128)(2,1)}, u32[]{:S(2)}) %copy-start) | copy-done | bytes 1048600
  8.7 0.9 %copy-done.4 = bf16[1,128,1024]{2,1,0:T(8,128)(2,1)S(1)} copy-done((bf16[1,128,1024]{2,1,0:T(8,128)(2,1)S(1)}, bf16[1,128,1024]{2,1,0:T(8,128)(2,1)}, u32[]{:S(2)}) %copy-start.4) | copy-done | bytes 262168
  9.6 0.7 copy-done.5
  10.3 0.7 copy-done.6
  11.0 1.8 %shard_map.68 = (bf16[4096,128]{1,0:T(8,128)(2,1)S(1)}, bf16[1024,128]{1,0:T(8,128)(2,1)S(1)}, s32[8,10]{1,0:T(8,128)S(1)}, s32[2,8]{1,0:T(2,128)S(1)}) custom-call(s32[8,10]{1,0:T(8,128)S(1)} %bitcast.9, s32[2,8]{1,0:T(2,128)S(1)} %bitcast.10, bf16[128,4096]{1,0:T(8,128)(2,1)S(1)} %bitcast.5, bf16[128,1024]{1,0:T(8,128)(2,1)S(1)} %bitcast.8), custom_call_target="tpu_custom_call" | custom-call | bytes 2097152 | tf_op jit(solution)/shard_map/pallas_call | solution.py:43
  12.8 1.5 %collective-permute-done.2.refs_1_ = bf16[320,128]{1,0:T(8,128)(2,1)S(1)} collective-permute-done((bf16[320,128]{1,0:T(8,128)(2,1)S(1)}, bf16[320,128]{1,0:T(8,128)(2,1)S(1)}, u32[]{:S(2)}, u32[]{:S(2)}) %collective-permute-start.2) | collective-permute-done | bytes 81952 | tf_op jit(solution)/shard_map/ppermute | solution.py:397
  14.3 2.5 %collective-permute-start.9 = (bf16[320,128]{1,0:T(8,128)(2,1)S(1)}, bf16[320,128]{1,0:T(8,128)(2,1)S(1)}, u32[]{:S(2)}, u32[]{:S(2)}) collective-permute-start(bf16[320,128]{1,0:T(8,128)(2,1)S(1)} %shard_map.70.refs_4_.refs_3_.refs_5_), channel_id=1, source_target_pairs={{0,24},{8,16},{16,8},{24,0},{1,25},{9,17},{17,9},{25,1},{2,26},{10... | collective-permute-start | bytes 245768 | tf_op jit(solution)/shard_map/ppermute | solution.py:400
  16.9 0.5 collective-permute-start.7
  17.4 0.5 collective-permute-start.5
  17.9 1.9 %collective-permute-done.9.refs_10_.refs_11_ = bf16[320,128]{1,0:T(8,128)(2,1)S(1)} collective-permute-done((bf16[320,128]{1,0:T(8,128)(2,1)S(1)}, bf16[320,128]{1,0:T(8,128)(2,1)S(1)}, u32[]{:S(2)}, u32[]{:S(2)}) %collective-permute-start.9) | collective-permute-done | bytes 81952 | tf_op jit(solution)/shard_map/ppermute | solution.py:400
  19.9 3.0 %collective-permute-start.13 = (bf16[640,128]{1,0:T(8,128)(2,1)S(1)}, bf16[640,128]{1,0:T(8,128)(2,1)S(1)}, u32[]{:S(2)}, u32[]{:S(2)}) collective-permute-start(bf16[640,128]{1,0:T(8,128)(2,1)S(1)} %shard_map.72.refs_0_), channel_id=1, source_target_pairs={{0,24},{8,16},{16,8},{24,0},{1,25},{9,17},{17,9},{25,1},{2,26},{10... | collective-permute-start | bytes 491528 | tf_op jit(solution)/shard_map/ppermute | solution.py:400
  22.8 0.6 collective-permute-start.12
  23.4 0.2 collective-permute-start.11
  23.6 0.5 collective-permute-start.6
  24.1 0.8 collective-permute-done.8.refs_9_.refs_10_
  24.9 0.2 collective-permute-done.6.refs_7_.refs_8_
  25.1 1.0 %shard_map.71 = (bf16[2560,128]{1,0:T(8,128)(2,1)S(1)}, bf16[128,256]{1,0:T(8,128)(2,1)S(1)}, bf16[128,128]{1,0:T(8,128)(2,1)S(1)}) custom-call(s32[8,10]{1,0:T(8,128)S(1)} %get-tuple-element.35.refs_3_.refs_0_, bf16[128,4096]{1,0:T(8,128)(2,1)S(1)} %bitcast.6, bf16[1280,128]{1,0:T(8,128)(2,1)S(1)} %copy-done.3, ...), custom_call_target="tpu_custom_call" | custom-call | flops 67108864 | bytes 3145728 | tf_op jit(solution)/shard_map/pallas_call | solution.py:43
  26.1 2.5 %collective-permute-start.16 = (bf16[128,256]{1,0:T(8,128)(2,1)S(1)}, bf16[128,256]{1,0:T(8,128)(2,1)S(1)}, u32[]{:S(2)}, u32[]{:S(2)}) collective-permute-start(bf16[128,256]{1,0:T(8,128)(2,1)S(1)} %get-tuple-element.38.refs_15_.refs_4_), channel_id=1, source_target_pairs={{0,6},{1,7},{2,4},{3,5},{4,2},{5,3},{6,0},{7,1},{8,14},{9,15},{10,... | collective-permute-start | bytes 196616 | tf_op jit(solution)/shard_map/ppermute | solution.py:397
  28.6 1.9 %collective-permute-start.14 = (bf16[128,256]{1,0:T(8,128)(2,1)S(1)}, bf16[128,256]{1,0:T(8,128)(2,1)S(1)}, u32[]{:S(2)}, u32[]{:S(2)}) collective-permute-start(bf16[128,256]{1,0:T(8,128)(2,1)S(1)} %get-tuple-element.38.refs_15_.refs_4_), channel_id=1, source_target_pairs={{0,2},{1,3},{2,0},{3,1},{4,6},{5,7},{6,4},{7,5},{8,10},{9,11},{10,... | collective-permute-start | bytes 196616 | tf_op jit(solution)/shard_map/ppermute | solution.py:397
  30.5 0.7 collective-permute-done.12.refs_2_
  31.2 0.4 collective-permute-done.11.refs_1_
  31.7 1.2 %collective-permute-done.16.refs_6_.refs_21_.refs_10_ = bf16[128,256]{1,0:T(8,128)(2,1)S(1)} collective-permute-done((bf16[128,256]{1,0:T(8,128)(2,1)S(1)}, bf16[128,256]{1,0:T(8,128)(2,1)S(1)}, u32[]{:S(2)}, u32[]{:S(2)}) %collective-permute-start.16) | collective-permute-done | bytes 65568 | tf_op jit(solution)/shard_map/ppermute | solution.py:397
  32.9 2.2 %collective-permute-done.15.refs_5_.refs_19_.refs_8_ = bf16[128,256]{1,0:T(8,128)(2,1)S(1)} collective-permute-done((bf16[128,256]{1,0:T(8,128)(2,1)S(1)}, bf16[128,256]{1,0:T(8,128)(2,1)S(1)}, u32[]{:S(2)}, u32[]{:S(2)}) %collective-permute-start.15) | collective-permute-done | bytes 65568 | tf_op jit(solution)/shard_map/ppermute | solution.py:397
  35.2 0.5 collective-permute-start.18
  35.8 0.4 collective-permute-start.20
  36.4 1.0 %collective-permute-done.18.refs_16_.refs_5_ = bf16[128,256]{1,0:T(8,128)(2,1)S(1)} collective-permute-done((bf16[128,256]{1,0:T(8,128)(2,1)S(1)}, bf16[128,256]{1,0:T(8,128)(2,1)S(1)}, u32[]{:S(2)}, u32[]{:S(2)}) %collective-permute-start.18) | collective-permute-done | bytes 65568 | tf_op jit(solution)/shard_map/ppermute | solution.py:391
  37.7 1.7 %shard_map.74 = (bf16[10240,128]{1,0:T(8,128)(2,1)S(1)}, bf16[1024,128]{1,0:T(8,128)(2,1)S(1)}, bf16[1024,128]{1,0:T(8,128)(2,1)S(1)}) custom-call(s32[8,10]{1,0:T(8,128)S(1)} %get-tuple-element.35.refs_3_.refs_0_, bf16[128,4096]{1,0:T(8,128)(2,1)S(1)} %bitcast.7, bf16[2560,128]{1,0:T(8,128)(2,1)S(1)} %get-tuple-element.37.refs_2_, ...), custom_call_target="tpu_custom_call" | custom-call | flops 268435456 | bytes 8388608 | tf_op jit(solution)/shard_map/pallas_call | solution.py:43
  39.4 0.2 collective-permute-start.24
  39.6 3.7 %shard_map.75 = (bf16[8,128,128]{2,1,0:T(8,128)(2,1)S(1)}, bf16[128,256]{1,0:T(8,128)(2,1)S(1)}, bf16[128,256]{1,0:T(8,128)(2,1)S(1)}, bf16[128,256]{1,0:T(8,128...) custom-call(s32[2,8]{1,0:T(2,128)S(1)} %get-tuple-element.36.refs_0_, ...), custom_call_target="tpu_custom_call" | custom-call | flops 671088640 | bytes 4194304 | tf_op jit(solution)/shard_map/pallas_call | solution.py:43
  43.3 0.4 collective-permute-start.27
  43.8 0.4 collective-permute-start.23
  44.3 0.3 collective-permute-done.27
  44.6 0.4 collective-permute-start.25
  45.0 0.5 collective-permute-done.29
  45.5 0.8 collective-permute-start.28
  46.3 2.4 %collective-permute-start.30 = (bf16[128,256]{1,0:T(8,128)(2,1)S(1)}, bf16[128,256]{1,0:T(8,128)(2,1)S(1)}, u32[]{:S(2)}, u32[]{:S(2)}) collective-permute-start(bf16[128,256]{1,0:T(8,128)(2,1)S(1)} %add_convert_fusion.1), channel_id=1, source_target_pairs={{0,6},{1,7},{2,4},{3,5},{4,2},{5,3},{6,0},{7,1},{8,14},{9,15},{10,... | collective-permute-start | bytes 196616 | tf_op jit(solution)/shard_map/ppermute | solution.py:397
  48.7 1.4 %shard_map.77 = (bf16[960,128]{1,0:T(8,128)(2,1)S(1)}, bf16[960,128]{1,0:T(8,128)(2,1)S(1)}, bf16[960,128]{1,0:T(8,128)(2,1)S(1)}, bf16[960,128]{1,0:T(8,128)(2,1)S(1)}) custom-call(s32[8,10]{1,0:T(8,128)S(1)} %get-tuple-element.35.refs_3_.refs_0_, bf16[4096,128]{1,0:T(8,128)(2,1)S(1)} %get-tuple-element.48.refs_1_, ...), custom_call_target="tpu_custom_call" | custom-call | flops 251658240 | bytes 4194304 | tf_op jit(solution)/shard_map/pallas_call | solution.py:43
  50.1 0.5 collective-permute-start.26
  50.5 1.9 %collective-permute-start.31 = (bf16[960,128]{1,0:T(8,128)(2,1)S(1)}, bf16[960,128]{1,0:T(8,128)(2,1)S(1)}, u32[]{:S(2)}, u32[]{:S(2)}) collective-permute-start(bf16[960,128]{1,0:T(8,128)(2,1)S(1)} %get-tuple-element.56), channel_id=1, source_target_pairs={{0,8},{8,0},{16,24},{24,16},{1,9},{9,1},{17,25},{25,17},{2,10},{10... | collective-permute-start | bytes 737288 | tf_op jit(solution)/shard_map/ppermute | solution.py:400
  52.4 1.5 %collective-permute-start.32 = (bf16[960,128]{1,0:T(8,128)(2,1)S(1)}, bf16[960,128]{1,0:T(8,128)(2,1)S(1)}, u32[]{:S(2)}, u32[]{:S(2)}) collective-permute-start(bf16[960,128]{1,0:T(8,128)(2,1)S(1)} %get-tuple-element.57), channel_id=1, source_target_pairs={{0,16},{8,24},{16,0},{24,8},{1,17},{9,25},{17,1},{25,9},{2,18},{10... | collective-permute-start | bytes 737288 | tf_op jit(solution)/shard_map/ppermute | solution.py:400
  53.9 2.4 %collective-permute-start.33 = (bf16[960,128]{1,0:T(8,128)(2,1)S(1)}, bf16[960,128]{1,0:T(8,128)(2,1)S(1)}, u32[]{:S(2)}, u32[]{:S(2)}) collective-permute-start(bf16[960,128]{1,0:T(8,128)(2,1)S(1)} %get-tuple-element.58), channel_id=1, source_target_pairs={{0,24},{8,16},{16,8},{24,0},{1,25},{9,17},{17,9},{25,1},{2,26},{10... | collective-permute-start | bytes 737288 | tf_op jit(solution)/shard_map/ppermute | solution.py:400
  56.6 1.2 %collective-permute-done.34.refs_6_ = bf16[2,128,128]{2,1,0:T(8,128)(2,1)S(1)} collective-permute-done((bf16[2,128,128]{2,1,0:T(8,128)(2,1)S(1)}, bf16[2,128,128]{2,1,0:T(8,128)(2,1)S(1)}, u32[]{:S(2)}, u32[]{:S(2)}) %collective-permute-start.34) | collective-permute-done | bytes 65568 | tf_op jit(solution)/shard_map/ppermute | solution.py:391
  57.8 1.0 %shard_map.81 = (bf16[320,128]{1,0:T(8,128)(2,1)S(1)}, bf16[320,128]{1,0:T(8,128)(2,1)S(1)}, bf16[320,128]{1,0:T(8,128)(2,1)S(1)}, bf16[320,128]{1,0:T(8,128)(2,1)S(1)}) custom-call(s32[8,10]{1,0:T(8,128)S(1)} %get-tuple-element.35.refs_3_.refs_0_, bf16[4096,128]{1,0:T(8,128)(2,1)S(1)} %get-tuple-element.48.refs_1_, ...), custom_call_target="tpu_custom_call" | custom-call | flops 83886080 | bytes 4194304 | tf_op jit(solution)/shard_map/pallas_call | solution.py:43
  58.8 0.7 collective-permute-start.35
  59.5 1.0 %collective-permute-start.36 = (bf16[320,128]{1,0:T(8,128)(2,1)S(1)}, bf16[320,128]{1,0:T(8,128)(2,1)S(1)}, u32[]{:S(2)}, u32[]{:S(2)}) collective-permute-start(bf16[320,128]{1,0:T(8,128)(2,1)S(1)} %get-tuple-element.61), channel_id=1, source_target_pairs={{0,16},{8,24},{16,0},{24,8},{1,17},{9,25},{17,1},{25,9},{2,18},{10... | collective-permute-start | bytes 245768 | tf_op jit(solution)/shard_map/ppermute | solution.py:400
  60.5 1.8 %collective-permute-start.37 = (bf16[320,128]{1,0:T(8,128)(2,1)S(1)}, bf16[320,128]{1,0:T(8,128)(2,1)S(1)}, u32[]{:S(2)}, u32[]{:S(2)}) collective-permute-start(bf16[320,128]{1,0:T(8,128)(2,1)S(1)} %shard_map.82), channel_id=1, source_target_pairs={{0,24},{8,16},{16,8},{24,0},{1,25},{9,17},{17,9},{25,1},{2,26},{10... | collective-permute-start | bytes 245768 | tf_op jit(solution)/shard_map/ppermute | solution.py:400
  62.3 3.0 %shard_map.80 = (bf16[128,4096]{1,0:T(8,128)(2,1)}, f32[8,128]{1,0:T(8,128)S(1)}) custom-call(s32[8,10]{1,0:T(8,128)S(1)} %get-tuple-element.35.refs_3_.refs_0_, bf16[8,128,128]{2,1,0:T(8,128)(2,1)S(1)} %get-tuple-element.42.refs_3_.refs_1_, bf16[2,128,128]{2,1,0:T(8,128)(2,1)S(1)} %shard_map.79.refs_2_.refs_5_, bf16[10240,128]{1,0:T(8,128)(2,1)S(1)} %get-tuple-element.54.refs_3_), custom_call_target="tpu_custom_call" | custom-call | flops 335544320 | bytes 4194304 | tf_op jit(solution)/shard_map/pallas_call | solution.py:43
  65.3 0.4 collective-permute-done.35.refs_5_
  65.6 2.5 %collective-permute-done.36.refs_6_ = bf16[320,128]{1,0:T(8,128)(2,1)S(1)} collective-permute-done((bf16[320,128]{1,0:T(8,128)(2,1)S(1)}, bf16[320,128]{1,0:T(8,128)(2,1)S(1)}, u32[]{:S(2)}, u32[]{:S(2)}) %collective-permute-start.36) | collective-permute-done | bytes 81952 | tf_op jit(solution)/shard_map/ppermute | solution.py:400
  68.1 0.3 shard_map.83
  68.4 1.7 %collective-permute-start.38 = (bf16[320,128]{1,0:T(8,128)(2,1)S(1)}, bf16[320,128]{1,0:T(8,128)(2,1)S(1)}, u32[]{:S(2)}, u32[]{:S(2)}) collective-permute-start(bf16[320,128]{1,0:T(8,128)(2,1)S(1)} %get-tuple-element.65), channel_id=1, source_target_pairs={{0,2},{1,3},{2,0},{3,1},{4,6},{5,7},{6,4},{7,5},{8,10},{9,11},{10,... | collective-permute-start | bytes 245768 | tf_op jit(solution)/shard_map/ppermute | solution.py:397
  70.1 1.4 %collective-permute-start.39 = (bf16[320,128]{1,0:T(8,128)(2,1)S(1)}, bf16[320,128]{1,0:T(8,128)(2,1)S(1)}, u32[]{:S(2)}, u32[]{:S(2)}) collective-permute-start(bf16[320,128]{1,0:T(8,128)(2,1)S(1)} %get-tuple-element.66), channel_id=1, source_target_pairs={{0,4},{1,5},{2,6},{3,7},{4,0},{5,1},{6,2},{7,3},{8,12},{9,13},{10,... | collective-permute-start | bytes 245768 | tf_op jit(solution)/shard_map/ppermute | solution.py:397
  71.5 1.4 %collective-permute-start.40 = (bf16[320,128]{1,0:T(8,128)(2,1)S(1)}, bf16[320,128]{1,0:T(8,128)(2,1)S(1)}, u32[]{:S(2)}, u32[]{:S(2)}) collective-permute-start(bf16[320,128]{1,0:T(8,128)(2,1)S(1)} %get-tuple-element.67), channel_id=1, source_target_pairs={{0,6},{1,7},{2,4},{3,5},{4,2},{5,3},{6,0},{7,1},{8,14},{9,15},{10,... | collective-permute-start | bytes 245768 | tf_op jit(solution)/shard_map/ppermute | solution.py:397
  72.9 0.9 %collective-permute-done.38 = bf16[320,128]{1,0:T(8,128)(2,1)S(1)} collective-permute-done((bf16[320,128]{1,0:T(8,128)(2,1)S(1)}, bf16[320,128]{1,0:T(8,128)(2,1)S(1)}, u32[]{:S(2)}, u32[]{:S(2)}) %collective-permute-start.38) | collective-permute-done | bytes 81952 | tf_op jit(solution)/shard_map/ppermute | solution.py:397
  73.8 4.9 %collective-permute-done.39 = bf16[320,128]{1,0:T(8,128)(2,1)S(1)} collective-permute-done((bf16[320,128]{1,0:T(8,128)(2,1)S(1)}, bf16[320,128]{1,0:T(8,128)(2,1)S(1)}, u32[]{:S(2)}, u32[]{:S(2)}) %collective-permute-start.39) | collective-permute-done | bytes 81952 | tf_op jit(solution)/shard_map/ppermute | solution.py:397
  78.8 1.9 %collective-permute-start.43 = (bf16[320,128]{1,0:T(8,128)(2,1)S(1)}, bf16[320,128]{1,0:T(8,128)(2,1)S(1)}, u32[]{:S(2)}, u32[]{:S(2)}) collective-permute-start(bf16[320,128]{1,0:T(8,128)(2,1)S(1)} %add_convert_fusion.refs_0_), channel_id=1, source_target_pairs={{0,24},{8,16},{16,8},{24,0},{1,25},{9,17},{17,9},{25,1},{2,26},{10... | collective-permute-start | bytes 245768 | tf_op jit(solution)/shard_map/ppermute | solution.py:400
  80.7 1.6 %collective-permute-start.41 = (bf16[320,128]{1,0:T(8,128)(2,1)S(1)}, bf16[320,128]{1,0:T(8,128)(2,1)S(1)}, u32[]{:S(2)}, u32[]{:S(2)}) collective-permute-start(bf16[320,128]{1,0:T(8,128)(2,1)S(1)} %add_convert_fusion.refs_0_), channel_id=1, source_target_pairs={{0,8},{8,0},{16,24},{24,16},{1,9},{9,1},{17,25},{25,17},{2,10},{10... | collective-permute-start | bytes 245768 | tf_op jit(solution)/shard_map/ppermute | solution.py:400
  82.3 1.9 %collective-permute-done.43.refs_3_ = bf16[320,128]{1,0:T(8,128)(2,1)S(1)} collective-permute-done((bf16[320,128]{1,0:T(8,128)(2,1)S(1)}, bf16[320,128]{1,0:T(8,128)(2,1)S(1)}, u32[]{:S(2)}, u32[]{:S(2)}) %collective-permute-start.43) | collective-permute-done | bytes 81952 | tf_op jit(solution)/shard_map/ppermute | solution.py:400
  84.2 1.0 %collective-permute-done.42.refs_2_ = bf16[320,128]{1,0:T(8,128)(2,1)S(1)} collective-permute-done((bf16[320,128]{1,0:T(8,128)(2,1)S(1)}, bf16[320,128]{1,0:T(8,128)(2,1)S(1)}, u32[]{:S(2)}, u32[]{:S(2)}) %collective-permute-start.42) | collective-permute-done | bytes 81952 | tf_op jit(solution)/shard_map/ppermute | solution.py:400
  85.2 0.9 %shard_map.84 = f32[1280,128]{1,0:T(8,128)} custom-call(bf16[320,128]{1,0:T(8,128)(2,1)S(1)} %add_convert_fusion.refs_0_, bf16[320,128]{1,0:T(8,128)(2,1)S(1)} %collective-permute-done.41.refs_1_, bf16[320,128]{1,0:T(8,128)(2,1)S(1)} %collective-permute-done.42.refs_2_, bf16[320,128]{1,0:T(8,128)(2,1)S(1)} %collective-permute-done.43.refs_3_), custom_call_target="tpu_custom_call" | custom-call | bytes 1048576 | tf_op jit(solution)/shard_map/pallas_call | solution.py:43
  (61 shorter events, 1.4 us)
Async XLA Ops:
  0.6 13.7 %collective-permute-start = (bf16[1280,128]{1,0:T(8,128)(2,1)}, bf16[1280,128]{1,0:T(8,128)(2,1)S(1)}, u32[]{:S(2)}, u32[]{:S(2)}) collective-permute-start(bf16[1280,128]{1,0:T(8,128)(2,1)} %refs_3_.1), channel_id=1, source_target_pairs={{0,1},{1,0},{2,3},{3,2},{4,5},{5,4},{6,7},{7,6},{8,9},{9,8},{10,11... | collective-permute-start | bytes 983048 | tf_op jit(solution)/shard_map/ppermute | solution.py:391
  1.1 1.0 %copy-start.2 = (bf16[1280,128]{1,0:T(8,128)(2,1)S(1)}, bf16[1280,128]{1,0:T(8,128)(2,1)}, u32[]{:S(2)}) copy-start(bf16[1280,128]{1,0:T(8,128)(2,1)} %refs_3_.1) | copy-start | bytes 983044
  2.1 22.9 %copy-start.3 = (bf16[1280,128]{1,0:T(8,128)(2,1)S(1)}, bf16[1280,128]{1,0:T(8,128)(2,1)}, u32[]{:S(2)}) copy-start(bf16[1280,128]{1,0:T(8,128)(2,1)} %refs_3_.1) | copy-start | bytes 983044
  2.1 10.7 %collective-permute-start.3 = (bf16[320,128]{1,0:T(8,128)(2,1)S(1)}, bf16[320,128]{1,0:T(8,128)(2,1)S(1)}, u32[]{:S(2)}, u32[]{:S(2)}) collective-permute-start(bf16[320,128]{1,0:T(8,128)(2,1)S(1)} %shard_map.69), channel_id=1, source_target_pairs={{0,6},{1,7},{2,4},{3,5},{4,2},{5,3},{6,0},{7,1},{8,14},{9,15},{10,... | collective-permute-start | bytes 245768 | tf_op jit(solution)/shard_map/ppermute | solution.py:397
  6.8 7.5 %collective-permute-start.2 = (bf16[320,128]{1,0:T(8,128)(2,1)S(1)}, bf16[320,128]{1,0:T(8,128)(2,1)S(1)}, u32[]{:S(2)}, u32[]{:S(2)}) collective-permute-start(bf16[320,128]{1,0:T(8,128)(2,1)S(1)} %shard_map.69), channel_id=1, source_target_pairs={{0,4},{1,5},{2,6},{3,7},{4,0},{5,1},{6,2},{7,3},{8,12},{9,13},{10,... | collective-permute-start | bytes 245768 | tf_op jit(solution)/shard_map/ppermute | solution.py:397
  6.8 7.5 %collective-permute-start.1 = (bf16[320,128]{1,0:T(8,128)(2,1)S(1)}, bf16[320,128]{1,0:T(8,128)(2,1)S(1)}, u32[]{:S(2)}, u32[]{:S(2)}) collective-permute-start(bf16[320,128]{1,0:T(8,128)(2,1)S(1)} %shard_map.69), channel_id=1, source_target_pairs={{0,2},{1,3},{2,0},{3,1},{4,6},{5,7},{6,4},{7,5},{8,10},{9,11},{10,... | collective-permute-start | bytes 245768 | tf_op jit(solution)/shard_map/ppermute | solution.py:397
  7.5 1.2 %copy-start = (bf16[1,128,4096]{2,1,0:T(8,128)(2,1)S(1)}, bf16[1,128,4096]{2,1,0:T(8,128)(2,1)}, u32[]{:S(2)}) copy-start(bf16[1,128,4096]{2,1,0:T(8,128)(2,1)} %param.5) | copy-start | bytes 3145732
  8.7 0.9 %copy-start.4 = (bf16[1,128,1024]{2,1,0:T(8,128)(2,1)S(1)}, bf16[1,128,1024]{2,1,0:T(8,128)(2,1)}, u32[]{:S(2)}) copy-start(bf16[1,128,1024]{2,1,0:T(8,128)(2,1)} %param.6) | copy-start | bytes 786436
  9.6 0.7 copy-start.5
  10.3 0.7 copy-start.6
  11.0 14.1 %copy-start.1 = (bf16[1,128,4096]{2,1,0:T(8,128)(2,1)S(1)}, bf16[1,128,4096]{2,1,0:T(8,128)(2,1)}, u32[]{:S(2)}) copy-start(bf16[1,128,4096]{2,1,0:T(8,128)(2,1)} %param.5) | copy-start | bytes 3145732
  14.3 5.5 %collective-permute-start.9 = (bf16[320,128]{1,0:T(8,128)(2,1)S(1)}, bf16[320,128]{1,0:T(8,128)(2,1)S(1)}, u32[]{:S(2)}, u32[]{:S(2)}) collective-permute-start(bf16[320,128]{1,0:T(8,128)(2,1)S(1)} %shard_map.70.refs_4_.refs_3_.refs_5_), channel_id=1, source_target_pairs={{0,24},{8,16},{16,8},{24,0},{1,25},{9,17},{17,9},{25,1},{2,26},{10... | collective-permute-start | bytes 245768 | tf_op jit(solution)/shard_map/ppermute | solution.py:400
  16.9 6.0 %collective-permute-start.7 = (bf16[320,128]{1,0:T(8,128)(2,1)S(1)}, bf16[320,128]{1,0:T(8,128)(2,1)S(1)}, u32[]{:S(2)}, u32[]{:S(2)}) collective-permute-start(bf16[320,128]{1,0:T(8,128)(2,1)S(1)} %shard_map.70.refs_4_.refs_3_.refs_5_), channel_id=1, source_target_pairs={{0,16},{8,24},{16,0},{24,8},{1,17},{9,25},{17,1},{25,9},{2,18},{10... | collective-permute-start | bytes 245768 | tf_op jit(solution)/shard_map/ppermute | solution.py:400
  17.4 6.1 %collective-permute-start.5 = (bf16[320,128]{1,0:T(8,128)(2,1)S(1)}, bf16[320,128]{1,0:T(8,128)(2,1)S(1)}, u32[]{:S(2)}, u32[]{:S(2)}) collective-permute-start(bf16[320,128]{1,0:T(8,128)(2,1)S(1)} %shard_map.70.refs_4_.refs_3_.refs_5_), channel_id=1, source_target_pairs={{0,8},{8,0},{16,24},{24,16},{1,9},{9,1},{17,25},{25,17},{2,10},{10... | collective-permute-start | bytes 245768 | tf_op jit(solution)/shard_map/ppermute | solution.py:400
  17.9 5.7 %collective-permute-start.4 = (bf16[320,128]{1,0:T(8,128)(2,1)S(1)}, bf16[320,128]{1,0:T(8,128)(2,1)S(1)}, u32[]{:S(2)}, u32[]{:S(2)}) collective-permute-start(bf16[320,128]{1,0:T(8,128)(2,1)S(1)} %shard_map.70.refs_4_.refs_3_.refs_5_), channel_id=1, source_target_pairs={{0,1},{1,0},{2,3},{3,2},{4,5},{5,4},{6,7},{7,6},{8,9},{9,8},{10,11... | collective-permute-start | bytes 245768 | tf_op jit(solution)/shard_map/ppermute | solution.py:391
  19.8 3.8 %collective-permute-start.10 = (bf16[320,128]{1,0:T(8,128)(2,1)S(1)}, bf16[320,128]{1,0:T(8,128)(2,1)S(1)}, u32[]{:S(2)}, u32[]{:S(2)}) collective-permute-start(bf16[320,128]{1,0:T(8,128)(2,1)S(1)} %collective-permute-done.9.refs_10_.refs_11_), channel_id=1, source_target_pairs={{0,1},{1,0},{2,3},{3,2},{4,5},{5,4},{6,7},{7,6},{8,9},{9,8},{10,11... | collective-permute-start | bytes 245768 | tf_op jit(solution)/shard_map/ppermute | solution.py:391
  19.9 8.7 %collective-permute-start.13 = (bf16[640,128]{1,0:T(8,128)(2,1)S(1)}, bf16[640,128]{1,0:T(8,128)(2,1)S(1)}, u32[]{:S(2)}, u32[]{:S(2)}) collective-permute-start(bf16[640,128]{1,0:T(8,128)(2,1)S(1)} %shard_map.72.refs_0_), channel_id=1, source_target_pairs={{0,24},{8,16},{16,8},{24,0},{1,25},{9,17},{17,9},{25,1},{2,26},{10... | collective-permute-start | bytes 491528 | tf_op jit(solution)/shard_map/ppermute | solution.py:400
  22.8 8.4 %collective-permute-start.12 = (bf16[640,128]{1,0:T(8,128)(2,1)S(1)}, bf16[640,128]{1,0:T(8,128)(2,1)S(1)}, u32[]{:S(2)}, u32[]{:S(2)}) collective-permute-start(bf16[640,128]{1,0:T(8,128)(2,1)S(1)} %shard_map.72.refs_0_), channel_id=1, source_target_pairs={{0,16},{8,24},{16,0},{24,8},{1,17},{9,25},{17,1},{25,9},{2,18},{10... | collective-permute-start | bytes 491528 | tf_op jit(solution)/shard_map/ppermute | solution.py:400
  23.4 8.2 %collective-permute-start.11 = (bf16[640,128]{1,0:T(8,128)(2,1)S(1)}, bf16[640,128]{1,0:T(8,128)(2,1)S(1)}, u32[]{:S(2)}, u32[]{:S(2)}) collective-permute-start(bf16[640,128]{1,0:T(8,128)(2,1)S(1)} %shard_map.72.refs_0_), channel_id=1, source_target_pairs={{0,8},{8,0},{16,24},{24,16},{1,9},{9,1},{17,25},{25,17},{2,10},{10... | collective-permute-start | bytes 491528 | tf_op jit(solution)/shard_map/ppermute | solution.py:400
  23.6 1.3 %collective-permute-start.8 = (bf16[320,128]{1,0:T(8,128)(2,1)S(1)}, bf16[320,128]{1,0:T(8,128)(2,1)S(1)}, u32[]{:S(2)}, u32[]{:S(2)}) collective-permute-start(bf16[320,128]{1,0:T(8,128)(2,1)S(1)} %collective-permute-done.7.refs_8_.refs_9_), channel_id=1, source_target_pairs={{0,1},{1,0},{2,3},{3,2},{4,5},{5,4},{6,7},{7,6},{8,9},{9,8},{10,11... | collective-permute-start | bytes 245768 | tf_op jit(solution)/shard_map/ppermute | solution.py:391
  23.6 1.4 %collective-permute-start.6 = (bf16[320,128]{1,0:T(8,128)(2,1)S(1)}, bf16[320,128]{1,0:T(8,128)(2,1)S(1)}, u32[]{:S(2)}, u32[]{:S(2)}) collective-permute-start(bf16[320,128]{1,0:T(8,128)(2,1)S(1)} %collective-permute-done.5.refs_6_.refs_7_), channel_id=1, source_target_pairs={{0,1},{1,0},{2,3},{3,2},{4,5},{5,4},{6,7},{7,6},{8,9},{9,8},{10,11... | collective-permute-start | bytes 245768 | tf_op jit(solution)/shard_map/ppermute | solution.py:391
  26.1 6.8 %collective-permute-start.16 = (bf16[128,256]{1,0:T(8,128)(2,1)S(1)}, bf16[128,256]{1,0:T(8,128)(2,1)S(1)}, u32[]{:S(2)}, u32[]{:S(2)}) collective-permute-start(bf16[128,256]{1,0:T(8,128)(2,1)S(1)} %get-tuple-element.38.refs_15_.refs_4_), channel_id=1, source_target_pairs={{0,6},{1,7},{2,4},{3,5},{4,2},{5,3},{6,0},{7,1},{8,14},{9,15},{10,... | collective-permute-start | bytes 196616 | tf_op jit(solution)/shard_map/ppermute | solution.py:397
  28.6 6.5 %collective-permute-start.15 = (bf16[128,256]{1,0:T(8,128)(2,1)S(1)}, bf16[128,256]{1,0:T(8,128)(2,1)S(1)}, u32[]{:S(2)}, u32[]{:S(2)}) collective-permute-start(bf16[128,256]{1,0:T(8,128)(2,1)S(1)} %get-tuple-element.38.refs_15_.refs_4_), channel_id=1, source_target_pairs={{0,4},{1,5},{2,6},{3,7},{4,0},{5,1},{6,2},{7,3},{8,12},{9,13},{10,... | collective-permute-start | bytes 196616 | tf_op jit(solution)/shard_map/ppermute | solution.py:397
  28.6 6.5 %collective-permute-start.14 = (bf16[128,256]{1,0:T(8,128)(2,1)S(1)}, bf16[128,256]{1,0:T(8,128)(2,1)S(1)}, u32[]{:S(2)}, u32[]{:S(2)}) collective-permute-start(bf16[128,256]{1,0:T(8,128)(2,1)S(1)} %get-tuple-element.38.refs_15_.refs_4_), channel_id=1, source_target_pairs={{0,2},{1,3},{2,0},{3,1},{4,6},{5,7},{6,4},{7,5},{8,10},{9,11},{10,... | collective-permute-start | bytes 196616 | tf_op jit(solution)/shard_map/ppermute | solution.py:397
  35.1 2.5 %collective-permute-start.17 = (bf16[2560,128]{1,0:T(8,128)(2,1)S(1)}, bf16[2560,128]{1,0:T(8,128)(2,1)S(1)}, u32[]{:S(2)}, u32[]{:S(2)}) collective-permute-start(bf16[2560,128]{1,0:T(8,128)(2,1)S(1)} %shard_map.73.refs_13_), channel_id=1, source_target_pairs={{0,1},{1,0},{2,3},{3,2},{4,5},{5,4},{6,7},{7,6},{8,9},{9,8},{10,11... | collective-permute-start | bytes 1966088 | tf_op jit(solution)/shard_map/ppermute | solution.py:391
  35.2 2.2 %collective-permute-start.18 = (bf16[128,256]{1,0:T(8,128)(2,1)S(1)}, bf16[128,256]{1,0:T(8,128)(2,1)S(1)}, u32[]{:S(2)}, u32[]{:S(2)}) collective-permute-start(bf16[128,256]{1,0:T(8,128)(2,1)S(1)} %get-tuple-element.38.refs_15_.refs_4_), channel_id=1, source_target_pairs={{0,1},{1,0},{2,3},{3,2},{4,5},{5,4},{6,7},{7,6},{8,9},{9,8},{10,11... | collective-permute-start | bytes 196616 | tf_op jit(solution)/shard_map/ppermute | solution.py:391
  35.7 1.8 %collective-permute-start.21 = (bf16[128,256]{1,0:T(8,128)(2,1)S(1)}, bf16[128,256]{1,0:T(8,128)(2,1)S(1)}, u32[]{:S(2)}, u32[]{:S(2)}) collective-permute-start(bf16[128,256]{1,0:T(8,128)(2,1)S(1)} %collective-permute-done.16.refs_6_.refs_21_.refs_10_), channel_id=1, source_target_pairs={{0,1},{1,0},{2,3},{3,2},{4,5},{5,4},{6,7},{7,6},{8,9},{9,8},{10,11... | collective-permute-start | bytes 196616 | tf_op jit(solution)/shard_map/ppermute | solution.py:391
  35.8 1.8 %collective-permute-start.20 = (bf16[128,256]{1,0:T(8,128)(2,1)S(1)}, bf16[128,256]{1,0:T(8,128)(2,1)S(1)}, u32[]{:S(2)}, u32[]{:S(2)}) collective-permute-start(bf16[128,256]{1,0:T(8,128)(2,1)S(1)} %collective-permute-done.15.refs_5_.refs_19_.refs_8_), channel_id=1, source_target_pairs={{0,1},{1,0},{2,3},{3,2},{4,5},{5,4},{6,7},{7,6},{8,9},{9,8},{10,11... | collective-permute-start | bytes 196616 | tf_op jit(solution)/shard_map/ppermute | solution.py:391
  36.2 1.5 %collective-permute-start.19 = (bf16[128,256]{1,0:T(8,128)(2,1)S(1)}, bf16[128,256]{1,0:T(8,128)(2,1)S(1)}, u32[]{:S(2)}, u32[]{:S(2)}) collective-permute-start(bf16[128,256]{1,0:T(8,128)(2,1)S(1)} %collective-permute-done.14.refs_4_.refs_17_.refs_6_), channel_id=1, source_target_pairs={{0,1},{1,0},{2,3},{3,2},{4,5},{5,4},{6,7},{7,6},{8,9},{9,8},{10,11... | collective-permute-start | bytes 196616 | tf_op jit(solution)/shard_map/ppermute | solution.py:391
  39.4 9.3 %collective-permute-start.24 = (bf16[4096,128]{1,0:T(8,128)(2,1)S(1)}, bf16[4096,128]{1,0:T(8,128)(2,1)S(1)}, u32[]{:S(2)}, u32[]{:S(2)}) collective-permute-start(bf16[4096,128]{1,0:T(8,128)(2,1)S(1)} %shard_map.76), channel_id=1, source_target_pairs={{0,1},{1,0},{2,3},{3,2},{4,5},{5,4},{6,7},{7,6},{8,9},{9,8},{10,11... | collective-permute-start | bytes 3145736 | tf_op jit(solution)/shard_map/ppermute | solution.py:391
  43.3 1.3 %collective-permute-start.27 = (bf16[128,256]{1,0:T(8,128)(2,1)S(1)}, bf16[128,256]{1,0:T(8,128)(2,1)S(1)}, u32[]{:S(2)}, u32[]{:S(2)}) collective-permute-start(bf16[128,256]{1,0:T(8,128)(2,1)S(1)} %get-tuple-element.51), channel_id=1, source_target_pairs={{0,1},{1,0},{2,3},{3,2},{4,5},{5,4},{6,7},{7,6},{8,9},{9,8},{10,11... | collective-permute-start | bytes 196616 | tf_op jit(solution)/shard_map/ppermute | solution.py:391
  43.7 8.7 %collective-permute-start.22 = (bf16[128,256]{1,0:T(8,128)(2,1)S(1)}, bf16[128,256]{1,0:T(8,128)(2,1)S(1)}, u32[]{:S(2)}, u32[]{:S(2)}) collective-permute-start(bf16[128,256]{1,0:T(8,128)(2,1)S(1)} %get-tuple-element.45), channel_id=1, source_target_pairs={{0,1},{1,0},{2,3},{3,2},{4,5},{5,4},{6,7},{7,6},{8,9},{9,8},{10,11... | collective-permute-start | bytes 196616 | tf_op jit(solution)/shard_map/ppermute | solution.py:391
  43.8 2.4 %collective-permute-start.23 = (bf16[128,256]{1,0:T(8,128)(2,1)S(1)}, bf16[128,256]{1,0:T(8,128)(2,1)S(1)}, u32[]{:S(2)}, u32[]{:S(2)}) collective-permute-start(bf16[128,256]{1,0:T(8,128)(2,1)S(1)} %get-tuple-element.47), channel_id=1, source_target_pairs={{0,1},{1,0},{2,3},{3,2},{4,5},{5,4},{6,7},{7,6},{8,9},{9,8},{10,11... | collective-permute-start | bytes 196616 | tf_op jit(solution)/shard_map/ppermute | solution.py:391
  44.2 1.3 %collective-permute-start.29 = (bf16[128,256]{1,0:T(8,128)(2,1)S(1)}, bf16[128,256]{1,0:T(8,128)(2,1)S(1)}, u32[]{:S(2)}, u32[]{:S(2)}) collective-permute-start(bf16[128,256]{1,0:T(8,128)(2,1)S(1)} %get-tuple-element.53), channel_id=1, source_target_pairs={{0,1},{1,0},{2,3},{3,2},{4,5},{5,4},{6,7},{7,6},{8,9},{9,8},{10,11... | collective-permute-start | bytes 196616 | tf_op jit(solution)/shard_map/ppermute | solution.py:391
  44.6 4.1 %collective-permute-start.25 = (bf16[8,128,128]{2,1,0:T(8,128)(2,1)S(1)}, bf16[8,128,128]{2,1,0:T(8,128)(2,1)S(1)}, u32[]{:S(2)}, u32[]{:S(2)}) collective-permute-start(bf16[8,128,128]{2,1,0:T(8,128)(2,1)S(1)} %get-tuple-element.42.refs_3_.refs_1_), channel_id=1, source_target_pairs={{0,1},{1,0},{2,3},{3,2},{4,5},{5,4},{6,7},{7,6},{8,9},{9,8},{10,11... | collective-permute-start | bytes 786440 | tf_op jit(solution)/shard_map/ppermute | solution.py:391
  45.5 8.4 %collective-permute-start.28 = (bf16[128,256]{1,0:T(8,128)(2,1)S(1)}, bf16[128,256]{1,0:T(8,128)(2,1)S(1)}, u32[]{:S(2)}, u32[]{:S(2)}) collective-permute-start(bf16[128,256]{1,0:T(8,128)(2,1)S(1)} %add_convert_fusion.2), channel_id=1, source_target_pairs={{0,4},{1,5},{2,6},{3,7},{4,0},{5,1},{6,2},{7,3},{8,12},{9,13},{10,... | collective-permute-start | bytes 196616 | tf_op jit(solution)/shard_map/ppermute | solution.py:397
  46.3 10.1 %collective-permute-start.30 = (bf16[128,256]{1,0:T(8,128)(2,1)S(1)}, bf16[128,256]{1,0:T(8,128)(2,1)S(1)}, u32[]{:S(2)}, u32[]{:S(2)}) collective-permute-start(bf16[128,256]{1,0:T(8,128)(2,1)S(1)} %add_convert_fusion.1), channel_id=1, source_target_pairs={{0,6},{1,7},{2,4},{3,5},{4,2},{5,3},{6,0},{7,1},{8,14},{9,15},{10,... | collective-permute-start | bytes 196616 | tf_op jit(solution)/shard_map/ppermute | solution.py:397
  50.1 6.3 %collective-permute-start.26 = (bf16[128,256]{1,0:T(8,128)(2,1)S(1)}, bf16[128,256]{1,0:T(8,128)(2,1)S(1)}, u32[]{:S(2)}, u32[]{:S(2)}) collective-permute-start(bf16[128,256]{1,0:T(8,128)(2,1)S(1)} %shard_map.78), channel_id=1, source_target_pairs={{0,2},{1,3},{2,0},{3,1},{4,6},{5,7},{6,4},{7,5},{8,10},{9,11},{10,... | collective-permute-start | bytes 196616 | tf_op jit(solution)/shard_map/ppermute | solution.py:397
  50.5 10.0 %collective-permute-start.31 = (bf16[960,128]{1,0:T(8,128)(2,1)S(1)}, bf16[960,128]{1,0:T(8,128)(2,1)S(1)}, u32[]{:S(2)}, u32[]{:S(2)}) collective-permute-start(bf16[960,128]{1,0:T(8,128)(2,1)S(1)} %get-tuple-element.56), channel_id=1, source_target_pairs={{0,8},{8,0},{16,24},{24,16},{1,9},{9,1},{17,25},{25,17},{2,10},{10... | collective-permute-start | bytes 737288 | tf_op jit(solution)/shard_map/ppermute | solution.py:400
  52.4 15.7 %collective-permute-start.32 = (bf16[960,128]{1,0:T(8,128)(2,1)S(1)}, bf16[960,128]{1,0:T(8,128)(2,1)S(1)}, u32[]{:S(2)}, u32[]{:S(2)}) collective-permute-start(bf16[960,128]{1,0:T(8,128)(2,1)S(1)} %get-tuple-element.57), channel_id=1, source_target_pairs={{0,16},{8,24},{16,0},{24,8},{1,17},{9,25},{17,1},{25,9},{2,18},{10... | collective-permute-start | bytes 737288 | tf_op jit(solution)/shard_map/ppermute | solution.py:400
  53.9 14.2 %collective-permute-start.33 = (bf16[960,128]{1,0:T(8,128)(2,1)S(1)}, bf16[960,128]{1,0:T(8,128)(2,1)S(1)}, u32[]{:S(2)}, u32[]{:S(2)}) collective-permute-start(bf16[960,128]{1,0:T(8,128)(2,1)S(1)} %get-tuple-element.58), channel_id=1, source_target_pairs={{0,24},{8,16},{16,8},{24,0},{1,25},{9,17},{17,9},{25,1},{2,26},{10... | collective-permute-start | bytes 737288 | tf_op jit(solution)/shard_map/ppermute | solution.py:400
  56.5 1.3 %collective-permute-start.34 = (bf16[2,128,128]{2,1,0:T(8,128)(2,1)S(1)}, bf16[2,128,128]{2,1,0:T(8,128)(2,1)S(1)}, u32[]{:S(2)}, u32[]{:S(2)}) collective-permute-start(bf16[2,128,128]{2,1,0:T(8,128)(2,1)S(1)} %shard_map.79.refs_2_.refs_5_), channel_id=1, source_target_pairs={{0,1},{1,0},{2,3},{3,2},{4,5},{5,4},{6,7},{7,6},{8,9},{9,8},{10,11... | collective-permute-start | bytes 196616 | tf_op jit(solution)/shard_map/ppermute | solution.py:391
  58.8 6.9 %collective-permute-start.35 = (bf16[320,128]{1,0:T(8,128)(2,1)S(1)}, bf16[320,128]{1,0:T(8,128)(2,1)S(1)}, u32[]{:S(2)}, u32[]{:S(2)}) collective-permute-start(bf16[320,128]{1,0:T(8,128)(2,1)S(1)} %get-tuple-element.60), channel_id=1, source_target_pairs={{0,8},{8,0},{16,24},{24,16},{1,9},{9,1},{17,25},{25,17},{2,10},{10... | collective-permute-start | bytes 245768 | tf_op jit(solution)/shard_map/ppermute | solution.py:400
  59.5 8.6 %collective-permute-start.36 = (bf16[320,128]{1,0:T(8,128)(2,1)S(1)}, bf16[320,128]{1,0:T(8,128)(2,1)S(1)}, u32[]{:S(2)}, u32[]{:S(2)}) collective-permute-start(bf16[320,128]{1,0:T(8,128)(2,1)S(1)} %get-tuple-element.61), channel_id=1, source_target_pairs={{0,16},{8,24},{16,0},{24,8},{1,17},{9,25},{17,1},{25,9},{2,18},{10... | collective-permute-start | bytes 245768 | tf_op jit(solution)/shard_map/ppermute | solution.py:400
  60.5 7.6 %collective-permute-start.37 = (bf16[320,128]{1,0:T(8,128)(2,1)S(1)}, bf16[320,128]{1,0:T(8,128)(2,1)S(1)}, u32[]{:S(2)}, u32[]{:S(2)}) collective-permute-start(bf16[320,128]{1,0:T(8,128)(2,1)S(1)} %shard_map.82), channel_id=1, source_target_pairs={{0,24},{8,16},{16,8},{24,0},{1,25},{9,17},{17,9},{25,1},{2,26},{10... | collective-permute-start | bytes 245768 | tf_op jit(solution)/shard_map/ppermute | solution.py:400
  68.4 5.4 %collective-permute-start.38 = (bf16[320,128]{1,0:T(8,128)(2,1)S(1)}, bf16[320,128]{1,0:T(8,128)(2,1)S(1)}, u32[]{:S(2)}, u32[]{:S(2)}) collective-permute-start(bf16[320,128]{1,0:T(8,128)(2,1)S(1)} %get-tuple-element.65), channel_id=1, source_target_pairs={{0,2},{1,3},{2,0},{3,1},{4,6},{5,7},{6,4},{7,5},{8,10},{9,11},{10,... | collective-permute-start | bytes 245768 | tf_op jit(solution)/shard_map/ppermute | solution.py:397
  70.1 8.6 %collective-permute-start.39 = (bf16[320,128]{1,0:T(8,128)(2,1)S(1)}, bf16[320,128]{1,0:T(8,128)(2,1)S(1)}, u32[]{:S(2)}, u32[]{:S(2)}) collective-permute-start(bf16[320,128]{1,0:T(8,128)(2,1)S(1)} %get-tuple-element.66), channel_id=1, source_target_pairs={{0,4},{1,5},{2,6},{3,7},{4,0},{5,1},{6,2},{7,3},{8,12},{9,13},{10,... | collective-permute-start | bytes 245768 | tf_op jit(solution)/shard_map/ppermute | solution.py:397
  71.5 7.2 %collective-permute-start.40 = (bf16[320,128]{1,0:T(8,128)(2,1)S(1)}, bf16[320,128]{1,0:T(8,128)(2,1)S(1)}, u32[]{:S(2)}, u32[]{:S(2)}) collective-permute-start(bf16[320,128]{1,0:T(8,128)(2,1)S(1)} %get-tuple-element.67), channel_id=1, source_target_pairs={{0,6},{1,7},{2,4},{3,5},{4,2},{5,3},{6,0},{7,1},{8,14},{9,15},{10,... | collective-permute-start | bytes 245768 | tf_op jit(solution)/shard_map/ppermute | solution.py:397
  78.8 5.4 %collective-permute-start.43 = (bf16[320,128]{1,0:T(8,128)(2,1)S(1)}, bf16[320,128]{1,0:T(8,128)(2,1)S(1)}, u32[]{:S(2)}, u32[]{:S(2)}) collective-permute-start(bf16[320,128]{1,0:T(8,128)(2,1)S(1)} %add_convert_fusion.refs_0_), channel_id=1, source_target_pairs={{0,24},{8,16},{16,8},{24,0},{1,25},{9,17},{17,9},{25,1},{2,26},{10... | collective-permute-start | bytes 245768 | tf_op jit(solution)/shard_map/ppermute | solution.py:400
  80.7 4.4 %collective-permute-start.42 = (bf16[320,128]{1,0:T(8,128)(2,1)S(1)}, bf16[320,128]{1,0:T(8,128)(2,1)S(1)}, u32[]{:S(2)}, u32[]{:S(2)}) collective-permute-start(bf16[320,128]{1,0:T(8,128)(2,1)S(1)} %add_convert_fusion.refs_0_), channel_id=1, source_target_pairs={{0,16},{8,24},{16,0},{24,8},{1,17},{9,25},{17,1},{25,9},{2,18},{10... | collective-permute-start | bytes 245768 | tf_op jit(solution)/shard_map/ppermute | solution.py:400
  80.7 4.4 %collective-permute-start.41 = (bf16[320,128]{1,0:T(8,128)(2,1)S(1)}, bf16[320,128]{1,0:T(8,128)(2,1)S(1)}, u32[]{:S(2)}, u32[]{:S(2)}) collective-permute-start(bf16[320,128]{1,0:T(8,128)(2,1)S(1)} %add_convert_fusion.refs_0_), channel_id=1, source_target_pairs={{0,8},{8,0},{16,24},{24,16},{1,9},{9,1},{17,25},{25,17},{2,10},{10... | collective-permute-start | bytes 245768 | tf_op jit(solution)/shard_map/ppermute | solution.py:400

commit v8 on v7

--- a/solution.py
+++ b/solution.py
@@ -224,7 +224,7 @@
     dq_ref = refs[2 * nz]
     keep = refs[2 * nz + 1 : 3 * nz + 1]
     send = refs[3 * nz + 1 : 4 * nz + 1]
-    kv, expo, dprob, acc, dq_t = refs[4 * nz + 1 :]
+    kv, expo, dprob, acc, dq_t, sums = refs[4 * nz + 1 :]
     half = NQ * SPAN
     me = lax.axis_index("ctx")
     zi, core = me // 2, me % 2
@@ -239,43 +239,60 @@
     length = kv.shape[0]
     key_row = lax.broadcasted_iota(jnp.int32, (keys, half), 0)
     query_at = lax.broadcasted_iota(jnp.int32, (keys, half), 1) % SPAN
+    def when_seen(p, at, body):
+        if at <= p * (length // 2):
+            body()
+        else:
+            pl.when(at < (spans[p, me] + 1) * SPAN)(body)
+
+    sums[...] = jnp.zeros_like(sums)
+    acc[length // 2 + keys :, :] = jnp.zeros((length // 2 - keys, 2 * HD), F32)
     for p in (1, 0):
-        reach = length if p == 1 else length // 2
-        sure = length // 2 if p == 1 else 0
-        q_part = qhat[p * half : (p + 1) * half, :]
-        up_part = up[p * half : (p + 1) * half, :]
+        base = 0 if p == 1 else length
         limit = query_at + spans[p, me] * SPAN
-        total = jnp.zeros((8, half), F32)
-        weighted = jnp.zeros((8, half), F32)
-        for at in range(0, reach, keys):
-            rows = slice(at, at + keys)
-            e = jnp.exp2(dot(kv[rows, :HD], q_part, ((1,), (1,))) * (SCALE * LOG2E))
-            if at + keys > sure:
-                e = jnp.where(key_row + at <= limit, e, 0.0)
-            dp = dot(kv[rows, HD:], up_part, ((1,), (1,)))
-            expo[rows, :] = e
-            dprob[rows, :] = dp
-            term = e.astype(BF16).astype(F32) * dp
-            total = total + jnp.sum(e.reshape(keys // 8, 8, half), axis=0)
-            weighted = weighted + jnp.sum(term.reshape(keys // 8, 8, half), axis=0)
-        inverse = 1.0 / jnp.sum(total, axis=0, keepdims=True)
-        delta = jnp.sum(weighted, axis=0, keepdims=True) * inverse
-        for at in range(0, reach, keys):
-            rows = slice(at, at + keys)
-            prob = expo[rows, :] * inverse
-            dscore = (prob * (dprob[rows, :] - delta) * SCALE).astype(BF16)
-            dkey, dvalue = dot(dscore, q_part), dot(prob.astype(BF16), up_part)
-            dq_term = dot(kv[rows, :HD].T, dscore)
-            if p == 1:
-                acc[rows, :HD] = dkey
-                acc[rows, HD:] = dvalue
-            else:
-                acc[rows, :HD] += dkey
-                acc[rows, HD:] += dvalue
-            if at == 0:
-                dq_t[...] = dq_term
-            else:
-                dq_t[...] += dq_term
+        for at in range(0, length // 2 * (p + 1), keys):
+
+            def forward():
+                q_part = qhat[p * half : (p + 1) * half, :]
+                up_part = up[p * half : (p + 1) * half, :]
+                rows, held = slice(at, at + keys), slice(base + at, base + at + keys)
+                e = jnp.exp2(dot(kv[rows, :HD], q_part, ((1,), (1,))) * (SCALE * LOG2E))
+                if at + keys > p * (length // 2):
+                    e = jnp.where(key_row + at <= limit, e, 0.0)
+                dp = dot(kv[rows, HD:], up_part, ((1,), (1,)))
+                expo[held, :] = e
+                dprob[held, :] = dp
+                term = e.astype(BF16).astype(F32) * dp
+                sums[2 * p] += jnp.sum(e.reshape(keys // 8, 8, half), axis=0)
+                sums[2 * p + 1] += jnp.sum(term.reshape(keys // 8, 8, half), axis=0)
+
+            when_seen(p, at, forward)
+    for p in (1, 0):
+        base = 0 if p == 1 else length
+        inverse = 1.0 / jnp.sum(sums[2 * p], axis=0, keepdims=True)
+        delta = jnp.sum(sums[2 * p + 1], axis=0, keepdims=True) * inverse
+        for at in range(0, length // 2 * (p + 1), keys):
+
+            def backward():
+                q_part = qhat[p * half : (p + 1) * half, :]
+                up_part = up[p * half : (p + 1) * half, :]
+                rows, held = slice(at, at + keys), slice(base + at, base + at + keys)
+                prob = expo[held, :] * inverse
+                dscore = (prob * (dprob[held, :] - delta) * SCALE).astype(BF16)
+                dkey, dvalue = dot(dscore, q_part), dot(prob.astype(BF16), up_part)
+                dq_term = dot(kv[rows, :HD].T, dscore)
+                if p == 1 and at <= length // 2:
+                    acc[rows, :HD] = dkey
+                    acc[rows, HD:] = dvalue
+                else:
+                    acc[rows, :HD] += dkey
+                    acc[rows, HD:] += dvalue
+                if at == 0:
+                    dq_t[...] = dq_term
+                else:
+                    dq_t[...] += dq_term
+
+            when_seen(p, at, backward)
         q_rows = q_ref[p * half : (p + 1) * half, :].astype(F32)
         dq = norm_backward(q_rows, inverse_rms(q_rows), dq_t[...].T).astype(BF16)
         for h in range(NQ):
@@ -479,16 +496,17 @@
         kv_pieces = both_cores([kv] + [swap_z(kv, k) for k in range(1, nz)])
 
     outs = call(
-        functools.partial(attend_kernel, nz, math.gcd(512, length // 2)),
+        functools.partial(attend_kernel, nz, math.gcd(256, length // 2)),
         (spans,),
         (query, qhat, up, *kv_pieces),
         [((NQ, tok, HD), BF16)] + [((tok, 2 * HD), BF16)] * (2 * nz),
         scratch=[
             pltpu.VMEM((length, 2 * HD), BF16),
-            pltpu.VMEM((length, half), F32),
-            pltpu.VMEM((length, half), F32),
+            pltpu.VMEM((length + length // 2, half), F32),
+            pltpu.VMEM((length + length // 2, half), F32),
             pltpu.VMEM((length, 2 * HD), F32),
             pltpu.VMEM((HD, half), F32),
+            pltpu.VMEM((4, 8, half), F32),
         ],
         flops=10 * tok * NQ * length * HD // 2,
         moved=4 * 2**20,

time: 86.3 us -> 86.2 us (level)
  no operation moved by 1% of the time
where the time goes in v8:
time: 86.2 us; the launch traced here: 86 us
  starting transfers between devices  41.9 us (49%)
  waiting for transfers between devices  23.8 us (28%)
  Pallas kernels  14.8 us (17%)
  local copies, waits for them, and re-layouts  4.59 us (5%)
    ppermute x15, starting transfers between devices, swap_dp(): return lax.ppermute(v, 'dp', [(i, i ^ k) for i in range(ndp)])  20.1 us
    ppermute x12, starting transfers between devices, swap_z(): return lax.ppermute(v, 'ctx', [(i, i ^ 2 * k) for i in range(nctx)])  17.8 us
    pallas_call x14, Pallas kernels, call(): pl.pallas_call(body, in_specs=[SMEM] * len(scalars) + [VMEM] * len(arrays...  14.8 us
    ppermute x12, waiting for transfers between devices, swap_z(): return lax.ppermute(v, 'ctx', [(i, i ^ 2 * k) for i in range(nctx)])  10.8 us
    ppermute x15, waiting for transfers between devices, swap_dp(): return lax.ppermute(v, 'dp', [(i, i ^ k) for i in range(ndp)])  8.74 us
    unnamed x15, local copies, waits for them, and re-layouts  4.59 us
    ppermute x17, waiting for transfers between devices, swap_core(): return lax.ppermute(v, 'ctx', [(i, i ^ 1) for i in range(nctx)])  4.23 us
    ppermute x17, starting transfers between devices, swap_core(): return lax.ppermute(v, 'ctx', [(i, i ^ 1) for i in range(nctx)])  3.9 us
  transfers between devices with their start and end apart: 44, of which 21 were waited for; matrix products, arithmetic and copies ran while one was open for 0% of the time, Pallas kernels for 14%

profile of v8, /device:TPU:0, one launch (start us, length us, event | category | flops | bytes accessed | tf_op | source)
XLA Modules:
  0.0 86.0 jit_solution(16240503009768051350)
XLA Ops:
  0.6 0.5 collective-permute-start
  1.1 1.0 %copy-done.2 = bf16[1280,128]{1,0:T(8,128)(2,1)S(1)} copy-done((bf16[1280,128]{1,0:T(8,128)(2,1)S(1)}, bf16[1280,128]{1,0:T(8,128)(2,1)}, u32[]{:S(2)}) %copy-start.2) | copy-done | bytes 327704
  2.1 4.7 %collective-permute-start.3 = (bf16[320,128]{1,0:T(8,128)(2,1)S(1)}, bf16[320,128]{1,0:T(8,128)(2,1)S(1)}, u32[]{:S(2)}, u32[]{:S(2)}) collective-permute-start(bf16[320,128]{1,0:T(8,128)(2,1)S(1)} %shard_map.69), channel_id=1, source_target_pairs={{0,6},{1,7},{2,4},{3,5},{4,2},{5,3},{6,0},{7,1},{8,14},{9,15},{10,... | collective-permute-start | bytes 245768 | tf_op jit(solution)/shard_map/ppermute | solution.py:414
  6.8 0.6 collective-permute-start.1
  7.5 1.2 %copy-done = bf16[1,128,4096]{2,1,0:T(8,128)(2,1)S(1)} copy-done((bf16[1,128,4096]{2,1,0:T(8,128)(2,1)S(1)}, bf16[1,128,4096]{2,1,0:T(8,128)(2,1)}, u32[]{:S(2)}) %copy-start) | copy-done | bytes 1048600
  8.7 0.9 %copy-done.4 = bf16[1,128,1024]{2,1,0:T(8,128)(2,1)S(1)} copy-done((bf16[1,128,1024]{2,1,0:T(8,128)(2,1)S(1)}, bf16[1,128,1024]{2,1,0:T(8,128)(2,1)}, u32[]{:S(2)}) %copy-start.4) | copy-done | bytes 262168
  9.6 0.7 copy-done.5
  10.3 0.7 copy-done.6
  11.0 1.8 %shard_map.68 = (bf16[4096,128]{1,0:T(8,128)(2,1)S(1)}, bf16[1024,128]{1,0:T(8,128)(2,1)S(1)}, s32[8,10]{1,0:T(8,128)S(1)}, s32[2,8]{1,0:T(2,128)S(1)}) custom-call(s32[8,10]{1,0:T(8,128)S(1)} %bitcast.9, s32[2,8]{1,0:T(2,128)S(1)} %bitcast.10, bf16[128,4096]{1,0:T(8,128)(2,1)S(1)} %bitcast.5, bf16[128,1024]{1,0:T(8,128)(2,1)S(1)} %bitcast.8), custom_call_target="tpu_custom_call" | custom-call | bytes 2097152 | tf_op jit(solution)/shard_map/pallas_call | solution.py:43
  12.8 1.5 %collective-permute-done.2.refs_1_ = bf16[320,128]{1,0:T(8,128)(2,1)S(1)} collective-permute-done((bf16[320,128]{1,0:T(8,128)(2,1)S(1)}, bf16[320,128]{1,0:T(8,128)(2,1)S(1)}, u32[]{:S(2)}, u32[]{:S(2)}) %collective-permute-start.2) | collective-permute-done | bytes 81952 | tf_op jit(solution)/shard_map/ppermute | solution.py:414
  14.3 2.5 %collective-permute-start.9 = (bf16[320,128]{1,0:T(8,128)(2,1)S(1)}, bf16[320,128]{1,0:T(8,128)(2,1)S(1)}, u32[]{:S(2)}, u32[]{:S(2)}) collective-permute-start(bf16[320,128]{1,0:T(8,128)(2,1)S(1)} %shard_map.70.refs_4_.refs_3_.refs_5_), channel_id=1, source_target_pairs={{0,24},{8,16},{16,8},{24,0},{1,25},{9,17},{17,9},{25,1},{2,26},{10... | collective-permute-start | bytes 245768 | tf_op jit(solution)/shard_map/ppermute | solution.py:417
  16.9 0.5 collective-permute-start.7
  17.4 0.5 collective-permute-start.5
  17.9 1.9 %collective-permute-done.9.refs_10_.refs_11_ = bf16[320,128]{1,0:T(8,128)(2,1)S(1)} collective-permute-done((bf16[320,128]{1,0:T(8,128)(2,1)S(1)}, bf16[320,128]{1,0:T(8,128)(2,1)S(1)}, u32[]{:S(2)}, u32[]{:S(2)}) %collective-permute-start.9) | collective-permute-done | bytes 81952 | tf_op jit(solution)/shard_map/ppermute | solution.py:417
  19.9 3.0 %collective-permute-start.13 = (bf16[640,128]{1,0:T(8,128)(2,1)S(1)}, bf16[640,128]{1,0:T(8,128)(2,1)S(1)}, u32[]{:S(2)}, u32[]{:S(2)}) collective-permute-start(bf16[640,128]{1,0:T(8,128)(2,1)S(1)} %shard_map.72.refs_0_), channel_id=1, source_target_pairs={{0,24},{8,16},{16,8},{24,0},{1,25},{9,17},{17,9},{25,1},{2,26},{10... | collective-permute-start | bytes 491528 | tf_op jit(solution)/shard_map/ppermute | solution.py:417
  22.8 0.6 collective-permute-start.12
  23.4 0.2 collective-permute-start.11
  23.6 0.5 collective-permute-start.6
  24.1 0.8 collective-permute-done.8.refs_9_.refs_10_
  24.9 0.2 collective-permute-done.6.refs_7_.refs_8_
  25.1 1.0 %shard_map.71 = (bf16[2560,128]{1,0:T(8,128)(2,1)S(1)}, bf16[128,256]{1,0:T(8,128)(2,1)S(1)}, bf16[128,128]{1,0:T(8,128)(2,1)S(1)}) custom-call(s32[8,10]{1,0:T(8,128)S(1)} %get-tuple-element.35.refs_3_.refs_0_, bf16[128,4096]{1,0:T(8,128)(2,1)S(1)} %bitcast.6, bf16[1280,128]{1,0:T(8,128)(2,1)S(1)} %copy-done.3, ...), custom_call_target="tpu_custom_call" | custom-call | flops 67108864 | bytes 3145728 | tf_op jit(solution)/shard_map/pallas_call | solution.py:43
  26.1 2.5 %collective-permute-start.16 = (bf16[128,256]{1,0:T(8,128)(2,1)S(1)}, bf16[128,256]{1,0:T(8,128)(2,1)S(1)}, u32[]{:S(2)}, u32[]{:S(2)}) collective-permute-start(bf16[128,256]{1,0:T(8,128)(2,1)S(1)} %get-tuple-element.38.refs_15_.refs_4_), channel_id=1, source_target_pairs={{0,6},{1,7},{2,4},{3,5},{4,2},{5,3},{6,0},{7,1},{8,14},{9,15},{10,... | collective-permute-start | bytes 196616 | tf_op jit(solution)/shard_map/ppermute | solution.py:414
  28.6 1.9 %collective-permute-start.14 = (bf16[128,256]{1,0:T(8,128)(2,1)S(1)}, bf16[128,256]{1,0:T(8,128)(2,1)S(1)}, u32[]{:S(2)}, u32[]{:S(2)}) collective-permute-start(bf16[128,256]{1,0:T(8,128)(2,1)S(1)} %get-tuple-element.38.refs_15_.refs_4_), channel_id=1, source_target_pairs={{0,2},{1,3},{2,0},{3,1},{4,6},{5,7},{6,4},{7,5},{8,10},{9,11},{10,... | collective-permute-start | bytes 196616 | tf_op jit(solution)/shard_map/ppermute | solution.py:414
  30.5 0.7 collective-permute-done.12.refs_2_
  31.2 0.4 collective-permute-done.11.refs_1_
  31.7 1.2 %collective-permute-done.16.refs_6_.refs_21_.refs_10_ = bf16[128,256]{1,0:T(8,128)(2,1)S(1)} collective-permute-done((bf16[128,256]{1,0:T(8,128)(2,1)S(1)}, bf16[128,256]{1,0:T(8,128)(2,1)S(1)}, u32[]{:S(2)}, u32[]{:S(2)}) %collective-permute-start.16) | collective-permute-done | bytes 65568 | tf_op jit(solution)/shard_map/ppermute | solution.py:414
  32.9 2.2 %collective-permute-done.15.refs_5_.refs_19_.refs_8_ = bf16[128,256]{1,0:T(8,128)(2,1)S(1)} collective-permute-done((bf16[128,256]{1,0:T(8,128)(2,1)S(1)}, bf16[128,256]{1,0:T(8,128)(2,1)S(1)}, u32[]{:S(2)}, u32[]{:S(2)}) %collective-permute-start.15) | collective-permute-done | bytes 65568 | tf_op jit(solution)/shard_map/ppermute | solution.py:414
  35.2 0.5 collective-permute-start.18
  35.8 0.4 collective-permute-start.20
  36.4 1.0 %collective-permute-done.18.refs_16_.refs_5_ = bf16[128,256]{1,0:T(8,128)(2,1)S(1)} collective-permute-done((bf16[128,256]{1,0:T(8,128)(2,1)S(1)}, bf16[128,256]{1,0:T(8,128)(2,1)S(1)}, u32[]{:S(2)}, u32[]{:S(2)}) %collective-permute-start.18) | collective-permute-done | bytes 65568 | tf_op jit(solution)/shard_map/ppermute | solution.py:408
  37.7 1.7 %shard_map.74 = (bf16[10240,128]{1,0:T(8,128)(2,1)S(1)}, bf16[1024,128]{1,0:T(8,128)(2,1)S(1)}, bf16[1024,128]{1,0:T(8,128)(2,1)S(1)}) custom-call(s32[8,10]{1,0:T(8,128)S(1)} %get-tuple-element.35.refs_3_.refs_0_, bf16[128,4096]{1,0:T(8,128)(2,1)S(1)} %bitcast.7, bf16[2560,128]{1,0:T(8,128)(2,1)S(1)} %get-tuple-element.37.refs_2_, ...), custom_call_target="tpu_custom_call" | custom-call | flops 268435456 | bytes 8388608 | tf_op jit(solution)/shard_map/pallas_call | solution.py:43
  39.4 0.2 collective-permute-start.24
  39.6 3.6 %shard_map.75 = (bf16[8,128,128]{2,1,0:T(8,128)(2,1)S(1)}, bf16[128,256]{1,0:T(8,128)(2,1)S(1)}, bf16[128,256]{1,0:T(8,128)(2,1)S(1)}, bf16[128,256]{1,0:T(8,128...) custom-call(s32[2,8]{1,0:T(2,128)S(1)} %get-tuple-element.36.refs_0_, ...), custom_call_target="tpu_custom_call" | custom-call | flops 671088640 | bytes 4194304 | tf_op jit(solution)/shard_map/pallas_call | solution.py:43
  43.2 0.4 collective-permute-start.27
  43.7 0.4 collective-permute-start.23
  44.3 0.3 collective-permute-done.27
  44.5 0.4 collective-permute-start.25
  44.9 0.5 collective-permute-done.29
  45.4 0.8 collective-permute-start.28
  46.2 2.4 %collective-permute-start.30 = (bf16[128,256]{1,0:T(8,128)(2,1)S(1)}, bf16[128,256]{1,0:T(8,128)(2,1)S(1)}, u32[]{:S(2)}, u32[]{:S(2)}) collective-permute-start(bf16[128,256]{1,0:T(8,128)(2,1)S(1)} %add_convert_fusion.1), channel_id=1, source_target_pairs={{0,6},{1,7},{2,4},{3,5},{4,2},{5,3},{6,0},{7,1},{8,14},{9,15},{10,... | collective-permute-start | bytes 196616 | tf_op jit(solution)/shard_map/ppermute | solution.py:414
  48.6 1.4 %shard_map.77 = (bf16[960,128]{1,0:T(8,128)(2,1)S(1)}, bf16[960,128]{1,0:T(8,128)(2,1)S(1)}, bf16[960,128]{1,0:T(8,128)(2,1)S(1)}, bf16[960,128]{1,0:T(8,128)(2,1)S(1)}) custom-call(s32[8,10]{1,0:T(8,128)S(1)} %get-tuple-element.35.refs_3_.refs_0_, bf16[4096,128]{1,0:T(8,128)(2,1)S(1)} %get-tuple-element.48.refs_1_, ...), custom_call_target="tpu_custom_call" | custom-call | flops 251658240 | bytes 4194304 | tf_op jit(solution)/shard_map/pallas_call | solution.py:43
  50.0 0.5 collective-permute-start.26
  50.5 1.9 %collective-permute-start.31 = (bf16[960,128]{1,0:T(8,128)(2,1)S(1)}, bf16[960,128]{1,0:T(8,128)(2,1)S(1)}, u32[]{:S(2)}, u32[]{:S(2)}) collective-permute-start(bf16[960,128]{1,0:T(8,128)(2,1)S(1)} %get-tuple-element.56), channel_id=1, source_target_pairs={{0,8},{8,0},{16,24},{24,16},{1,9},{9,1},{17,25},{25,17},{2,10},{10... | collective-permute-start | bytes 737288 | tf_op jit(solution)/shard_map/ppermute | solution.py:417
  52.3 1.5 %collective-permute-start.32 = (bf16[960,128]{1,0:T(8,128)(2,1)S(1)}, bf16[960,128]{1,0:T(8,128)(2,1)S(1)}, u32[]{:S(2)}, u32[]{:S(2)}) collective-permute-start(bf16[960,128]{1,0:T(8,128)(2,1)S(1)} %get-tuple-element.57), channel_id=1, source_target_pairs={{0,16},{8,24},{16,0},{24,8},{1,17},{9,25},{17,1},{25,9},{2,18},{10... | collective-permute-start | bytes 737288 | tf_op jit(solution)/shard_map/ppermute | solution.py:417
  53.8 2.4 %collective-permute-start.33 = (bf16[960,128]{1,0:T(8,128)(2,1)S(1)}, bf16[960,128]{1,0:T(8,128)(2,1)S(1)}, u32[]{:S(2)}, u32[]{:S(2)}) collective-permute-start(bf16[960,128]{1,0:T(8,128)(2,1)S(1)} %get-tuple-element.58), channel_id=1, source_target_pairs={{0,24},{8,16},{16,8},{24,0},{1,25},{9,17},{17,9},{25,1},{2,26},{10... | collective-permute-start | bytes 737288 | tf_op jit(solution)/shard_map/ppermute | solution.py:417
  56.5 1.2 %collective-permute-done.34.refs_6_ = bf16[2,128,128]{2,1,0:T(8,128)(2,1)S(1)} collective-permute-done((bf16[2,128,128]{2,1,0:T(8,128)(2,1)S(1)}, bf16[2,128,128]{2,1,0:T(8,128)(2,1)S(1)}, u32[]{:S(2)}, u32[]{:S(2)}) %collective-permute-start.34) | collective-permute-done | bytes 65568 | tf_op jit(solution)/shard_map/ppermute | solution.py:408
  57.7 1.0 %shard_map.81 = (bf16[320,128]{1,0:T(8,128)(2,1)S(1)}, bf16[320,128]{1,0:T(8,128)(2,1)S(1)}, bf16[320,128]{1,0:T(8,128)(2,1)S(1)}, bf16[320,128]{1,0:T(8,128)(2,1)S(1)}) custom-call(s32[8,10]{1,0:T(8,128)S(1)} %get-tuple-element.35.refs_3_.refs_0_, bf16[4096,128]{1,0:T(8,128)(2,1)S(1)} %get-tuple-element.48.refs_1_, ...), custom_call_target="tpu_custom_call" | custom-call | flops 83886080 | bytes 4194304 | tf_op jit(solution)/shard_map/pallas_call | solution.py:43
  58.7 0.7 collective-permute-start.35
  59.4 1.0 %collective-permute-start.36 = (bf16[320,128]{1,0:T(8,128)(2,1)S(1)}, bf16[320,128]{1,0:T(8,128)(2,1)S(1)}, u32[]{:S(2)}, u32[]{:S(2)}) collective-permute-start(bf16[320,128]{1,0:T(8,128)(2,1)S(1)} %get-tuple-element.61), channel_id=1, source_target_pairs={{0,16},{8,24},{16,0},{24,8},{1,17},{9,25},{17,1},{25,9},{2,18},{10... | collective-permute-start | bytes 245768 | tf_op jit(solution)/shard_map/ppermute | solution.py:417
  60.4 1.8 %collective-permute-start.37 = (bf16[320,128]{1,0:T(8,128)(2,1)S(1)}, bf16[320,128]{1,0:T(8,128)(2,1)S(1)}, u32[]{:S(2)}, u32[]{:S(2)}) collective-permute-start(bf16[320,128]{1,0:T(8,128)(2,1)S(1)} %shard_map.82), channel_id=1, source_target_pairs={{0,24},{8,16},{16,8},{24,0},{1,25},{9,17},{17,9},{25,1},{2,26},{10... | collective-permute-start | bytes 245768 | tf_op jit(solution)/shard_map/ppermute | solution.py:417
  62.2 3.0 %shard_map.80 = (bf16[128,4096]{1,0:T(8,128)(2,1)}, f32[8,128]{1,0:T(8,128)S(1)}) custom-call(s32[8,10]{1,0:T(8,128)S(1)} %get-tuple-element.35.refs_3_.refs_0_, bf16[8,128,128]{2,1,0:T(8,128)(2,1)S(1)} %get-tuple-element.42.refs_3_.refs_1_, bf16[2,128,128]{2,1,0:T(8,128)(2,1)S(1)} %shard_map.79.refs_2_.refs_5_, bf16[10240,128]{1,0:T(8,128)(2,1)S(1)} %get-tuple-element.54.refs_3_), custom_call_target="tpu_custom_call" | custom-call | flops 335544320 | bytes 4194304 | tf_op jit(solution)/shard_map/pallas_call | solution.py:43
  65.2 0.3 collective-permute-done.35.refs_5_
  65.5 2.5 %collective-permute-done.36.refs_6_ = bf16[320,128]{1,0:T(8,128)(2,1)S(1)} collective-permute-done((bf16[320,128]{1,0:T(8,128)(2,1)S(1)}, bf16[320,128]{1,0:T(8,128)(2,1)S(1)}, u32[]{:S(2)}, u32[]{:S(2)}) %collective-permute-start.36) | collective-permute-done | bytes 81952 | tf_op jit(solution)/shard_map/ppermute | solution.py:417
  68.0 0.3 shard_map.83
  68.3 1.7 %collective-permute-start.38 = (bf16[320,128]{1,0:T(8,128)(2,1)S(1)}, bf16[320,128]{1,0:T(8,128)(2,1)S(1)}, u32[]{:S(2)}, u32[]{:S(2)}) collective-permute-start(bf16[320,128]{1,0:T(8,128)(2,1)S(1)} %get-tuple-element.65), channel_id=1, source_target_pairs={{0,2},{1,3},{2,0},{3,1},{4,6},{5,7},{6,4},{7,5},{8,10},{9,11},{10,... | collective-permute-start | bytes 245768 | tf_op jit(solution)/shard_map/ppermute | solution.py:414
  70.0 1.4 %collective-permute-start.39 = (bf16[320,128]{1,0:T(8,128)(2,1)S(1)}, bf16[320,128]{1,0:T(8,128)(2,1)S(1)}, u32[]{:S(2)}, u32[]{:S(2)}) collective-permute-start(bf16[320,128]{1,0:T(8,128)(2,1)S(1)} %get-tuple-element.66), channel_id=1, source_target_pairs={{0,4},{1,5},{2,6},{3,7},{4,0},{5,1},{6,2},{7,3},{8,12},{9,13},{10,... | collective-permute-start | bytes 245768 | tf_op jit(solution)/shard_map/ppermute | solution.py:414
  71.4 1.4 %collective-permute-start.40 = (bf16[320,128]{1,0:T(8,128)(2,1)S(1)}, bf16[320,128]{1,0:T(8,128)(2,1)S(1)}, u32[]{:S(2)}, u32[]{:S(2)}) collective-permute-start(bf16[320,128]{1,0:T(8,128)(2,1)S(1)} %get-tuple-element.67), channel_id=1, source_target_pairs={{0,6},{1,7},{2,4},{3,5},{4,2},{5,3},{6,0},{7,1},{8,14},{9,15},{10,... | collective-permute-start | bytes 245768 | tf_op jit(solution)/shard_map/ppermute | solution.py:414
  72.8 0.9 %collective-permute-done.38 = bf16[320,128]{1,0:T(8,128)(2,1)S(1)} collective-permute-done((bf16[320,128]{1,0:T(8,128)(2,1)S(1)}, bf16[320,128]{1,0:T(8,128)(2,1)S(1)}, u32[]{:S(2)}, u32[]{:S(2)}) %collective-permute-start.38) | collective-permute-done | bytes 81952 | tf_op jit(solution)/shard_map/ppermute | solution.py:414
  73.7 4.9 %collective-permute-done.39 = bf16[320,128]{1,0:T(8,128)(2,1)S(1)} collective-permute-done((bf16[320,128]{1,0:T(8,128)(2,1)S(1)}, bf16[320,128]{1,0:T(8,128)(2,1)S(1)}, u32[]{:S(2)}, u32[]{:S(2)}) %collective-permute-start.39) | collective-permute-done | bytes 81952 | tf_op jit(solution)/shard_map/ppermute | solution.py:414
  78.7 1.9 %collective-permute-start.43 = (bf16[320,128]{1,0:T(8,128)(2,1)S(1)}, bf16[320,128]{1,0:T(8,128)(2,1)S(1)}, u32[]{:S(2)}, u32[]{:S(2)}) collective-permute-start(bf16[320,128]{1,0:T(8,128)(2,1)S(1)} %add_convert_fusion.refs_0_), channel_id=1, source_target_pairs={{0,24},{8,16},{16,8},{24,0},{1,25},{9,17},{17,9},{25,1},{2,26},{10... | collective-permute-start | bytes 245768 | tf_op jit(solution)/shard_map/ppermute | solution.py:417
  80.6 1.6 %collective-permute-start.41 = (bf16[320,128]{1,0:T(8,128)(2,1)S(1)}, bf16[320,128]{1,0:T(8,128)(2,1)S(1)}, u32[]{:S(2)}, u32[]{:S(2)}) collective-permute-start(bf16[320,128]{1,0:T(8,128)(2,1)S(1)} %add_convert_fusion.refs_0_), channel_id=1, source_target_pairs={{0,8},{8,0},{16,24},{24,16},{1,9},{9,1},{17,25},{25,17},{2,10},{10... | collective-permute-start | bytes 245768 | tf_op jit(solution)/shard_map/ppermute | solution.py:417
  82.3 1.9 %collective-permute-done.43.refs_3_ = bf16[320,128]{1,0:T(8,128)(2,1)S(1)} collective-permute-done((bf16[320,128]{1,0:T(8,128)(2,1)S(1)}, bf16[320,128]{1,0:T(8,128)(2,1)S(1)}, u32[]{:S(2)}, u32[]{:S(2)}) %collective-permute-start.43) | collective-permute-done | bytes 81952 | tf_op jit(solution)/shard_map/ppermute | solution.py:417
  84.1 1.0 %collective-permute-done.42.refs_2_ = bf16[320,128]{1,0:T(8,128)(2,1)S(1)} collective-permute-done((bf16[320,128]{1,0:T(8,128)(2,1)S(1)}, bf16[320,128]{1,0:T(8,128)(2,1)S(1)}, u32[]{:S(2)}, u32[]{:S(2)}) %collective-permute-start.42) | collective-permute-done | bytes 81952 | tf_op jit(solution)/shard_map/ppermute | solution.py:417
  85.1 0.9 %shard_map.84 = f32[1280,128]{1,0:T(8,128)} custom-call(bf16[320,128]{1,0:T(8,128)(2,1)S(1)} %add_convert_fusion.refs_0_, bf16[320,128]{1,0:T(8,128)(2,1)S(1)} %collective-permute-done.41.refs_1_, bf16[320,128]{1,0:T(8,128)(2,1)S(1)} %collective-permute-done.42.refs_2_, bf16[320,128]{1,0:T(8,128)(2,1)S(1)} %collective-permute-done.43.refs_3_), custom_call_target="tpu_custom_call" | custom-call | bytes 1048576 | tf_op jit(solution)/shard_map/pallas_call | solution.py:43
  (61 shorter events, 1.4 us)
Async XLA Ops:
  0.6 13.7 %collective-permute-start = (bf16[1280,128]{1,0:T(8,128)(2,1)}, bf16[1280,128]{1,0:T(8,128)(2,1)S(1)}, u32[]{:S(2)}, u32[]{:S(2)}) collective-permute-start(bf16[1280,128]{1,0:T(8,128)(2,1)} %refs_3_.1), channel_id=1, source_target_pairs={{0,1},{1,0},{2,3},{3,2},{4,5},{5,4},{6,7},{7,6},{8,9},{9,8},{10,11... | collective-permute-start | bytes 983048 | tf_op jit(solution)/shard_map/ppermute | solution.py:408
  1.1 1.0 %copy-start.2 = (bf16[1280,128]{1,0:T(8,128)(2,1)S(1)}, bf16[1280,128]{1,0:T(8,128)(2,1)}, u32[]{:S(2)}) copy-start(bf16[1280,128]{1,0:T(8,128)(2,1)} %refs_3_.1) | copy-start | bytes 983044
  2.1 22.9 %copy-start.3 = (bf16[1280,128]{1,0:T(8,128)(2,1)S(1)}, bf16[1280,128]{1,0:T(8,128)(2,1)}, u32[]{:S(2)}) copy-start(bf16[1280,128]{1,0:T(8,128)(2,1)} %refs_3_.1) | copy-start | bytes 983044
  2.1 10.7 %collective-permute-start.3 = (bf16[320,128]{1,0:T(8,128)(2,1)S(1)}, bf16[320,128]{1,0:T(8,128)(2,1)S(1)}, u32[]{:S(2)}, u32[]{:S(2)}) collective-permute-start(bf16[320,128]{1,0:T(8,128)(2,1)S(1)} %shard_map.69), channel_id=1, source_target_pairs={{0,6},{1,7},{2,4},{3,5},{4,2},{5,3},{6,0},{7,1},{8,14},{9,15},{10,... | collective-permute-start | bytes 245768 | tf_op jit(solution)/shard_map/ppermute | solution.py:414
  6.8 7.5 %collective-permute-start.2 = (bf16[320,128]{1,0:T(8,128)(2,1)S(1)}, bf16[320,128]{1,0:T(8,128)(2,1)S(1)}, u32[]{:S(2)}, u32[]{:S(2)}) collective-permute-start(bf16[320,128]{1,0:T(8,128)(2,1)S(1)} %shard_map.69), channel_id=1, source_target_pairs={{0,4},{1,5},{2,6},{3,7},{4,0},{5,1},{6,2},{7,3},{8,12},{9,13},{10,... | collective-permute-start | bytes 245768 | tf_op jit(solution)/shard_map/ppermute | solution.py:414
  6.8 7.5 %collective-permute-start.1 = (bf16[320,128]{1,0:T(8,128)(2,1)S(1)}, bf16[320,128]{1,0:T(8,128)(2,1)S(1)}, u32[]{:S(2)}, u32[]{:S(2)}) collective-permute-start(bf16[320,128]{1,0:T(8,128)(2,1)S(1)} %shard_map.69), channel_id=1, source_target_pairs={{0,2},{1,3},{2,0},{3,1},{4,6},{5,7},{6,4},{7,5},{8,10},{9,11},{10,... | collective-permute-start | bytes 245768 | tf_op jit(solution)/shard_map/ppermute | solution.py:414
  7.5 1.2 %copy-start = (bf16[1,128,4096]{2,1,0:T(8,128)(2,1)S(1)}, bf16[1,128,4096]{2,1,0:T(8,128)(2,1)}, u32[]{:S(2)}) copy-start(bf16[1,128,4096]{2,1,0:T(8,128)(2,1)} %param.5) | copy-start | bytes 3145732
  8.7 0.9 %copy-start.4 = (bf16[1,128,1024]{2,1,0:T(8,128)(2,1)S(1)}, bf16[1,128,1024]{2,1,0:T(8,128)(2,1)}, u32[]{:S(2)}) copy-start(bf16[1,128,1024]{2,1,0:T(8,128)(2,1)} %param.6) | copy-start | bytes 786436
  9.6 0.7 copy-start.5
  10.3 0.7 copy-start.6
  11.0 14.1 %copy-start.1 = (bf16[1,128,4096]{2,1,0:T(8,128)(2,1)S(1)}, bf16[1,128,4096]{2,1,0:T(8,128)(2,1)}, u32[]{:S(2)}) copy-start(bf16[1,128,4096]{2,1,0:T(8,128)(2,1)} %param.5) | copy-start | bytes 3145732
  14.3 5.5 %collective-permute-start.9 = (bf16[320,128]{1,0:T(8,128)(2,1)S(1)}, bf16[320,128]{1,0:T(8,128)(2,1)S(1)}, u32[]{:S(2)}, u32[]{:S(2)}) collective-permute-start(bf16[320,128]{1,0:T(8,128)(2,1)S(1)} %shard_map.70.refs_4_.refs_3_.refs_5_), channel_id=1, source_target_pairs={{0,24},{8,16},{16,8},{24,0},{1,25},{9,17},{17,9},{25,1},{2,26},{10... | collective-permute-start | bytes 245768 | tf_op jit(solution)/shard_map/ppermute | solution.py:417
  16.9 6.0 %collective-permute-start.7 = (bf16[320,128]{1,0:T(8,128)(2,1)S(1)}, bf16[320,128]{1,0:T(8,128)(2,1)S(1)}, u32[]{:S(2)}, u32[]{:S(2)}) collective-permute-start(bf16[320,128]{1,0:T(8,128)(2,1)S(1)} %shard_map.70.refs_4_.refs_3_.refs_5_), channel_id=1, source_target_pairs={{0,16},{8,24},{16,0},{24,8},{1,17},{9,25},{17,1},{25,9},{2,18},{10... | collective-permute-start | bytes 245768 | tf_op jit(solution)/shard_map/ppermute | solution.py:417
  17.4 6.1 %collective-permute-start.5 = (bf16[320,128]{1,0:T(8,128)(2,1)S(1)}, bf16[320,128]{1,0:T(8,128)(2,1)S(1)}, u32[]{:S(2)}, u32[]{:S(2)}) collective-permute-start(bf16[320,128]{1,0:T(8,128)(2,1)S(1)} %shard_map.70.refs_4_.refs_3_.refs_5_), channel_id=1, source_target_pairs={{0,8},{8,0},{16,24},{24,16},{1,9},{9,1},{17,25},{25,17},{2,10},{10... | collective-permute-start | bytes 245768 | tf_op jit(solution)/shard_map/ppermute | solution.py:417
  17.9 5.7 %collective-permute-start.4 = (bf16[320,128]{1,0:T(8,128)(2,1)S(1)}, bf16[320,128]{1,0:T(8,128)(2,1)S(1)}, u32[]{:S(2)}, u32[]{:S(2)}) collective-permute-start(bf16[320,128]{1,0:T(8,128)(2,1)S(1)} %shard_map.70.refs_4_.refs_3_.refs_5_), channel_id=1, source_target_pairs={{0,1},{1,0},{2,3},{3,2},{4,5},{5,4},{6,7},{7,6},{8,9},{9,8},{10,11... | collective-permute-start | bytes 245768 | tf_op jit(solution)/shard_map/ppermute | solution.py:408
  19.8 3.8 %collective-permute-start.10 = (bf16[320,128]{1,0:T(8,128)(2,1)S(1)}, bf16[320,128]{1,0:T(8,128)(2,1)S(1)}, u32[]{:S(2)}, u32[]{:S(2)}) collective-permute-start(bf16[320,128]{1,0:T(8,128)(2,1)S(1)} %collective-permute-done.9.refs_10_.refs_11_), channel_id=1, source_target_pairs={{0,1},{1,0},{2,3},{3,2},{4,5},{5,4},{6,7},{7,6},{8,9},{9,8},{10,11... | collective-permute-start | bytes 245768 | tf_op jit(solution)/shard_map/ppermute | solution.py:408
  19.9 8.7 %collective-permute-start.13 = (bf16[640,128]{1,0:T(8,128)(2,1)S(1)}, bf16[640,128]{1,0:T(8,128)(2,1)S(1)}, u32[]{:S(2)}, u32[]{:S(2)}) collective-permute-start(bf16[640,128]{1,0:T(8,128)(2,1)S(1)} %shard_map.72.refs_0_), channel_id=1, source_target_pairs={{0,24},{8,16},{16,8},{24,0},{1,25},{9,17},{17,9},{25,1},{2,26},{10... | collective-permute-start | bytes 491528 | tf_op jit(solution)/shard_map/ppermute | solution.py:417
  22.8 8.4 %collective-permute-start.12 = (bf16[640,128]{1,0:T(8,128)(2,1)S(1)}, bf16[640,128]{1,0:T(8,128)(2,1)S(1)}, u32[]{:S(2)}, u32[]{:S(2)}) collective-permute-start(bf16[640,128]{1,0:T(8,128)(2,1)S(1)} %shard_map.72.refs_0_), channel_id=1, source_target_pairs={{0,16},{8,24},{16,0},{24,8},{1,17},{9,25},{17,1},{25,9},{2,18},{10... | collective-permute-start | bytes 491528 | tf_op jit(solution)/shard_map/ppermute | solution.py:417
  23.4 8.2 %collective-permute-start.11 = (bf16[640,128]{1,0:T(8,128)(2,1)S(1)}, bf16[640,128]{1,0:T(8,128)(2,1)S(1)}, u32[]{:S(2)}, u32[]{:S(2)}) collective-permute-start(bf16[640,128]{1,0:T(8,128)(2,1)S(1)} %shard_map.72.refs_0_), channel_id=1, source_target_pairs={{0,8},{8,0},{16,24},{24,16},{1,9},{9,1},{17,25},{25,17},{2,10},{10... | collective-permute-start | bytes 491528 | tf_op jit(solution)/shard_map/ppermute | solution.py:417
  23.6 1.3 %collective-permute-start.8 = (bf16[320,128]{1,0:T(8,128)(2,1)S(1)}, bf16[320,128]{1,0:T(8,128)(2,1)S(1)}, u32[]{:S(2)}, u32[]{:S(2)}) collective-permute-start(bf16[320,128]{1,0:T(8,128)(2,1)S(1)} %collective-permute-done.7.refs_8_.refs_9_), channel_id=1, source_target_pairs={{0,1},{1,0},{2,3},{3,2},{4,5},{5,4},{6,7},{7,6},{8,9},{9,8},{10,11... | collective-permute-start | bytes 245768 | tf_op jit(solution)/shard_map/ppermute | solution.py:408
  23.6 1.4 %collective-permute-start.6 = (bf16[320,128]{1,0:T(8,128)(2,1)S(1)}, bf16[320,128]{1,0:T(8,128)(2,1)S(1)}, u32[]{:S(2)}, u32[]{:S(2)}) collective-permute-start(bf16[320,128]{1,0:T(8,128)(2,1)S(1)} %collective-permute-done.5.refs_6_.refs_7_), channel_id=1, source_target_pairs={{0,1},{1,0},{2,3},{3,2},{4,5},{5,4},{6,7},{7,6},{8,9},{9,8},{10,11... | collective-permute-start | bytes 245768 | tf_op jit(solution)/shard_map/ppermute | solution.py:408
  26.1 6.8 %collective-permute-start.16 = (bf16[128,256]{1,0:T(8,128)(2,1)S(1)}, bf16[128,256]{1,0:T(8,128)(2,1)S(1)}, u32[]{:S(2)}, u32[]{:S(2)}) collective-permute-start(bf16[128,256]{1,0:T(8,128)(2,1)S(1)} %get-tuple-element.38.refs_15_.refs_4_), channel_id=1, source_target_pairs={{0,6},{1,7},{2,4},{3,5},{4,2},{5,3},{6,0},{7,1},{8,14},{9,15},{10,... | collective-permute-start | bytes 196616 | tf_op jit(solution)/shard_map/ppermute | solution.py:414
  28.6 6.5 %collective-permute-start.15 = (bf16[128,256]{1,0:T(8,128)(2,1)S(1)}, bf16[128,256]{1,0:T(8,128)(2,1)S(1)}, u32[]{:S(2)}, u32[]{:S(2)}) collective-permute-start(bf16[128,256]{1,0:T(8,128)(2,1)S(1)} %get-tuple-element.38.refs_15_.refs_4_), channel_id=1, source_target_pairs={{0,4},{1,5},{2,6},{3,7},{4,0},{5,1},{6,2},{7,3},{8,12},{9,13},{10,... | collective-permute-start | bytes 196616 | tf_op jit(solution)/shard_map/ppermute | solution.py:414
  28.6 6.5 %collective-permute-start.14 = (bf16[128,256]{1,0:T(8,128)(2,1)S(1)}, bf16[128,256]{1,0:T(8,128)(2,1)S(1)}, u32[]{:S(2)}, u32[]{:S(2)}) collective-permute-start(bf16[128,256]{1,0:T(8,128)(2,1)S(1)} %get-tuple-element.38.refs_15_.refs_4_), channel_id=1, source_target_pairs={{0,2},{1,3},{2,0},{3,1},{4,6},{5,7},{6,4},{7,5},{8,10},{9,11},{10,... | collective-permute-start | bytes 196616 | tf_op jit(solution)/shard_map/ppermute | solution.py:414
  35.1 2.5 %collective-permute-start.17 = (bf16[2560,128]{1,0:T(8,128)(2,1)S(1)}, bf16[2560,128]{1,0:T(8,128)(2,1)S(1)}, u32[]{:S(2)}, u32[]{:S(2)}) collective-permute-start(bf16[2560,128]{1,0:T(8,128)(2,1)S(1)} %shard_map.73.refs_13_), channel_id=1, source_target_pairs={{0,1},{1,0},{2,3},{3,2},{4,5},{5,4},{6,7},{7,6},{8,9},{9,8},{10,11... | collective-permute-start | bytes 1966088 | tf_op jit(solution)/shard_map/ppermute | solution.py:408
  35.2 2.2 %collective-permute-start.18 = (bf16[128,256]{1,0:T(8,128)(2,1)S(1)}, bf16[128,256]{1,0:T(8,128)(2,1)S(1)}, u32[]{:S(2)}, u32[]{:S(2)}) collective-permute-start(bf16[128,256]{1,0:T(8,128)(2,1)S(1)} %get-tuple-element.38.refs_15_.refs_4_), channel_id=1, source_target_pairs={{0,1},{1,0},{2,3},{3,2},{4,5},{5,4},{6,7},{7,6},{8,9},{9,8},{10,11... | collective-permute-start | bytes 196616 | tf_op jit(solution)/shard_map/ppermute | solution.py:408
  35.7 1.8 %collective-permute-start.21 = (bf16[128,256]{1,0:T(8,128)(2,1)S(1)}, bf16[128,256]{1,0:T(8,128)(2,1)S(1)}, u32[]{:S(2)}, u32[]{:S(2)}) collective-permute-start(bf16[128,256]{1,0:T(8,128)(2,1)S(1)} %collective-permute-done.16.refs_6_.refs_21_.refs_10_), channel_id=1, source_target_pairs={{0,1},{1,0},{2,3},{3,2},{4,5},{5,4},{6,7},{7,6},{8,9},{9,8},{10,11... | collective-permute-start | bytes 196616 | tf_op jit(solution)/shard_map/ppermute | solution.py:408
  35.8 1.8 %collective-permute-start.20 = (bf16[128,256]{1,0:T(8,128)(2,1)S(1)}, bf16[128,256]{1,0:T(8,128)(2,1)S(1)}, u32[]{:S(2)}, u32[]{:S(2)}) collective-permute-start(bf16[128,256]{1,0:T(8,128)(2,1)S(1)} %collective-permute-done.15.refs_5_.refs_19_.refs_8_), channel_id=1, source_target_pairs={{0,1},{1,0},{2,3},{3,2},{4,5},{5,4},{6,7},{7,6},{8,9},{9,8},{10,11... | collective-permute-start | bytes 196616 | tf_op jit(solution)/shard_map/ppermute | solution.py:408
  36.2 1.5 %collective-permute-start.19 = (bf16[128,256]{1,0:T(8,128)(2,1)S(1)}, bf16[128,256]{1,0:T(8,128)(2,1)S(1)}, u32[]{:S(2)}, u32[]{:S(2)}) collective-permute-start(bf16[128,256]{1,0:T(8,128)(2,1)S(1)} %collective-permute-done.14.refs_4_.refs_17_.refs_6_), channel_id=1, source_target_pairs={{0,1},{1,0},{2,3},{3,2},{4,5},{5,4},{6,7},{7,6},{8,9},{9,8},{10,11... | collective-permute-start | bytes 196616 | tf_op jit(solution)/shard_map/ppermute | solution.py:408
  39.4 9.2 %collective-permute-start.24 = (bf16[4096,128]{1,0:T(8,128)(2,1)S(1)}, bf16[4096,128]{1,0:T(8,128)(2,1)S(1)}, u32[]{:S(2)}, u32[]{:S(2)}) collective-permute-start(bf16[4096,128]{1,0:T(8,128)(2,1)S(1)} %shard_map.76), channel_id=1, source_target_pairs={{0,1},{1,0},{2,3},{3,2},{4,5},{5,4},{6,7},{7,6},{8,9},{9,8},{10,11... | collective-permute-start | bytes 3145736 | tf_op jit(solution)/shard_map/ppermute | solution.py:408
  43.2 1.3 %collective-permute-start.27 = (bf16[128,256]{1,0:T(8,128)(2,1)S(1)}, bf16[128,256]{1,0:T(8,128)(2,1)S(1)}, u32[]{:S(2)}, u32[]{:S(2)}) collective-permute-start(bf16[128,256]{1,0:T(8,128)(2,1)S(1)} %get-tuple-element.51), channel_id=1, source_target_pairs={{0,1},{1,0},{2,3},{3,2},{4,5},{5,4},{6,7},{7,6},{8,9},{9,8},{10,11... | collective-permute-start | bytes 196616 | tf_op jit(solution)/shard_map/ppermute | solution.py:408
  43.6 8.7 %collective-permute-start.22 = (bf16[128,256]{1,0:T(8,128)(2,1)S(1)}, bf16[128,256]{1,0:T(8,128)(2,1)S(1)}, u32[]{:S(2)}, u32[]{:S(2)}) collective-permute-start(bf16[128,256]{1,0:T(8,128)(2,1)S(1)} %get-tuple-element.45), channel_id=1, source_target_pairs={{0,1},{1,0},{2,3},{3,2},{4,5},{5,4},{6,7},{7,6},{8,9},{9,8},{10,11... | collective-permute-start | bytes 196616 | tf_op jit(solution)/shard_map/ppermute | solution.py:408
  43.7 2.4 %collective-permute-start.23 = (bf16[128,256]{1,0:T(8,128)(2,1)S(1)}, bf16[128,256]{1,0:T(8,128)(2,1)S(1)}, u32[]{:S(2)}, u32[]{:S(2)}) collective-permute-start(bf16[128,256]{1,0:T(8,128)(2,1)S(1)} %get-tuple-element.47), channel_id=1, source_target_pairs={{0,1},{1,0},{2,3},{3,2},{4,5},{5,4},{6,7},{7,6},{8,9},{9,8},{10,11... | collective-permute-start | bytes 196616 | tf_op jit(solution)/shard_map/ppermute | solution.py:408
  44.1 1.3 %collective-permute-start.29 = (bf16[128,256]{1,0:T(8,128)(2,1)S(1)}, bf16[128,256]{1,0:T(8,128)(2,1)S(1)}, u32[]{:S(2)}, u32[]{:S(2)}) collective-permute-start(bf16[128,256]{1,0:T(8,128)(2,1)S(1)} %get-tuple-element.53), channel_id=1, source_target_pairs={{0,1},{1,0},{2,3},{3,2},{4,5},{5,4},{6,7},{7,6},{8,9},{9,8},{10,11... | collective-permute-start | bytes 196616 | tf_op jit(solution)/shard_map/ppermute | solution.py:408
  44.5 4.0 %collective-permute-start.25 = (bf16[8,128,128]{2,1,0:T(8,128)(2,1)S(1)}, bf16[8,128,128]{2,1,0:T(8,128)(2,1)S(1)}, u32[]{:S(2)}, u32[]{:S(2)}) collective-permute-start(bf16[8,128,128]{2,1,0:T(8,128)(2,1)S(1)} %get-tuple-element.42.refs_3_.refs_1_), channel_id=1, source_target_pairs={{0,1},{1,0},{2,3},{3,2},{4,5},{5,4},{6,7},{7,6},{8,9},{9,8},{10,11... | collective-permute-start | bytes 786440 | tf_op jit(solution)/shard_map/ppermute | solution.py:408
  45.4 8.4 %collective-permute-start.28 = (bf16[128,256]{1,0:T(8,128)(2,1)S(1)}, bf16[128,256]{1,0:T(8,128)(2,1)S(1)}, u32[]{:S(2)}, u32[]{:S(2)}) collective-permute-start(bf16[128,256]{1,0:T(8,128)(2,1)S(1)} %add_convert_fusion.2), channel_id=1, source_target_pairs={{0,4},{1,5},{2,6},{3,7},{4,0},{5,1},{6,2},{7,3},{8,12},{9,13},{10,... | collective-permute-start | bytes 196616 | tf_op jit(solution)/shard_map/ppermute | solution.py:414
  46.2 10.1 %collective-permute-start.30 = (bf16[128,256]{1,0:T(8,128)(2,1)S(1)}, bf16[128,256]{1,0:T(8,128)(2,1)S(1)}, u32[]{:S(2)}, u32[]{:S(2)}) collective-permute-start(bf16[128,256]{1,0:T(8,128)(2,1)S(1)} %add_convert_fusion.1), channel_id=1, source_target_pairs={{0,6},{1,7},{2,4},{3,5},{4,2},{5,3},{6,0},{7,1},{8,14},{9,15},{10,... | collective-permute-start | bytes 196616 | tf_op jit(solution)/shard_map/ppermute | solution.py:414
  50.0 6.3 %collective-permute-start.26 = (bf16[128,256]{1,0:T(8,128)(2,1)S(1)}, bf16[128,256]{1,0:T(8,128)(2,1)S(1)}, u32[]{:S(2)}, u32[]{:S(2)}) collective-permute-start(bf16[128,256]{1,0:T(8,128)(2,1)S(1)} %shard_map.78), channel_id=1, source_target_pairs={{0,2},{1,3},{2,0},{3,1},{4,6},{5,7},{6,4},{7,5},{8,10},{9,11},{10,... | collective-permute-start | bytes 196616 | tf_op jit(solution)/shard_map/ppermute | solution.py:414
  50.5 10.0 %collective-permute-start.31 = (bf16[960,128]{1,0:T(8,128)(2,1)S(1)}, bf16[960,128]{1,0:T(8,128)(2,1)S(1)}, u32[]{:S(2)}, u32[]{:S(2)}) collective-permute-start(bf16[960,128]{1,0:T(8,128)(2,1)S(1)} %get-tuple-element.56), channel_id=1, source_target_pairs={{0,8},{8,0},{16,24},{24,16},{1,9},{9,1},{17,25},{25,17},{2,10},{10... | collective-permute-start | bytes 737288 | tf_op jit(solution)/shard_map/ppermute | solution.py:417
  52.3 15.7 %collective-permute-start.32 = (bf16[960,128]{1,0:T(8,128)(2,1)S(1)}, bf16[960,128]{1,0:T(8,128)(2,1)S(1)}, u32[]{:S(2)}, u32[]{:S(2)}) collective-permute-start(bf16[960,128]{1,0:T(8,128)(2,1)S(1)} %get-tuple-element.57), channel_id=1, source_target_pairs={{0,16},{8,24},{16,0},{24,8},{1,17},{9,25},{17,1},{25,9},{2,18},{10... | collective-permute-start | bytes 737288 | tf_op jit(solution)/shard_map/ppermute | solution.py:417
  53.8 14.2 %collective-permute-start.33 = (bf16[960,128]{1,0:T(8,128)(2,1)S(1)}, bf16[960,128]{1,0:T(8,128)(2,1)S(1)}, u32[]{:S(2)}, u32[]{:S(2)}) collective-permute-start(bf16[960,128]{1,0:T(8,128)(2,1)S(1)} %get-tuple-element.58), channel_id=1, source_target_pairs={{0,24},{8,16},{16,8},{24,0},{1,25},{9,17},{17,9},{25,1},{2,26},{10... | collective-permute-start | bytes 737288 | tf_op jit(solution)/shard_map/ppermute | solution.py:417
  56.4 1.3 %collective-permute-start.34 = (bf16[2,128,128]{2,1,0:T(8,128)(2,1)S(1)}, bf16[2,128,128]{2,1,0:T(8,128)(2,1)S(1)}, u32[]{:S(2)}, u32[]{:S(2)}) collective-permute-start(bf16[2,128,128]{2,1,0:T(8,128)(2,1)S(1)} %shard_map.79.refs_2_.refs_5_), channel_id=1, source_target_pairs={{0,1},{1,0},{2,3},{3,2},{4,5},{5,4},{6,7},{7,6},{8,9},{9,8},{10,11... | collective-permute-start | bytes 196616 | tf_op jit(solution)/shard_map/ppermute | solution.py:408
  58.7 6.9 %collective-permute-start.35 = (bf16[320,128]{1,0:T(8,128)(2,1)S(1)}, bf16[320,128]{1,0:T(8,128)(2,1)S(1)}, u32[]{:S(2)}, u32[]{:S(2)}) collective-permute-start(bf16[320,128]{1,0:T(8,128)(2,1)S(1)} %get-tuple-element.60), channel_id=1, source_target_pairs={{0,8},{8,0},{16,24},{24,16},{1,9},{9,1},{17,25},{25,17},{2,10},{10... | collective-permute-start | bytes 245768 | tf_op jit(solution)/shard_map/ppermute | solution.py:417
  59.4 8.6 %collective-permute-start.36 = (bf16[320,128]{1,0:T(8,128)(2,1)S(1)}, bf16[320,128]{1,0:T(8,128)(2,1)S(1)}, u32[]{:S(2)}, u32[]{:S(2)}) collective-permute-start(bf16[320,128]{1,0:T(8,128)(2,1)S(1)} %get-tuple-element.61), channel_id=1, source_target_pairs={{0,16},{8,24},{16,0},{24,8},{1,17},{9,25},{17,1},{25,9},{2,18},{10... | collective-permute-start | bytes 245768 | tf_op jit(solution)/shard_map/ppermute | solution.py:417
  60.4 7.6 %collective-permute-start.37 = (bf16[320,128]{1,0:T(8,128)(2,1)S(1)}, bf16[320,128]{1,0:T(8,128)(2,1)S(1)}, u32[]{:S(2)}, u32[]{:S(2)}) collective-permute-start(bf16[320,128]{1,0:T(8,128)(2,1)S(1)} %shard_map.82), channel_id=1, source_target_pairs={{0,24},{8,16},{16,8},{24,0},{1,25},{9,17},{17,9},{25,1},{2,26},{10... | collective-permute-start | bytes 245768 | tf_op jit(solution)/shard_map/ppermute | solution.py:417
  68.3 5.4 %collective-permute-start.38 = (bf16[320,128]{1,0:T(8,128)(2,1)S(1)}, bf16[320,128]{1,0:T(8,128)(2,1)S(1)}, u32[]{:S(2)}, u32[]{:S(2)}) collective-permute-start(bf16[320,128]{1,0:T(8,128)(2,1)S(1)} %get-tuple-element.65), channel_id=1, source_target_pairs={{0,2},{1,3},{2,0},{3,1},{4,6},{5,7},{6,4},{7,5},{8,10},{9,11},{10,... | collective-permute-start | bytes 245768 | tf_op jit(solution)/shard_map/ppermute | solution.py:414
  70.0 8.7 %collective-permute-start.39 = (bf16[320,128]{1,0:T(8,128)(2,1)S(1)}, bf16[320,128]{1,0:T(8,128)(2,1)S(1)}, u32[]{:S(2)}, u32[]{:S(2)}) collective-permute-start(bf16[320,128]{1,0:T(8,128)(2,1)S(1)} %get-tuple-element.66), channel_id=1, source_target_pairs={{0,4},{1,5},{2,6},{3,7},{4,0},{5,1},{6,2},{7,3},{8,12},{9,13},{10,... | collective-permute-start | bytes 245768 | tf_op jit(solution)/shard_map/ppermute | solution.py:414
  71.4 7.2 %collective-permute-start.40 = (bf16[320,128]{1,0:T(8,128)(2,1)S(1)}, bf16[320,128]{1,0:T(8,128)(2,1)S(1)}, u32[]{:S(2)}, u32[]{:S(2)}) collective-permute-start(bf16[320,128]{1,0:T(8,128)(2,1)S(1)} %get-tuple-element.67), channel_id=1, source_target_pairs={{0,6},{1,7},{2,4},{3,5},{4,2},{5,3},{6,0},{7,1},{8,14},{9,15},{10,... | collective-permute-start | bytes 245768 | tf_op jit(solution)/shard_map/ppermute | solution.py:414
  78.7 5.4 %collective-permute-start.43 = (bf16[320,128]{1,0:T(8,128)(2,1)S(1)}, bf16[320,128]{1,0:T(8,128)(2,1)S(1)}, u32[]{:S(2)}, u32[]{:S(2)}) collective-permute-start(bf16[320,128]{1,0:T(8,128)(2,1)S(1)} %add_convert_fusion.refs_0_), channel_id=1, source_target_pairs={{0,24},{8,16},{16,8},{24,0},{1,25},{9,17},{17,9},{25,1},{2,26},{10... | collective-permute-start | bytes 245768 | tf_op jit(solution)/shard_map/ppermute | solution.py:417
  80.6 4.4 %collective-permute-start.42 = (bf16[320,128]{1,0:T(8,128)(2,1)S(1)}, bf16[320,128]{1,0:T(8,128)(2,1)S(1)}, u32[]{:S(2)}, u32[]{:S(2)}) collective-permute-start(bf16[320,128]{1,0:T(8,128)(2,1)S(1)} %add_convert_fusion.refs_0_), channel_id=1, source_target_pairs={{0,16},{8,24},{16,0},{24,8},{1,17},{9,25},{17,1},{25,9},{2,18},{10... | collective-permute-start | bytes 245768 | tf_op jit(solution)/shard_map/ppermute | solution.py:417
  80.6 4.4 %collective-permute-start.41 = (bf16[320,128]{1,0:T(8,128)(2,1)S(1)}, bf16[320,128]{1,0:T(8,128)(2,1)S(1)}, u32[]{:S(2)}, u32[]{:S(2)}) collective-permute-start(bf16[320,128]{1,0:T(8,128)(2,1)S(1)} %add_convert_fusion.refs_0_), channel_id=1, source_target_pairs={{0,8},{8,0},{16,24},{24,16},{1,9},{9,1},{17,25},{25,17},{2,10},{10... | collective-permute-start | bytes 245768 | tf_op jit(solution)/shard_map/ppermute | solution.py:417

commit v9 on v7

--- a/solution.py
+++ b/solution.py
@@ -239,8 +239,10 @@
     length = kv.shape[0]
     key_row = lax.broadcasted_iota(jnp.int32, (keys, half), 0)
     query_at = lax.broadcasted_iota(jnp.int32, (keys, half), 1) % SPAN
+    found = {}
     for p in (1, 0):
         reach = length if p == 1 else length // 2
+        base = 0 if p == 1 else length
         sure = length // 2 if p == 1 else 0
         q_part = qhat[p * half : (p + 1) * half, :]
         up_part = up[p * half : (p + 1) * half, :]
@@ -253,17 +255,24 @@
             if at + keys > sure:
                 e = jnp.where(key_row + at <= limit, e, 0.0)
             dp = dot(kv[rows, HD:], up_part, ((1,), (1,)))
-            expo[rows, :] = e
-            dprob[rows, :] = dp
+            expo[base + at : base + at + keys, :] = e
+            dprob[base + at : base + at + keys, :] = dp
             term = e.astype(BF16).astype(F32) * dp
             total = total + jnp.sum(e.reshape(keys // 8, 8, half), axis=0)
             weighted = weighted + jnp.sum(term.reshape(keys // 8, 8, half), axis=0)
         inverse = 1.0 / jnp.sum(total, axis=0, keepdims=True)
-        delta = jnp.sum(weighted, axis=0, keepdims=True) * inverse
+        found[p] = (inverse, jnp.sum(weighted, axis=0, keepdims=True) * inverse)
+    for p in (1, 0):
+        reach = length if p == 1 else length // 2
+        base = 0 if p == 1 else length
+        q_part = qhat[p * half : (p + 1) * half, :]
+        up_part = up[p * half : (p + 1) * half, :]
+        inverse, delta = found[p]
         for at in range(0, reach, keys):
             rows = slice(at, at + keys)
-            prob = expo[rows, :] * inverse
-            dscore = (prob * (dprob[rows, :] - delta) * SCALE).astype(BF16)
+            held = slice(base + at, base + at + keys)
+            prob = expo[held, :] * inverse
+            dscore = (prob * (dprob[held, :] - delta) * SCALE).astype(BF16)
             dkey, dvalue = dot(dscore, q_part), dot(prob.astype(BF16), up_part)
             dq_term = dot(kv[rows, :HD].T, dscore)
             if p == 1:
@@ -485,8 +494,8 @@
         [((NQ, tok, HD), BF16)] + [((tok, 2 * HD), BF16)] * (2 * nz),
         scratch=[
             pltpu.VMEM((length, 2 * HD), BF16),
-            pltpu.VMEM((length, half), F32),
-            pltpu.VMEM((length, half), F32),
+            pltpu.VMEM((length + length // 2, half), F32),
+            pltpu.VMEM((length + length // 2, half), F32),
             pltpu.VMEM((length, 2 * HD), F32),
             pltpu.VMEM((HD, half), F32),
         ],

time: 86.3 us -> 86.3 us (level)
  no operation moved by 1% of the time
where the time goes in v9:
time: 86.3 us; the launch traced here: 86 us
  starting transfers between devices  41.9 us (49%)
  waiting for transfers between devices  23.8 us (28%)
  Pallas kernels  14.8 us (17%)
  local copies, waits for them, and re-layouts  4.59 us (5%)
    ppermute x15, starting transfers between devices, swap_dp(): return lax.ppermute(v, 'dp', [(i, i ^ k) for i in range(ndp)])  20.1 us
    ppermute x12, starting transfers between devices, swap_z(): return lax.ppermute(v, 'ctx', [(i, i ^ 2 * k) for i in range(nctx)])  17.8 us
    pallas_call x14, Pallas kernels, call(): pl.pallas_call(body, in_specs=[SMEM] * len(scalars) + [VMEM] * len(arrays...  14.8 us
    ppermute x12, waiting for transfers between devices, swap_z(): return lax.ppermute(v, 'ctx', [(i, i ^ 2 * k) for i in range(nctx)])  10.8 us
    ppermute x15, waiting for transfers between devices, swap_dp(): return lax.ppermute(v, 'dp', [(i, i ^ k) for i in range(ndp)])  8.74 us
    unnamed x15, local copies, waits for them, and re-layouts  4.59 us
    ppermute x17, waiting for transfers between devices, swap_core(): return lax.ppermute(v, 'ctx', [(i, i ^ 1) for i in range(nctx)])  4.23 us
    ppermute x17, starting transfers between devices, swap_core(): return lax.ppermute(v, 'ctx', [(i, i ^ 1) for i in range(nctx)])  3.91 us
  transfers between devices with their start and end apart: 44, of which 21 were waited for; matrix products, arithmetic and copies ran while one was open for 0% of the time, Pallas kernels for 14%

profile of v9, /device:TPU:0, one launch (start us, length us, event | category | flops | bytes accessed | tf_op | source)
XLA Modules:
  0.0 86.0 jit_solution(1161295610527814503)
XLA Ops:
  0.6 0.5 collective-permute-start
  1.1 1.0 %copy-done.2 = bf16[1280,128]{1,0:T(8,128)(2,1)S(1)} copy-done((bf16[1280,128]{1,0:T(8,128)(2,1)S(1)}, bf16[1280,128]{1,0:T(8,128)(2,1)}, u32[]{:S(2)}) %copy-start.2) | copy-done | bytes 327704
  2.1 4.7 %collective-permute-start.3 = (bf16[320,128]{1,0:T(8,128)(2,1)S(1)}, bf16[320,128]{1,0:T(8,128)(2,1)S(1)}, u32[]{:S(2)}, u32[]{:S(2)}) collective-permute-start(bf16[320,128]{1,0:T(8,128)(2,1)S(1)} %shard_map.69), channel_id=1, source_target_pairs={{0,6},{1,7},{2,4},{3,5},{4,2},{5,3},{6,0},{7,1},{8,14},{9,15},{10,... | collective-permute-start | bytes 245768 | tf_op jit(solution)/shard_map/ppermute | solution.py:406
  6.8 0.6 collective-permute-start.1
  7.5 1.2 %copy-done = bf16[1,128,4096]{2,1,0:T(8,128)(2,1)S(1)} copy-done((bf16[1,128,4096]{2,1,0:T(8,128)(2,1)S(1)}, bf16[1,128,4096]{2,1,0:T(8,128)(2,1)}, u32[]{:S(2)}) %copy-start) | copy-done | bytes 1048600
  8.7 0.9 %copy-done.4 = bf16[1,128,1024]{2,1,0:T(8,128)(2,1)S(1)} copy-done((bf16[1,128,1024]{2,1,0:T(8,128)(2,1)S(1)}, bf16[1,128,1024]{2,1,0:T(8,128)(2,1)}, u32[]{:S(2)}) %copy-start.4) | copy-done | bytes 262168
  9.6 0.7 copy-done.5
  10.3 0.7 copy-done.6
  11.0 1.8 %shard_map.68 = (bf16[4096,128]{1,0:T(8,128)(2,1)S(1)}, bf16[1024,128]{1,0:T(8,128)(2,1)S(1)}, s32[8,10]{1,0:T(8,128)S(1)}, s32[2,8]{1,0:T(2,128)S(1)}) custom-call(s32[8,10]{1,0:T(8,128)S(1)} %bitcast.9, s32[2,8]{1,0:T(2,128)S(1)} %bitcast.10, bf16[128,4096]{1,0:T(8,128)(2,1)S(1)} %bitcast.5, bf16[128,1024]{1,0:T(8,128)(2,1)S(1)} %bitcast.8), custom_call_target="tpu_custom_call" | custom-call | bytes 2097152 | tf_op jit(solution)/shard_map/pallas_call | solution.py:43
  12.8 1.5 %collective-permute-done.2.refs_1_ = bf16[320,128]{1,0:T(8,128)(2,1)S(1)} collective-permute-done((bf16[320,128]{1,0:T(8,128)(2,1)S(1)}, bf16[320,128]{1,0:T(8,128)(2,1)S(1)}, u32[]{:S(2)}, u32[]{:S(2)}) %collective-permute-start.2) | collective-permute-done | bytes 81952 | tf_op jit(solution)/shard_map/ppermute | solution.py:406
  14.3 2.5 %collective-permute-start.9 = (bf16[320,128]{1,0:T(8,128)(2,1)S(1)}, bf16[320,128]{1,0:T(8,128)(2,1)S(1)}, u32[]{:S(2)}, u32[]{:S(2)}) collective-permute-start(bf16[320,128]{1,0:T(8,128)(2,1)S(1)} %shard_map.70.refs_4_.refs_3_.refs_5_), channel_id=1, source_target_pairs={{0,24},{8,16},{16,8},{24,0},{1,25},{9,17},{17,9},{25,1},{2,26},{10... | collective-permute-start | bytes 245768 | tf_op jit(solution)/shard_map/ppermute | solution.py:409
  16.9 0.5 collective-permute-start.7
  17.4 0.5 collective-permute-start.5
  17.9 1.9 %collective-permute-done.9.refs_10_.refs_11_ = bf16[320,128]{1,0:T(8,128)(2,1)S(1)} collective-permute-done((bf16[320,128]{1,0:T(8,128)(2,1)S(1)}, bf16[320,128]{1,0:T(8,128)(2,1)S(1)}, u32[]{:S(2)}, u32[]{:S(2)}) %collective-permute-start.9) | collective-permute-done | bytes 81952 | tf_op jit(solution)/shard_map/ppermute | solution.py:409
  19.9 3.0 %collective-permute-start.13 = (bf16[640,128]{1,0:T(8,128)(2,1)S(1)}, bf16[640,128]{1,0:T(8,128)(2,1)S(1)}, u32[]{:S(2)}, u32[]{:S(2)}) collective-permute-start(bf16[640,128]{1,0:T(8,128)(2,1)S(1)} %shard_map.72.refs_0_), channel_id=1, source_target_pairs={{0,24},{8,16},{16,8},{24,0},{1,25},{9,17},{17,9},{25,1},{2,26},{10... | collective-permute-start | bytes 491528 | tf_op jit(solution)/shard_map/ppermute | solution.py:409
  22.8 0.6 collective-permute-start.12
  23.4 0.2 collective-permute-start.11
  23.6 0.5 collective-permute-start.6
  24.1 0.8 collective-permute-done.8.refs_9_.refs_10_
  24.9 0.2 collective-permute-done.6.refs_7_.refs_8_
  25.1 1.0 %shard_map.71 = (bf16[2560,128]{1,0:T(8,128)(2,1)S(1)}, bf16[128,256]{1,0:T(8,128)(2,1)S(1)}, bf16[128,128]{1,0:T(8,128)(2,1)S(1)}) custom-call(s32[8,10]{1,0:T(8,128)S(1)} %get-tuple-element.35.refs_3_.refs_0_, bf16[128,4096]{1,0:T(8,128)(2,1)S(1)} %bitcast.6, bf16[1280,128]{1,0:T(8,128)(2,1)S(1)} %copy-done.3, ...), custom_call_target="tpu_custom_call" | custom-call | flops 67108864 | bytes 3145728 | tf_op jit(solution)/shard_map/pallas_call | solution.py:43
  26.0 2.5 %collective-permute-start.16 = (bf16[128,256]{1,0:T(8,128)(2,1)S(1)}, bf16[128,256]{1,0:T(8,128)(2,1)S(1)}, u32[]{:S(2)}, u32[]{:S(2)}) collective-permute-start(bf16[128,256]{1,0:T(8,128)(2,1)S(1)} %get-tuple-element.38.refs_15_.refs_4_), channel_id=1, source_target_pairs={{0,6},{1,7},{2,4},{3,5},{4,2},{5,3},{6,0},{7,1},{8,14},{9,15},{10,... | collective-permute-start | bytes 196616 | tf_op jit(solution)/shard_map/ppermute | solution.py:406
  28.6 1.9 %collective-permute-start.14 = (bf16[128,256]{1,0:T(8,128)(2,1)S(1)}, bf16[128,256]{1,0:T(8,128)(2,1)S(1)}, u32[]{:S(2)}, u32[]{:S(2)}) collective-permute-start(bf16[128,256]{1,0:T(8,128)(2,1)S(1)} %get-tuple-element.38.refs_15_.refs_4_), channel_id=1, source_target_pairs={{0,2},{1,3},{2,0},{3,1},{4,6},{5,7},{6,4},{7,5},{8,10},{9,11},{10,... | collective-permute-start | bytes 196616 | tf_op jit(solution)/shard_map/ppermute | solution.py:406
  30.5 0.7 collective-permute-done.12.refs_2_
  31.2 0.4 collective-permute-done.11.refs_1_
  31.7 1.2 %collective-permute-done.16.refs_6_.refs_21_.refs_10_ = bf16[128,256]{1,0:T(8,128)(2,1)S(1)} collective-permute-done((bf16[128,256]{1,0:T(8,128)(2,1)S(1)}, bf16[128,256]{1,0:T(8,128)(2,1)S(1)}, u32[]{:S(2)}, u32[]{:S(2)}) %collective-permute-start.16) | collective-permute-done | bytes 65568 | tf_op jit(solution)/shard_map/ppermute | solution.py:406
  32.9 2.2 %collective-permute-done.15.refs_5_.refs_19_.refs_8_ = bf16[128,256]{1,0:T(8,128)(2,1)S(1)} collective-permute-done((bf16[128,256]{1,0:T(8,128)(2,1)S(1)}, bf16[128,256]{1,0:T(8,128)(2,1)S(1)}, u32[]{:S(2)}, u32[]{:S(2)}) %collective-permute-start.15) | collective-permute-done | bytes 65568 | tf_op jit(solution)/shard_map/ppermute | solution.py:406
  35.2 0.5 collective-permute-start.18
  35.8 0.4 collective-permute-start.20
  36.4 1.0 %collective-permute-done.18.refs_16_.refs_5_ = bf16[128,256]{1,0:T(8,128)(2,1)S(1)} collective-permute-done((bf16[128,256]{1,0:T(8,128)(2,1)S(1)}, bf16[128,256]{1,0:T(8,128)(2,1)S(1)}, u32[]{:S(2)}, u32[]{:S(2)}) %collective-permute-start.18) | collective-permute-done | bytes 65568 | tf_op jit(solution)/shard_map/ppermute | solution.py:400
  37.7 1.7 %shard_map.74 = (bf16[10240,128]{1,0:T(8,128)(2,1)S(1)}, bf16[1024,128]{1,0:T(8,128)(2,1)S(1)}, bf16[1024,128]{1,0:T(8,128)(2,1)S(1)}) custom-call(s32[8,10]{1,0:T(8,128)S(1)} %get-tuple-element.35.refs_3_.refs_0_, bf16[128,4096]{1,0:T(8,128)(2,1)S(1)} %bitcast.7, bf16[2560,128]{1,0:T(8,128)(2,1)S(1)} %get-tuple-element.37.refs_2_, ...), custom_call_target="tpu_custom_call" | custom-call | flops 268435456 | bytes 8388608 | tf_op jit(solution)/shard_map/pallas_call | solution.py:43
  39.4 0.2 collective-permute-start.24
  39.6 3.6 %shard_map.75 = (bf16[8,128,128]{2,1,0:T(8,128)(2,1)S(1)}, bf16[128,256]{1,0:T(8,128)(2,1)S(1)}, bf16[128,256]{1,0:T(8,128)(2,1)S(1)}, bf16[128,256]{1,0:T(8,128...) custom-call(s32[2,8]{1,0:T(2,128)S(1)} %get-tuple-element.36.refs_0_, ...), custom_call_target="tpu_custom_call" | custom-call | flops 671088640 | bytes 4194304 | tf_op jit(solution)/shard_map/pallas_call | solution.py:43
  43.2 0.4 collective-permute-start.27
  43.8 0.4 collective-permute-start.23
  44.3 0.3 collective-permute-done.27
  44.5 0.4 collective-permute-start.25
  44.9 0.5 collective-permute-done.29
  45.4 0.8 collective-permute-start.28
  46.2 2.4 %collective-permute-start.30 = (bf16[128,256]{1,0:T(8,128)(2,1)S(1)}, bf16[128,256]{1,0:T(8,128)(2,1)S(1)}, u32[]{:S(2)}, u32[]{:S(2)}) collective-permute-start(bf16[128,256]{1,0:T(8,128)(2,1)S(1)} %add_convert_fusion.1), channel_id=1, source_target_pairs={{0,6},{1,7},{2,4},{3,5},{4,2},{5,3},{6,0},{7,1},{8,14},{9,15},{10,... | collective-permute-start | bytes 196616 | tf_op jit(solution)/shard_map/ppermute | solution.py:406
  48.6 1.4 %shard_map.77 = (bf16[960,128]{1,0:T(8,128)(2,1)S(1)}, bf16[960,128]{1,0:T(8,128)(2,1)S(1)}, bf16[960,128]{1,0:T(8,128)(2,1)S(1)}, bf16[960,128]{1,0:T(8,128)(2,1)S(1)}) custom-call(s32[8,10]{1,0:T(8,128)S(1)} %get-tuple-element.35.refs_3_.refs_0_, bf16[4096,128]{1,0:T(8,128)(2,1)S(1)} %get-tuple-element.48.refs_1_, ...), custom_call_target="tpu_custom_call" | custom-call | flops 251658240 | bytes 4194304 | tf_op jit(solution)/shard_map/pallas_call | solution.py:43
  50.0 0.5 collective-permute-start.26
  50.5 1.9 %collective-permute-start.31 = (bf16[960,128]{1,0:T(8,128)(2,1)S(1)}, bf16[960,128]{1,0:T(8,128)(2,1)S(1)}, u32[]{:S(2)}, u32[]{:S(2)}) collective-permute-start(bf16[960,128]{1,0:T(8,128)(2,1)S(1)} %get-tuple-element.56), channel_id=1, source_target_pairs={{0,8},{8,0},{16,24},{24,16},{1,9},{9,1},{17,25},{25,17},{2,10},{10... | collective-permute-start | bytes 737288 | tf_op jit(solution)/shard_map/ppermute | solution.py:409
  52.4 1.5 %collective-permute-start.32 = (bf16[960,128]{1,0:T(8,128)(2,1)S(1)}, bf16[960,128]{1,0:T(8,128)(2,1)S(1)}, u32[]{:S(2)}, u32[]{:S(2)}) collective-permute-start(bf16[960,128]{1,0:T(8,128)(2,1)S(1)} %get-tuple-element.57), channel_id=1, source_target_pairs={{0,16},{8,24},{16,0},{24,8},{1,17},{9,25},{17,1},{25,9},{2,18},{10... | collective-permute-start | bytes 737288 | tf_op jit(solution)/shard_map/ppermute | solution.py:409
  53.8 2.4 %collective-permute-start.33 = (bf16[960,128]{1,0:T(8,128)(2,1)S(1)}, bf16[960,128]{1,0:T(8,128)(2,1)S(1)}, u32[]{:S(2)}, u32[]{:S(2)}) collective-permute-start(bf16[960,128]{1,0:T(8,128)(2,1)S(1)} %get-tuple-element.58), channel_id=1, source_target_pairs={{0,24},{8,16},{16,8},{24,0},{1,25},{9,17},{17,9},{25,1},{2,26},{10... | collective-permute-start | bytes 737288 | tf_op jit(solution)/shard_map/ppermute | solution.py:409
  56.5 1.2 %collective-permute-done.34.refs_6_ = bf16[2,128,128]{2,1,0:T(8,128)(2,1)S(1)} collective-permute-done((bf16[2,128,128]{2,1,0:T(8,128)(2,1)S(1)}, bf16[2,128,128]{2,1,0:T(8,128)(2,1)S(1)}, u32[]{:S(2)}, u32[]{:S(2)}) %collective-permute-start.34) | collective-permute-done | bytes 65568 | tf_op jit(solution)/shard_map/ppermute | solution.py:400
  57.7 1.0 %shard_map.81 = (bf16[320,128]{1,0:T(8,128)(2,1)S(1)}, bf16[320,128]{1,0:T(8,128)(2,1)S(1)}, bf16[320,128]{1,0:T(8,128)(2,1)S(1)}, bf16[320,128]{1,0:T(8,128)(2,1)S(1)}) custom-call(s32[8,10]{1,0:T(8,128)S(1)} %get-tuple-element.35.refs_3_.refs_0_, bf16[4096,128]{1,0:T(8,128)(2,1)S(1)} %get-tuple-element.48.refs_1_, ...), custom_call_target="tpu_custom_call" | custom-call | flops 83886080 | bytes 4194304 | tf_op jit(solution)/shard_map/pallas_call | solution.py:43
  58.7 0.7 collective-permute-start.35
  59.4 1.0 %collective-permute-start.36 = (bf16[320,128]{1,0:T(8,128)(2,1)S(1)}, bf16[320,128]{1,0:T(8,128)(2,1)S(1)}, u32[]{:S(2)}, u32[]{:S(2)}) collective-permute-start(bf16[320,128]{1,0:T(8,128)(2,1)S(1)} %get-tuple-element.61), channel_id=1, source_target_pairs={{0,16},{8,24},{16,0},{24,8},{1,17},{9,25},{17,1},{25,9},{2,18},{10... | collective-permute-start | bytes 245768 | tf_op jit(solution)/shard_map/ppermute | solution.py:409
  60.5 1.8 %collective-permute-start.37 = (bf16[320,128]{1,0:T(8,128)(2,1)S(1)}, bf16[320,128]{1,0:T(8,128)(2,1)S(1)}, u32[]{:S(2)}, u32[]{:S(2)}) collective-permute-start(bf16[320,128]{1,0:T(8,128)(2,1)S(1)} %shard_map.82), channel_id=1, source_target_pairs={{0,24},{8,16},{16,8},{24,0},{1,25},{9,17},{17,9},{25,1},{2,26},{10... | collective-permute-start | bytes 245768 | tf_op jit(solution)/shard_map/ppermute | solution.py:409
  62.2 3.0 %shard_map.80 = (bf16[128,4096]{1,0:T(8,128)(2,1)}, f32[8,128]{1,0:T(8,128)S(1)}) custom-call(s32[8,10]{1,0:T(8,128)S(1)} %get-tuple-element.35.refs_3_.refs_0_, bf16[8,128,128]{2,1,0:T(8,128)(2,1)S(1)} %get-tuple-element.42.refs_3_.refs_1_, bf16[2,128,128]{2,1,0:T(8,128)(2,1)S(1)} %shard_map.79.refs_2_.refs_5_, bf16[10240,128]{1,0:T(8,128)(2,1)S(1)} %get-tuple-element.54.refs_3_), custom_call_target="tpu_custom_call" | custom-call | flops 335544320 | bytes 4194304 | tf_op jit(solution)/shard_map/pallas_call | solution.py:43
  65.2 0.3 collective-permute-done.35.refs_5_
  65.6 2.5 %collective-permute-done.36.refs_6_ = bf16[320,128]{1,0:T(8,128)(2,1)S(1)} collective-permute-done((bf16[320,128]{1,0:T(8,128)(2,1)S(1)}, bf16[320,128]{1,0:T(8,128)(2,1)S(1)}, u32[]{:S(2)}, u32[]{:S(2)}) %collective-permute-start.36) | collective-permute-done | bytes 81952 | tf_op jit(solution)/shard_map/ppermute | solution.py:409
  68.0 0.3 shard_map.83
  68.3 1.7 %collective-permute-start.38 = (bf16[320,128]{1,0:T(8,128)(2,1)S(1)}, bf16[320,128]{1,0:T(8,128)(2,1)S(1)}, u32[]{:S(2)}, u32[]{:S(2)}) collective-permute-start(bf16[320,128]{1,0:T(8,128)(2,1)S(1)} %get-tuple-element.65), channel_id=1, source_target_pairs={{0,2},{1,3},{2,0},{3,1},{4,6},{5,7},{6,4},{7,5},{8,10},{9,11},{10,... | collective-permute-start | bytes 245768 | tf_op jit(solution)/shard_map/ppermute | solution.py:406
  70.0 1.4 %collective-permute-start.39 = (bf16[320,128]{1,0:T(8,128)(2,1)S(1)}, bf16[320,128]{1,0:T(8,128)(2,1)S(1)}, u32[]{:S(2)}, u32[]{:S(2)}) collective-permute-start(bf16[320,128]{1,0:T(8,128)(2,1)S(1)} %get-tuple-element.66), channel_id=1, source_target_pairs={{0,4},{1,5},{2,6},{3,7},{4,0},{5,1},{6,2},{7,3},{8,12},{9,13},{10,... | collective-permute-start | bytes 245768 | tf_op jit(solution)/shard_map/ppermute | solution.py:406
  71.4 1.4 %collective-permute-start.40 = (bf16[320,128]{1,0:T(8,128)(2,1)S(1)}, bf16[320,128]{1,0:T(8,128)(2,1)S(1)}, u32[]{:S(2)}, u32[]{:S(2)}) collective-permute-start(bf16[320,128]{1,0:T(8,128)(2,1)S(1)} %get-tuple-element.67), channel_id=1, source_target_pairs={{0,6},{1,7},{2,4},{3,5},{4,2},{5,3},{6,0},{7,1},{8,14},{9,15},{10,... | collective-permute-start | bytes 245768 | tf_op jit(solution)/shard_map/ppermute | solution.py:406
  72.8 0.9 %collective-permute-done.38 = bf16[320,128]{1,0:T(8,128)(2,1)S(1)} collective-permute-done((bf16[320,128]{1,0:T(8,128)(2,1)S(1)}, bf16[320,128]{1,0:T(8,128)(2,1)S(1)}, u32[]{:S(2)}, u32[]{:S(2)}) %collective-permute-start.38) | collective-permute-done | bytes 81952 | tf_op jit(solution)/shard_map/ppermute | solution.py:406
  73.7 4.9 %collective-permute-done.39 = bf16[320,128]{1,0:T(8,128)(2,1)S(1)} collective-permute-done((bf16[320,128]{1,0:T(8,128)(2,1)S(1)}, bf16[320,128]{1,0:T(8,128)(2,1)S(1)}, u32[]{:S(2)}, u32[]{:S(2)}) %collective-permute-start.39) | collective-permute-done | bytes 81952 | tf_op jit(solution)/shard_map/ppermute | solution.py:406
  78.7 1.9 %collective-permute-start.43 = (bf16[320,128]{1,0:T(8,128)(2,1)S(1)}, bf16[320,128]{1,0:T(8,128)(2,1)S(1)}, u32[]{:S(2)}, u32[]{:S(2)}) collective-permute-start(bf16[320,128]{1,0:T(8,128)(2,1)S(1)} %add_convert_fusion.refs_0_), channel_id=1, source_target_pairs={{0,24},{8,16},{16,8},{24,0},{1,25},{9,17},{17,9},{25,1},{2,26},{10... | collective-permute-start | bytes 245768 | tf_op jit(solution)/shard_map/ppermute | solution.py:409
  80.7 1.6 %collective-permute-start.41 = (bf16[320,128]{1,0:T(8,128)(2,1)S(1)}, bf16[320,128]{1,0:T(8,128)(2,1)S(1)}, u32[]{:S(2)}, u32[]{:S(2)}) collective-permute-start(bf16[320,128]{1,0:T(8,128)(2,1)S(1)} %add_convert_fusion.refs_0_), channel_id=1, source_target_pairs={{0,8},{8,0},{16,24},{24,16},{1,9},{9,1},{17,25},{25,17},{2,10},{10... | collective-permute-start | bytes 245768 | tf_op jit(solution)/shard_map/ppermute | solution.py:409
  82.3 1.9 %collective-permute-done.43.refs_3_ = bf16[320,128]{1,0:T(8,128)(2,1)S(1)} collective-permute-done((bf16[320,128]{1,0:T(8,128)(2,1)S(1)}, bf16[320,128]{1,0:T(8,128)(2,1)S(1)}, u32[]{:S(2)}, u32[]{:S(2)}) %collective-permute-start.43) | collective-permute-done | bytes 81952 | tf_op jit(solution)/shard_map/ppermute | solution.py:409
  84.1 1.0 %collective-permute-done.42.refs_2_ = bf16[320,128]{1,0:T(8,128)(2,1)S(1)} collective-permute-done((bf16[320,128]{1,0:T(8,128)(2,1)S(1)}, bf16[320,128]{1,0:T(8,128)(2,1)S(1)}, u32[]{:S(2)}, u32[]{:S(2)}) %collective-permute-start.42) | collective-permute-done | bytes 81952 | tf_op jit(solution)/shard_map/ppermute | solution.py:409
  85.1 0.9 %shard_map.84 = f32[1280,128]{1,0:T(8,128)} custom-call(bf16[320,128]{1,0:T(8,128)(2,1)S(1)} %add_convert_fusion.refs_0_, bf16[320,128]{1,0:T(8,128)(2,1)S(1)} %collective-permute-done.41.refs_1_, bf16[320,128]{1,0:T(8,128)(2,1)S(1)} %collective-permute-done.42.refs_2_, bf16[320,128]{1,0:T(8,128)(2,1)S(1)} %collective-permute-done.43.refs_3_), custom_call_target="tpu_custom_call" | custom-call | bytes 1048576 | tf_op jit(solution)/shard_map/pallas_call | solution.py:43
  (61 shorter events, 1.4 us)
Async XLA Ops:
  0.6 13.7 %collective-permute-start = (bf16[1280,128]{1,0:T(8,128)(2,1)}, bf16[1280,128]{1,0:T(8,128)(2,1)S(1)}, u32[]{:S(2)}, u32[]{:S(2)}) collective-permute-start(bf16[1280,128]{1,0:T(8,128)(2,1)} %refs_3_.1), channel_id=1, source_target_pairs={{0,1},{1,0},{2,3},{3,2},{4,5},{5,4},{6,7},{7,6},{8,9},{9,8},{10,11... | collective-permute-start | bytes 983048 | tf_op jit(solution)/shard_map/ppermute | solution.py:400
  1.1 1.0 %copy-start.2 = (bf16[1280,128]{1,0:T(8,128)(2,1)S(1)}, bf16[1280,128]{1,0:T(8,128)(2,1)}, u32[]{:S(2)}) copy-start(bf16[1280,128]{1,0:T(8,128)(2,1)} %refs_3_.1) | copy-start | bytes 983044
  2.1 22.9 %copy-start.3 = (bf16[1280,128]{1,0:T(8,128)(2,1)S(1)}, bf16[1280,128]{1,0:T(8,128)(2,1)}, u32[]{:S(2)}) copy-start(bf16[1280,128]{1,0:T(8,128)(2,1)} %refs_3_.1) | copy-start | bytes 983044
  2.1 10.7 %collective-permute-start.3 = (bf16[320,128]{1,0:T(8,128)(2,1)S(1)}, bf16[320,128]{1,0:T(8,128)(2,1)S(1)}, u32[]{:S(2)}, u32[]{:S(2)}) collective-permute-start(bf16[320,128]{1,0:T(8,128)(2,1)S(1)} %shard_map.69), channel_id=1, source_target_pairs={{0,6},{1,7},{2,4},{3,5},{4,2},{5,3},{6,0},{7,1},{8,14},{9,15},{10,... | collective-permute-start | bytes 245768 | tf_op jit(solution)/shard_map/ppermute | solution.py:406
  6.8 7.5 %collective-permute-start.2 = (bf16[320,128]{1,0:T(8,128)(2,1)S(1)}, bf16[320,128]{1,0:T(8,128)(2,1)S(1)}, u32[]{:S(2)}, u32[]{:S(2)}) collective-permute-start(bf16[320,128]{1,0:T(8,128)(2,1)S(1)} %shard_map.69), channel_id=1, source_target_pairs={{0,4},{1,5},{2,6},{3,7},{4,0},{5,1},{6,2},{7,3},{8,12},{9,13},{10,... | collective-permute-start | bytes 245768 | tf_op jit(solution)/shard_map/ppermute | solution.py:406
  6.8 7.5 %collective-permute-start.1 = (bf16[320,128]{1,0:T(8,128)(2,1)S(1)}, bf16[320,128]{1,0:T(8,128)(2,1)S(1)}, u32[]{:S(2)}, u32[]{:S(2)}) collective-permute-start(bf16[320,128]{1,0:T(8,128)(2,1)S(1)} %shard_map.69), channel_id=1, source_target_pairs={{0,2},{1,3},{2,0},{3,1},{4,6},{5,7},{6,4},{7,5},{8,10},{9,11},{10,... | collective-permute-start | bytes 245768 | tf_op jit(solution)/shard_map/ppermute | solution.py:406
  7.5 1.2 %copy-start = (bf16[1,128,4096]{2,1,0:T(8,128)(2,1)S(1)}, bf16[1,128,4096]{2,1,0:T(8,128)(2,1)}, u32[]{:S(2)}) copy-start(bf16[1,128,4096]{2,1,0:T(8,128)(2,1)} %param.5) | copy-start | bytes 3145732
  8.7 0.9 %copy-start.4 = (bf16[1,128,1024]{2,1,0:T(8,128)(2,1)S(1)}, bf16[1,128,1024]{2,1,0:T(8,128)(2,1)}, u32[]{:S(2)}) copy-start(bf16[1,128,1024]{2,1,0:T(8,128)(2,1)} %param.6) | copy-start | bytes 786436
  9.6 0.7 copy-start.5
  10.3 0.7 copy-start.6
  11.0 14.1 %copy-start.1 = (bf16[1,128,4096]{2,1,0:T(8,128)(2,1)S(1)}, bf16[1,128,4096]{2,1,0:T(8,128)(2,1)}, u32[]{:S(2)}) copy-start(bf16[1,128,4096]{2,1,0:T(8,128)(2,1)} %param.5) | copy-start | bytes 3145732
  14.3 5.5 %collective-permute-start.9 = (bf16[320,128]{1,0:T(8,128)(2,1)S(1)}, bf16[320,128]{1,0:T(8,128)(2,1)S(1)}, u32[]{:S(2)}, u32[]{:S(2)}) collective-permute-start(bf16[320,128]{1,0:T(8,128)(2,1)S(1)} %shard_map.70.refs_4_.refs_3_.refs_5_), channel_id=1, source_target_pairs={{0,24},{8,16},{16,8},{24,0},{1,25},{9,17},{17,9},{25,1},{2,26},{10... | collective-permute-start | bytes 245768 | tf_op jit(solution)/shard_map/ppermute | solution.py:409
  16.9 6.0 %collective-permute-start.7 = (bf16[320,128]{1,0:T(8,128)(2,1)S(1)}, bf16[320,128]{1,0:T(8,128)(2,1)S(1)}, u32[]{:S(2)}, u32[]{:S(2)}) collective-permute-start(bf16[320,128]{1,0:T(8,128)(2,1)S(1)} %shard_map.70.refs_4_.refs_3_.refs_5_), channel_id=1, source_target_pairs={{0,16},{8,24},{16,0},{24,8},{1,17},{9,25},{17,1},{25,9},{2,18},{10... | collective-permute-start | bytes 245768 | tf_op jit(solution)/shard_map/ppermute | solution.py:409
  17.4 6.1 %collective-permute-start.5 = (bf16[320,128]{1,0:T(8,128)(2,1)S(1)}, bf16[320,128]{1,0:T(8,128)(2,1)S(1)}, u32[]{:S(2)}, u32[]{:S(2)}) collective-permute-start(bf16[320,128]{1,0:T(8,128)(2,1)S(1)} %shard_map.70.refs_4_.refs_3_.refs_5_), channel_id=1, source_target_pairs={{0,8},{8,0},{16,24},{24,16},{1,9},{9,1},{17,25},{25,17},{2,10},{10... | collective-permute-start | bytes 245768 | tf_op jit(solution)/shard_map/ppermute | solution.py:409
  17.9 5.7 %collective-permute-start.4 = (bf16[320,128]{1,0:T(8,128)(2,1)S(1)}, bf16[320,128]{1,0:T(8,128)(2,1)S(1)}, u32[]{:S(2)}, u32[]{:S(2)}) collective-permute-start(bf16[320,128]{1,0:T(8,128)(2,1)S(1)} %shard_map.70.refs_4_.refs_3_.refs_5_), channel_id=1, source_target_pairs={{0,1},{1,0},{2,3},{3,2},{4,5},{5,4},{6,7},{7,6},{8,9},{9,8},{10,11... | collective-permute-start | bytes 245768 | tf_op jit(solution)/shard_map/ppermute | solution.py:400
  19.8 3.8 %collective-permute-start.10 = (bf16[320,128]{1,0:T(8,128)(2,1)S(1)}, bf16[320,128]{1,0:T(8,128)(2,1)S(1)}, u32[]{:S(2)}, u32[]{:S(2)}) collective-permute-start(bf16[320,128]{1,0:T(8,128)(2,1)S(1)} %collective-permute-done.9.refs_10_.refs_11_), channel_id=1, source_target_pairs={{0,1},{1,0},{2,3},{3,2},{4,5},{5,4},{6,7},{7,6},{8,9},{9,8},{10,11... | collective-permute-start | bytes 245768 | tf_op jit(solution)/shard_map/ppermute | solution.py:400
  19.9 8.7 %collective-permute-start.13 = (bf16[640,128]{1,0:T(8,128)(2,1)S(1)}, bf16[640,128]{1,0:T(8,128)(2,1)S(1)}, u32[]{:S(2)}, u32[]{:S(2)}) collective-permute-start(bf16[640,128]{1,0:T(8,128)(2,1)S(1)} %shard_map.72.refs_0_), channel_id=1, source_target_pairs={{0,24},{8,16},{16,8},{24,0},{1,25},{9,17},{17,9},{25,1},{2,26},{10... | collective-permute-start | bytes 491528 | tf_op jit(solution)/shard_map/ppermute | solution.py:409
  22.8 8.4 %collective-permute-start.12 = (bf16[640,128]{1,0:T(8,128)(2,1)S(1)}, bf16[640,128]{1,0:T(8,128)(2,1)S(1)}, u32[]{:S(2)}, u32[]{:S(2)}) collective-permute-start(bf16[640,128]{1,0:T(8,128)(2,1)S(1)} %shard_map.72.refs_0_), channel_id=1, source_target_pairs={{0,16},{8,24},{16,0},{24,8},{1,17},{9,25},{17,1},{25,9},{2,18},{10... | collective-permute-start | bytes 491528 | tf_op jit(solution)/shard_map/ppermute | solution.py:409
  23.4 8.2 %collective-permute-start.11 = (bf16[640,128]{1,0:T(8,128)(2,1)S(1)}, bf16[640,128]{1,0:T(8,128)(2,1)S(1)}, u32[]{:S(2)}, u32[]{:S(2)}) collective-permute-start(bf16[640,128]{1,0:T(8,128)(2,1)S(1)} %shard_map.72.refs_0_), channel_id=1, source_target_pairs={{0,8},{8,0},{16,24},{24,16},{1,9},{9,1},{17,25},{25,17},{2,10},{10... | collective-permute-start | bytes 491528 | tf_op jit(solution)/shard_map/ppermute | solution.py:409
  23.6 1.3 %collective-permute-start.8 = (bf16[320,128]{1,0:T(8,128)(2,1)S(1)}, bf16[320,128]{1,0:T(8,128)(2,1)S(1)}, u32[]{:S(2)}, u32[]{:S(2)}) collective-permute-start(bf16[320,128]{1,0:T(8,128)(2,1)S(1)} %collective-permute-done.7.refs_8_.refs_9_), channel_id=1, source_target_pairs={{0,1},{1,0},{2,3},{3,2},{4,5},{5,4},{6,7},{7,6},{8,9},{9,8},{10,11... | collective-permute-start | bytes 245768 | tf_op jit(solution)/shard_map/ppermute | solution.py:400
  23.6 1.4 %collective-permute-start.6 = (bf16[320,128]{1,0:T(8,128)(2,1)S(1)}, bf16[320,128]{1,0:T(8,128)(2,1)S(1)}, u32[]{:S(2)}, u32[]{:S(2)}) collective-permute-start(bf16[320,128]{1,0:T(8,128)(2,1)S(1)} %collective-permute-done.5.refs_6_.refs_7_), channel_id=1, source_target_pairs={{0,1},{1,0},{2,3},{3,2},{4,5},{5,4},{6,7},{7,6},{8,9},{9,8},{10,11... | collective-permute-start | bytes 245768 | tf_op jit(solution)/shard_map/ppermute | solution.py:400
  26.0 6.8 %collective-permute-start.16 = (bf16[128,256]{1,0:T(8,128)(2,1)S(1)}, bf16[128,256]{1,0:T(8,128)(2,1)S(1)}, u32[]{:S(2)}, u32[]{:S(2)}) collective-permute-start(bf16[128,256]{1,0:T(8,128)(2,1)S(1)} %get-tuple-element.38.refs_15_.refs_4_), channel_id=1, source_target_pairs={{0,6},{1,7},{2,4},{3,5},{4,2},{5,3},{6,0},{7,1},{8,14},{9,15},{10,... | collective-permute-start | bytes 196616 | tf_op jit(solution)/shard_map/ppermute | solution.py:406
  28.6 6.5 %collective-permute-start.15 = (bf16[128,256]{1,0:T(8,128)(2,1)S(1)}, bf16[128,256]{1,0:T(8,128)(2,1)S(1)}, u32[]{:S(2)}, u32[]{:S(2)}) collective-permute-start(bf16[128,256]{1,0:T(8,128)(2,1)S(1)} %get-tuple-element.38.refs_15_.refs_4_), channel_id=1, source_target_pairs={{0,4},{1,5},{2,6},{3,7},{4,0},{5,1},{6,2},{7,3},{8,12},{9,13},{10,... | collective-permute-start | bytes 196616 | tf_op jit(solution)/shard_map/ppermute | solution.py:406
  28.6 6.5 %collective-permute-start.14 = (bf16[128,256]{1,0:T(8,128)(2,1)S(1)}, bf16[128,256]{1,0:T(8,128)(2,1)S(1)}, u32[]{:S(2)}, u32[]{:S(2)}) collective-permute-start(bf16[128,256]{1,0:T(8,128)(2,1)S(1)} %get-tuple-element.38.refs_15_.refs_4_), channel_id=1, source_target_pairs={{0,2},{1,3},{2,0},{3,1},{4,6},{5,7},{6,4},{7,5},{8,10},{9,11},{10,... | collective-permute-start | bytes 196616 | tf_op jit(solution)/shard_map/ppermute | solution.py:406
  35.1 2.5 %collective-permute-start.17 = (bf16[2560,128]{1,0:T(8,128)(2,1)S(1)}, bf16[2560,128]{1,0:T(8,128)(2,1)S(1)}, u32[]{:S(2)}, u32[]{:S(2)}) collective-permute-start(bf16[2560,128]{1,0:T(8,128)(2,1)S(1)} %shard_map.73.refs_13_), channel_id=1, source_target_pairs={{0,1},{1,0},{2,3},{3,2},{4,5},{5,4},{6,7},{7,6},{8,9},{9,8},{10,11... | collective-permute-start | bytes 1966088 | tf_op jit(solution)/shard_map/ppermute | solution.py:400
  35.2 2.2 %collective-permute-start.18 = (bf16[128,256]{1,0:T(8,128)(2,1)S(1)}, bf16[128,256]{1,0:T(8,128)(2,1)S(1)}, u32[]{:S(2)}, u32[]{:S(2)}) collective-permute-start(bf16[128,256]{1,0:T(8,128)(2,1)S(1)} %get-tuple-element.38.refs_15_.refs_4_), channel_id=1, source_target_pairs={{0,1},{1,0},{2,3},{3,2},{4,5},{5,4},{6,7},{7,6},{8,9},{9,8},{10,11... | collective-permute-start | bytes 196616 | tf_op jit(solution)/shard_map/ppermute | solution.py:400
  35.7 1.8 %collective-permute-start.21 = (bf16[128,256]{1,0:T(8,128)(2,1)S(1)}, bf16[128,256]{1,0:T(8,128)(2,1)S(1)}, u32[]{:S(2)}, u32[]{:S(2)}) collective-permute-start(bf16[128,256]{1,0:T(8,128)(2,1)S(1)} %collective-permute-done.16.refs_6_.refs_21_.refs_10_), channel_id=1, source_target_pairs={{0,1},{1,0},{2,3},{3,2},{4,5},{5,4},{6,7},{7,6},{8,9},{9,8},{10,11... | collective-permute-start | bytes 196616 | tf_op jit(solution)/shard_map/ppermute | solution.py:400
  35.8 1.8 %collective-permute-start.20 = (bf16[128,256]{1,0:T(8,128)(2,1)S(1)}, bf16[128,256]{1,0:T(8,128)(2,1)S(1)}, u32[]{:S(2)}, u32[]{:S(2)}) collective-permute-start(bf16[128,256]{1,0:T(8,128)(2,1)S(1)} %collective-permute-done.15.refs_5_.refs_19_.refs_8_), channel_id=1, source_target_pairs={{0,1},{1,0},{2,3},{3,2},{4,5},{5,4},{6,7},{7,6},{8,9},{9,8},{10,11... | collective-permute-start | bytes 196616 | tf_op jit(solution)/shard_map/ppermute | solution.py:400
  36.2 1.5 %collective-permute-start.19 = (bf16[128,256]{1,0:T(8,128)(2,1)S(1)}, bf16[128,256]{1,0:T(8,128)(2,1)S(1)}, u32[]{:S(2)}, u32[]{:S(2)}) collective-permute-start(bf16[128,256]{1,0:T(8,128)(2,1)S(1)} %collective-permute-done.14.refs_4_.refs_17_.refs_6_), channel_id=1, source_target_pairs={{0,1},{1,0},{2,3},{3,2},{4,5},{5,4},{6,7},{7,6},{8,9},{9,8},{10,11... | collective-permute-start | bytes 196616 | tf_op jit(solution)/shard_map/ppermute | solution.py:400
  39.4 9.2 %collective-permute-start.24 = (bf16[4096,128]{1,0:T(8,128)(2,1)S(1)}, bf16[4096,128]{1,0:T(8,128)(2,1)S(1)}, u32[]{:S(2)}, u32[]{:S(2)}) collective-permute-start(bf16[4096,128]{1,0:T(8,128)(2,1)S(1)} %shard_map.76), channel_id=1, source_target_pairs={{0,1},{1,0},{2,3},{3,2},{4,5},{5,4},{6,7},{7,6},{8,9},{9,8},{10,11... | collective-permute-start | bytes 3145736 | tf_op jit(solution)/shard_map/ppermute | solution.py:400
  43.2 1.3 %collective-permute-start.27 = (bf16[128,256]{1,0:T(8,128)(2,1)S(1)}, bf16[128,256]{1,0:T(8,128)(2,1)S(1)}, u32[]{:S(2)}, u32[]{:S(2)}) collective-permute-start(bf16[128,256]{1,0:T(8,128)(2,1)S(1)} %get-tuple-element.51), channel_id=1, source_target_pairs={{0,1},{1,0},{2,3},{3,2},{4,5},{5,4},{6,7},{7,6},{8,9},{9,8},{10,11... | collective-permute-start | bytes 196616 | tf_op jit(solution)/shard_map/ppermute | solution.py:400
  43.6 8.7 %collective-permute-start.22 = (bf16[128,256]{1,0:T(8,128)(2,1)S(1)}, bf16[128,256]{1,0:T(8,128)(2,1)S(1)}, u32[]{:S(2)}, u32[]{:S(2)}) collective-permute-start(bf16[128,256]{1,0:T(8,128)(2,1)S(1)} %get-tuple-element.45), channel_id=1, source_target_pairs={{0,1},{1,0},{2,3},{3,2},{4,5},{5,4},{6,7},{7,6},{8,9},{9,8},{10,11... | collective-permute-start | bytes 196616 | tf_op jit(solution)/shard_map/ppermute | solution.py:400
  43.8 2.4 %collective-permute-start.23 = (bf16[128,256]{1,0:T(8,128)(2,1)S(1)}, bf16[128,256]{1,0:T(8,128)(2,1)S(1)}, u32[]{:S(2)}, u32[]{:S(2)}) collective-permute-start(bf16[128,256]{1,0:T(8,128)(2,1)S(1)} %get-tuple-element.47), channel_id=1, source_target_pairs={{0,1},{1,0},{2,3},{3,2},{4,5},{5,4},{6,7},{7,6},{8,9},{9,8},{10,11... | collective-permute-start | bytes 196616 | tf_op jit(solution)/shard_map/ppermute | solution.py:400
  44.1 1.3 %collective-permute-start.29 = (bf16[128,256]{1,0:T(8,128)(2,1)S(1)}, bf16[128,256]{1,0:T(8,128)(2,1)S(1)}, u32[]{:S(2)}, u32[]{:S(2)}) collective-permute-start(bf16[128,256]{1,0:T(8,128)(2,1)S(1)} %get-tuple-element.53), channel_id=1, source_target_pairs={{0,1},{1,0},{2,3},{3,2},{4,5},{5,4},{6,7},{7,6},{8,9},{9,8},{10,11... | collective-permute-start | bytes 196616 | tf_op jit(solution)/shard_map/ppermute | solution.py:400
  44.5 4.1 %collective-permute-start.25 = (bf16[8,128,128]{2,1,0:T(8,128)(2,1)S(1)}, bf16[8,128,128]{2,1,0:T(8,128)(2,1)S(1)}, u32[]{:S(2)}, u32[]{:S(2)}) collective-permute-start(bf16[8,128,128]{2,1,0:T(8,128)(2,1)S(1)} %get-tuple-element.42.refs_3_.refs_1_), channel_id=1, source_target_pairs={{0,1},{1,0},{2,3},{3,2},{4,5},{5,4},{6,7},{7,6},{8,9},{9,8},{10,11... | collective-permute-start | bytes 786440 | tf_op jit(solution)/shard_map/ppermute | solution.py:400
  45.4 8.4 %collective-permute-start.28 = (bf16[128,256]{1,0:T(8,128)(2,1)S(1)}, bf16[128,256]{1,0:T(8,128)(2,1)S(1)}, u32[]{:S(2)}, u32[]{:S(2)}) collective-permute-start(bf16[128,256]{1,0:T(8,128)(2,1)S(1)} %add_convert_fusion.2), channel_id=1, source_target_pairs={{0,4},{1,5},{2,6},{3,7},{4,0},{5,1},{6,2},{7,3},{8,12},{9,13},{10,... | collective-permute-start | bytes 196616 | tf_op jit(solution)/shard_map/ppermute | solution.py:406
  46.2 10.1 %collective-permute-start.30 = (bf16[128,256]{1,0:T(8,128)(2,1)S(1)}, bf16[128,256]{1,0:T(8,128)(2,1)S(1)}, u32[]{:S(2)}, u32[]{:S(2)}) collective-permute-start(bf16[128,256]{1,0:T(8,128)(2,1)S(1)} %add_convert_fusion.1), channel_id=1, source_target_pairs={{0,6},{1,7},{2,4},{3,5},{4,2},{5,3},{6,0},{7,1},{8,14},{9,15},{10,... | collective-permute-start | bytes 196616 | tf_op jit(solution)/shard_map/ppermute | solution.py:406
  50.0 6.3 %collective-permute-start.26 = (bf16[128,256]{1,0:T(8,128)(2,1)S(1)}, bf16[128,256]{1,0:T(8,128)(2,1)S(1)}, u32[]{:S(2)}, u32[]{:S(2)}) collective-permute-start(bf16[128,256]{1,0:T(8,128)(2,1)S(1)} %shard_map.78), channel_id=1, source_target_pairs={{0,2},{1,3},{2,0},{3,1},{4,6},{5,7},{6,4},{7,5},{8,10},{9,11},{10,... | collective-permute-start | bytes 196616 | tf_op jit(solution)/shard_map/ppermute | solution.py:406
  50.5 10.0 %collective-permute-start.31 = (bf16[960,128]{1,0:T(8,128)(2,1)S(1)}, bf16[960,128]{1,0:T(8,128)(2,1)S(1)}, u32[]{:S(2)}, u32[]{:S(2)}) collective-permute-start(bf16[960,128]{1,0:T(8,128)(2,1)S(1)} %get-tuple-element.56), channel_id=1, source_target_pairs={{0,8},{8,0},{16,24},{24,16},{1,9},{9,1},{17,25},{25,17},{2,10},{10... | collective-permute-start | bytes 737288 | tf_op jit(solution)/shard_map/ppermute | solution.py:409
  52.4 15.7 %collective-permute-start.32 = (bf16[960,128]{1,0:T(8,128)(2,1)S(1)}, bf16[960,128]{1,0:T(8,128)(2,1)S(1)}, u32[]{:S(2)}, u32[]{:S(2)}) collective-permute-start(bf16[960,128]{1,0:T(8,128)(2,1)S(1)} %get-tuple-element.57), channel_id=1, source_target_pairs={{0,16},{8,24},{16,0},{24,8},{1,17},{9,25},{17,1},{25,9},{2,18},{10... | collective-permute-start | bytes 737288 | tf_op jit(solution)/shard_map/ppermute | solution.py:409
  53.8 14.2 %collective-permute-start.33 = (bf16[960,128]{1,0:T(8,128)(2,1)S(1)}, bf16[960,128]{1,0:T(8,128)(2,1)S(1)}, u32[]{:S(2)}, u32[]{:S(2)}) collective-permute-start(bf16[960,128]{1,0:T(8,128)(2,1)S(1)} %get-tuple-element.58), channel_id=1, source_target_pairs={{0,24},{8,16},{16,8},{24,0},{1,25},{9,17},{17,9},{25,1},{2,26},{10... | collective-permute-start | bytes 737288 | tf_op jit(solution)/shard_map/ppermute | solution.py:409
  56.4 1.3 %collective-permute-start.34 = (bf16[2,128,128]{2,1,0:T(8,128)(2,1)S(1)}, bf16[2,128,128]{2,1,0:T(8,128)(2,1)S(1)}, u32[]{:S(2)}, u32[]{:S(2)}) collective-permute-start(bf16[2,128,128]{2,1,0:T(8,128)(2,1)S(1)} %shard_map.79.refs_2_.refs_5_), channel_id=1, source_target_pairs={{0,1},{1,0},{2,3},{3,2},{4,5},{5,4},{6,7},{7,6},{8,9},{9,8},{10,11... | collective-permute-start | bytes 196616 | tf_op jit(solution)/shard_map/ppermute | solution.py:400
  58.7 6.9 %collective-permute-start.35 = (bf16[320,128]{1,0:T(8,128)(2,1)S(1)}, bf16[320,128]{1,0:T(8,128)(2,1)S(1)}, u32[]{:S(2)}, u32[]{:S(2)}) collective-permute-start(bf16[320,128]{1,0:T(8,128)(2,1)S(1)} %get-tuple-element.60), channel_id=1, source_target_pairs={{0,8},{8,0},{16,24},{24,16},{1,9},{9,1},{17,25},{25,17},{2,10},{10... | collective-permute-start | bytes 245768 | tf_op jit(solution)/shard_map/ppermute | solution.py:409
  59.4 8.6 %collective-permute-start.36 = (bf16[320,128]{1,0:T(8,128)(2,1)S(1)}, bf16[320,128]{1,0:T(8,128)(2,1)S(1)}, u32[]{:S(2)}, u32[]{:S(2)}) collective-permute-start(bf16[320,128]{1,0:T(8,128)(2,1)S(1)} %get-tuple-element.61), channel_id=1, source_target_pairs={{0,16},{8,24},{16,0},{24,8},{1,17},{9,25},{17,1},{25,9},{2,18},{10... | collective-permute-start | bytes 245768 | tf_op jit(solution)/shard_map/ppermute | solution.py:409
  60.5 7.6 %collective-permute-start.37 = (bf16[320,128]{1,0:T(8,128)(2,1)S(1)}, bf16[320,128]{1,0:T(8,128)(2,1)S(1)}, u32[]{:S(2)}, u32[]{:S(2)}) collective-permute-start(bf16[320,128]{1,0:T(8,128)(2,1)S(1)} %shard_map.82), channel_id=1, source_target_pairs={{0,24},{8,16},{16,8},{24,0},{1,25},{9,17},{17,9},{25,1},{2,26},{10... | collective-permute-start | bytes 245768 | tf_op jit(solution)/shard_map/ppermute | solution.py:409
  68.3 5.4 %collective-permute-start.38 = (bf16[320,128]{1,0:T(8,128)(2,1)S(1)}, bf16[320,128]{1,0:T(8,128)(2,1)S(1)}, u32[]{:S(2)}, u32[]{:S(2)}) collective-permute-start(bf16[320,128]{1,0:T(8,128)(2,1)S(1)} %get-tuple-element.65), channel_id=1, source_target_pairs={{0,2},{1,3},{2,0},{3,1},{4,6},{5,7},{6,4},{7,5},{8,10},{9,11},{10,... | collective-permute-start | bytes 245768 | tf_op jit(solution)/shard_map/ppermute | solution.py:406
  70.0 8.7 %collective-permute-start.39 = (bf16[320,128]{1,0:T(8,128)(2,1)S(1)}, bf16[320,128]{1,0:T(8,128)(2,1)S(1)}, u32[]{:S(2)}, u32[]{:S(2)}) collective-permute-start(bf16[320,128]{1,0:T(8,128)(2,1)S(1)} %get-tuple-element.66), channel_id=1, source_target_pairs={{0,4},{1,5},{2,6},{3,7},{4,0},{5,1},{6,2},{7,3},{8,12},{9,13},{10,... | collective-permute-start | bytes 245768 | tf_op jit(solution)/shard_map/ppermute | solution.py:406
  71.4 7.2 %collective-permute-start.40 = (bf16[320,128]{1,0:T(8,128)(2,1)S(1)}, bf16[320,128]{1,0:T(8,128)(2,1)S(1)}, u32[]{:S(2)}, u32[]{:S(2)}) collective-permute-start(bf16[320,128]{1,0:T(8,128)(2,1)S(1)} %get-tuple-element.67), channel_id=1, source_target_pairs={{0,6},{1,7},{2,4},{3,5},{4,2},{5,3},{6,0},{7,1},{8,14},{9,15},{10,... | collective-permute-start | bytes 245768 | tf_op jit(solution)/shard_map/ppermute | solution.py:406
  78.7 5.4 %collective-permute-start.43 = (bf16[320,128]{1,0:T(8,128)(2,1)S(1)}, bf16[320,128]{1,0:T(8,128)(2,1)S(1)}, u32[]{:S(2)}, u32[]{:S(2)}) collective-permute-start(bf16[320,128]{1,0:T(8,128)(2,1)S(1)} %add_convert_fusion.refs_0_), channel_id=1, source_target_pairs={{0,24},{8,16},{16,8},{24,0},{1,25},{9,17},{17,9},{25,1},{2,26},{10... | collective-permute-start | bytes 245768 | tf_op jit(solution)/shard_map/ppermute | solution.py:409
  80.7 4.4 %collective-permute-start.42 = (bf16[320,128]{1,0:T(8,128)(2,1)S(1)}, bf16[320,128]{1,0:T(8,128)(2,1)S(1)}, u32[]{:S(2)}, u32[]{:S(2)}) collective-permute-start(bf16[320,128]{1,0:T(8,128)(2,1)S(1)} %add_convert_fusion.refs_0_), channel_id=1, source_target_pairs={{0,16},{8,24},{16,0},{24,8},{1,17},{9,25},{17,1},{25,9},{2,18},{10... | collective-permute-start | bytes 245768 | tf_op jit(solution)/shard_map/ppermute | solution.py:409
  80.7 4.4 %collective-permute-start.41 = (bf16[320,128]{1,0:T(8,128)(2,1)S(1)}, bf16[320,128]{1,0:T(8,128)(2,1)S(1)}, u32[]{:S(2)}, u32[]{:S(2)}) collective-permute-start(bf16[320,128]{1,0:T(8,128)(2,1)S(1)} %add_convert_fusion.refs_0_), channel_id=1, source_target_pairs={{0,8},{8,0},{16,24},{24,16},{1,9},{9,1},{17,25},{25,17},{2,10},{10... | collective-permute-start | bytes 245768 | tf_op jit(solution)/shard_map/ppermute | solution.py:409
